TPU v7x, 32 devices: a whole 2x2x4 slice. The times are simulated.
32 devices in a mesh: pair: 8 (over z, x), virt: 4 (over y, core).
Axes of the slice: x: 2, y: 2, z: 4, core: 2. Of those that a mesh axis runs over, the one named last changes fastest.
Arguments:
- amplitudes: bfloat16 [8192, 8, 1024], P('pair', 'virt'), may hold values from -6 to 6
- tile_mask: int32 [8192, 8], P('pair', 'virt'), may hold values from 0 to 1
- integrals: bfloat16 [8, 1024, 1024], P('virt', 'pair'), may hold values from -0.0625 to 0.0625
- pair_energy: float32 [8192], P(('pair', 'virt')), may hold values from -2 to -0.5
- virt_energy: float32 [1024], replicated, may hold values from 0.5 to 3
Outputs:
- update: bfloat16 [8192, 1024], P(('pair', 'virt'))
All inputs are finite; a program needn't handle non-finite values.
Results may differ from a plain program's by a relative error of at most 0.011.
Values may be sent and summed in bfloat16 or wider, within the bound.
No kernel may reach another device: no remote copies, remote signals or barrier semaphores. Data moves between devices by JAX's collectives and lax.ppermute only.
A program may use at most 64 MiB of HBM per device.

v0:
```python
import jax
import jax.numpy as jnp
from jax import lax
from jax.sharding import PartitionSpec as P


def on_device(amplitudes, tile_mask, integrals, pair_energy, virt_energy):
    masked = amplitudes * tile_mask.astype(jnp.bfloat16)[:, :, None]
    partial_value = jnp.einsum(
        "ptk,tkn->pn",
        masked,
        lax.all_gather(integrals, "pair", axis=1, tiled=True),
        preferred_element_type=jnp.float32,
    )
    ladder = lax.psum_scatter(
        partial_value.astype(jnp.bfloat16), "virt", scatter_dimension=0, tiled=True
    ).astype(jnp.float32)
    denom = virt_energy[None, :] - pair_energy[:, None]
    return (ladder / denom).astype(jnp.bfloat16)


def solution(mesh):
    placed = (
        P("pair", "virt", None),
        P("pair", "virt"),
        P("virt", "pair", None),
        P(("pair", "virt")),
        P(),
    )
    return jax.shard_map(
        on_device, mesh=mesh, in_specs=placed, out_specs=P(("pair", "virt"), None), check_vma=False
    )
```

profile of v0, /device:TPU:0, one launch (start us, length us, event | category | flops | bytes accessed | tf_op | source)
XLA Modules:
  0.0 133.8 jit_solution(1826553211772932355)
XLA Ops:
  6.5 0.0 all-gather.2.cloned.1.call-start
  6.5 0.7 all-gather.2.cloned.1.call-update
  7.3 0.0 reduce-scatter.2.cloned.1.call-start
  7.3 0.7 convert_element_type.12
  8.0 0.2 copy.6
  8.2 8.0 %broadcast_multiply_fusion = bf16[1024,2,1024]{2,1,0:T(2,128)(2,1)} fusion(bf16[1024,2,1024]{2,1,0:T(2,128)(2,1)} %param.5, bf16[1024,2]{1,0:T(8,128)(2,1)S(1)} %copy.6), kind=kLoop, calls=%fused_computation.3 | loop fusion | flops 2097152 | bytes 8392704 | tf_op jit(solution)/shard_map/mul | solution.py:8
  16.2 0.0 copy-start
  16.2 0.0 copy-start.1
  16.2 69.4 %all-gather.2.cloned.1.call-done = bf16[2,1024,1024]{2,1,0:T(8,128)(2,1)} async-done(((bf16[2,128,1024]{2,1,0:T(8,128)(2,1)}), bf16[2,1024,1024]{2,1,0:T(8,128)(2,1)}) %all-gather.2.cloned.1.call-update) | async-done | bytes 4194320 | tf_op jit(solution)/shard_map/all_gather | solution.py:12
  85.6 9.3 %bitcast_convert_fusion = bf16[1024,1024]{1,0:T(8,128)(2,1)} fusion(bf16[2,1024,1024]{2,1,0:T(8,128)(2,1)} %all-gather.2.cloned.1.call-done, bf16[1024,2,1024]{2,1,0:T(2,128)(2,1)} %broadcast_multiply_fusion), kind=kOutput, calls=%fused_computation | convolution fusion | flops 4296015872 | bytes 10485760 | tf_op jit(solution)/shard_map/ptk,tkn->pn/dot_general | solution.py:9
  95.0 0.0 reduce-scatter.2.cloned.1.call-update
  95.0 29.9 %reduce-scatter.2.cloned.1.call-done = bf16[256,1024]{1,0:T(8,128)(2,1)} async-done(((bf16[1024,1024]{1,0:T(8,128)(2,1)}), bf16[256,1024]{1,0:T(8,128)(2,1)}) %reduce-scatter.2.cloned.1.call-update) | async-done | bytes 524304 | tf_op jit(solution)/shard_map/reduce_scatter | solution.py:15
  124.9 0.0 copy-done
  124.9 0.0 copy-done.1
  124.9 2.1 %divide_convert_fusion = bf16[256,1024]{1,0:T(8,128)(2,1)} fusion(bf16[256,1024]{1,0:T(8,128)(2,1)} %reduce-scatter.2.cloned.1.call-done, f32[256]{0:T(256)S(1)} %copy-done.1, f32[1024]{0:T(1024)S(1)} %copy-done), kind=kLoop, calls=%fused_computation.4 | loop fusion | flops 1048576 | bytes 1053696 | tf_op jit(solution)/shard_map/convert_element_type | solution.py:19
Async XLA Ops:
  6.5 79.1 %all-gather.2.cloned.1.call-start = ((), (), s32[]{:S(2)}) async-start(), calls=%async_computation.1 | async-start | bytes 4718592 | tf_op jit(solution)/shard_map/all_gather | solution.py:12
  7.3 117.6 %reduce-scatter.2.cloned.1.call-start = ((), (), s32[]{:S(2)}) async-start(), calls=%async_computation.2 | async-start | bytes 2621440 | tf_op jit(solution)/shard_map/reduce_scatter | solution.py:15
  16.2 108.6 %copy-start = (f32[1024]{0:T(1024)S(1)}, f32[1024]{0:T(1024)}, u32[]{:S(2)}) copy-start(f32[1024]{0:T(1024)} %param.9) | copy-start | bytes 12292
  16.2 108.6 %copy-start.1 = (f32[256]{0:T(256)S(1)}, f32[256]{0:T(256)}, u32[]{:S(2)}) copy-start(f32[256]{0:T(256)} %param.8) | copy-start | bytes 3076
Sparse Core Ops, SparseCore 0:
  9.5 76.0 all-gather.1
  95.1 29.7 reduce-scatter.1
where the time goes:
time: 134 us
  waiting for transfers between devices  100 us (75%)
  between operations  13.4 us (10%)
  other arithmetic  10.8 us (8%)
  matrix products  9.32 us (7%)
    all_gather x1, waiting for transfers between devices, on_device(): lax.all_gather(integrals, 'pair', axis=1, tiled=True)  69.4 us
    reduce_scatter x1, waiting for transfers between devices, on_device(): lax.psum_scatter(partial_value.astype(jnp.bfloat16), 'virt', scatter_dime...  29.9 us
    dot_general x1, matrix products, on_device(): jnp.einsum('ptk,tkn->pn', masked, lax.all_gather(integrals, 'pair', axis=...  9.32 us
    mul x1, other arithmetic, on_device(): masked = amplitudes * tile_mask.astype(jnp.bfloat16)[:, :, None]  8.03 us
  transfers between devices with their start and end apart: 2, of which 2 were waited for; matrix products, arithmetic and copies ran while one was open for 7% of the time, Pallas kernels for 0%

commit v1 on v0

v1 whole, which is shorter than its diff:
```python
import functools

import jax
import jax.numpy as jnp
from jax import lax
from jax.experimental import pallas as pl
from jax.experimental.pallas import tpu as pltpu
from jax.sharding import PartitionSpec as P

BF16 = jnp.bfloat16
F32 = jnp.float32


def plain(amplitudes, tile_mask, integrals, pair_energy, virt_energy):
    masked = amplitudes * tile_mask.astype(BF16)[:, :, None]
    partial_value = jnp.einsum(
        "ptk,tkn->pn",
        masked,
        lax.all_gather(integrals, "pair", axis=1, tiled=True),
        preferred_element_type=F32,
    )
    ladder = lax.psum_scatter(partial_value.astype(BF16), "virt", scatter_dimension=0, tiled=True).astype(F32)
    denom = virt_energy[None, :] - pair_energy[:, None]
    return (ladder / denom).astype(BF16)


def line(z_pairs, flip=False):
    return [(a * 2 + x, b * 2 + (1 - x if flip else x)) for a, b in z_pairs for x in range(2)]


Z1 = line([(0, 1), (1, 0), (2, 3), (3, 2)])
Z2 = line([(0, 2), (2, 0), (1, 3), (3, 1)])
ZMID = line([(1, 2), (2, 1)])
ZEND = line([(1, 0), (2, 3)])
XALL = line([(z, z) for z in range(4)], True)
XMID = line([(1, 1), (2, 2)], True)
XEND = line([(0, 0), (3, 3)], True)
CORE = [(0, 1), (1, 0), (2, 3), (3, 2)]
YHOP = [(0, 2), (2, 0), (1, 3), (3, 1)]


def over_pair(value, hops):
    return lax.ppermute(value, "pair", hops)


def over_virt(value, hops):
    return lax.ppermute(value, "virt", hops)


def after(value, *others):
    return lax.optimization_barrier((value,) + others)[0]


def products(places, rows, a, blocks, ends, total=None, finish=False):
    depth, columns = blocks[0].shape if blocks else ends[0][0].shape
    n_blocks = len(blocks) + len(ends)
    row = a.shape[1] // 4
    refs_in = list(blocks) + [e for pair in ends for e in pair]

    def body(places_ref, rows_ref, a_ref, *refs):
        ins = refs[: len(refs_in)]
        rest = refs[len(refs_in):]
        if total is not None:
            acc = rest[0][0]
            rest = rest[1:]
        else:
            acc = jnp.zeros((row, columns), F32)
        for k in range(n_blocks):
            if k < len(blocks):
                block = ins[k][...]
            else:
                e = len(blocks) + 2 * (k - len(blocks))
                block = ins[e][...] + ins[e + 1][...]
            acc += jnp.dot(a_ref[places_ref[k]], block, preferred_element_type=F32)
        if not finish:
            rest[0][0] = acc
            return
        step = pl.program_id(0)

        @pl.when(step < 2)
        def _():
            rest[0][0] = acc.astype(BF16)

        @pl.when(step >= 2)
        def _():
            rest[1][0] = acc

    in_specs = [pl.BlockSpec((a.shape[0], row, depth), lambda i, p, r: (0, r[i], 0))]
    in_specs += [pl.BlockSpec((depth, columns), lambda i, p, r: (0, 0))] * len(refs_in)
    operands = [a] + refs_in
    if total is not None:
        in_specs.append(pl.BlockSpec((1, row, columns), lambda i, p, r: (i, 0, 0)))
        operands.append(total)
    if finish:
        out_specs = [
            pl.BlockSpec((1, row, columns), lambda i, p, r: (jnp.minimum(i, 1), 0, 0)),
            pl.BlockSpec((1, row, columns), lambda i, p, r: (jnp.maximum(i - 2, 0), 0, 0)),
        ]
        out_shape = [
            jax.ShapeDtypeStruct((2, row, columns), BF16),
            jax.ShapeDtypeStruct((2, row, columns), F32),
        ]
    else:
        out_specs = pl.BlockSpec((1, row, columns), lambda i, p, r: (i, 0, 0))
        out_shape = jax.ShapeDtypeStruct((4, row, columns), F32)
    return pl.pallas_call(
        body,
        grid_spec=pltpu.PrefetchScalarGridSpec(
            num_scalar_prefetch=2, grid=(4,), in_specs=in_specs, out_specs=out_specs
        ),
        out_shape=out_shape,
        compiler_params=pltpu.CompilerParams(vmem_limit_bytes=48 * 2**20),
        cost_estimate=pl.CostEstimate(
            flops=2 * a.shape[1] * depth * n_blocks * columns,
            bytes_accessed=2 * a.size + 2 * n_blocks * depth * columns,
            transcendentals=0,
        ),
    )(places, rows, *operands)


def scheduled(cut, amplitudes, tile_mask, integrals, pair_energy, virt_energy):
    pairs, tiles, wide = amplitudes.shape
    depth, columns = integrals.shape[1:]
    pair, virt = lax.axis_index("pair"), lax.axis_index("virt")
    z, x = pair // 2, pair % 2
    y, core = virt // 2, virt % 2
    corner = (z == 0) | (z == 3)

    def ab(v):
        return v.reshape(tiles * depth, v.shape[-1])

    x0 = over_pair(integrals, XALL)
    own_a, own_b = integrals[:, :, :cut], integrals[:, :, cut:]
    p1a = over_pair(own_a, Z1)
    p2a = over_pair(own_a, Z2)

    masked = amplitudes * tile_mask.astype(BF16)[:, :, None]
    a = masked.reshape(pairs, tiles, 8, depth).transpose(2, 0, 1, 3).reshape(8, pairs, tiles * depth)

    x1a = over_pair(p1a, XALL)
    p1b = over_pair(after(own_b, p1a), Z1)
    p3ea = over_pair(p2a, ZEND)
    x2a = over_pair(p2a, XALL)
    p2b = over_pair(after(own_b, p2a), Z2)
    p3ma = over_pair(after(own_a, p1b), ZMID)
    x1b = over_pair(x0[:, :, cut:], Z1)
    x2b = over_pair(p2b, XALL)
    p3eb = over_pair(p2b, ZEND)
    p3mb = over_pair(after(own_b, p2b), ZMID)
    x3ea = over_pair(p3ea, XEND)
    x3ma = over_pair(p3ma, XMID)
    x3eb = over_pair(p3eb, XEND)
    x3mb = over_pair(p3mb, XMID)

    near, far = z ^ 1, z ^ 2
    third = z ^ 3
    zs = jnp.stack([z, z, near, near, far, far, third, third])
    xs = jnp.stack([x, 1 - x] * 4)
    places = (zs * 2 + xs).astype(jnp.int32)
    rows = jnp.stack(
        [2 * (1 - y) + 1 - core, 2 * y + 1 - core, 2 * (1 - y) + core, 2 * y + core]
    ).astype(jnp.int32)

    first = [ab(v) for v in (own_a, x0[:, :, :cut], p1a, x1a, p2a, x2a)]
    send_a, keep_a = products(
        places, rows, a, first, [(ab(p3ma), ab(p3ea)), (ab(x3ma), ab(x3ea))], finish=True
    )
    got_a = over_virt(send_a, CORE)
    there_a = over_virt((keep_a[0] + got_a[0].astype(F32)).astype(BF16), YHOP)

    second = [ab(v) for v in (own_b, x0[:, :, cut:], p1b, x1b, p2b, x2b)]
    total_b = products(places[:7], rows, a, second, [(ab(p3mb), ab(p3eb))])
    send_b, keep_b = products(places[7:], rows, a, [], [(ab(x3mb), ab(x3eb))], total=total_b, finish=True)
    got_b = over_virt(send_b, CORE)
    there_b = over_virt((keep_b[0] + got_b[0].astype(F32)).astype(BF16), YHOP)

    ladder = jnp.concatenate(
        [
            keep_a[1] + got_a[1].astype(F32) + there_a.astype(F32),
            keep_b[1] + got_b[1].astype(F32) + there_b.astype(F32),
        ],
        axis=1,
    )
    denom = virt_energy[None, :] - pair_energy[:, None]
    return (ladder / denom).astype(BF16)


def solution(mesh):
    placed = (
        P("pair", "virt", None),
        P("pair", "virt"),
        P("virt", "pair", None),
        P(("pair", "virt")),
        P(),
    )
    here = mesh.shape["pair"] == 8 and mesh.shape["virt"] == 4
    return jax.shard_map(
        functools.partial(scheduled, 640) if here else plain,
        mesh=mesh,
        in_specs=placed,
        out_specs=P(("pair", "virt"), None),
        check_vma=False,
    )
```

time: 134 us -> 104 us (0.78)
  waiting for transfers between devices: 100 us -> 34.5 us
  starting transfers between devices: 0.04 us -> 30.3 us
  Pallas kernels: 0 us -> 16.1 us
  between operations: 13.4 us -> 0.25 us
  local copies, waits for them, and re-layouts: 0.21 us -> 11.7 us
  matrix products: 9.32 us -> 0 us
    all_gather x1 -> x0, waiting for transfers between devices: 69.4 us -> none  [on_device(): lax.all_gather(integrals, 'pair', axis=1, tiled=True)]
    ppermute x0 -> x21, waiting for transfers between devices: none -> 34.5 us  [the longest x17 21.2 us: over_pair(): return lax.ppermute(value, 'pair', hops)]
    ppermute x0 -> x21, starting transfers between devices: none -> 30.3 us  [the longest x17 27.5 us: over_pair(): return lax.ppermute(value, 'pair', hops)]
    reduce_scatter x1 -> x0, waiting for transfers between devices: 29.9 us -> none  [on_device(): lax.psum_scatter(partial_value.astype(jnp.bfloat16), 'virt', scatter_dime...]
    pallas_call x0 -> x3, Pallas kernels: none -> 16.1 us  [products(): pl.pallas_call(body, grid_spec=pltpu.PrefetchScalarGridSpec(num_scalar_pr...]
    dot_general x1 -> x0, matrix products: 9.32 us -> none  [on_device(): jnp.einsum('ptk,tkn->pn', masked, lax.all_gather(integrals, 'pair', axis=...]
    transpose x0 -> x1, other arithmetic: none -> 8.31 us  [scheduled(): masked.reshape(pairs, tiles, 8, depth).transpose(2, 0, 1, 3)]
    mul x1 -> x0, other arithmetic: 8.03 us -> none  [on_device(): masked = amplitudes * tile_mask.astype(jnp.bfloat16)[:, :, None]]
  transfers between devices with their start and end apart: 2 -> 21, of which waited for: 2 -> 8; matrix products, arithmetic and copies ran while one was open for 7% -> 19% of each run, Pallas kernels for 0% -> 16%
where the time goes in v1:
time: 104 us; the launch traced here: 103 us
  waiting for transfers between devices  34.5 us (33%)
  starting transfers between devices  30.3 us (29%)
  Pallas kernels  16.1 us (15%)
  local copies, waits for them, and re-layouts  11.7 us (11%)
  other arithmetic  10.4 us (10%)
    ppermute x17, starting transfers between devices, over_pair(): return lax.ppermute(value, 'pair', hops)  27.5 us
    ppermute x17, waiting for transfers between devices, over_pair(): return lax.ppermute(value, 'pair', hops)  21.2 us
    pallas_call x3, Pallas kernels, products(): pl.pallas_call(body, grid_spec=pltpu.PrefetchScalarGridSpec(num_scalar_pr...  16.1 us
    ppermute x4, waiting for transfers between devices, over_virt(): return lax.ppermute(value, 'virt', hops)  13.3 us
    transpose x1, other arithmetic, scheduled(): masked.reshape(pairs, tiles, 8, depth).transpose(2, 0, 1, 3)  8.31 us
    reshape x1, local copies, waits for them, and re-layouts, scheduled(): masked.reshape(pairs, tiles, 8, depth).transpose(2, 0, 1, 3)  7.65 us
    ppermute x4, starting transfers between devices, over_virt(): return lax.ppermute(value, 'virt', hops)  2.78 us
  transfers between devices with their start and end apart: 21, of which 8 were waited for; matrix products, arithmetic and copies ran while one was open for 19% of the time, Pallas kernels for 16%

profile of v1, /device:TPU:0, one launch (start us, length us, event | category | flops | bytes accessed | tf_op | source)
XLA Modules:
  0.0 103.1 jit_solution(4798287037943604466)
XLA Ops:
  0.0 1.0 slice.43
  1.0 4.1 %collective-permute-start.3 = (bf16[2,128,640]{2,1,0:T(8,128)(2,1)S(1)}, bf16[2,128,640]{2,1,0:T(8,128)(2,1)S(1)}, u32[]{:S(2)}, u32[]{:S(2)}) collective-permute-start(bf16[2,128,640]{2,1,0:T(8,128)(2,1)S(1)} %slice.43), channel_id=1, source_target_pairs={{0,16},{4,20},{16,0},{20,4},{8,24},{12,28},{24,8},{28,12},{1,17},{... | collective-permute-start | bytes 983048 | tf_op jit(solution)/shard_map/ppermute | solution.py:43
  5.1 1.6 %collective-permute-start.1 = (bf16[2,128,640]{2,1,0:T(8,128)(2,1)S(1)}, bf16[2,128,640]{2,1,0:T(8,128)(2,1)S(1)}, u32[]{:S(2)}, u32[]{:S(2)}) collective-permute-start(bf16[2,128,640]{2,1,0:T(8,128)(2,1)S(1)} %slice.43), channel_id=1, source_target_pairs={{0,8},{4,12},{8,0},{12,4},{16,24},{20,28},{24,16},{28,20},{1,9},{5... | collective-permute-start | bytes 983048 | tf_op jit(solution)/shard_map/ppermute | solution.py:43
  6.7 1.5 %collective-permute-start = (bf16[2,128,1024]{2,1,0:T(8,128)(2,1)}, bf16[2,128,1024]{2,1,0:T(8,128)(2,1)S(1)}, u32[]{:S(2)}, u32[]{:S(2)}) collective-permute-start(bf16[2,128,1024]{2,1,0:T(8,128)(2,1)} %param.7), channel_id=1, source_target_pairs={{0,4},{4,0},{8,12},{12,8},{16,20},{20,16},{24,28},{28,24},{1,5},{5... | collective-permute-start | bytes 1572872 | tf_op jit(solution)/shard_map/ppermute | solution.py:43
  8.2 1.0 slice.45
  9.2 10.8 %collective-permute-done.3 = bf16[2,128,640]{2,1,0:T(8,128)(2,1)S(1)} collective-permute-done((bf16[2,128,640]{2,1,0:T(8,128)(2,1)S(1)}, bf16[2,128,640]{2,1,0:T(8,128)(2,1)S(1)}, u32[]{:S(2)}, u32[]{:S(2)}) %collective-permute-start.3) | collective-permute-done | bytes 327712 | tf_op jit(solution)/shard_map/ppermute | solution.py:43
  19.9 0.0 collective-permute-start.12
  19.9 0.2 collective-permute-done.1
  20.1 3.8 %collective-permute-start.5 = (bf16[2,128,384]{2,1,0:T(8,128)(2,1)S(1)}, bf16[2,128,384]{2,1,0:T(8,128)(2,1)S(1)}, u32[]{:S(2)}, u32[]{:S(2)}) collective-permute-start(bf16[2,128,384]{2,1,0:T(8,128)(2,1)S(1)} %slice.45), channel_id=1, source_target_pairs={{0,8},{4,12},{8,0},{12,4},{16,24},{20,28},{24,16},{28,20},{1,9},{5... | collective-permute-start | bytes 589832 | tf_op jit(solution)/shard_map/ppermute | solution.py:43
  23.9 0.7 convert_element_type.40
  24.6 0.2 copy.6
  24.9 1.3 %collective-permute-start.7 = (bf16[2,128,640]{2,1,0:T(8,128)(2,1)S(1)}, bf16[2,128,640]{2,1,0:T(8,128)(2,1)S(1)}, u32[]{:S(2)}, u32[]{:S(2)}) collective-permute-start(bf16[2,128,640]{2,1,0:T(8,128)(2,1)S(1)} %collective-permute-done.3), channel_id=1, source_target_pairs={{8,0},{12,4},{16,24},{20,28},{9,1},{13,5},{17,25},{21,29},{10,2},{... | collective-permute-start | bytes 983048 | tf_op jit(solution)/shard_map/ppermute | solution.py:43
  26.2 5.0 %collective-permute-done.12 = bf16[2,128,384]{2,1,0:T(8,128)(2,1)S(1)} collective-permute-done((bf16[2,128,384]{2,1,0:T(8,128)(2,1)S(1)}, bf16[2,128,384]{2,1,0:T(8,128)(2,1)S(1)}, u32[]{:S(2)}, u32[]{:S(2)}) %collective-permute-start.12) | collective-permute-done | bytes 196640 | tf_op jit(solution)/shard_map/ppermute | solution.py:43
  31.2 0.7 collective-permute-start.13
  31.9 0.0 collective-permute-done
  31.9 0.0 copy-start
  31.9 1.3 %collective-permute-start.17 = (bf16[2,128,384]{2,1,0:T(8,128)(2,1)S(1)}, bf16[2,128,384]{2,1,0:T(8,128)(2,1)S(1)}, u32[]{:S(2)}, u32[]{:S(2)}) collective-permute-start(bf16[2,128,384]{2,1,0:T(8,128)(2,1)S(1)} %slice.60), channel_id=1, source_target_pairs={{0,8},{4,12},{8,0},{12,4},{16,24},{20,28},{24,16},{28,20},{1,9},{5... | collective-permute-start | bytes 589832 | tf_op jit(solution)/shard_map/ppermute | solution.py:43
  33.3 0.0 collective-permute-done.5
  33.3 0.7 collective-permute-start.6
  33.9 1.3 %collective-permute-start.15 = (bf16[2,128,384]{2,1,0:T(8,128)(2,1)S(1)}, bf16[2,128,384]{2,1,0:T(8,128)(2,1)S(1)}, u32[]{:S(2)}, u32[]{:S(2)}) collective-permute-start(bf16[2,128,384]{2,1,0:T(8,128)(2,1)S(1)} %collective-permute-done.12), channel_id=1, source_target_pairs={{8,0},{12,4},{16,24},{20,28},{9,1},{13,5},{17,25},{21,29},{10,2},{... | collective-permute-start | bytes 589832 | tf_op jit(solution)/shard_map/ppermute | solution.py:43
  35.2 8.3 %bitcast_bitcast_fusion = bf16[8,1024,2,128]{3,2,1,0:T(2,128)(2,1)} fusion(bf16[1024,2,1024]{2,1,0:T(2,128)(2,1)} %param.5, bf16[1024,2]{1,0:T(8,128)(2,1)S(1)} %copy.6), kind=kLoop, calls=%fused_computation | loop fusion | flops 2097152 | bytes 8392704 | tf_op jit(solution)/shard_map/transpose | solution.py:138
  43.5 0.1 stack.56
  43.6 0.1 stack.53
  43.7 0.0 collective-permute-done.7
  43.7 1.3 %collective-permute-start.2 = (bf16[2,128,640]{2,1,0:T(8,128)(2,1)S(1)}, bf16[2,128,640]{2,1,0:T(8,128)(2,1)S(1)}, u32[]{:S(2)}, u32[]{:S(2)}) collective-permute-start(bf16[2,128,640]{2,1,0:T(8,128)(2,1)S(1)} %collective-permute-done.1), channel_id=1, source_target_pairs={{0,4},{4,0},{8,12},{12,8},{16,20},{20,16},{24,28},{28,24},{1,5},{5... | collective-permute-start | bytes 983048 | tf_op jit(solution)/shard_map/ppermute | solution.py:43
  45.0 0.0 collective-permute-done.13
  45.0 0.8 collective-permute-start.4
  45.8 0.9 collective-permute-done.15
  46.7 1.2 %collective-permute-start.18 = (bf16[2,128,384]{2,1,0:T(8,128)(2,1)S(1)}, bf16[2,128,384]{2,1,0:T(8,128)(2,1)S(1)}, u32[]{:S(2)}, u32[]{:S(2)}) collective-permute-start(bf16[2,128,384]{2,1,0:T(8,128)(2,1)S(1)} %collective-permute-done.12), channel_id=1, source_target_pairs={{0,4},{4,0},{8,12},{12,8},{16,20},{20,16},{24,28},{28,24},{1,5},{5... | collective-permute-start | bytes 589832 | tf_op jit(solution)/shard_map/ppermute | solution.py:43
  48.0 0.0 collective-permute-done.17
  48.0 2.7 %collective-permute-start.9 = (bf16[2,128,640]{2,1,0:T(8,128)(2,1)S(1)}, bf16[2,128,640]{2,1,0:T(8,128)(2,1)}, u32[]{:S(2)}, u32[]{:S(2)}) collective-permute-start(bf16[2,128,640]{2,1,0:T(8,128)(2,1)S(1)} %collective-permute-done.7), channel_id=1, source_target_pairs={{0,4},{4,0},{24,28},{28,24},{1,5},{5,1},{25,29},{29,25},{2,6},{6,2... | collective-permute-start | bytes 983048 | tf_op jit(solution)/shard_map/ppermute | solution.py:43
  50.7 0.0 collective-permute-done.6
  50.7 1.4 %collective-permute-start.8 = (bf16[2,128,640]{2,1,0:T(8,128)(2,1)S(1)}, bf16[2,128,640]{2,1,0:T(8,128)(2,1)}, u32[]{:S(2)}, u32[]{:S(2)}) collective-permute-start(bf16[2,128,640]{2,1,0:T(8,128)(2,1)S(1)} %collective-permute-done.6), channel_id=1, source_target_pairs={{8,12},{12,8},{16,20},{20,16},{9,13},{13,9},{17,21},{21,17},{10,14... | collective-permute-start | bytes 983048 | tf_op jit(solution)/shard_map/ppermute | solution.py:43
  52.1 0.6 slice.50.places_ref
  52.7 7.7 %reshape.80.a_ref = bf16[8,1024,256]{2,1,0:T(8,128)(2,1)} reshape(bf16[8,1024,2,128]{3,2,1,0:T(2,128)(2,1)} %bitcast_bitcast_fusion) | data formatting | bytes 8388608 | tf_op jit(solution)/shard_map/reshape | solution.py:138
  60.3 0.1 pad_add_fusion.rows_ref
  60.4 1.0 slice.57
  61.4 4.2 %collective-permute-done.18 = bf16[2,128,384]{2,1,0:T(8,128)(2,1)S(1)} collective-permute-done((bf16[2,128,384]{2,1,0:T(8,128)(2,1)S(1)}, bf16[2,128,384]{2,1,0:T(8,128)(2,1)S(1)}, u32[]{:S(2)}, u32[]{:S(2)}) %collective-permute-start.18) | collective-permute-done | bytes 196640 | tf_op jit(solution)/shard_map/ppermute | solution.py:43
  65.7 0.7 collective-permute-start.14
  66.3 5.1 %shard_map.56.refs_2_ = f32[4,256,384]{2,1,0:T(8,128)S(1)} custom-call(s32[7]{0:T(128)S(1)} %bitcast.58, s32[4]{0:T(128)S(1)} %pad_add_fusion.rows_ref, bf16[8,1024,256]{2,1,0:T(8,128)(2,1)} %reshape.80.a_ref, bf16[256,384]{1,0:T(8,128)(2,1)S(1)} %bitcast.46, bf16[256,384]{1,0:T(8,128)(2,1)S(1)} %bitcast.47, bf16[256,384]{1,0:T(8,128)(2,1)S(1)} %bitcast.55, ...), custom_call_target="tpu_custom_call" | custom-call | flops 1409286144 | bytes 5570560 | tf_op jit(solution)/shard_map/pallas_call | solution.py:106
  71.4 0.0 collective-permute-done.2
  71.4 3.2 %collective-permute-start.16 = (bf16[2,128,384]{2,1,0:T(8,128)(2,1)S(1)}, bf16[2,128,384]{2,1,0:T(8,128)(2,1)S(1)}, u32[]{:S(2)}, u32[]{:S(2)}) collective-permute-start(bf16[2,128,384]{2,1,0:T(8,128)(2,1)S(1)} %collective-permute-done.15), channel_id=1, source_target_pairs={{0,4},{4,0},{24,28},{28,24},{1,5},{5,1},{25,29},{29,25},{2,6},{6,2... | collective-permute-start | bytes 589832 | tf_op jit(solution)/shard_map/ppermute | solution.py:43
  74.6 0.0 collective-permute-done.4
  74.6 0.0 collective-permute-done.9
  74.6 0.0 collective-permute-done.8
  74.6 6.5 %shard_map.55 = (bf16[2,256,640]{2,1,0:T(8,128)(2,1)S(1)}, f32[2,256,640]{2,1,0:T(8,128)S(1)}) custom-call(s32[8]{0:T(128)S(1)} %multiply_add_fusion.places_ref, s32[4]{0:T(128)S(1)} %pad_add_fusion.rows_ref, bf16[8,1024,256]{2,1,0:T(8,128)(2,1)} %reshape.80.a_ref, bf16[256,640]{1,0:T(8,128)(2,1)S(1)} %bitcast.48, bf16[256,640]{1,0:T(8,128)(2,1)S(1)} %bitcast.49, ...), custom_call_target="tpu_custom_call" | custom-call | flops 2684354560 | bytes 6815744 | tf_op jit(solution)/shard_map/pallas_call | solution.py:106
  81.1 0.1 collective-permute-start.10
  81.2 0.0 collective-permute-done.14
  81.2 0.0 collective-permute-done.16
  81.2 0.0 copy-start.1
  81.2 0.0 copy-start.2
  81.2 4.6 %shard_map.57 = (bf16[2,256,384]{2,1,0:T(8,128)(2,1)S(1)}, f32[2,256,384]{2,1,0:T(8,128)S(1)}) custom-call(s32[1]{0:T(128)} %slice.50.places_ref, s32[4]{0:T(128)S(1)} %pad_add_fusion.rows_ref, bf16[8,1024,256]{2,1,0:T(8,128)(2,1)} %reshape.80.a_ref, bf16[256,384]{1,0:T(8,128)(2,1)S(1)} %bitcast.50, bf16[256,384]{1,0:T(8,128)(2,1)S(1)} %bitcast.51, ...), custom_call_target="tpu_custom_call" | custom-call | flops 201326592 | bytes 4390912 | tf_op jit(solution)/shard_map/pallas_call | solution.py:106
  85.8 0.5 collective-permute-start.19
  86.3 1.3 %collective-permute-done.19 = bf16[2,256,384]{2,1,0:T(8,128)(2,1)S(1)} collective-permute-done((bf16[2,256,384]{2,1,0:T(8,128)(2,1)S(1)}, bf16[2,256,384]{2,1,0:T(8,128)(2,1)S(1)}, u32[]{:S(2)}, u32[]{:S(2)}) %collective-permute-start.19) | collective-permute-done | bytes 393248 | tf_op jit(solution)/shard_map/ppermute | solution.py:47
  87.7 1.6 %collective-permute-start.20 = (bf16[256,384]{1,0:T(8,128)(2,1)S(1)}, bf16[256,384]{1,0:T(8,128)(2,1)S(1)}, u32[]{:S(2)}, u32[]{:S(2)}) collective-permute-start(bf16[256,384]{1,0:T(8,128)(2,1)S(1)} %fusion.2), channel_id=1, source_target_pairs={{0,2},{2,0},{1,3},{3,1},{4,6},{6,4},{5,7},{7,5},{8,10},{10,8},{9,1... | collective-permute-start | bytes 589832 | tf_op jit(solution)/shard_map/ppermute | solution.py:47
  89.3 0.0 collective-permute-done.10
  89.3 0.1 fusion.1
  89.4 0.6 collective-permute-start.11
  90.0 5.5 %collective-permute-done.20 = bf16[256,384]{1,0:T(8,128)(2,1)S(1)} collective-permute-done((bf16[256,384]{1,0:T(8,128)(2,1)S(1)}, bf16[256,384]{1,0:T(8,128)(2,1)S(1)}, u32[]{:S(2)}, u32[]{:S(2)}) %collective-permute-start.20) | collective-permute-done | bytes 196640 | tf_op jit(solution)/shard_map/ppermute | solution.py:47
  95.5 0.1 bitcast_add_fusion.1
  95.6 6.4 %collective-permute-done.11 = bf16[256,640]{1,0:T(8,128)(2,1)S(1)} collective-permute-done((bf16[256,640]{1,0:T(8,128)(2,1)S(1)}, bf16[256,640]{1,0:T(8,128)(2,1)S(1)}, u32[]{:S(2)}, u32[]{:S(2)}) %collective-permute-start.11) | collective-permute-done | bytes 327712 | tf_op jit(solution)/shard_map/ppermute | solution.py:47
  102.0 0.1 bitcast_add_fusion
  102.1 0.0 copy-done.1
  102.1 1.0 fusion
  (5 shorter events, 0.1 us)
Async XLA Ops:
  1.0 18.9 %collective-permute-start.3 = (bf16[2,128,640]{2,1,0:T(8,128)(2,1)S(1)}, bf16[2,128,640]{2,1,0:T(8,128)(2,1)S(1)}, u32[]{:S(2)}, u32[]{:S(2)}) collective-permute-start(bf16[2,128,640]{2,1,0:T(8,128)(2,1)S(1)} %slice.43), channel_id=1, source_target_pairs={{0,16},{4,20},{16,0},{20,4},{8,24},{12,28},{24,8},{28,12},{1,17},{... | collective-permute-start | bytes 983048 | tf_op jit(solution)/shard_map/ppermute | solution.py:43
  5.1 15.0 %collective-permute-start.1 = (bf16[2,128,640]{2,1,0:T(8,128)(2,1)S(1)}, bf16[2,128,640]{2,1,0:T(8,128)(2,1)S(1)}, u32[]{:S(2)}, u32[]{:S(2)}) collective-permute-start(bf16[2,128,640]{2,1,0:T(8,128)(2,1)S(1)} %slice.43), channel_id=1, source_target_pairs={{0,8},{4,12},{8,0},{12,4},{16,24},{20,28},{24,16},{28,20},{1,9},{5... | collective-permute-start | bytes 983048 | tf_op jit(solution)/shard_map/ppermute | solution.py:43
  6.7 25.2 %collective-permute-start = (bf16[2,128,1024]{2,1,0:T(8,128)(2,1)}, bf16[2,128,1024]{2,1,0:T(8,128)(2,1)S(1)}, u32[]{:S(2)}, u32[]{:S(2)}) collective-permute-start(bf16[2,128,1024]{2,1,0:T(8,128)(2,1)} %param.7), channel_id=1, source_target_pairs={{0,4},{4,0},{8,12},{12,8},{16,20},{20,16},{24,28},{28,24},{1,5},{5... | collective-permute-start | bytes 1572872 | tf_op jit(solution)/shard_map/ppermute | solution.py:43
  19.9 11.2 %collective-permute-start.12 = (bf16[2,128,384]{2,1,0:T(8,128)(2,1)S(1)}, bf16[2,128,384]{2,1,0:T(8,128)(2,1)S(1)}, u32[]{:S(2)}, u32[]{:S(2)}) collective-permute-start(bf16[2,128,384]{2,1,0:T(8,128)(2,1)S(1)} %slice.45), channel_id=1, source_target_pairs={{0,16},{4,20},{16,0},{20,4},{8,24},{12,28},{24,8},{28,12},{1,17},{... | collective-permute-start | bytes 589832 | tf_op jit(solution)/shard_map/ppermute | solution.py:43
  20.1 13.1 %collective-permute-start.5 = (bf16[2,128,384]{2,1,0:T(8,128)(2,1)S(1)}, bf16[2,128,384]{2,1,0:T(8,128)(2,1)S(1)}, u32[]{:S(2)}, u32[]{:S(2)}) collective-permute-start(bf16[2,128,384]{2,1,0:T(8,128)(2,1)S(1)} %slice.45), channel_id=1, source_target_pairs={{0,8},{4,12},{8,0},{12,4},{16,24},{20,28},{24,16},{28,20},{1,9},{5... | collective-permute-start | bytes 589832 | tf_op jit(solution)/shard_map/ppermute | solution.py:43
  24.9 18.9 %collective-permute-start.7 = (bf16[2,128,640]{2,1,0:T(8,128)(2,1)S(1)}, bf16[2,128,640]{2,1,0:T(8,128)(2,1)S(1)}, u32[]{:S(2)}, u32[]{:S(2)}) collective-permute-start(bf16[2,128,640]{2,1,0:T(8,128)(2,1)S(1)} %collective-permute-done.3), channel_id=1, source_target_pairs={{8,0},{12,4},{16,24},{20,28},{9,1},{13,5},{17,25},{21,29},{10,2},{... | collective-permute-start | bytes 983048 | tf_op jit(solution)/shard_map/ppermute | solution.py:43
  31.2 13.8 %collective-permute-start.13 = (bf16[2,128,384]{2,1,0:T(8,128)(2,1)S(1)}, bf16[2,128,384]{2,1,0:T(8,128)(2,1)S(1)}, u32[]{:S(2)}, u32[]{:S(2)}) collective-permute-start(bf16[2,128,384]{2,1,0:T(8,128)(2,1)S(1)} %slice.45), channel_id=1, source_target_pairs={{8,16},{12,20},{16,8},{20,12},{9,17},{13,21},{17,9},{21,13},{10,18... | collective-permute-start | bytes 589832 | tf_op jit(solution)/shard_map/ppermute | solution.py:43
  31.9 1.4 %copy-start = (bf16[2,128,1024]{2,1,0:T(8,128)(2,1)}, bf16[2,128,1024]{2,1,0:T(8,128)(2,1)S(1)}, u32[]{:S(2)}) copy-start(bf16[2,128,1024]{2,1,0:T(8,128)(2,1)S(1)} %collective-permute-done) | copy-start | bytes 1572868
  31.9 16.1 %collective-permute-start.17 = (bf16[2,128,384]{2,1,0:T(8,128)(2,1)S(1)}, bf16[2,128,384]{2,1,0:T(8,128)(2,1)S(1)}, u32[]{:S(2)}, u32[]{:S(2)}) collective-permute-start(bf16[2,128,384]{2,1,0:T(8,128)(2,1)S(1)} %slice.60), channel_id=1, source_target_pairs={{0,8},{4,12},{8,0},{12,4},{16,24},{20,28},{24,16},{28,20},{1,9},{5... | collective-permute-start | bytes 589832 | tf_op jit(solution)/shard_map/ppermute | solution.py:43
  33.3 17.4 %collective-permute-start.6 = (bf16[2,128,640]{2,1,0:T(8,128)(2,1)S(1)}, bf16[2,128,640]{2,1,0:T(8,128)(2,1)S(1)}, u32[]{:S(2)}, u32[]{:S(2)}) collective-permute-start(bf16[2,128,640]{2,1,0:T(8,128)(2,1)S(1)} %slice.43), channel_id=1, source_target_pairs={{8,16},{12,20},{16,8},{20,12},{9,17},{13,21},{17,9},{21,13},{10,18... | collective-permute-start | bytes 983048 | tf_op jit(solution)/shard_map/ppermute | solution.py:43
  33.9 12.8 %collective-permute-start.15 = (bf16[2,128,384]{2,1,0:T(8,128)(2,1)S(1)}, bf16[2,128,384]{2,1,0:T(8,128)(2,1)S(1)}, u32[]{:S(2)}, u32[]{:S(2)}) collective-permute-start(bf16[2,128,384]{2,1,0:T(8,128)(2,1)S(1)} %collective-permute-done.12), channel_id=1, source_target_pairs={{8,0},{12,4},{16,24},{20,28},{9,1},{13,5},{17,25},{21,29},{10,2},{... | collective-permute-start | bytes 589832 | tf_op jit(solution)/shard_map/ppermute | solution.py:43
  43.7 27.7 %collective-permute-start.2 = (bf16[2,128,640]{2,1,0:T(8,128)(2,1)S(1)}, bf16[2,128,640]{2,1,0:T(8,128)(2,1)S(1)}, u32[]{:S(2)}, u32[]{:S(2)}) collective-permute-start(bf16[2,128,640]{2,1,0:T(8,128)(2,1)S(1)} %collective-permute-done.1), channel_id=1, source_target_pairs={{0,4},{4,0},{8,12},{12,8},{16,20},{20,16},{24,28},{28,24},{1,5},{5... | collective-permute-start | bytes 983048 | tf_op jit(solution)/shard_map/ppermute | solution.py:43
  45.0 29.5 %collective-permute-start.4 = (bf16[2,128,640]{2,1,0:T(8,128)(2,1)S(1)}, bf16[2,128,640]{2,1,0:T(8,128)(2,1)}, u32[]{:S(2)}, u32[]{:S(2)}) collective-permute-start(bf16[2,128,640]{2,1,0:T(8,128)(2,1)S(1)} %collective-permute-done.3), channel_id=1, source_target_pairs={{0,4},{4,0},{8,12},{12,8},{16,20},{20,16},{24,28},{28,24},{1,5},{5... | collective-permute-start | bytes 983048 | tf_op jit(solution)/shard_map/ppermute | solution.py:43
  46.7 19.0 %collective-permute-start.18 = (bf16[2,128,384]{2,1,0:T(8,128)(2,1)S(1)}, bf16[2,128,384]{2,1,0:T(8,128)(2,1)S(1)}, u32[]{:S(2)}, u32[]{:S(2)}) collective-permute-start(bf16[2,128,384]{2,1,0:T(8,128)(2,1)S(1)} %collective-permute-done.12), channel_id=1, source_target_pairs={{0,4},{4,0},{8,12},{12,8},{16,20},{20,16},{24,28},{28,24},{1,5},{5... | collective-permute-start | bytes 589832 | tf_op jit(solution)/shard_map/ppermute | solution.py:43
  48.0 26.6 %collective-permute-start.9 = (bf16[2,128,640]{2,1,0:T(8,128)(2,1)S(1)}, bf16[2,128,640]{2,1,0:T(8,128)(2,1)}, u32[]{:S(2)}, u32[]{:S(2)}) collective-permute-start(bf16[2,128,640]{2,1,0:T(8,128)(2,1)S(1)} %collective-permute-done.7), channel_id=1, source_target_pairs={{0,4},{4,0},{24,28},{28,24},{1,5},{5,1},{25,29},{29,25},{2,6},{6,2... | collective-permute-start | bytes 983048 | tf_op jit(solution)/shard_map/ppermute | solution.py:43
  50.7 23.9 %collective-permute-start.8 = (bf16[2,128,640]{2,1,0:T(8,128)(2,1)S(1)}, bf16[2,128,640]{2,1,0:T(8,128)(2,1)}, u32[]{:S(2)}, u32[]{:S(2)}) collective-permute-start(bf16[2,128,640]{2,1,0:T(8,128)(2,1)S(1)} %collective-permute-done.6), channel_id=1, source_target_pairs={{8,12},{12,8},{16,20},{20,16},{9,13},{13,9},{17,21},{21,17},{10,14... | collective-permute-start | bytes 983048 | tf_op jit(solution)/shard_map/ppermute | solution.py:43
  65.7 15.5 %collective-permute-start.14 = (bf16[2,128,384]{2,1,0:T(8,128)(2,1)S(1)}, bf16[2,128,384]{2,1,0:T(8,128)(2,1)S(1)}, u32[]{:S(2)}, u32[]{:S(2)}) collective-permute-start(bf16[2,128,384]{2,1,0:T(8,128)(2,1)S(1)} %collective-permute-done.13), channel_id=1, source_target_pairs={{8,12},{12,8},{16,20},{20,16},{9,13},{13,9},{17,21},{21,17},{10,14... | collective-permute-start | bytes 589832 | tf_op jit(solution)/shard_map/ppermute | solution.py:43
  71.4 9.8 %collective-permute-start.16 = (bf16[2,128,384]{2,1,0:T(8,128)(2,1)S(1)}, bf16[2,128,384]{2,1,0:T(8,128)(2,1)S(1)}, u32[]{:S(2)}, u32[]{:S(2)}) collective-permute-start(bf16[2,128,384]{2,1,0:T(8,128)(2,1)S(1)} %collective-permute-done.15), channel_id=1, source_target_pairs={{0,4},{4,0},{24,28},{28,24},{1,5},{5,1},{25,29},{29,25},{2,6},{6,2... | collective-permute-start | bytes 589832 | tf_op jit(solution)/shard_map/ppermute | solution.py:43
  81.1 8.2 %collective-permute-start.10 = (bf16[2,256,640]{2,1,0:T(8,128)(2,1)S(1)}, bf16[2,256,640]{2,1,0:T(8,128)(2,1)S(1)}, u32[]{:S(2)}, u32[]{:S(2)}) collective-permute-start(bf16[2,256,640]{2,1,0:T(8,128)(2,1)S(1)} %get-tuple-element.16), channel_id=1, source_target_pairs={{0,1},{1,0},{2,3},{3,2},{4,5},{5,4},{6,7},{7,6},{8,9},{9,8},{10,11... | collective-permute-start | bytes 1966088 | tf_op jit(solution)/shard_map/ppermute | solution.py:47
  81.2 20.9 %copy-start.1 = (f32[1024]{0:T(1024)S(1)}, f32[1024]{0:T(1024)}, u32[]{:S(2)}) copy-start(f32[1024]{0:T(1024)} %param.9) | copy-start | bytes 12292
  81.2 20.9 %copy-start.2 = (f32[256]{0:T(256)S(1)}, f32[256]{0:T(256)}, u32[]{:S(2)}) copy-start(f32[256]{0:T(256)} %param.8) | copy-start | bytes 3076
  85.8 1.9 %collective-permute-start.19 = (bf16[2,256,384]{2,1,0:T(8,128)(2,1)S(1)}, bf16[2,256,384]{2,1,0:T(8,128)(2,1)S(1)}, u32[]{:S(2)}, u32[]{:S(2)}) collective-permute-start(bf16[2,256,384]{2,1,0:T(8,128)(2,1)S(1)} %get-tuple-element.20), channel_id=1, source_target_pairs={{0,1},{1,0},{2,3},{3,2},{4,5},{5,4},{6,7},{7,6},{8,9},{9,8},{10,11... | collective-permute-start | bytes 1179656 | tf_op jit(solution)/shard_map/ppermute | solution.py:47
  87.7 7.8 %collective-permute-start.20 = (bf16[256,384]{1,0:T(8,128)(2,1)S(1)}, bf16[256,384]{1,0:T(8,128)(2,1)S(1)}, u32[]{:S(2)}, u32[]{:S(2)}) collective-permute-start(bf16[256,384]{1,0:T(8,128)(2,1)S(1)} %fusion.2), channel_id=1, source_target_pairs={{0,2},{2,0},{1,3},{3,1},{4,6},{6,4},{5,7},{7,5},{8,10},{10,8},{9,1... | collective-permute-start | bytes 589832 | tf_op jit(solution)/shard_map/ppermute | solution.py:47
  89.4 12.6 %collective-permute-start.11 = (bf16[256,640]{1,0:T(8,128)(2,1)S(1)}, bf16[256,640]{1,0:T(8,128)(2,1)S(1)}, u32[]{:S(2)}, u32[]{:S(2)}) collective-permute-start(bf16[256,640]{1,0:T(8,128)(2,1)S(1)} %fusion.1), channel_id=1, source_target_pairs={{0,2},{2,0},{1,3},{3,1},{4,6},{6,4},{5,7},{7,5},{8,10},{10,8},{9,1... | collective-permute-start | bytes 983048 | tf_op jit(solution)/shard_map/ppermute | solution.py:47

commit v2 on v0

v2 whole, which is shorter than its diff:
```python
import jax
import jax.numpy as jnp
from jax import lax
from jax.experimental import pallas as pl
from jax.experimental.pallas import tpu as pltpu
from jax.sharding import PartitionSpec as P

BF16 = jnp.bfloat16
F32 = jnp.float32


def plain(amplitudes, tile_mask, integrals, pair_energy, virt_energy):
    masked = amplitudes * tile_mask.astype(BF16)[:, :, None]
    partial_value = jnp.einsum(
        "ptk,tkn->pn",
        masked,
        lax.all_gather(integrals, "pair", axis=1, tiled=True),
        preferred_element_type=F32,
    )
    ladder = lax.psum_scatter(partial_value.astype(BF16), "virt", scatter_dimension=0, tiled=True).astype(F32)
    denom = virt_energy[None, :] - pair_energy[:, None]
    return (ladder / denom).astype(BF16)


RING = [0, 2, 4, 6, 7, 5, 3, 1]
EVEN = [(RING[i], RING[i ^ 1]) for i in range(8)]
ODD = [(RING[i], RING[(i + 2 * (i % 2) - 1) % 8]) for i in range(8)]
CORE = [(0, 1), (1, 0), (2, 3), (3, 2)]
YHOP = [(0, 2), (2, 0), (1, 3), (3, 1)]


def over_pair(value, hops):
    return lax.ppermute(value, "pair", hops)


def over_virt(value, hops):
    return lax.ppermute(value, "virt", hops)


def tie(*values):
    return lax.optimization_barrier(values)


def products(table, slots, a, blocks, span, total=None, finish=False):
    blocks = [b if isinstance(b, list) else [b] for b in blocks]
    flat = [v for b in blocks for v in b]
    tiles, depth = flat[0].shape[:2]
    lo, hi = span
    columns = hi - lo
    row = a.shape[1] // 4

    def body(table_ref, a_ref, *refs):
        ins, outs = list(refs[: len(flat)]), refs[len(flat):]
        if total is not None:
            total_ref, outs = outs[0], outs[1:]
        groups = [[ins.pop(0) for _ in b] for b in blocks]

        def sums(i):
            here = pl.ds(pl.multiple_of(table_ref[8 + i] * row, row), row)
            left, right = [], []
            for slot, group in zip(slots, groups):
                cols = pl.ds(pl.multiple_of(table_ref[slot] * depth, depth), depth)
                left += [a_ref[t, here, cols] for t in range(tiles)]
                pieces = [r[:, :, lo:hi] if r.shape[2] > columns else r[...] for r in group]
                block = pieces[0] if len(pieces) == 1 else jnp.concatenate(pieces, axis=2)
                right.append(block.reshape(tiles * depth, columns))
            acc = jnp.dot(
                jnp.concatenate(left, axis=1), jnp.concatenate(right, axis=0), preferred_element_type=F32
            )
            return acc if total is None else acc + total_ref[i, :, lo:hi]

        if finish:

            @pl.loop(0, 2)
            def _(i):
                outs[0][i] = sums(i).astype(BF16)

            @pl.loop(2, 4)
            def _(i):
                outs[1][i - 2] = sums(i)

        else:

            @pl.loop(0, 4)
            def _(i):
                outs[0][i] = sums(i)

    vmem = pl.BlockSpec(memory_space=pltpu.VMEM)
    smem = pl.BlockSpec(memory_space=pltpu.SMEM)
    operands = [a] + flat + ([] if total is None else [total])
    if finish:
        out_shape = [
            jax.ShapeDtypeStruct((2, row, columns), BF16),
            jax.ShapeDtypeStruct((2, row, columns), F32),
        ]
    else:
        out_shape = [jax.ShapeDtypeStruct((4, row, columns), F32)]
    out = pl.pallas_call(
        body,
        in_specs=[smem] + [vmem] * len(operands),
        out_specs=[vmem] * len(out_shape),
        out_shape=out_shape,
        compiler_params=pltpu.CompilerParams(vmem_limit_bytes=20 * 2**20),
        cost_estimate=pl.CostEstimate(
            flops=2 * a.shape[1] * tiles * depth * len(blocks) * columns,
            bytes_accessed=2 * a.size + 2 * len(flat) * tiles * depth * columns,
            transcendentals=0,
        ),
    )(table, *operands)
    return out if finish else out[0]


def device_table():
    even, odd = dict(EVEN), dict(ODD)
    places = []
    for p in range(8):
        slots = [p, even[p], odd[p], odd[even[p]], even[odd[p]], even[odd[even[p]]], odd[even[odd[p]]]]
        places.append(slots + [sum(range(8)) - sum(slots)])
    every = [places[p] + [v ^ s for s in (3, 1, 2, 0)] for p in range(8) for v in range(4)]
    me = lax.axis_index(("pair", "virt"))
    return lax.dynamic_index_in_dim(jnp.array(every, jnp.int32), me, keepdims=False)


def scheduled(amplitudes, tile_mask, integrals, pair_energy, virt_energy):
    table = device_table()
    columns = integrals.shape[2]
    half, quarter = columns // 2, columns // 4
    span_a, span_b = (0, half), (half, columns)

    def part(v, span):
        return v[:, :, span[0] : span[1]]

    e1, o1 = over_pair(integrals, EVEN), over_pair(integrals, ODD)
    masked = amplitudes * tile_mask.astype(BF16)[:, :, None]
    a = masked.transpose(1, 0, 2)
    e1, a, table = tie(e1, a, table)

    def second(span):
        return over_pair(part(o1, span), EVEN), over_pair(part(e1, span), ODD)

    def third(e2, o2):
        return over_pair(o2, EVEN), over_pair(e2, ODD)

    def fourth(e3, o3):
        return [over_pair(o3[:, :, :quarter], EVEN), over_pair(e3[:, :, quarter:], ODD)]

    e2a, o2a = second(span_a)
    e2b, o2b = second(span_b)
    e3a, o3a = third(e2a, o2a)
    e3b, o3b = third(e2b, o2b)
    total = products(table, [0, 1, 2], a, [integrals, e1, o1], (0, columns))
    e3a, o3a, e2b, o2b, total = tie(e3a, o3a, e2b, o2b, total)
    lasta = fourth(e3a, o3a)
    lasta[0], lasta[1], e3b, o3b = tie(lasta[0], lasta[1], e3b, o3b)
    lastb = fourth(e3b, o3b)

    def shared(blocks, span):
        return products(table, [3, 4, 5, 6, 7], a, blocks, span, total=total, finish=True)

    send_a, keep_a = shared([e2a, o2a, e3a, o3a, lasta], span_a)
    got_a = over_virt(send_a, CORE)
    send_b, keep_b = shared([e2b, o2b, e3b, o3b, lastb], span_b)
    got_a, send_b = tie(got_a, send_b)
    there_a = over_virt((keep_a[0] + got_a[0].astype(F32)).astype(BF16), YHOP)
    got_b = over_virt(send_b, CORE)
    there_b = over_virt((keep_b[0] + got_b[0].astype(F32)).astype(BF16), YHOP)

    ladder = jnp.concatenate(
        [
            keep_a[1] + got_a[1].astype(F32) + there_a.astype(F32),
            keep_b[1] + got_b[1].astype(F32) + there_b.astype(F32),
        ],
        axis=1,
    )
    denom = virt_energy[None, :] - pair_energy[:, None]
    return (ladder / denom).astype(BF16)


def solution(mesh):
    placed = (
        P("pair", "virt", None),
        P("pair", "virt"),
        P("virt", "pair", None),
        P(("pair", "virt")),
        P(),
    )
    here = mesh.shape["pair"] == 8 and mesh.shape["virt"] == 4
    return jax.shard_map(
        scheduled if here else plain,
        mesh=mesh,
        in_specs=placed,
        out_specs=P(("pair", "virt"), None),
        check_vma=False,
    )
```

time: 134 us -> 72.9 us (0.54)
  waiting for transfers between devices: 100 us -> 32.9 us
  starting transfers between devices: 0.04 us -> 23.9 us
  between operations: 13.4 us -> 0.17 us
  matrix products: 9.32 us -> 0 us
  Pallas kernels: 0 us -> 8.14 us
  other arithmetic: 10.8 us -> 6.72 us
    all_gather x1 -> x0, waiting for transfers between devices: 69.4 us -> none  [on_device(): lax.all_gather(integrals, 'pair', axis=1, tiled=True)]
    ppermute x0 -> x18, waiting for transfers between devices: none -> 32.9 us  [the longest x14 21.9 us: over_pair(): return lax.ppermute(value, 'pair', hops)]
    reduce_scatter x1 -> x0, waiting for transfers between devices: 29.9 us -> none  [on_device(): lax.psum_scatter(partial_value.astype(jnp.bfloat16), 'virt', scatter_dime...]
    ppermute x0 -> x18, starting transfers between devices: none -> 23.9 us  [the longest x14 20.6 us: over_pair(): return lax.ppermute(value, 'pair', hops)]
    dot_general x1 -> x0, matrix products: 9.32 us -> none  [on_device(): jnp.einsum('ptk,tkn->pn', masked, lax.all_gather(integrals, 'pair', axis=...]
    pallas_call x0 -> x3, Pallas kernels: none -> 8.14 us  [products(): pl.pallas_call(body, in_specs=[smem] + [vmem] * len(operands), out_specs=...]
    mul x1 -> x0, other arithmetic: 8.03 us -> none  [on_device(): masked = amplitudes * tile_mask.astype(jnp.bfloat16)[:, :, None]]
    transpose x0 -> x1, other arithmetic: none -> 4.65 us  [scheduled(): a = masked.transpose(1, 0, 2)]
  transfers between devices with their start and end apart: 2 -> 18, of which waited for: 2 -> 14; matrix products, arithmetic and copies ran while one was open for 7% -> 9% of each run, Pallas kernels for 0% -> 8%
where the time goes in v2:
time: 72.9 us; the launch traced here: 72.7 us
  waiting for transfers between devices  32.9 us (45%)
  starting transfers between devices  23.9 us (33%)
  Pallas kernels  8.14 us (11%)
  other arithmetic  6.72 us (9%)
  local copies, waits for them, and re-layouts  0.82 us (1%)
    ppermute x14, waiting for transfers between devices, over_pair(): return lax.ppermute(value, 'pair', hops)  21.9 us
    ppermute x14, starting transfers between devices, over_pair(): return lax.ppermute(value, 'pair', hops)  20.6 us
    ppermute x4, waiting for transfers between devices, over_virt(): return lax.ppermute(value, 'virt', hops)  11.1 us
    pallas_call x3, Pallas kernels, products(): pl.pallas_call(body, in_specs=[smem] + [vmem] * len(operands), out_specs=...  8.14 us
    transpose x1, other arithmetic, scheduled(): a = masked.transpose(1, 0, 2)  4.65 us
    ppermute x4, starting transfers between devices, over_virt(): return lax.ppermute(value, 'virt', hops)  3.29 us
  transfers between devices with their start and end apart: 18, of which 14 were waited for; matrix products, arithmetic and copies ran while one was open for 9% of the time, Pallas kernels for 8%

profile of v2, /device:TPU:0, one launch (start us, length us, event | category | flops | bytes accessed | tf_op | source)
XLA Modules:
  0.0 72.7 jit_solution(8193570995793876569)
XLA Ops:
  0.0 3.0 %collective-permute-start = (bf16[2,128,1024]{2,1,0:T(8,128)(2,1)}, bf16[2,128,1024]{2,1,0:T(8,128)(2,1)S(1)}, u32[]{:S(2)}, u32[]{:S(2)}) collective-permute-start(bf16[2,128,1024]{2,1,0:T(8,128)(2,1)} %refs_0_.1), channel_id=1, source_target_pairs={{0,8},{8,0},{16,24},{24,16},{28,20},{20,28},{12,4},{4,12},{1,9},{9... | collective-permute-start | bytes 1572872 | tf_op jit(solution)/shard_map/ppermute | solution.py:33
  3.0 1.5 %collective-permute-start.1 = (bf16[2,128,1024]{2,1,0:T(8,128)(2,1)}, bf16[2,128,1024]{2,1,0:T(8,128)(2,1)S(1)}, u32[]{:S(2)}, u32[]{:S(2)}) collective-permute-start(bf16[2,128,1024]{2,1,0:T(8,128)(2,1)} %refs_0_.1), channel_id=1, source_target_pairs={{0,4},{8,16},{16,8},{24,28},{28,24},{20,12},{12,20},{4,0},{1,5},{9... | collective-permute-start | bytes 1572872 | tf_op jit(solution)/shard_map/ppermute | solution.py:33
  4.5 0.7 convert_element_type.40
  5.2 0.7 dynamic-slice_bitcast_fusion.table_ref
  5.9 0.0 copy-start
  5.9 4.7 %fusion.a_ref = bf16[2,1024,1024]{2,1,0:T(8,128)(2,1)S(1)} fusion(bf16[1024,2,1024]{2,1,0:T(2,128)(2,1)} %param.6, bf16[1024,2]{0,1:T(2,128)(2,1)S(1)} %convert_element_type.40), kind=kLoop, calls=%fused_computation.1 | loop fusion | flops 2097152 | bytes 8392704 | tf_op jit(solution)/shard_map/transpose | solution.py:135
  10.6 6.0 %collective-permute-done.1.refs_2_ = bf16[2,128,1024]{2,1,0:T(8,128)(2,1)S(1)} collective-permute-done((bf16[2,128,1024]{2,1,0:T(8,128)(2,1)}, bf16[2,128,1024]{2,1,0:T(8,128)(2,1)S(1)}, u32[]{:S(2)}, u32[]{:S(2)}) %collective-permute-start.1) | collective-permute-done | bytes 524320 | tf_op jit(solution)/shard_map/ppermute | solution.py:33
  16.7 1.5 %collective-permute-start.2 = (bf16[2,128,512]{2,1,0:T(8,128)(2,1)S(1)}, bf16[2,128,512]{2,1,0:T(8,128)(2,1)S(1)}, u32[]{:S(2)}, u32[]{:S(2)}) collective-permute-start(bf16[2,128,512]{2,1,0:T(8,128)(2,1)S(1)} %get-tuple-element.44), channel_id=1, source_target_pairs={{0,8},{8,0},{16,24},{24,16},{28,20},{20,28},{12,4},{4,12},{1,9},{9... | collective-permute-start | bytes 786440 | tf_op jit(solution)/shard_map/ppermute | solution.py:33
  18.2 0.0 collective-permute-done.refs_1_
  18.2 1.6 %collective-permute-start.3 = (bf16[2,128,512]{2,1,0:T(8,128)(2,1)S(1)}, bf16[2,128,512]{2,1,0:T(8,128)(2,1)S(1)}, u32[]{:S(2)}, u32[]{:S(2)}) collective-permute-start(bf16[2,128,512]{2,1,0:T(8,128)(2,1)S(1)} %get-tuple-element.42), channel_id=1, source_target_pairs={{0,4},{8,16},{16,8},{24,28},{28,24},{20,12},{12,20},{4,0},{1,5},{9... | collective-permute-start | bytes 786440 | tf_op jit(solution)/shard_map/ppermute | solution.py:33
  19.8 0.7 collective-permute-start.6
  20.4 1.5 %collective-permute-start.7 = (bf16[2,128,512]{2,1,0:T(8,128)(2,1)S(1)}, bf16[2,128,512]{2,1,0:T(8,128)(2,1)S(1)}, u32[]{:S(2)}, u32[]{:S(2)}) collective-permute-start(bf16[2,128,512]{2,1,0:T(8,128)(2,1)S(1)} %get-tuple-element.41), channel_id=1, source_target_pairs={{0,4},{8,16},{16,8},{24,28},{28,24},{20,12},{12,20},{4,0},{1,5},{9... | collective-permute-start | bytes 786440 | tf_op jit(solution)/shard_map/ppermute | solution.py:33
  21.9 4.0 %collective-permute-done.2.refs_0_ = bf16[2,128,512]{2,1,0:T(8,128)(2,1)S(1)} collective-permute-done((bf16[2,128,512]{2,1,0:T(8,128)(2,1)S(1)}, bf16[2,128,512]{2,1,0:T(8,128)(2,1)S(1)}, u32[]{:S(2)}, u32[]{:S(2)}) %collective-permute-start.2) | collective-permute-done | bytes 262176 | tf_op jit(solution)/shard_map/ppermute | solution.py:33
  26.0 1.5 %collective-permute-start.5 = (bf16[2,128,512]{2,1,0:T(8,128)(2,1)S(1)}, bf16[2,128,512]{2,1,0:T(8,128)(2,1)S(1)}, u32[]{:S(2)}, u32[]{:S(2)}) collective-permute-start(bf16[2,128,512]{2,1,0:T(8,128)(2,1)S(1)} %collective-permute-done.2.refs_0_), channel_id=1, source_target_pairs={{0,4},{8,16},{16,8},{24,28},{28,24},{20,12},{12,20},{4,0},{1,5},{9... | collective-permute-start | bytes 786440 | tf_op jit(solution)/shard_map/ppermute | solution.py:33
  27.5 0.1 collective-permute-done.3.refs_1_
  27.5 1.6 %collective-permute-start.4 = (bf16[2,128,512]{2,1,0:T(8,128)(2,1)S(1)}, bf16[2,128,512]{2,1,0:T(8,128)(2,1)S(1)}, u32[]{:S(2)}, u32[]{:S(2)}) collective-permute-start(bf16[2,128,512]{2,1,0:T(8,128)(2,1)S(1)} %collective-permute-done.3.refs_1_), channel_id=1, source_target_pairs={{0,8},{8,0},{16,24},{24,16},{28,20},{20,28},{12,4},{4,12},{1,9},{9... | collective-permute-start | bytes 786440 | tf_op jit(solution)/shard_map/ppermute | solution.py:33
  29.1 2.5 %collective-permute-done.6.refs_0_ = bf16[2,128,512]{2,1,0:T(8,128)(2,1)S(1)} collective-permute-done((bf16[2,128,512]{2,1,0:T(8,128)(2,1)S(1)}, bf16[2,128,512]{2,1,0:T(8,128)(2,1)S(1)}, u32[]{:S(2)}, u32[]{:S(2)}) %collective-permute-start.6) | collective-permute-done | bytes 262176 | tf_op jit(solution)/shard_map/ppermute | solution.py:33
  31.6 1.5 %collective-permute-start.11 = (bf16[2,128,512]{2,1,0:T(8,128)(2,1)S(1)}, bf16[2,128,512]{2,1,0:T(8,128)(2,1)S(1)}, u32[]{:S(2)}, u32[]{:S(2)}) collective-permute-start(bf16[2,128,512]{2,1,0:T(8,128)(2,1)S(1)} %collective-permute-done.6.refs_0_), channel_id=1, source_target_pairs={{0,4},{8,16},{16,8},{24,28},{28,24},{20,12},{12,20},{4,0},{1,5},{9... | collective-permute-start | bytes 786440 | tf_op jit(solution)/shard_map/ppermute | solution.py:33
  33.1 0.1 collective-permute-done.7.refs_1_
  33.2 1.6 %collective-permute-start.10 = (bf16[2,128,512]{2,1,0:T(8,128)(2,1)S(1)}, bf16[2,128,512]{2,1,0:T(8,128)(2,1)S(1)}, u32[]{:S(2)}, u32[]{:S(2)}) collective-permute-start(bf16[2,128,512]{2,1,0:T(8,128)(2,1)S(1)} %collective-permute-done.7.refs_1_), channel_id=1, source_target_pairs={{0,8},{8,0},{16,24},{24,16},{28,20},{20,28},{12,4},{4,12},{1,9},{9... | collective-permute-start | bytes 786440 | tf_op jit(solution)/shard_map/ppermute | solution.py:33
  34.7 0.0 copy-done
  34.7 2.9 %shard_map.64.refs_6_ = f32[4,256,1024]{2,1,0:T(8,128)S(1)} custom-call(s32[12]{0:T(128)S(1)} %dynamic-slice_bitcast_fusion.table_ref, bf16[2,1024,1024]{2,1,0:T(8,128)(2,1)S(1)} %fusion.a_ref, bf16[2,128,1024]{2,1,0:T(8,128)(2,1)S(1)} %copy-done, bf16[2,128,1024]{2,1,0:T(8,128)(2,1)S(1)} %collective-permute-done.refs_1_, ...), custom_call_target="tpu_custom_call" | custom-call | flops 1610612736 | bytes 5767168 | tf_op jit(solution)/shard_map/pallas_call | solution.py:98
  37.6 1.1 %collective-permute-done.5.refs_3_ = bf16[2,128,512]{2,1,0:T(8,128)(2,1)S(1)} collective-permute-done((bf16[2,128,512]{2,1,0:T(8,128)(2,1)S(1)}, bf16[2,128,512]{2,1,0:T(8,128)(2,1)S(1)}, u32[]{:S(2)}, u32[]{:S(2)}) %collective-permute-start.5) | collective-permute-done | bytes 262176 | tf_op jit(solution)/shard_map/ppermute | solution.py:33
  38.8 0.0 collective-permute-done.4.refs_2_
  38.8 0.6 collective-permute-start.8
  39.4 1.5 %collective-permute-start.9 = (bf16[2,128,256]{2,1,0:T(8,128)(2,1)S(1)}, bf16[2,128,256]{2,1,0:T(8,128)(2,1)S(1)}, u32[]{:S(2)}, u32[]{:S(2)}) collective-permute-start(bf16[2,128,256]{2,1,0:T(8,128)(2,1)S(1)} %slice.53), channel_id=1, source_target_pairs={{0,4},{8,16},{16,8},{24,28},{28,24},{20,12},{12,20},{4,0},{1,5},{9... | collective-permute-start | bytes 393224 | tf_op jit(solution)/shard_map/ppermute | solution.py:33
  40.9 2.5 %collective-permute-done.11.refs_3_ = bf16[2,128,512]{2,1,0:T(8,128)(2,1)S(1)} collective-permute-done((bf16[2,128,512]{2,1,0:T(8,128)(2,1)S(1)}, bf16[2,128,512]{2,1,0:T(8,128)(2,1)S(1)}, u32[]{:S(2)}, u32[]{:S(2)}) %collective-permute-start.11) | collective-permute-done | bytes 262176 | tf_op jit(solution)/shard_map/ppermute | solution.py:33
  43.4 0.0 collective-permute-done.10.refs_2_
  43.4 0.4 collective-permute-done.8.refs_4_
  43.8 1.0 %collective-permute-done.9.refs_5_ = bf16[2,128,256]{2,1,0:T(8,128)(2,1)S(1)} collective-permute-done((bf16[2,128,256]{2,1,0:T(8,128)(2,1)S(1)}, bf16[2,128,256]{2,1,0:T(8,128)(2,1)S(1)}, u32[]{:S(2)}, u32[]{:S(2)}) %collective-permute-start.9) | collective-permute-done | bytes 131104 | tf_op jit(solution)/shard_map/ppermute | solution.py:33
  44.8 2.6 %shard_map.65 = (bf16[2,256,512]{2,1,0:T(8,128)(2,1)S(1)}, f32[2,256,512]{2,1,0:T(8,128)S(1)}) custom-call(s32[12]{0:T(128)S(1)} %dynamic-slice_bitcast_fusion.table_ref, bf16[2,1024,1024]{2,1,0:T(8,128)(2,1)S(1)} %fusion.a_ref, bf16[2,128,512]{2,1,0:T(8,128)(2,1)S(1)} %collective-permute-done.2.refs_0_, ...), custom_call_target="tpu_custom_call" | custom-call | flops 1342177280 | bytes 5767168 | tf_op jit(solution)/shard_map/pallas_call | solution.py:98
  47.5 0.1 collective-permute-start.12
  47.6 1.1 %collective-permute-start.13 = (bf16[2,128,256]{2,1,0:T(8,128)(2,1)S(1)}, bf16[2,128,256]{2,1,0:T(8,128)(2,1)S(1)}, u32[]{:S(2)}, u32[]{:S(2)}) collective-permute-start(bf16[2,128,256]{2,1,0:T(8,128)(2,1)S(1)} %slice.55), channel_id=1, source_target_pairs={{0,8},{8,0},{16,24},{24,16},{28,20},{20,28},{12,4},{4,12},{1,9},{9... | collective-permute-start | bytes 393224 | tf_op jit(solution)/shard_map/ppermute | solution.py:33
  48.7 1.5 %collective-permute-start.14 = (bf16[2,128,256]{2,1,0:T(8,128)(2,1)S(1)}, bf16[2,128,256]{2,1,0:T(8,128)(2,1)S(1)}, u32[]{:S(2)}, u32[]{:S(2)}) collective-permute-start(bf16[2,128,256]{2,1,0:T(8,128)(2,1)S(1)} %slice.56), channel_id=1, source_target_pairs={{0,4},{8,16},{16,8},{24,28},{28,24},{20,12},{12,20},{4,0},{1,5},{9... | collective-permute-start | bytes 393224 | tf_op jit(solution)/shard_map/ppermute | solution.py:33
  50.2 3.4 %collective-permute-done.13.refs_4_ = bf16[2,128,256]{2,1,0:T(8,128)(2,1)S(1)} collective-permute-done((bf16[2,128,256]{2,1,0:T(8,128)(2,1)S(1)}, bf16[2,128,256]{2,1,0:T(8,128)(2,1)S(1)}, u32[]{:S(2)}, u32[]{:S(2)}) %collective-permute-start.13) | collective-permute-done | bytes 131104 | tf_op jit(solution)/shard_map/ppermute | solution.py:33
  53.5 0.8 %collective-permute-done.14.refs_5_ = bf16[2,128,256]{2,1,0:T(8,128)(2,1)S(1)} collective-permute-done((bf16[2,128,256]{2,1,0:T(8,128)(2,1)S(1)}, bf16[2,128,256]{2,1,0:T(8,128)(2,1)S(1)}, u32[]{:S(2)}, u32[]{:S(2)}) %collective-permute-start.14) | collective-permute-done | bytes 131104 | tf_op jit(solution)/shard_map/ppermute | solution.py:33
  54.3 2.6 %shard_map.66 = (bf16[2,256,512]{2,1,0:T(8,128)(2,1)S(1)}, f32[2,256,512]{2,1,0:T(8,128)S(1)}) custom-call(s32[12]{0:T(128)S(1)} %dynamic-slice_bitcast_fusion.table_ref, bf16[2,1024,1024]{2,1,0:T(8,128)(2,1)S(1)} %fusion.a_ref, bf16[2,128,512]{2,1,0:T(8,128)(2,1)S(1)} %collective-permute-done.6.refs_0_, ...), custom_call_target="tpu_custom_call" | custom-call | flops 1342177280 | bytes 5767168 | tf_op jit(solution)/shard_map/pallas_call | solution.py:98
  57.0 0.0 copy-start.1
  57.0 0.0 copy-start.2
  57.0 0.0 collective-permute-done.12
  57.0 0.1 collective-permute-start.16
  57.1 0.1 fusion.2
  57.2 1.6 %collective-permute-start.15 = (bf16[256,512]{1,0:T(8,128)(2,1)S(1)}, bf16[256,512]{1,0:T(8,128)(2,1)S(1)}, u32[]{:S(2)}, u32[]{:S(2)}) collective-permute-start(bf16[256,512]{1,0:T(8,128)(2,1)S(1)} %fusion.2), channel_id=1, source_target_pairs={{0,2},{2,0},{1,3},{3,1},{4,6},{6,4},{5,7},{7,5},{8,10},{10,8},{9,1... | collective-permute-start | bytes 786440 | tf_op jit(solution)/shard_map/ppermute | solution.py:37
  58.7 0.2 collective-permute-done.16
  59.0 0.1 fusion.3
  59.0 1.6 %collective-permute-start.17 = (bf16[256,512]{1,0:T(8,128)(2,1)S(1)}, bf16[256,512]{1,0:T(8,128)(2,1)S(1)}, u32[]{:S(2)}, u32[]{:S(2)}) collective-permute-start(bf16[256,512]{1,0:T(8,128)(2,1)S(1)} %fusion.3), channel_id=1, source_target_pairs={{0,2},{2,0},{1,3},{3,1},{4,6},{6,4},{5,7},{7,5},{8,10},{10,8},{9,1... | collective-permute-start | bytes 786440 | tf_op jit(solution)/shard_map/ppermute | solution.py:37
  60.6 5.7 %collective-permute-done.15 = bf16[256,512]{1,0:T(8,128)(2,1)S(1)} collective-permute-done((bf16[256,512]{1,0:T(8,128)(2,1)S(1)}, bf16[256,512]{1,0:T(8,128)(2,1)S(1)}, u32[]{:S(2)}, u32[]{:S(2)}) %collective-permute-start.15) | collective-permute-done | bytes 262176 | tf_op jit(solution)/shard_map/ppermute | solution.py:37
  66.3 0.1 bitcast_add_fusion.1
  66.4 5.1 %collective-permute-done.17 = bf16[256,512]{1,0:T(8,128)(2,1)S(1)} collective-permute-done((bf16[256,512]{1,0:T(8,128)(2,1)S(1)}, bf16[256,512]{1,0:T(8,128)(2,1)S(1)}, u32[]{:S(2)}, u32[]{:S(2)}) %collective-permute-start.17) | collective-permute-done | bytes 262176 | tf_op jit(solution)/shard_map/ppermute | solution.py:37
  71.5 0.1 bitcast_add_fusion
  71.7 0.0 copy-done.1
  71.7 0.0 copy-done.2
  71.7 1.0 %fusion.1 = bf16[256,1024]{1,0:T(8,128)(2,1)} fusion(f32[256,512]{1,0:T(8,128)S(1)} %bitcast_add_fusion, f32[256,512]{1,0:T(8,128)S(1)} %bitcast_add_fusion.1, f32[256]{0:T(256)S(1)} %copy-done.2, f32[1024]{0:T(1024)S(1)} %copy-done.1), kind=kLoop, calls=%fused_computation.3 | loop fusion | flops 1048576 | bytes 1577984 | tf_op jit(solution)/shard_map/convert_element_type | solution.py:176
  (6 shorter events, 0.1 us)
Async XLA Ops:
  0.0 18.2 %collective-permute-start = (bf16[2,128,1024]{2,1,0:T(8,128)(2,1)}, bf16[2,128,1024]{2,1,0:T(8,128)(2,1)S(1)}, u32[]{:S(2)}, u32[]{:S(2)}) collective-permute-start(bf16[2,128,1024]{2,1,0:T(8,128)(2,1)} %refs_0_.1), channel_id=1, source_target_pairs={{0,8},{8,0},{16,24},{24,16},{28,20},{20,28},{12,4},{4,12},{1,9},{9... | collective-permute-start | bytes 1572872 | tf_op jit(solution)/shard_map/ppermute | solution.py:33
  3.0 13.6 %collective-permute-start.1 = (bf16[2,128,1024]{2,1,0:T(8,128)(2,1)}, bf16[2,128,1024]{2,1,0:T(8,128)(2,1)S(1)}, u32[]{:S(2)}, u32[]{:S(2)}) collective-permute-start(bf16[2,128,1024]{2,1,0:T(8,128)(2,1)} %refs_0_.1), channel_id=1, source_target_pairs={{0,4},{8,16},{16,8},{24,28},{28,24},{20,12},{12,20},{4,0},{1,5},{9... | collective-permute-start | bytes 1572872 | tf_op jit(solution)/shard_map/ppermute | solution.py:33
  5.9 28.8 %copy-start = (bf16[2,128,1024]{2,1,0:T(8,128)(2,1)S(1)}, bf16[2,128,1024]{2,1,0:T(8,128)(2,1)}, u32[]{:S(2)}) copy-start(bf16[2,128,1024]{2,1,0:T(8,128)(2,1)} %refs_0_.1) | copy-start | bytes 1572868
  16.7 9.3 %collective-permute-start.2 = (bf16[2,128,512]{2,1,0:T(8,128)(2,1)S(1)}, bf16[2,128,512]{2,1,0:T(8,128)(2,1)S(1)}, u32[]{:S(2)}, u32[]{:S(2)}) collective-permute-start(bf16[2,128,512]{2,1,0:T(8,128)(2,1)S(1)} %get-tuple-element.44), channel_id=1, source_target_pairs={{0,8},{8,0},{16,24},{24,16},{28,20},{20,28},{12,4},{4,12},{1,9},{9... | collective-permute-start | bytes 786440 | tf_op jit(solution)/shard_map/ppermute | solution.py:33
  18.2 9.3 %collective-permute-start.3 = (bf16[2,128,512]{2,1,0:T(8,128)(2,1)S(1)}, bf16[2,128,512]{2,1,0:T(8,128)(2,1)S(1)}, u32[]{:S(2)}, u32[]{:S(2)}) collective-permute-start(bf16[2,128,512]{2,1,0:T(8,128)(2,1)S(1)} %get-tuple-element.42), channel_id=1, source_target_pairs={{0,4},{8,16},{16,8},{24,28},{28,24},{20,12},{12,20},{4,0},{1,5},{9... | collective-permute-start | bytes 786440 | tf_op jit(solution)/shard_map/ppermute | solution.py:33
  19.8 11.8 %collective-permute-start.6 = (bf16[2,128,512]{2,1,0:T(8,128)(2,1)S(1)}, bf16[2,128,512]{2,1,0:T(8,128)(2,1)S(1)}, u32[]{:S(2)}, u32[]{:S(2)}) collective-permute-start(bf16[2,128,512]{2,1,0:T(8,128)(2,1)S(1)} %get-tuple-element.43), channel_id=1, source_target_pairs={{0,8},{8,0},{16,24},{24,16},{28,20},{20,28},{12,4},{4,12},{1,9},{9... | collective-permute-start | bytes 786440 | tf_op jit(solution)/shard_map/ppermute | solution.py:33
  20.4 12.7 %collective-permute-start.7 = (bf16[2,128,512]{2,1,0:T(8,128)(2,1)S(1)}, bf16[2,128,512]{2,1,0:T(8,128)(2,1)S(1)}, u32[]{:S(2)}, u32[]{:S(2)}) collective-permute-start(bf16[2,128,512]{2,1,0:T(8,128)(2,1)S(1)} %get-tuple-element.41), channel_id=1, source_target_pairs={{0,4},{8,16},{16,8},{24,28},{28,24},{20,12},{12,20},{4,0},{1,5},{9... | collective-permute-start | bytes 786440 | tf_op jit(solution)/shard_map/ppermute | solution.py:33
  26.0 12.8 %collective-permute-start.5 = (bf16[2,128,512]{2,1,0:T(8,128)(2,1)S(1)}, bf16[2,128,512]{2,1,0:T(8,128)(2,1)S(1)}, u32[]{:S(2)}, u32[]{:S(2)}) collective-permute-start(bf16[2,128,512]{2,1,0:T(8,128)(2,1)S(1)} %collective-permute-done.2.refs_0_), channel_id=1, source_target_pairs={{0,4},{8,16},{16,8},{24,28},{28,24},{20,12},{12,20},{4,0},{1,5},{9... | collective-permute-start | bytes 786440 | tf_op jit(solution)/shard_map/ppermute | solution.py:33
  27.5 11.2 %collective-permute-start.4 = (bf16[2,128,512]{2,1,0:T(8,128)(2,1)S(1)}, bf16[2,128,512]{2,1,0:T(8,128)(2,1)S(1)}, u32[]{:S(2)}, u32[]{:S(2)}) collective-permute-start(bf16[2,128,512]{2,1,0:T(8,128)(2,1)S(1)} %collective-permute-done.3.refs_1_), channel_id=1, source_target_pairs={{0,8},{8,0},{16,24},{24,16},{28,20},{20,28},{12,4},{4,12},{1,9},{9... | collective-permute-start | bytes 786440 | tf_op jit(solution)/shard_map/ppermute | solution.py:33
  31.6 11.8 %collective-permute-start.11 = (bf16[2,128,512]{2,1,0:T(8,128)(2,1)S(1)}, bf16[2,128,512]{2,1,0:T(8,128)(2,1)S(1)}, u32[]{:S(2)}, u32[]{:S(2)}) collective-permute-start(bf16[2,128,512]{2,1,0:T(8,128)(2,1)S(1)} %collective-permute-done.6.refs_0_), channel_id=1, source_target_pairs={{0,4},{8,16},{16,8},{24,28},{28,24},{20,12},{12,20},{4,0},{1,5},{9... | collective-permute-start | bytes 786440 | tf_op jit(solution)/shard_map/ppermute | solution.py:33
  33.2 10.3 %collective-permute-start.10 = (bf16[2,128,512]{2,1,0:T(8,128)(2,1)S(1)}, bf16[2,128,512]{2,1,0:T(8,128)(2,1)S(1)}, u32[]{:S(2)}, u32[]{:S(2)}) collective-permute-start(bf16[2,128,512]{2,1,0:T(8,128)(2,1)S(1)} %collective-permute-done.7.refs_1_), channel_id=1, source_target_pairs={{0,8},{8,0},{16,24},{24,16},{28,20},{20,28},{12,4},{4,12},{1,9},{9... | collective-permute-start | bytes 786440 | tf_op jit(solution)/shard_map/ppermute | solution.py:33
  38.8 5.0 %collective-permute-start.8 = (bf16[2,128,256]{2,1,0:T(8,128)(2,1)S(1)}, bf16[2,128,256]{2,1,0:T(8,128)(2,1)S(1)}, u32[]{:S(2)}, u32[]{:S(2)}) collective-permute-start(bf16[2,128,256]{2,1,0:T(8,128)(2,1)S(1)} %slice.52), channel_id=1, source_target_pairs={{0,8},{8,0},{16,24},{24,16},{28,20},{20,28},{12,4},{4,12},{1,9},{9... | collective-permute-start | bytes 393224 | tf_op jit(solution)/shard_map/ppermute | solution.py:33
  39.4 5.4 %collective-permute-start.9 = (bf16[2,128,256]{2,1,0:T(8,128)(2,1)S(1)}, bf16[2,128,256]{2,1,0:T(8,128)(2,1)S(1)}, u32[]{:S(2)}, u32[]{:S(2)}) collective-permute-start(bf16[2,128,256]{2,1,0:T(8,128)(2,1)S(1)} %slice.53), channel_id=1, source_target_pairs={{0,4},{8,16},{16,8},{24,28},{28,24},{20,12},{12,20},{4,0},{1,5},{9... | collective-permute-start | bytes 393224 | tf_op jit(solution)/shard_map/ppermute | solution.py:33
  47.5 9.5 %collective-permute-start.12 = (bf16[2,256,512]{2,1,0:T(8,128)(2,1)S(1)}, bf16[2,256,512]{2,1,0:T(8,128)(2,1)S(1)}, u32[]{:S(2)}, u32[]{:S(2)}) collective-permute-start(bf16[2,256,512]{2,1,0:T(8,128)(2,1)S(1)} %get-tuple-element.32), channel_id=1, source_target_pairs={{0,1},{1,0},{2,3},{3,2},{4,5},{5,4},{6,7},{7,6},{8,9},{9,8},{10,11... | collective-permute-start | bytes 1572872 | tf_op jit(solution)/shard_map/ppermute | solution.py:37
  47.6 6.0 %collective-permute-start.13 = (bf16[2,128,256]{2,1,0:T(8,128)(2,1)S(1)}, bf16[2,128,256]{2,1,0:T(8,128)(2,1)S(1)}, u32[]{:S(2)}, u32[]{:S(2)}) collective-permute-start(bf16[2,128,256]{2,1,0:T(8,128)(2,1)S(1)} %slice.55), channel_id=1, source_target_pairs={{0,8},{8,0},{16,24},{24,16},{28,20},{20,28},{12,4},{4,12},{1,9},{9... | collective-permute-start | bytes 393224 | tf_op jit(solution)/shard_map/ppermute | solution.py:33
  48.7 5.6 %collective-permute-start.14 = (bf16[2,128,256]{2,1,0:T(8,128)(2,1)S(1)}, bf16[2,128,256]{2,1,0:T(8,128)(2,1)S(1)}, u32[]{:S(2)}, u32[]{:S(2)}) collective-permute-start(bf16[2,128,256]{2,1,0:T(8,128)(2,1)S(1)} %slice.56), channel_id=1, source_target_pairs={{0,4},{8,16},{16,8},{24,28},{28,24},{20,12},{12,20},{4,0},{1,5},{9... | collective-permute-start | bytes 393224 | tf_op jit(solution)/shard_map/ppermute | solution.py:33
  57.0 14.7 %copy-start.1 = (f32[1024]{0:T(1024)S(1)}, f32[1024]{0:T(1024)}, u32[]{:S(2)}) copy-start(f32[1024]{0:T(1024)} %param.10) | copy-start | bytes 12292
  57.0 14.7 %copy-start.2 = (f32[256]{0:T(256)S(1)}, f32[256]{0:T(256)}, u32[]{:S(2)}) copy-start(f32[256]{0:T(256)} %param.9) | copy-start | bytes 3076
  57.0 2.0 %collective-permute-start.16 = (bf16[2,256,512]{2,1,0:T(8,128)(2,1)S(1)}, bf16[2,256,512]{2,1,0:T(8,128)(2,1)S(1)}, u32[]{:S(2)}, u32[]{:S(2)}) collective-permute-start(bf16[2,256,512]{2,1,0:T(8,128)(2,1)S(1)} %get-tuple-element.40), channel_id=1, source_target_pairs={{0,1},{1,0},{2,3},{3,2},{4,5},{5,4},{6,7},{7,6},{8,9},{9,8},{10,11... | collective-permute-start | bytes 1572872 | tf_op jit(solution)/shard_map/ppermute | solution.py:37
  57.2 9.2 %collective-permute-start.15 = (bf16[256,512]{1,0:T(8,128)(2,1)S(1)}, bf16[256,512]{1,0:T(8,128)(2,1)S(1)}, u32[]{:S(2)}, u32[]{:S(2)}) collective-permute-start(bf16[256,512]{1,0:T(8,128)(2,1)S(1)} %fusion.2), channel_id=1, source_target_pairs={{0,2},{2,0},{1,3},{3,1},{4,6},{6,4},{5,7},{7,5},{8,10},{10,8},{9,1... | collective-permute-start | bytes 786440 | tf_op jit(solution)/shard_map/ppermute | solution.py:37
  59.0 12.5 %collective-permute-start.17 = (bf16[256,512]{1,0:T(8,128)(2,1)S(1)}, bf16[256,512]{1,0:T(8,128)(2,1)S(1)}, u32[]{:S(2)}, u32[]{:S(2)}) collective-permute-start(bf16[256,512]{1,0:T(8,128)(2,1)S(1)} %fusion.3), channel_id=1, source_target_pairs={{0,2},{2,0},{1,3},{3,1},{4,6},{6,4},{5,7},{7,5},{8,10},{10,8},{9,1... | collective-permute-start | bytes 786440 | tf_op jit(solution)/shard_map/ppermute | solution.py:37

commit v3 on v2

--- a/solution.py
+++ b/solution.py
@@ -1,3 +1,5 @@
+import functools
+
 import jax
 import jax.numpy as jnp
 from jax import lax
@@ -41,7 +43,7 @@
     return lax.optimization_barrier(values)
 
 
-def products(table, slots, a, blocks, span, total=None, finish=False):
+def products(table, slots, a, blocks, span, total=None, finish=False, weight=1):
     blocks = [b if isinstance(b, list) else [b] for b in blocks]
     flat = [v for b in blocks for v in b]
     tiles, depth = flat[0].shape[:2]
@@ -54,45 +56,30 @@
         if total is not None:
             total_ref, outs = outs[0], outs[1:]
         groups = [[ins.pop(0) for _ in b] for b in blocks]
-
-        def sums(i):
+        for i in range(4):
             here = pl.ds(pl.multiple_of(table_ref[8 + i] * row, row), row)
             left, right = [], []
             for slot, group in zip(slots, groups):
                 cols = pl.ds(pl.multiple_of(table_ref[slot] * depth, depth), depth)
                 left += [a_ref[t, here, cols] for t in range(tiles)]
-                pieces = [r[:, :, lo:hi] if r.shape[2] > columns else r[...] for r in group]
+                pieces = [r[:, :, lo:hi] if len(group) == 1 and r.shape[2] > columns else r[...] for r in group]
                 block = pieces[0] if len(pieces) == 1 else jnp.concatenate(pieces, axis=2)
                 right.append(block.reshape(tiles * depth, columns))
             acc = jnp.dot(
                 jnp.concatenate(left, axis=1), jnp.concatenate(right, axis=0), preferred_element_type=F32
             )
-            return acc if total is None else acc + total_ref[i, :, lo:hi]
-
-        if finish:
-
-            @pl.loop(0, 2)
-            def _(i):
-                outs[0][i] = sums(i).astype(BF16)
-
-            @pl.loop(2, 4)
-            def _(i):
-                outs[1][i - 2] = sums(i)
-
-        else:
-
-            @pl.loop(0, 4)
-            def _(i):
-                outs[0][i] = sums(i)
+            if total is not None:
+                acc += total_ref[i, :, lo:hi] if total.shape[2] > columns else total_ref[i]
+            if not finish:
+                outs[0][i] = acc
+            else:
+                outs[i][...] = acc.astype(outs[i].dtype)
 
     vmem = pl.BlockSpec(memory_space=pltpu.VMEM)
     smem = pl.BlockSpec(memory_space=pltpu.SMEM)
     operands = [a] + flat + ([] if total is None else [total])
     if finish:
-        out_shape = [
-            jax.ShapeDtypeStruct((2, row, columns), BF16),
-            jax.ShapeDtypeStruct((2, row, columns), F32),
-        ]
+        out_shape = [jax.ShapeDtypeStruct((row, columns), t) for t in (BF16, BF16, F32, F32)]
     else:
         out_shape = [jax.ShapeDtypeStruct((4, row, columns), F32)]
     out = pl.pallas_call(
@@ -102,7 +89,7 @@
         out_shape=out_shape,
         compiler_params=pltpu.CompilerParams(vmem_limit_bytes=20 * 2**20),
         cost_estimate=pl.CostEstimate(
-            flops=2 * a.shape[1] * tiles * depth * len(blocks) * columns,
+            flops=weight * 2 * a.shape[1] * tiles * depth * len(blocks) * columns,
             bytes_accessed=2 * a.size + 2 * len(flat) * tiles * depth * columns,
             transcendentals=0,
         ),
@@ -121,11 +108,10 @@
     return lax.dynamic_index_in_dim(jnp.array(every, jnp.int32), me, keepdims=False)
 
 
-def scheduled(amplitudes, tile_mask, integrals, pair_energy, virt_energy):
+def scheduled(cut, amplitudes, tile_mask, integrals, pair_energy, virt_energy):
     table = device_table()
     columns = integrals.shape[2]
-    half, quarter = columns // 2, columns // 4
-    span_a, span_b = (0, half), (half, columns)
+    span_a, span_b = (0, cut), (cut, columns)
 
     def part(v, span):
         return v[:, :, span[0] : span[1]]
@@ -142,33 +128,39 @@
         return over_pair(o2, EVEN), over_pair(e2, ODD)
 
     def fourth(e3, o3):
-        return [over_pair(o3[:, :, :quarter], EVEN), over_pair(e3[:, :, quarter:], ODD)]
+        middle = e3.shape[2] // 2
+        return [over_pair(o3[:, :, :middle], EVEN), over_pair(e3[:, :, middle:], ODD)]
 
     e2a, o2a = second(span_a)
     e2b, o2b = second(span_b)
+    total = products(table, [0, 1, 2], a, [integrals, e1, o1], (0, columns))
+    o2a, e2a, total = tie(o2a, e2a, total)
     e3a, o3a = third(e2a, o2a)
     e3b, o3b = third(e2b, o2b)
-    total = products(table, [0, 1, 2], a, [integrals, e1, o1], (0, columns))
-    e3a, o3a, e2b, o2b, total = tie(e3a, o3a, e2b, o2b, total)
-    lasta = fourth(e3a, o3a)
-    lasta[0], lasta[1], e3b, o3b = tie(lasta[0], lasta[1], e3b, o3b)
-    lastb = fourth(e3b, o3b)
+    total = products(table, [3, 4], a, [[e2a, e2b], [o2a, o2b]], (0, columns), total=total)
+    e3a, o3a, total = tie(e3a, o3a, total)
+    last_a = fourth(e3a, o3a)
 
-    def shared(blocks, span):
-        return products(table, [3, 4, 5, 6, 7], a, blocks, span, total=total, finish=True)
-
-    send_a, keep_a = shared([e2a, o2a, e3a, o3a, lasta], span_a)
-    got_a = over_virt(send_a, CORE)
-    send_b, keep_b = shared([e2b, o2b, e3b, o3b, lastb], span_b)
-    got_a, send_b = tie(got_a, send_b)
-    there_a = over_virt((keep_a[0] + got_a[0].astype(F32)).astype(BF16), YHOP)
-    got_b = over_virt(send_b, CORE)
-    there_b = over_virt((keep_b[0] + got_b[0].astype(F32)).astype(BF16), YHOP)
+    total_a = products(table, [5, 6], a, [e3a, o3a], span_a, total=total, weight=20)
+    e3b, o3b, total_a = tie(e3b, o3b, total_a)
+    last_b = fourth(e3b, o3b)
+    total_b = products(table, [5, 6], a, [e3b, o3b], span_b, total=total)
+    there_a, here_a, keep_there_a, keep_here_a = products(
+        table, [7], a, [last_a], span_a, total=total_a, finish=True
+    )
+    got_there_a, got_here_a = over_virt(there_a, CORE), over_virt(here_a, CORE)
+    there_b, here_b, keep_there_b, keep_here_b = products(
+        table, [7], a, [last_b], span_b, total=total_b, finish=True, weight=20
+    )
+    got_there_a, there_b = tie(got_there_a, there_b)
+    from_y_a = over_virt((keep_there_a + got_there_a.astype(F32)).astype(BF16), YHOP)
+    got_there_b, got_here_b = over_virt(there_b, CORE), over_virt(here_b, CORE)
+    from_y_b = over_virt((keep_there_b + got_there_b.astype(F32)).astype(BF16), YHOP)
 
     ladder = jnp.concatenate(
         [
-            keep_a[1] + got_a[1].astype(F32) + there_a.astype(F32),
-            keep_b[1] + got_b[1].astype(F32) + there_b.astype(F32),
+            keep_here_a + got_here_a.astype(F32) + from_y_a.astype(F32),
+            keep_here_b + got_here_b.astype(F32) + from_y_b.astype(F32),
         ],
         axis=1,
     )
@@ -186,7 +178,7 @@
     )
     here = mesh.shape["pair"] == 8 and mesh.shape["virt"] == 4
     return jax.shard_map(
-        scheduled if here else plain,
+        functools.partial(scheduled, 512) if here else plain,
         mesh=mesh,
         in_specs=placed,
         out_specs=P(("pair", "virt"), None),

time: 72.9 us -> 67 us (0.919)
  waiting for transfers between devices: 32.9 us -> 23.1 us
  starting transfers between devices: 23.9 us -> 27.1 us
    ppermute x14, waiting for transfers between devices: 21.9 us -> 11.8 us  [over_pair(): return lax.ppermute(value, 'pair', hops)]
    ppermute x14, starting transfers between devices: 20.6 us -> 24 us  [over_pair(): return lax.ppermute(value, 'pair', hops)]
    pallas_call x3 -> x6, Pallas kernels: 8.14 us -> 8.8 us  [products(): pl.pallas_call(body, in_specs=[smem] + [vmem] * len(operands), out_specs=...]
    ppermute x4 -> x6, waiting for transfers between devices: 11.1 us -> 11.2 us  [over_virt(): return lax.ppermute(value, 'virt', hops)]
    ppermute x4 -> x6, starting transfers between devices: 3.29 us -> 3.16 us  [over_virt(): return lax.ppermute(value, 'virt', hops)]
  transfers between devices with their start and end apart: 18 -> 20, of which waited for: 14 -> 9; matrix products, arithmetic and copies ran while one was open for 9% -> 10% of each run, Pallas kernels for 8% -> 13%
where the time goes in v3:
time: 67 us; the launch traced here: 66.7 us
  starting transfers between devices  27.1 us (40%)
  waiting for transfers between devices  23.1 us (34%)
  Pallas kernels  8.8 us (13%)
  other arithmetic  6.72 us (10%)
  local copies, waits for them, and re-layouts  0.82 us (1%)
    ppermute x14, starting transfers between devices, over_pair(): return lax.ppermute(value, 'pair', hops)  24 us
    ppermute x14, waiting for transfers between devices, over_pair(): return lax.ppermute(value, 'pair', hops)  11.8 us
    ppermute x6, waiting for transfers between devices, over_virt(): return lax.ppermute(value, 'virt', hops)  11.2 us
    pallas_call x6, Pallas kernels, products(): pl.pallas_call(body, in_specs=[smem] + [vmem] * len(operands), out_specs=...  8.8 us
    transpose x1, other arithmetic, scheduled(): a = masked.transpose(1, 0, 2)  4.65 us
    ppermute x6, starting transfers between devices, over_virt(): return lax.ppermute(value, 'virt', hops)  3.16 us
  transfers between devices with their start and end apart: 20, of which 9 were waited for; matrix products, arithmetic and copies ran while one was open for 10% of the time, Pallas kernels for 13%

profile of v3, /device:TPU:0, one launch (start us, length us, event | category | flops | bytes accessed | tf_op | source)
XLA Modules:
  0.0 66.7 jit_solution(5721356997502864463)
XLA Ops:
  0.0 3.0 %collective-permute-start = (bf16[2,128,1024]{2,1,0:T(8,128)(2,1)}, bf16[2,128,1024]{2,1,0:T(8,128)(2,1)S(1)}, u32[]{:S(2)}, u32[]{:S(2)}) collective-permute-start(bf16[2,128,1024]{2,1,0:T(8,128)(2,1)} %refs_0_.1), channel_id=1, source_target_pairs={{0,8},{8,0},{16,24},{24,16},{28,20},{20,28},{12,4},{4,12},{1,9},{9... | collective-permute-start | bytes 1572872 | tf_op jit(solution)/shard_map/ppermute | solution.py:35
  3.0 1.5 %collective-permute-start.2 = (bf16[2,128,1024]{2,1,0:T(8,128)(2,1)}, bf16[2,128,1024]{2,1,0:T(8,128)(2,1)S(1)}, u32[]{:S(2)}, u32[]{:S(2)}) collective-permute-start(bf16[2,128,1024]{2,1,0:T(8,128)(2,1)} %refs_0_.1), channel_id=1, source_target_pairs={{0,4},{8,16},{16,8},{24,28},{28,24},{20,12},{12,20},{4,0},{1,5},{9... | collective-permute-start | bytes 1572872 | tf_op jit(solution)/shard_map/ppermute | solution.py:35
  4.5 0.7 %convert_element_type.30 = bf16[1024,2]{0,1:T(2,128)(2,1)S(1)} convert(s32[1024,2]{0,1:T(2,128)} %param.7) | non-fusion elementwise | flops 2048 | bytes 12288 | tf_op jit(solution)/shard_map/convert_element_type | solution.py:120
  5.2 0.7 %dynamic-slice_bitcast_fusion.table_ref = s32[12]{0:T(128)S(1)} fusion(s32[32,12]{1,0:T(8,128)} %constant.19.clone, s32[]{:T(128)S(6)} %select_n.4), kind=kLoop, calls=%fused_computation.8 | loop fusion | bytes 100 | tf_op jit(solution)/shard_map/jit(dynamic_index_in_dim)/squeeze | solution.py:108
  5.9 0.0 copy-start
  5.9 4.7 %fusion.a_ref = bf16[2,1024,1024]{2,1,0:T(8,128)(2,1)S(1)} fusion(bf16[1024,2,1024]{2,1,0:T(2,128)(2,1)} %param.6, bf16[1024,2]{0,1:T(2,128)(2,1)S(1)} %convert_element_type.30), kind=kLoop, calls=%fused_computation.1 | loop fusion | flops 2097152 | bytes 8392704 | tf_op jit(solution)/shard_map/transpose | solution.py:121
  10.6 4.6 %collective-permute-done.refs_1_ = bf16[2,128,1024]{2,1,0:T(8,128)(2,1)S(1)} collective-permute-done((bf16[2,128,1024]{2,1,0:T(8,128)(2,1)}, bf16[2,128,1024]{2,1,0:T(8,128)(2,1)S(1)}, u32[]{:S(2)}, u32[]{:S(2)}) %collective-permute-start) | collective-permute-done | bytes 524320 | tf_op jit(solution)/shard_map/ppermute | solution.py:35
  15.2 1.7 %collective-permute-start.1 = (bf16[2,128,512]{2,1,0:T(8,128)(2,1)S(1)}, bf16[2,128,512]{2,1,0:T(8,128)(2,1)S(1)}, u32[]{:S(2)}, u32[]{:S(2)}) collective-permute-start(bf16[2,128,512]{2,1,0:T(8,128)(2,1)S(1)} %get-tuple-element.51), channel_id=1, source_target_pairs={{0,4},{8,16},{16,8},{24,28},{28,24},{20,12},{12,20},{4,0},{1,5},{9... | collective-permute-start | bytes 786440 | tf_op jit(solution)/shard_map/ppermute | solution.py:35
  16.9 0.0 collective-permute-done.2.refs_2_
  17.0 1.7 %collective-permute-start.3 = (bf16[2,128,512]{2,1,0:T(8,128)(2,1)S(1)}, bf16[2,128,512]{2,1,0:T(8,128)(2,1)S(1)}, u32[]{:S(2)}, u32[]{:S(2)}) collective-permute-start(bf16[2,128,512]{2,1,0:T(8,128)(2,1)S(1)} %get-tuple-element.49), channel_id=1, source_target_pairs={{0,8},{8,0},{16,24},{24,16},{28,20},{20,28},{12,4},{4,12},{1,9},{9... | collective-permute-start | bytes 786440 | tf_op jit(solution)/shard_map/ppermute | solution.py:35
  18.7 1.5 %collective-permute-start.7 = (bf16[2,128,512]{2,1,0:T(8,128)(2,1)S(1)}, bf16[2,128,512]{2,1,0:T(8,128)(2,1)S(1)}, u32[]{:S(2)}, u32[]{:S(2)}) collective-permute-start(bf16[2,128,512]{2,1,0:T(8,128)(2,1)S(1)} %get-tuple-element.52), channel_id=1, source_target_pairs={{0,4},{8,16},{16,8},{24,28},{28,24},{20,12},{12,20},{4,0},{1,5},{9... | collective-permute-start | bytes 786440 | tf_op jit(solution)/shard_map/ppermute | solution.py:35
  20.2 1.6 %collective-permute-start.6 = (bf16[2,128,512]{2,1,0:T(8,128)(2,1)S(1)}, bf16[2,128,512]{2,1,0:T(8,128)(2,1)S(1)}, u32[]{:S(2)}, u32[]{:S(2)}) collective-permute-start(bf16[2,128,512]{2,1,0:T(8,128)(2,1)S(1)} %get-tuple-element.50), channel_id=1, source_target_pairs={{0,8},{8,0},{16,24},{24,16},{28,20},{20,28},{12,4},{4,12},{1,9},{9... | collective-permute-start | bytes 786440 | tf_op jit(solution)/shard_map/ppermute | solution.py:35
  21.8 0.0 copy-done
  21.8 2.3 %shard_map.64.refs_4_ = f32[4,256,1024]{2,1,0:T(8,128)S(1)} custom-call(s32[12]{0:T(128)S(1)} %dynamic-slice_bitcast_fusion.table_ref, bf16[2,1024,1024]{2,1,0:T(8,128)(2,1)S(1)} %fusion.a_ref, bf16[2,128,1024]{2,1,0:T(8,128)(2,1)S(1)} %copy-done, bf16[2,128,1024]{2,1,0:T(8,128)(2,1)S(1)} %collective-permute-done.refs_1_, ...), custom_call_target="tpu_custom_call" | custom-call | flops 1610612736 | bytes 5767168 | tf_op jit(solution)/shard_map/pallas_call | solution.py:85
  24.1 0.4 collective-permute-done.1.refs_2_
  24.5 1.8 %collective-permute-done.3.refs_0_ = bf16[2,128,512]{2,1,0:T(8,128)(2,1)S(1)} collective-permute-done((bf16[2,128,512]{2,1,0:T(8,128)(2,1)S(1)}, bf16[2,128,512]{2,1,0:T(8,128)(2,1)S(1)}, u32[]{:S(2)}, u32[]{:S(2)}) %collective-permute-start.3) | collective-permute-done | bytes 262176 | tf_op jit(solution)/shard_map/ppermute | solution.py:35
  26.3 1.7 %collective-permute-start.4 = (bf16[2,128,512]{2,1,0:T(8,128)(2,1)S(1)}, bf16[2,128,512]{2,1,0:T(8,128)(2,1)S(1)}, u32[]{:S(2)}, u32[]{:S(2)}) collective-permute-start(bf16[2,128,512]{2,1,0:T(8,128)(2,1)S(1)} %collective-permute-done.1.refs_2_), channel_id=1, source_target_pairs={{0,8},{8,0},{16,24},{24,16},{28,20},{20,28},{12,4},{4,12},{1,9},{9... | collective-permute-start | bytes 786440 | tf_op jit(solution)/shard_map/ppermute | solution.py:35
  27.9 1.5 %collective-permute-start.5 = (bf16[2,128,512]{2,1,0:T(8,128)(2,1)S(1)}, bf16[2,128,512]{2,1,0:T(8,128)(2,1)S(1)}, u32[]{:S(2)}, u32[]{:S(2)}) collective-permute-start(bf16[2,128,512]{2,1,0:T(8,128)(2,1)S(1)} %collective-permute-done.3.refs_0_), channel_id=1, source_target_pairs={{0,4},{8,16},{16,8},{24,28},{28,24},{20,12},{12,20},{4,0},{1,5},{9... | collective-permute-start | bytes 786440 | tf_op jit(solution)/shard_map/ppermute | solution.py:35
  29.4 0.7 %collective-permute-done.7.refs_3_ = bf16[2,128,512]{2,1,0:T(8,128)(2,1)S(1)} collective-permute-done((bf16[2,128,512]{2,1,0:T(8,128)(2,1)S(1)}, bf16[2,128,512]{2,1,0:T(8,128)(2,1)S(1)}, u32[]{:S(2)}, u32[]{:S(2)}) %collective-permute-start.7) | collective-permute-done | bytes 262176 | tf_op jit(solution)/shard_map/ppermute | solution.py:35
  30.1 1.7 %collective-permute-start.10 = (bf16[2,128,512]{2,1,0:T(8,128)(2,1)S(1)}, bf16[2,128,512]{2,1,0:T(8,128)(2,1)S(1)}, u32[]{:S(2)}, u32[]{:S(2)}) collective-permute-start(bf16[2,128,512]{2,1,0:T(8,128)(2,1)S(1)} %collective-permute-done.7.refs_3_), channel_id=1, source_target_pairs={{0,8},{8,0},{16,24},{24,16},{28,20},{20,28},{12,4},{4,12},{1,9},{9... | collective-permute-start | bytes 786440 | tf_op jit(solution)/shard_map/ppermute | solution.py:35
  31.9 0.0 collective-permute-done.6.refs_1_
  31.9 1.5 %collective-permute-start.11 = (bf16[2,128,512]{2,1,0:T(8,128)(2,1)S(1)}, bf16[2,128,512]{2,1,0:T(8,128)(2,1)S(1)}, u32[]{:S(2)}, u32[]{:S(2)}) collective-permute-start(bf16[2,128,512]{2,1,0:T(8,128)(2,1)S(1)} %collective-permute-done.6.refs_1_), channel_id=1, source_target_pairs={{0,4},{8,16},{16,8},{24,28},{28,24},{20,12},{12,20},{4,0},{1,5},{9... | collective-permute-start | bytes 786440 | tf_op jit(solution)/shard_map/ppermute | solution.py:35
  33.4 1.8 %shard_map.65.refs_2_ = f32[4,256,1024]{2,1,0:T(8,128)S(1)} custom-call(s32[12]{0:T(128)S(1)} %dynamic-slice_bitcast_fusion.table_ref, bf16[2,1024,1024]{2,1,0:T(8,128)(2,1)S(1)} %fusion.a_ref, bf16[2,128,512]{2,1,0:T(8,128)(2,1)S(1)} %collective-permute-done.3.refs_0_, bf16[2,128,512]{2,1,0:T(8,128)(2,1)S(1)} %collective-permute-done.6.refs_1_, ...), custom_call_target="tpu_custom_call" | custom-call | flops 1073741824 | bytes 6291456 | tf_op jit(solution)/shard_map/pallas_call | solution.py:85
  35.2 2.3 %collective-permute-done.4.refs_0_ = bf16[2,128,512]{2,1,0:T(8,128)(2,1)S(1)} collective-permute-done((bf16[2,128,512]{2,1,0:T(8,128)(2,1)S(1)}, bf16[2,128,512]{2,1,0:T(8,128)(2,1)S(1)}, u32[]{:S(2)}, u32[]{:S(2)}) %collective-permute-start.4) | collective-permute-done | bytes 262176 | tf_op jit(solution)/shard_map/ppermute | solution.py:35
  37.5 0.0 collective-permute-done.5.refs_1_
  37.5 1.7 %collective-permute-start.8 = (bf16[2,128,256]{2,1,0:T(8,128)(2,1)S(1)}, bf16[2,128,256]{2,1,0:T(8,128)(2,1)S(1)}, u32[]{:S(2)}, u32[]{:S(2)}) collective-permute-start(bf16[2,128,256]{2,1,0:T(8,128)(2,1)S(1)} %slice.28), channel_id=1, source_target_pairs={{0,8},{8,0},{16,24},{24,16},{28,20},{20,28},{12,4},{4,12},{1,9},{9... | collective-permute-start | bytes 393224 | tf_op jit(solution)/shard_map/ppermute | solution.py:35
  39.3 1.6 %collective-permute-start.9 = (bf16[2,128,256]{2,1,0:T(8,128)(2,1)S(1)}, bf16[2,128,256]{2,1,0:T(8,128)(2,1)S(1)}, u32[]{:S(2)}, u32[]{:S(2)}) collective-permute-start(bf16[2,128,256]{2,1,0:T(8,128)(2,1)S(1)} %slice.29), channel_id=1, source_target_pairs={{0,4},{8,16},{16,8},{24,28},{28,24},{20,12},{12,20},{4,0},{1,5},{9... | collective-permute-start | bytes 393224 | tf_op jit(solution)/shard_map/ppermute | solution.py:35
  40.8 1.3 %shard_map.66.refs_2_ = f32[4,256,512]{2,1,0:T(8,128)S(1)} custom-call(s32[12]{0:T(128)S(1)} %dynamic-slice_bitcast_fusion.table_ref, bf16[2,1024,1024]{2,1,0:T(8,128)(2,1)S(1)} %fusion.a_ref, bf16[2,128,512]{2,1,0:T(8,128)(2,1)S(1)} %collective-permute-done.4.refs_0_, bf16[2,128,512]{2,1,0:T(8,128)(2,1)S(1)} %collective-permute-done.5.refs_1_, ...), custom_call_target="tpu_custom_call" | custom-call | flops 10737418240 | bytes 4718592 | tf_op jit(solution)/shard_map/pallas_call | solution.py:85
  42.1 1.0 %collective-permute-done.10.refs_0_ = bf16[2,128,512]{2,1,0:T(8,128)(2,1)S(1)} collective-permute-done((bf16[2,128,512]{2,1,0:T(8,128)(2,1)S(1)}, bf16[2,128,512]{2,1,0:T(8,128)(2,1)S(1)}, u32[]{:S(2)}, u32[]{:S(2)}) %collective-permute-start.10) | collective-permute-done | bytes 262176 | tf_op jit(solution)/shard_map/ppermute | solution.py:35
  43.1 0.0 collective-permute-done.11.refs_1_
  43.2 1.7 %collective-permute-start.14 = (bf16[2,128,256]{2,1,0:T(8,128)(2,1)S(1)}, bf16[2,128,256]{2,1,0:T(8,128)(2,1)S(1)}, u32[]{:S(2)}, u32[]{:S(2)}) collective-permute-start(bf16[2,128,256]{2,1,0:T(8,128)(2,1)S(1)} %slice.30), channel_id=1, source_target_pairs={{0,8},{8,0},{16,24},{24,16},{28,20},{20,28},{12,4},{4,12},{1,9},{9... | collective-permute-start | bytes 393224 | tf_op jit(solution)/shard_map/ppermute | solution.py:35
  44.9 1.6 %collective-permute-start.15 = (bf16[2,128,256]{2,1,0:T(8,128)(2,1)S(1)}, bf16[2,128,256]{2,1,0:T(8,128)(2,1)S(1)}, u32[]{:S(2)}, u32[]{:S(2)}) collective-permute-start(bf16[2,128,256]{2,1,0:T(8,128)(2,1)S(1)} %slice.31), channel_id=1, source_target_pairs={{0,4},{8,16},{16,8},{24,28},{28,24},{20,12},{12,20},{4,0},{1,5},{9... | collective-permute-start | bytes 393224 | tf_op jit(solution)/shard_map/ppermute | solution.py:35
  46.5 1.3 %shard_map.68.refs_2_ = f32[4,256,512]{2,1,0:T(8,128)S(1)} custom-call(s32[12]{0:T(128)S(1)} %dynamic-slice_bitcast_fusion.table_ref, bf16[2,1024,1024]{2,1,0:T(8,128)(2,1)S(1)} %fusion.a_ref, bf16[2,128,512]{2,1,0:T(8,128)(2,1)S(1)} %collective-permute-done.10.refs_0_, bf16[2,128,512]{2,1,0:T(8,128)(2,1)S(1)} %collective-permute-done.11.refs_1_, ...), custom_call_target="tpu_custom_call" | custom-call | flops 536870912 | bytes 4718592 | tf_op jit(solution)/shard_map/pallas_call | solution.py:85
  47.8 0.0 collective-permute-done.8.refs_0_
  47.8 0.0 collective-permute-done.9.refs_1_
  47.8 1.0 %shard_map.67 = (bf16[256,512]{1,0:T(8,128)(2,1)S(1)}, bf16[256,512]{1,0:T(8,128)(2,1)S(1)}, f32[256,512]{1,0:T(8,128)S(1)}, f32[256,512]{1,0:T(8,128)S(1)}) custom-call(s32[12]{0:T(128)S(1)} %dynamic-slice_bitcast_fusion.table_ref, bf16[2,1024,1024]{2,1,0:T(8,128)(2,1)S(1)} %fusion.a_ref, bf16[2,128,256]{2,1,0:T(8,128)(2,1)S(1)} %collective-permute-done.8.refs_0_, ...), custom_call_target="tpu_custom_call" | custom-call | flops 268435456 | bytes 4718592 | tf_op jit(solution)/shard_map/pallas_call | solution.py:85
  48.8 0.1 collective-permute-start.13
  48.9 0.0 collective-permute-done.14.refs_0_
  48.9 1.0 %collective-permute-done.15.refs_1_ = bf16[2,128,256]{2,1,0:T(8,128)(2,1)S(1)} collective-permute-done((bf16[2,128,256]{2,1,0:T(8,128)(2,1)S(1)}, bf16[2,128,256]{2,1,0:T(8,128)(2,1)S(1)}, u32[]{:S(2)}, u32[]{:S(2)}) %collective-permute-start.15) | collective-permute-done | bytes 131104 | tf_op jit(solution)/shard_map/ppermute | solution.py:35
  49.9 1.0 %shard_map.69 = (bf16[256,512]{1,0:T(8,128)(2,1)S(1)}, bf16[256,512]{1,0:T(8,128)(2,1)S(1)}, f32[256,512]{1,0:T(8,128)S(1)}, f32[256,512]{1,0:T(8,128)S(1)}) custom-call(s32[12]{0:T(128)S(1)} %dynamic-slice_bitcast_fusion.table_ref, bf16[2,1024,1024]{2,1,0:T(8,128)(2,1)S(1)} %fusion.a_ref, bf16[2,128,256]{2,1,0:T(8,128)(2,1)S(1)} %collective-permute-done.14.refs_0_, ...), custom_call_target="tpu_custom_call" | custom-call | flops 5368709120 | bytes 4718592 | tf_op jit(solution)/shard_map/pallas_call | solution.py:85
  50.9 0.0 copy-start.1
  51.0 0.0 copy-start.2
  51.0 0.0 collective-permute-done.13
  51.0 0.1 collective-permute-start.18
  51.1 0.5 collective-permute-start.12
  51.6 0.1 add_convert_fusion.1
  51.6 1.6 %collective-permute-start.16 = (bf16[256,512]{1,0:T(8,128)(2,1)S(1)}, bf16[256,512]{1,0:T(8,128)(2,1)S(1)}, u32[]{:S(2)}, u32[]{:S(2)}) collective-permute-start(bf16[256,512]{1,0:T(8,128)(2,1)S(1)} %add_convert_fusion.1), channel_id=1, source_target_pairs={{0,2},{2,0},{1,3},{3,1},{4,6},{6,4},{5,7},{7,5},{8,10},{10,8},{9,1... | collective-permute-start | bytes 786440 | tf_op jit(solution)/shard_map/ppermute | solution.py:39
  53.2 0.0 collective-permute-start.17
  53.2 0.0 collective-permute-done.18
  53.2 0.1 add_convert_fusion
  53.3 0.9 %collective-permute-start.19 = (bf16[256,512]{1,0:T(8,128)(2,1)S(1)}, bf16[256,512]{1,0:T(8,128)(2,1)S(1)}, u32[]{:S(2)}, u32[]{:S(2)}) collective-permute-start(bf16[256,512]{1,0:T(8,128)(2,1)S(1)} %add_convert_fusion), channel_id=1, source_target_pairs={{0,2},{2,0},{1,3},{3,1},{4,6},{6,4},{5,7},{7,5},{8,10},{10,8},{9,1... | collective-permute-start | bytes 786440 | tf_op jit(solution)/shard_map/ppermute | solution.py:39
  54.2 0.0 collective-permute-done.12
  54.3 6.6 %collective-permute-done.16 = bf16[256,512]{1,0:T(8,128)(2,1)S(1)} collective-permute-done((bf16[256,512]{1,0:T(8,128)(2,1)S(1)}, bf16[256,512]{1,0:T(8,128)(2,1)S(1)}, u32[]{:S(2)}, u32[]{:S(2)}) %collective-permute-start.16) | collective-permute-done | bytes 262176 | tf_op jit(solution)/shard_map/ppermute | solution.py:39
  60.9 0.1 convert_add_fusion.1
  61.0 0.0 collective-permute-done.17
  61.0 4.6 %collective-permute-done.19 = bf16[256,512]{1,0:T(8,128)(2,1)S(1)} collective-permute-done((bf16[256,512]{1,0:T(8,128)(2,1)S(1)}, bf16[256,512]{1,0:T(8,128)(2,1)S(1)}, u32[]{:S(2)}, u32[]{:S(2)}) %collective-permute-start.19) | collective-permute-done | bytes 262176 | tf_op jit(solution)/shard_map/ppermute | solution.py:39
  65.6 0.1 convert_add_fusion
  65.7 0.0 copy-done.1
  65.7 0.0 copy-done.2
  65.7 1.0 %fusion.1 = bf16[256,1024]{1,0:T(8,128)(2,1)} fusion(f32[256,512]{1,0:T(8,128)S(1)} %convert_add_fusion, f32[256,512]{1,0:T(8,128)S(1)} %convert_add_fusion.1, f32[256]{0:T(256)S(1)} %copy-done.2, f32[1024]{0:T(1024)S(1)} %copy-done.1), kind=kLoop, calls=%fused_computation.3 | loop fusion | flops 1048576 | bytes 1577984 | tf_op jit(solution)/shard_map/convert_element_type | solution.py:168
  (6 shorter events, 0.1 us)
Async XLA Ops:
  0.0 15.2 %collective-permute-start = (bf16[2,128,1024]{2,1,0:T(8,128)(2,1)}, bf16[2,128,1024]{2,1,0:T(8,128)(2,1)S(1)}, u32[]{:S(2)}, u32[]{:S(2)}) collective-permute-start(bf16[2,128,1024]{2,1,0:T(8,128)(2,1)} %refs_0_.1), channel_id=1, source_target_pairs={{0,8},{8,0},{16,24},{24,16},{28,20},{20,28},{12,4},{4,12},{1,9},{9... | collective-permute-start | bytes 1572872 | tf_op jit(solution)/shard_map/ppermute | solution.py:35
  3.0 13.9 %collective-permute-start.2 = (bf16[2,128,1024]{2,1,0:T(8,128)(2,1)}, bf16[2,128,1024]{2,1,0:T(8,128)(2,1)S(1)}, u32[]{:S(2)}, u32[]{:S(2)}) collective-permute-start(bf16[2,128,1024]{2,1,0:T(8,128)(2,1)} %refs_0_.1), channel_id=1, source_target_pairs={{0,4},{8,16},{16,8},{24,28},{28,24},{20,12},{12,20},{4,0},{1,5},{9... | collective-permute-start | bytes 1572872 | tf_op jit(solution)/shard_map/ppermute | solution.py:35
  5.9 15.9 %copy-start = (bf16[2,128,1024]{2,1,0:T(8,128)(2,1)S(1)}, bf16[2,128,1024]{2,1,0:T(8,128)(2,1)}, u32[]{:S(2)}) copy-start(bf16[2,128,1024]{2,1,0:T(8,128)(2,1)} %refs_0_.1) | copy-start | bytes 1572868
  15.2 9.3 %collective-permute-start.1 = (bf16[2,128,512]{2,1,0:T(8,128)(2,1)S(1)}, bf16[2,128,512]{2,1,0:T(8,128)(2,1)S(1)}, u32[]{:S(2)}, u32[]{:S(2)}) collective-permute-start(bf16[2,128,512]{2,1,0:T(8,128)(2,1)S(1)} %get-tuple-element.51), channel_id=1, source_target_pairs={{0,4},{8,16},{16,8},{24,28},{28,24},{20,12},{12,20},{4,0},{1,5},{9... | collective-permute-start | bytes 786440 | tf_op jit(solution)/shard_map/ppermute | solution.py:35
  17.0 9.3 %collective-permute-start.3 = (bf16[2,128,512]{2,1,0:T(8,128)(2,1)S(1)}, bf16[2,128,512]{2,1,0:T(8,128)(2,1)S(1)}, u32[]{:S(2)}, u32[]{:S(2)}) collective-permute-start(bf16[2,128,512]{2,1,0:T(8,128)(2,1)S(1)} %get-tuple-element.49), channel_id=1, source_target_pairs={{0,8},{8,0},{16,24},{24,16},{28,20},{20,28},{12,4},{4,12},{1,9},{9... | collective-permute-start | bytes 786440 | tf_op jit(solution)/shard_map/ppermute | solution.py:35
  18.7 11.4 %collective-permute-start.7 = (bf16[2,128,512]{2,1,0:T(8,128)(2,1)S(1)}, bf16[2,128,512]{2,1,0:T(8,128)(2,1)S(1)}, u32[]{:S(2)}, u32[]{:S(2)}) collective-permute-start(bf16[2,128,512]{2,1,0:T(8,128)(2,1)S(1)} %get-tuple-element.52), channel_id=1, source_target_pairs={{0,4},{8,16},{16,8},{24,28},{28,24},{20,12},{12,20},{4,0},{1,5},{9... | collective-permute-start | bytes 786440 | tf_op jit(solution)/shard_map/ppermute | solution.py:35
  20.2 11.7 %collective-permute-start.6 = (bf16[2,128,512]{2,1,0:T(8,128)(2,1)S(1)}, bf16[2,128,512]{2,1,0:T(8,128)(2,1)S(1)}, u32[]{:S(2)}, u32[]{:S(2)}) collective-permute-start(bf16[2,128,512]{2,1,0:T(8,128)(2,1)S(1)} %get-tuple-element.50), channel_id=1, source_target_pairs={{0,8},{8,0},{16,24},{24,16},{28,20},{20,28},{12,4},{4,12},{1,9},{9... | collective-permute-start | bytes 786440 | tf_op jit(solution)/shard_map/ppermute | solution.py:35
  26.3 11.2 %collective-permute-start.4 = (bf16[2,128,512]{2,1,0:T(8,128)(2,1)S(1)}, bf16[2,128,512]{2,1,0:T(8,128)(2,1)S(1)}, u32[]{:S(2)}, u32[]{:S(2)}) collective-permute-start(bf16[2,128,512]{2,1,0:T(8,128)(2,1)S(1)} %collective-permute-done.1.refs_2_), channel_id=1, source_target_pairs={{0,8},{8,0},{16,24},{24,16},{28,20},{20,28},{12,4},{4,12},{1,9},{9... | collective-permute-start | bytes 786440 | tf_op jit(solution)/shard_map/ppermute | solution.py:35
  27.9 9.6 %collective-permute-start.5 = (bf16[2,128,512]{2,1,0:T(8,128)(2,1)S(1)}, bf16[2,128,512]{2,1,0:T(8,128)(2,1)S(1)}, u32[]{:S(2)}, u32[]{:S(2)}) collective-permute-start(bf16[2,128,512]{2,1,0:T(8,128)(2,1)S(1)} %collective-permute-done.3.refs_0_), channel_id=1, source_target_pairs={{0,4},{8,16},{16,8},{24,28},{28,24},{20,12},{12,20},{4,0},{1,5},{9... | collective-permute-start | bytes 786440 | tf_op jit(solution)/shard_map/ppermute | solution.py:35
  30.1 13.0 %collective-permute-start.10 = (bf16[2,128,512]{2,1,0:T(8,128)(2,1)S(1)}, bf16[2,128,512]{2,1,0:T(8,128)(2,1)S(1)}, u32[]{:S(2)}, u32[]{:S(2)}) collective-permute-start(bf16[2,128,512]{2,1,0:T(8,128)(2,1)S(1)} %collective-permute-done.7.refs_3_), channel_id=1, source_target_pairs={{0,8},{8,0},{16,24},{24,16},{28,20},{20,28},{12,4},{4,12},{1,9},{9... | collective-permute-start | bytes 786440 | tf_op jit(solution)/shard_map/ppermute | solution.py:35
  31.9 11.2 %collective-permute-start.11 = (bf16[2,128,512]{2,1,0:T(8,128)(2,1)S(1)}, bf16[2,128,512]{2,1,0:T(8,128)(2,1)S(1)}, u32[]{:S(2)}, u32[]{:S(2)}) collective-permute-start(bf16[2,128,512]{2,1,0:T(8,128)(2,1)S(1)} %collective-permute-done.6.refs_1_), channel_id=1, source_target_pairs={{0,4},{8,16},{16,8},{24,28},{28,24},{20,12},{12,20},{4,0},{1,5},{9... | collective-permute-start | bytes 786440 | tf_op jit(solution)/shard_map/ppermute | solution.py:35
  37.5 10.2 %collective-permute-start.8 = (bf16[2,128,256]{2,1,0:T(8,128)(2,1)S(1)}, bf16[2,128,256]{2,1,0:T(8,128)(2,1)S(1)}, u32[]{:S(2)}, u32[]{:S(2)}) collective-permute-start(bf16[2,128,256]{2,1,0:T(8,128)(2,1)S(1)} %slice.28), channel_id=1, source_target_pairs={{0,8},{8,0},{16,24},{24,16},{28,20},{20,28},{12,4},{4,12},{1,9},{9... | collective-permute-start | bytes 393224 | tf_op jit(solution)/shard_map/ppermute | solution.py:35
  39.3 8.5 %collective-permute-start.9 = (bf16[2,128,256]{2,1,0:T(8,128)(2,1)S(1)}, bf16[2,128,256]{2,1,0:T(8,128)(2,1)S(1)}, u32[]{:S(2)}, u32[]{:S(2)}) collective-permute-start(bf16[2,128,256]{2,1,0:T(8,128)(2,1)S(1)} %slice.29), channel_id=1, source_target_pairs={{0,4},{8,16},{16,8},{24,28},{28,24},{20,12},{12,20},{4,0},{1,5},{9... | collective-permute-start | bytes 393224 | tf_op jit(solution)/shard_map/ppermute | solution.py:35
  43.2 5.7 %collective-permute-start.14 = (bf16[2,128,256]{2,1,0:T(8,128)(2,1)S(1)}, bf16[2,128,256]{2,1,0:T(8,128)(2,1)S(1)}, u32[]{:S(2)}, u32[]{:S(2)}) collective-permute-start(bf16[2,128,256]{2,1,0:T(8,128)(2,1)S(1)} %slice.30), channel_id=1, source_target_pairs={{0,8},{8,0},{16,24},{24,16},{28,20},{20,28},{12,4},{4,12},{1,9},{9... | collective-permute-start | bytes 393224 | tf_op jit(solution)/shard_map/ppermute | solution.py:35
  44.9 5.0 %collective-permute-start.15 = (bf16[2,128,256]{2,1,0:T(8,128)(2,1)S(1)}, bf16[2,128,256]{2,1,0:T(8,128)(2,1)S(1)}, u32[]{:S(2)}, u32[]{:S(2)}) collective-permute-start(bf16[2,128,256]{2,1,0:T(8,128)(2,1)S(1)} %slice.31), channel_id=1, source_target_pairs={{0,4},{8,16},{16,8},{24,28},{28,24},{20,12},{12,20},{4,0},{1,5},{9... | collective-permute-start | bytes 393224 | tf_op jit(solution)/shard_map/ppermute | solution.py:35
  48.8 2.2 %collective-permute-start.13 = (bf16[256,512]{1,0:T(8,128)(2,1)S(1)}, bf16[256,512]{1,0:T(8,128)(2,1)S(1)}, u32[]{:S(2)}, u32[]{:S(2)}) collective-permute-start(bf16[256,512]{1,0:T(8,128)(2,1)S(1)} %get-tuple-element.40), channel_id=1, source_target_pairs={{0,1},{1,0},{2,3},{3,2},{4,5},{5,4},{6,7},{7,6},{8,9},{9,8},{10,11... | collective-permute-start | bytes 786440 | tf_op jit(solution)/shard_map/ppermute | solution.py:39
  50.9 14.8 %copy-start.1 = (f32[1024]{0:T(1024)S(1)}, f32[1024]{0:T(1024)}, u32[]{:S(2)}) copy-start(f32[1024]{0:T(1024)} %param.10) | copy-start | bytes 12292
  51.0 14.8 %copy-start.2 = (f32[256]{0:T(256)S(1)}, f32[256]{0:T(256)}, u32[]{:S(2)}) copy-start(f32[256]{0:T(256)} %param.9) | copy-start | bytes 3076
  51.0 2.3 %collective-permute-start.18 = (bf16[256,512]{1,0:T(8,128)(2,1)S(1)}, bf16[256,512]{1,0:T(8,128)(2,1)S(1)}, u32[]{:S(2)}, u32[]{:S(2)}) collective-permute-start(bf16[256,512]{1,0:T(8,128)(2,1)S(1)} %get-tuple-element.48), channel_id=1, source_target_pairs={{0,1},{1,0},{2,3},{3,2},{4,5},{5,4},{6,7},{7,6},{8,9},{9,8},{10,11... | collective-permute-start | bytes 786440 | tf_op jit(solution)/shard_map/ppermute | solution.py:39
  51.1 3.2 %collective-permute-start.12 = (bf16[256,512]{1,0:T(8,128)(2,1)S(1)}, bf16[256,512]{1,0:T(8,128)(2,1)S(1)}, u32[]{:S(2)}, u32[]{:S(2)}) collective-permute-start(bf16[256,512]{1,0:T(8,128)(2,1)S(1)} %get-tuple-element.38), channel_id=1, source_target_pairs={{0,1},{1,0},{2,3},{3,2},{4,5},{5,4},{6,7},{7,6},{8,9},{9,8},{10,11... | collective-permute-start | bytes 786440 | tf_op jit(solution)/shard_map/ppermute | solution.py:39
  51.6 9.2 %collective-permute-start.16 = (bf16[256,512]{1,0:T(8,128)(2,1)S(1)}, bf16[256,512]{1,0:T(8,128)(2,1)S(1)}, u32[]{:S(2)}, u32[]{:S(2)}) collective-permute-start(bf16[256,512]{1,0:T(8,128)(2,1)S(1)} %add_convert_fusion.1), channel_id=1, source_target_pairs={{0,2},{2,0},{1,3},{3,1},{4,6},{6,4},{5,7},{7,5},{8,10},{10,8},{9,1... | collective-permute-start | bytes 786440 | tf_op jit(solution)/shard_map/ppermute | solution.py:39
  53.2 7.8 %collective-permute-start.17 = (bf16[256,512]{1,0:T(8,128)(2,1)S(1)}, bf16[256,512]{1,0:T(8,128)(2,1)S(1)}, u32[]{:S(2)}, u32[]{:S(2)}) collective-permute-start(bf16[256,512]{1,0:T(8,128)(2,1)S(1)} %get-tuple-element.46), channel_id=1, source_target_pairs={{0,1},{1,0},{2,3},{3,2},{4,5},{5,4},{6,7},{7,6},{8,9},{9,8},{10,11... | collective-permute-start | bytes 786440 | tf_op jit(solution)/shard_map/ppermute | solution.py:39
  53.3 12.3 %collective-permute-start.19 = (bf16[256,512]{1,0:T(8,128)(2,1)S(1)}, bf16[256,512]{1,0:T(8,128)(2,1)S(1)}, u32[]{:S(2)}, u32[]{:S(2)}) collective-permute-start(bf16[256,512]{1,0:T(8,128)(2,1)S(1)} %add_convert_fusion), channel_id=1, source_target_pairs={{0,2},{2,0},{1,3},{3,1},{4,6},{6,4},{5,7},{7,5},{8,10},{10,8},{9,1... | collective-permute-start | bytes 786440 | tf_op jit(solution)/shard_map/ppermute | solution.py:39

commit v4 on v3

--- a/solution.py
+++ b/solution.py
@@ -1,5 +1,3 @@
-import functools
-
 import jax
 import jax.numpy as jnp
 from jax import lax
@@ -37,6 +35,50 @@
 
 def over_virt(value, hops):
     return lax.ppermute(value, "virt", hops)
+
+
+def arranged(amplitudes, tile_mask):
+    pairs, tiles, wide = amplitudes.shape
+    rows = 128
+
+    def body(amplitudes_ref, mask_ref, out_ref):
+        apart = lax.broadcasted_iota(jnp.int32, (rows, rows * tiles), 1) - tiles * lax.broadcasted_iota(
+            jnp.int32, (rows, rows * tiles), 0
+        )
+        for at in range(0, pairs, rows):
+            here = pl.ds(at, rows)
+            mixed = amplitudes_ref[here].reshape(rows * tiles, wide)
+            mask = jnp.transpose(jnp.concatenate([mask_ref[:, here].astype(F32)] * (8 // tiles), axis=0))
+            for t in range(tiles):
+                chosen = jnp.where(apart == t, mask[:, t : t + 1], 0.0).astype(BF16)
+                out_ref[t, here] = jnp.dot(chosen, mixed, preferred_element_type=F32).astype(BF16)
+
+    vmem = pl.BlockSpec(memory_space=pltpu.VMEM)
+    return pl.pallas_call(
+        body,
+        in_specs=[vmem, vmem],
+        out_specs=vmem,
+        out_shape=jax.ShapeDtypeStruct((tiles, pairs, wide), BF16),
+        compiler_params=pltpu.CompilerParams(vmem_limit_bytes=12 * 2**20),
+        cost_estimate=pl.CostEstimate(
+            flops=4 * rows * tiles * amplitudes.size, bytes_accessed=4 * amplitudes.size, transcendentals=0
+        ),
+    )(amplitudes, tile_mask.T)
+
+
+def added(kept, got):
+    def body(kept_ref, got_ref, out_ref):
+        out_ref[...] = (kept_ref[...] + got_ref[...].astype(F32)).astype(BF16)
+
+    vmem = pl.BlockSpec(memory_space=pltpu.VMEM)
+    return pl.pallas_call(
+        body,
+        in_specs=[vmem, vmem],
+        out_specs=vmem,
+        out_shape=jax.ShapeDtypeStruct(kept.shape, BF16),
+        compiler_params=pltpu.CompilerParams(vmem_limit_bytes=4 * 2**20),
+        cost_estimate=pl.CostEstimate(flops=0, bytes_accessed=0, transcendentals=0),
+    )(kept, got)
 
 
 def tie(*values):
@@ -62,24 +104,24 @@
             for slot, group in zip(slots, groups):
                 cols = pl.ds(pl.multiple_of(table_ref[slot] * depth, depth), depth)
                 left += [a_ref[t, here, cols] for t in range(tiles)]
-                pieces = [r[:, :, lo:hi] if len(group) == 1 and r.shape[2] > columns else r[...] for r in group]
-                block = pieces[0] if len(pieces) == 1 else jnp.concatenate(pieces, axis=2)
+                sides = [r[:, :, lo:hi] if len(group) == 1 and r.shape[2] > columns else r[...] for r in group]
+                block = sides[0] if len(sides) == 1 else jnp.concatenate(sides, axis=2)
                 right.append(block.reshape(tiles * depth, columns))
             acc = jnp.dot(
                 jnp.concatenate(left, axis=1), jnp.concatenate(right, axis=0), preferred_element_type=F32
             )
             if total is not None:
                 acc += total_ref[i, :, lo:hi] if total.shape[2] > columns else total_ref[i]
-            if not finish:
+            if finish:
+                outs[i - 1][...] = acc.astype(outs[i - 1].dtype)
+            else:
                 outs[0][i] = acc
-            else:
-                outs[i][...] = acc.astype(outs[i].dtype)
 
     vmem = pl.BlockSpec(memory_space=pltpu.VMEM)
     smem = pl.BlockSpec(memory_space=pltpu.SMEM)
     operands = [a] + flat + ([] if total is None else [total])
     if finish:
-        out_shape = [jax.ShapeDtypeStruct((row, columns), t) for t in (BF16, BF16, F32, F32)]
+        out_shape = [jax.ShapeDtypeStruct((row, columns), t) for t in (BF16, F32, F32, BF16)]
     else:
         out_shape = [jax.ShapeDtypeStruct((4, row, columns), F32)]
     out = pl.pallas_call(
@@ -90,7 +132,7 @@
         compiler_params=pltpu.CompilerParams(vmem_limit_bytes=20 * 2**20),
         cost_estimate=pl.CostEstimate(
             flops=weight * 2 * a.shape[1] * tiles * depth * len(blocks) * columns,
-            bytes_accessed=2 * a.size + 2 * len(flat) * tiles * depth * columns,
+            bytes_accessed=min(weight, 1) * (2 * a.size + 2 * len(flat) * tiles * depth * columns),
             transcendentals=0,
         ),
     )(table, *operands)
@@ -108,54 +150,45 @@
     return lax.dynamic_index_in_dim(jnp.array(every, jnp.int32), me, keepdims=False)
 
 
-def scheduled(cut, amplitudes, tile_mask, integrals, pair_energy, virt_energy):
+def scheduled(amplitudes, tile_mask, integrals, pair_energy, virt_energy):
     table = device_table()
     columns = integrals.shape[2]
-    span_a, span_b = (0, cut), (cut, columns)
+    span_a, span_b = (0, columns // 2), (columns // 2, columns)
 
     def part(v, span):
         return v[:, :, span[0] : span[1]]
 
-    e1, o1 = over_pair(integrals, EVEN), over_pair(integrals, ODD)
-    masked = amplitudes * tile_mask.astype(BF16)[:, :, None]
-    a = masked.transpose(1, 0, 2)
-    e1, a, table = tie(e1, a, table)
-
-    def second(span):
-        return over_pair(part(o1, span), EVEN), over_pair(part(e1, span), ODD)
-
-    def third(e2, o2):
-        return over_pair(o2, EVEN), over_pair(e2, ODD)
-
-    def fourth(e3, o3):
-        middle = e3.shape[2] // 2
-        return [over_pair(o3[:, :, :middle], EVEN), over_pair(e3[:, :, middle:], ODD)]
-
-    e2a, o2a = second(span_a)
-    e2b, o2b = second(span_b)
-    total = products(table, [0, 1, 2], a, [integrals, e1, o1], (0, columns))
+    e1 = over_pair(integrals, EVEN)
+    o1a, o1b = over_pair(part(integrals, span_a), ODD), over_pair(part(integrals, span_b), ODD)
+    a = arranged(amplitudes, tile_mask)
+    o1b, a, table = tie(o1b, a, table)
+    e2a, o2a = over_pair(o1a, EVEN), over_pair(part(e1, span_a), ODD)
+    e2b, o2b = over_pair(o1b, EVEN), over_pair(part(e1, span_b), ODD)
+    total = products(table, [0, 1, 2], a, [integrals, e1, [o1a, o1b]], (0, columns))
     o2a, e2a, total = tie(o2a, e2a, total)
-    e3a, o3a = third(e2a, o2a)
-    e3b, o3b = third(e2b, o2b)
+    e3a, o3a = over_pair(o2a, EVEN), over_pair(e2a, ODD)
+    e3b, o3b = over_pair(o2b, EVEN), over_pair(e2b, ODD)
     total = products(table, [3, 4], a, [[e2a, e2b], [o2a, o2b]], (0, columns), total=total)
     e3a, o3a, total = tie(e3a, o3a, total)
-    last_a = fourth(e3a, o3a)
-
+    last_a = over_pair(o3a, EVEN)
     total_a = products(table, [5, 6], a, [e3a, o3a], span_a, total=total, weight=20)
-    e3b, o3b, total_a = tie(e3b, o3b, total_a)
-    last_b = fourth(e3b, o3b)
+    e3b, total_a = tie(e3b, total_a)
+    last_b = over_pair(e3b, ODD)
     total_b = products(table, [5, 6], a, [e3b, o3b], span_b, total=total)
-    there_a, here_a, keep_there_a, keep_here_a = products(
+
+    here_a, keep_there_a, keep_here_a, there_a = products(
         table, [7], a, [last_a], span_a, total=total_a, finish=True
     )
-    got_there_a, got_here_a = over_virt(there_a, CORE), over_virt(here_a, CORE)
-    there_b, here_b, keep_there_b, keep_here_b = products(
+    got_there_a = over_virt(there_a, CORE)
+    here_b, keep_there_b, keep_here_b, there_b = products(
         table, [7], a, [last_b], span_b, total=total_b, finish=True, weight=20
     )
-    got_there_a, there_b = tie(got_there_a, there_b)
-    from_y_a = over_virt((keep_there_a + got_there_a.astype(F32)).astype(BF16), YHOP)
-    got_there_b, got_here_b = over_virt(there_b, CORE), over_virt(here_b, CORE)
-    from_y_b = over_virt((keep_there_b + got_there_b.astype(F32)).astype(BF16), YHOP)
+    mine_a = added(keep_there_a, got_there_a)
+    mine_a, there_b = tie(mine_a, there_b)
+    from_y_a = over_virt(mine_a, YHOP)
+    got_there_b = over_virt(there_b, CORE)
+    from_y_b = over_virt(added(keep_there_b, got_there_b), YHOP)
+    got_here_a, got_here_b = over_virt(here_a, CORE), over_virt(here_b, CORE)
 
     ladder = jnp.concatenate(
         [
@@ -178,7 +211,7 @@
     )
     here = mesh.shape["pair"] == 8 and mesh.shape["virt"] == 4
     return jax.shard_map(
-        functools.partial(scheduled, 512) if here else plain,
+        scheduled if here else plain,
         mesh=mesh,
         in_specs=placed,
         out_specs=P(("pair", "virt"), None),

time: 67 us -> 63.7 us (0.951)
  other arithmetic: 6.72 us -> 1.21 us
  local copies, waits for them, and re-layouts: 0.82 us -> 4.69 us
  Pallas kernels: 8.8 us -> 10.8 us
  waiting for transfers between devices: 23.1 us -> 21.2 us
  starting transfers between devices: 27.1 us -> 25.3 us
    transpose x1 -> x0, other arithmetic: 4.65 us -> none  [scheduled(): a = masked.transpose(1, 0, 2)]
    unnamed x6 -> x10, local copies, waits for them, and re-layouts: 0.02 us -> 2.9 us
    ppermute x14 -> x13, starting transfers between devices: 24 us -> 21.7 us  [over_pair(): return lax.ppermute(value, 'pair', hops)]
    pallas_call x0 -> x3, Pallas kernels: none -> 1.95 us  [the longest x1 1.85 us: arranged(): pl.pallas_call(body, in_specs=[vmem, vmem], out_specs=vmem, out_shape=jax...]
    ppermute x14 -> x13, waiting for transfers between devices: 11.8 us -> 10.3 us  [over_pair(): return lax.ppermute(value, 'pair', hops)]
    slice x2, local copies, waits for them, and re-layouts: 0.08 us -> 1.1 us  [part(): return v[:, :, span[0]:span[1]]]
    convert_element_type x3 -> x0, other arithmetic: 0.86 us -> none  [the longest x1 0.7 us: scheduled(): masked = amplitudes * tile_mask.astype(BF16)[:, :, None]]
  transfers between devices with their start and end apart: 20 -> 19, of which waited for: 9 -> 10; matrix products, arithmetic and copies ran while one was open for 10% -> 3% of each run, Pallas kernels for 13% -> 17%
where the time goes in v4:
time: 63.7 us; the launch traced here: 63.5 us
  starting transfers between devices  25.3 us (40%)
  waiting for transfers between devices  21.2 us (33%)
  Pallas kernels  10.8 us (17%)
  local copies, waits for them, and re-layouts  4.69 us (7%)
  other arithmetic  1.21 us (2%)
    ppermute x13, starting transfers between devices, over_pair(): return lax.ppermute(value, 'pair', hops)  21.7 us
    ppermute x6, waiting for transfers between devices, over_virt(): return lax.ppermute(value, 'virt', hops)  10.9 us
    ppermute x13, waiting for transfers between devices, over_pair(): return lax.ppermute(value, 'pair', hops)  10.3 us
    pallas_call x6, Pallas kernels, products(): pl.pallas_call(body, in_specs=[smem] + [vmem] * len(operands), out_specs=...  8.9 us
    ppermute x6, starting transfers between devices, over_virt(): return lax.ppermute(value, 'virt', hops)  3.61 us
    unnamed x10, local copies, waits for them, and re-layouts  2.9 us
    pallas_call x1, Pallas kernels, arranged(): pl.pallas_call(body, in_specs=[vmem, vmem], out_specs=vmem, out_shape=jax...  1.85 us
  transfers between devices with their start and end apart: 19, of which 10 were waited for; matrix products, arithmetic and copies ran while one was open for 3% of the time, Pallas kernels for 17%

profile of v4, /device:TPU:0, one launch (start us, length us, event | category | flops | bytes accessed | tf_op | source)
XLA Modules:
  0.0 63.5 jit_solution(15090564437320304346)
XLA Ops:
  0.0 3.0 %collective-permute-start.1 = (bf16[2,128,1024]{2,1,0:T(8,128)(2,1)}, bf16[2,128,1024]{2,1,0:T(8,128)(2,1)S(1)}, u32[]{:S(2)}, u32[]{:S(2)}) collective-permute-start(bf16[2,128,1024]{2,1,0:T(8,128)(2,1)} %refs_0_.1), channel_id=1, source_target_pairs={{0,8},{8,0},{16,24},{24,16},{28,20},{20,28},{12,4},{4,12},{1,9},{9... | collective-permute-start | bytes 1572872 | tf_op jit(solution)/shard_map/ppermute | solution.py:33
  3.0 1.1 %fusion.1 = (bf16[2,128,512]{2,1,0:T(8,128)(2,1)S(1)}, bf16[2,128,512]{2,1,0:T(8,128)(2,1)S(1)}) fusion(bf16[2,128,1024]{2,1,0:T(8,128)(2,1)} %refs_0_.1), kind=kLoop, calls=%fused_computation.5 | loop fusion | bytes 1048576 | tf_op jit(solution)/shard_map/slice | solution.py:159
  4.1 1.6 %collective-permute-start.3 = (bf16[2,128,512]{2,1,0:T(8,128)(2,1)S(1)}, bf16[2,128,512]{2,1,0:T(8,128)(2,1)S(1)}, u32[]{:S(2)}, u32[]{:S(2)}) collective-permute-start(bf16[2,128,512]{2,1,0:T(8,128)(2,1)S(1)} %get-tuple-element.47), channel_id=1, source_target_pairs={{0,4},{8,16},{16,8},{24,28},{28,24},{20,12},{12,20},{4,0},{1,5},{9... | collective-permute-start | bytes 786440 | tf_op jit(solution)/shard_map/ppermute | solution.py:33
  5.6 0.5 collective-permute-start
  6.2 0.0 copy-start
  6.2 2.2 %copy-done = bf16[1024,2,1024]{2,1,0:T(2,128)(2,1)S(1)} copy-done((bf16[1024,2,1024]{2,1,0:T(2,128)(2,1)S(1)}, bf16[1024,2,1024]{2,1,0:T(2,128)(2,1)}, u32[]{:S(2)}) %copy-start) | copy-done | bytes 4194328
  8.4 0.0 copy-start.2
  8.4 0.7 %copy-done.2 = s32[1024,2]{0,1:T(2,128)S(1)} copy-done((s32[1024,2]{0,1:T(2,128)S(1)}, s32[1024,2]{0,1:T(2,128)}, u32[]{:S(2)}) %copy-start.2) | copy-done | bytes 8216
  9.1 0.0 copy-start.1
  9.1 1.8 %shard_map.64.a_ref = bf16[2,1024,1024]{2,1,0:T(8,128)(2,1)S(1)} custom-call(bf16[1024,2,1024]{2,1,0:T(2,128)(2,1)S(1)} %copy-done, s32[2,1024]{1,0:T(2,128)S(1)} %bitcast.3), custom_call_target="tpu_custom_call" | custom-call | flops 2147483648 | bytes 8388608 | tf_op jit(solution)/shard_map/pallas_call | solution.py:57
  10.9 2.5 %collective-permute-done.3.refs_2_ = bf16[2,128,512]{2,1,0:T(8,128)(2,1)S(1)} collective-permute-done((bf16[2,128,512]{2,1,0:T(8,128)(2,1)S(1)}, bf16[2,128,512]{2,1,0:T(8,128)(2,1)S(1)}, u32[]{:S(2)}, u32[]{:S(2)}) %collective-permute-start.3) | collective-permute-done | bytes 262176 | tf_op jit(solution)/shard_map/ppermute | solution.py:33
  13.4 1.1 %collective-permute-start.4 = (bf16[2,128,512]{2,1,0:T(8,128)(2,1)S(1)}, bf16[2,128,512]{2,1,0:T(8,128)(2,1)S(1)}, u32[]{:S(2)}, u32[]{:S(2)}) collective-permute-start(bf16[2,128,512]{2,1,0:T(8,128)(2,1)S(1)} %collective-permute-done.3.refs_2_), channel_id=1, source_target_pairs={{0,8},{8,0},{16,24},{24,16},{28,20},{20,28},{12,4},{4,12},{1,9},{9... | collective-permute-start | bytes 786440 | tf_op jit(solution)/shard_map/ppermute | solution.py:33
  14.5 1.5 %collective-permute-done.1.refs_1_ = bf16[2,128,1024]{2,1,0:T(8,128)(2,1)S(1)} collective-permute-done((bf16[2,128,1024]{2,1,0:T(8,128)(2,1)}, bf16[2,128,1024]{2,1,0:T(8,128)(2,1)S(1)}, u32[]{:S(2)}, u32[]{:S(2)}) %collective-permute-start.1) | collective-permute-done | bytes 524320 | tf_op jit(solution)/shard_map/ppermute | solution.py:33
  16.0 2.0 %collective-permute-start.2 = (bf16[2,128,512]{2,1,0:T(8,128)(2,1)S(1)}, bf16[2,128,512]{2,1,0:T(8,128)(2,1)S(1)}, u32[]{:S(2)}, u32[]{:S(2)}) collective-permute-start(bf16[2,128,512]{2,1,0:T(8,128)(2,1)S(1)} %get-tuple-element.49), channel_id=1, source_target_pairs={{0,4},{8,16},{16,8},{24,28},{28,24},{20,12},{12,20},{4,0},{1,5},{9... | collective-permute-start | bytes 786440 | tf_op jit(solution)/shard_map/ppermute | solution.py:33
  18.1 0.7 %dynamic-slice_bitcast_fusion.table_ref = s32[12]{0:T(128)S(1)} fusion(s32[32,12]{1,0:T(8,128)} %constant.19.clone, s32[]{:T(128)S(6)} %select_n.4), kind=kLoop, calls=%fused_computation.4 | loop fusion | bytes 100 | tf_op jit(solution)/shard_map/jit(dynamic_index_in_dim)/squeeze | solution.py:150
  18.8 0.0 collective-permute-done.refs_3_
  18.8 1.7 %collective-permute-start.7 = (bf16[2,128,512]{2,1,0:T(8,128)(2,1)S(1)}, bf16[2,128,512]{2,1,0:T(8,128)(2,1)S(1)}, u32[]{:S(2)}, u32[]{:S(2)}) collective-permute-start(bf16[2,128,512]{2,1,0:T(8,128)(2,1)S(1)} %collective-permute-done.refs_3_), channel_id=1, source_target_pairs={{0,8},{8,0},{16,24},{24,16},{28,20},{20,28},{12,4},{4,12},{1,9},{9... | collective-permute-start | bytes 786440 | tf_op jit(solution)/shard_map/ppermute | solution.py:33
  20.4 1.5 %collective-permute-start.8 = (bf16[2,128,512]{2,1,0:T(8,128)(2,1)S(1)}, bf16[2,128,512]{2,1,0:T(8,128)(2,1)S(1)}, u32[]{:S(2)}, u32[]{:S(2)}) collective-permute-start(bf16[2,128,512]{2,1,0:T(8,128)(2,1)S(1)} %get-tuple-element.50), channel_id=1, source_target_pairs={{0,4},{8,16},{16,8},{24,28},{28,24},{20,12},{12,20},{4,0},{1,5},{9... | collective-permute-start | bytes 786440 | tf_op jit(solution)/shard_map/ppermute | solution.py:33
  21.9 0.0 copy-done.1
  21.9 2.4 %shard_map.65.refs_4_ = f32[4,256,1024]{2,1,0:T(8,128)S(1)} custom-call(s32[12]{0:T(128)S(1)} %dynamic-slice_bitcast_fusion.table_ref, bf16[2,1024,1024]{2,1,0:T(8,128)(2,1)S(1)} %shard_map.64.a_ref, bf16[2,128,1024]{2,1,0:T(8,128)(2,1)S(1)} %copy-done.1, bf16[2,128,1024]{2,1,0:T(8,128)(2,1)S(1)} %collective-permute-done.1.refs_1_, ...), custom_call_target="tpu_custom_call" | custom-call | flops 1610612736 | bytes 6291456 | tf_op jit(solution)/shard_map/pallas_call | solution.py:127
  24.3 0.0 collective-permute-done.4.refs_0_
  24.3 1.0 %collective-permute-done.2.refs_2_ = bf16[2,128,512]{2,1,0:T(8,128)(2,1)S(1)} collective-permute-done((bf16[2,128,512]{2,1,0:T(8,128)(2,1)S(1)}, bf16[2,128,512]{2,1,0:T(8,128)(2,1)S(1)}, u32[]{:S(2)}, u32[]{:S(2)}) %collective-permute-start.2) | collective-permute-done | bytes 262176 | tf_op jit(solution)/shard_map/ppermute | solution.py:33
  25.3 2.1 %collective-permute-start.5 = (bf16[2,128,512]{2,1,0:T(8,128)(2,1)S(1)}, bf16[2,128,512]{2,1,0:T(8,128)(2,1)S(1)}, u32[]{:S(2)}, u32[]{:S(2)}) collective-permute-start(bf16[2,128,512]{2,1,0:T(8,128)(2,1)S(1)} %collective-permute-done.2.refs_2_), channel_id=1, source_target_pairs={{0,8},{8,0},{16,24},{24,16},{28,20},{20,28},{12,4},{4,12},{1,9},{9... | collective-permute-start | bytes 786440 | tf_op jit(solution)/shard_map/ppermute | solution.py:33
  27.4 1.5 %collective-permute-start.6 = (bf16[2,128,512]{2,1,0:T(8,128)(2,1)S(1)}, bf16[2,128,512]{2,1,0:T(8,128)(2,1)S(1)}, u32[]{:S(2)}, u32[]{:S(2)}) collective-permute-start(bf16[2,128,512]{2,1,0:T(8,128)(2,1)S(1)} %collective-permute-done.4.refs_0_), channel_id=1, source_target_pairs={{0,4},{8,16},{16,8},{24,28},{28,24},{20,12},{12,20},{4,0},{1,5},{9... | collective-permute-start | bytes 786440 | tf_op jit(solution)/shard_map/ppermute | solution.py:33
  28.9 0.0 collective-permute-done.7.refs_1_
  28.9 0.8 %collective-permute-start.14 = (bf16[2,128,512]{2,1,0:T(8,128)(2,1)S(1)}, bf16[2,128,512]{2,1,0:T(8,128)(2,1)S(1)}, u32[]{:S(2)}, u32[]{:S(2)}) collective-permute-start(bf16[2,128,512]{2,1,0:T(8,128)(2,1)S(1)} %collective-permute-done.7.refs_1_), channel_id=1, source_target_pairs={{0,4},{8,16},{16,8},{24,28},{28,24},{20,12},{12,20},{4,0},{1,5},{9... | collective-permute-start | bytes 786440 | tf_op jit(solution)/shard_map/ppermute | solution.py:33
  29.7 1.2 %collective-permute-done.8.refs_3_ = bf16[2,128,512]{2,1,0:T(8,128)(2,1)S(1)} collective-permute-done((bf16[2,128,512]{2,1,0:T(8,128)(2,1)S(1)}, bf16[2,128,512]{2,1,0:T(8,128)(2,1)S(1)}, u32[]{:S(2)}, u32[]{:S(2)}) %collective-permute-start.8) | collective-permute-done | bytes 262176 | tf_op jit(solution)/shard_map/ppermute | solution.py:33
  31.0 2.1 %collective-permute-start.10 = (bf16[2,128,512]{2,1,0:T(8,128)(2,1)S(1)}, bf16[2,128,512]{2,1,0:T(8,128)(2,1)S(1)}, u32[]{:S(2)}, u32[]{:S(2)}) collective-permute-start(bf16[2,128,512]{2,1,0:T(8,128)(2,1)S(1)} %collective-permute-done.8.refs_3_), channel_id=1, source_target_pairs={{0,8},{8,0},{16,24},{24,16},{28,20},{20,28},{12,4},{4,12},{1,9},{9... | collective-permute-start | bytes 786440 | tf_op jit(solution)/shard_map/ppermute | solution.py:33
  33.0 1.9 %shard_map.66.refs_2_ = f32[4,256,1024]{2,1,0:T(8,128)S(1)} custom-call(s32[12]{0:T(128)S(1)} %dynamic-slice_bitcast_fusion.table_ref, bf16[2,1024,1024]{2,1,0:T(8,128)(2,1)S(1)} %shard_map.64.a_ref, bf16[2,128,512]{2,1,0:T(8,128)(2,1)S(1)} %collective-permute-done.4.refs_0_, bf16[2,128,512]{2,1,0:T(8,128)(2,1)S(1)} %collective-permute-done.7.refs_1_, ...), custom_call_target="tpu_custom_call" | custom-call | flops 1073741824 | bytes 6291456 | tf_op jit(solution)/shard_map/pallas_call | solution.py:127
  34.9 0.0 collective-permute-done.5.refs_0_
  34.9 1.7 %collective-permute-done.6.refs_1_ = bf16[2,128,512]{2,1,0:T(8,128)(2,1)S(1)} collective-permute-done((bf16[2,128,512]{2,1,0:T(8,128)(2,1)S(1)}, bf16[2,128,512]{2,1,0:T(8,128)(2,1)S(1)}, u32[]{:S(2)}, u32[]{:S(2)}) %collective-permute-start.6) | collective-permute-done | bytes 262176 | tf_op jit(solution)/shard_map/ppermute | solution.py:33
  36.6 2.0 %collective-permute-start.9 = (bf16[2,128,512]{2,1,0:T(8,128)(2,1)S(1)}, bf16[2,128,512]{2,1,0:T(8,128)(2,1)S(1)}, u32[]{:S(2)}, u32[]{:S(2)}) collective-permute-start(bf16[2,128,512]{2,1,0:T(8,128)(2,1)S(1)} %collective-permute-done.6.refs_1_), channel_id=1, source_target_pairs={{0,8},{8,0},{16,24},{24,16},{28,20},{20,28},{12,4},{4,12},{1,9},{9... | collective-permute-start | bytes 786440 | tf_op jit(solution)/shard_map/ppermute | solution.py:33
  38.6 1.3 %shard_map.67.refs_1_ = f32[4,256,512]{2,1,0:T(8,128)S(1)} custom-call(s32[12]{0:T(128)S(1)} %dynamic-slice_bitcast_fusion.table_ref, bf16[2,1024,1024]{2,1,0:T(8,128)(2,1)S(1)} %shard_map.64.a_ref, bf16[2,128,512]{2,1,0:T(8,128)(2,1)S(1)} %collective-permute-done.5.refs_0_, bf16[2,128,512]{2,1,0:T(8,128)(2,1)S(1)} %collective-permute-done.6.refs_1_, ...), custom_call_target="tpu_custom_call" | custom-call | flops 10737418240 | bytes 4718592 | tf_op jit(solution)/shard_map/pallas_call | solution.py:127
  39.9 0.3 collective-permute-done.10.refs_0_
  40.2 1.9 %collective-permute-start.13 = (bf16[2,128,512]{2,1,0:T(8,128)(2,1)S(1)}, bf16[2,128,512]{2,1,0:T(8,128)(2,1)S(1)}, u32[]{:S(2)}, u32[]{:S(2)}) collective-permute-start(bf16[2,128,512]{2,1,0:T(8,128)(2,1)S(1)} %collective-permute-done.10.refs_0_), channel_id=1, source_target_pairs={{0,4},{8,16},{16,8},{24,28},{28,24},{20,12},{12,20},{4,0},{1,5},{9... | collective-permute-start | bytes 786440 | tf_op jit(solution)/shard_map/ppermute | solution.py:33
  42.1 0.2 collective-permute-done.14.refs_1_
  42.3 1.3 %shard_map.70.refs_1_ = f32[4,256,512]{2,1,0:T(8,128)S(1)} custom-call(s32[12]{0:T(128)S(1)} %dynamic-slice_bitcast_fusion.table_ref, bf16[2,1024,1024]{2,1,0:T(8,128)(2,1)S(1)} %shard_map.64.a_ref, bf16[2,128,512]{2,1,0:T(8,128)(2,1)S(1)} %collective-permute-done.10.refs_0_, bf16[2,128,512]{2,1,0:T(8,128)(2,1)S(1)} %collective-permute-done.14.refs_1_, ...), custom_call_target="tpu_custom_call" | custom-call | flops 536870912 | bytes 4718592 | tf_op jit(solution)/shard_map/pallas_call | solution.py:127
  43.6 0.0 collective-permute-done.9.refs_0_
  43.6 1.0 %shard_map.68 = (bf16[256,512]{1,0:T(8,128)(2,1)S(1)}, f32[256,512]{1,0:T(8,128)S(1)}, f32[256,512]{1,0:T(8,128)S(1)}, bf16[256,512]{1,0:T(8,128)(2,1)S(1)}) custom-call(s32[12]{0:T(128)S(1)} %dynamic-slice_bitcast_fusion.table_ref, bf16[2,1024,1024]{2,1,0:T(8,128)(2,1)S(1)} %shard_map.64.a_ref, bf16[2,128,512]{2,1,0:T(8,128)(2,1)S(1)} %collective-permute-done.9.refs_0_, ...), custom_call_target="tpu_custom_call" | custom-call | flops 268435456 | bytes 4456448 | tf_op jit(solution)/shard_map/pallas_call | solution.py:127
  44.6 0.1 collective-permute-start.12
  44.7 1.9 %collective-permute-done.13.refs_0_ = bf16[2,128,512]{2,1,0:T(8,128)(2,1)S(1)} collective-permute-done((bf16[2,128,512]{2,1,0:T(8,128)(2,1)S(1)}, bf16[2,128,512]{2,1,0:T(8,128)(2,1)S(1)}, u32[]{:S(2)}, u32[]{:S(2)}) %collective-permute-start.13) | collective-permute-done | bytes 262176 | tf_op jit(solution)/shard_map/ppermute | solution.py:33
  46.6 1.0 %shard_map.71 = (bf16[256,512]{1,0:T(8,128)(2,1)S(1)}, f32[256,512]{1,0:T(8,128)S(1)}, f32[256,512]{1,0:T(8,128)S(1)}, bf16[256,512]{1,0:T(8,128)(2,1)S(1)}) custom-call(s32[12]{0:T(128)S(1)} %dynamic-slice_bitcast_fusion.table_ref, bf16[2,1024,1024]{2,1,0:T(8,128)(2,1)S(1)} %shard_map.64.a_ref, bf16[2,128,512]{2,1,0:T(8,128)(2,1)S(1)} %collective-permute-done.13.refs_0_, ...), custom_call_target="tpu_custom_call" | custom-call | flops 5368709120 | bytes 4456448 | tf_op jit(solution)/shard_map/pallas_call | solution.py:127
  47.6 0.0 copy-start.3
  47.6 0.0 copy-start.4
  47.6 0.0 collective-permute-done.12.got_ref
  47.7 0.1 collective-permute-start.17
  47.8 0.5 collective-permute-start.11
  48.3 1.9 %collective-permute-start.15 = (bf16[256,512]{1,0:T(8,128)(2,1)S(1)}, bf16[256,512]{1,0:T(8,128)(2,1)S(1)}, u32[]{:S(2)}, u32[]{:S(2)}) collective-permute-start(bf16[256,512]{1,0:T(8,128)(2,1)S(1)} %shard_map.69), channel_id=1, source_target_pairs={{0,2},{2,0},{1,3},{3,1},{4,6},{6,4},{5,7},{7,5},{8,10},{10,8},{9,1... | collective-permute-start | bytes 786440 | tf_op jit(solution)/shard_map/ppermute | solution.py:37
  50.2 0.0 collective-permute-start.16
  50.2 0.0 collective-permute-done.17.got_ref
  50.2 0.1 shard_map.72
  50.2 1.1 %collective-permute-start.18 = (bf16[256,512]{1,0:T(8,128)(2,1)S(1)}, bf16[256,512]{1,0:T(8,128)(2,1)S(1)}, u32[]{:S(2)}, u32[]{:S(2)}) collective-permute-start(bf16[256,512]{1,0:T(8,128)(2,1)S(1)} %shard_map.72), channel_id=1, source_target_pairs={{0,2},{2,0},{1,3},{3,1},{4,6},{6,4},{5,7},{7,5},{8,10},{10,8},{9,1... | collective-permute-start | bytes 786440 | tf_op jit(solution)/shard_map/ppermute | solution.py:37
  51.3 0.0 collective-permute-done.11
  51.3 6.1 %collective-permute-done.15 = bf16[256,512]{1,0:T(8,128)(2,1)S(1)} collective-permute-done((bf16[256,512]{1,0:T(8,128)(2,1)S(1)}, bf16[256,512]{1,0:T(8,128)(2,1)S(1)}, u32[]{:S(2)}, u32[]{:S(2)}) %collective-permute-start.15) | collective-permute-done | bytes 262176 | tf_op jit(solution)/shard_map/ppermute | solution.py:37
  57.4 0.1 convert_add_fusion.1
  57.5 0.0 collective-permute-done.16
  57.5 4.8 %collective-permute-done.18 = bf16[256,512]{1,0:T(8,128)(2,1)S(1)} collective-permute-done((bf16[256,512]{1,0:T(8,128)(2,1)S(1)}, bf16[256,512]{1,0:T(8,128)(2,1)S(1)}, u32[]{:S(2)}, u32[]{:S(2)}) %collective-permute-start.18) | collective-permute-done | bytes 262176 | tf_op jit(solution)/shard_map/ppermute | solution.py:37
  62.3 0.1 convert_add_fusion
  62.4 0.0 copy-done.3
  62.4 0.0 copy-done.4
  62.4 1.0 %fusion = bf16[256,1024]{1,0:T(8,128)(2,1)} fusion(f32[256,512]{1,0:T(8,128)S(1)} %convert_add_fusion, f32[256,512]{1,0:T(8,128)S(1)} %convert_add_fusion.1, f32[256]{0:T(256)S(1)} %copy-done.4, f32[1024]{0:T(1024)S(1)} %copy-done.3), kind=kLoop, calls=%fused_computation.1 | loop fusion | flops 1048576 | bytes 1577984 | tf_op jit(solution)/shard_map/convert_element_type | solution.py:201
  (2 shorter events, 0.1 us)
Async XLA Ops:
  0.0 16.0 %collective-permute-start.1 = (bf16[2,128,1024]{2,1,0:T(8,128)(2,1)}, bf16[2,128,1024]{2,1,0:T(8,128)(2,1)S(1)}, u32[]{:S(2)}, u32[]{:S(2)}) collective-permute-start(bf16[2,128,1024]{2,1,0:T(8,128)(2,1)} %refs_0_.1), channel_id=1, source_target_pairs={{0,8},{8,0},{16,24},{24,16},{28,20},{20,28},{12,4},{4,12},{1,9},{9... | collective-permute-start | bytes 1572872 | tf_op jit(solution)/shard_map/ppermute | solution.py:33
  4.1 9.3 %collective-permute-start.3 = (bf16[2,128,512]{2,1,0:T(8,128)(2,1)S(1)}, bf16[2,128,512]{2,1,0:T(8,128)(2,1)S(1)}, u32[]{:S(2)}, u32[]{:S(2)}) collective-permute-start(bf16[2,128,512]{2,1,0:T(8,128)(2,1)S(1)} %get-tuple-element.47), channel_id=1, source_target_pairs={{0,4},{8,16},{16,8},{24,28},{28,24},{20,12},{12,20},{4,0},{1,5},{9... | collective-permute-start | bytes 786440 | tf_op jit(solution)/shard_map/ppermute | solution.py:33
  5.6 13.1 %collective-permute-start = (bf16[2,128,512]{2,1,0:T(8,128)(2,1)S(1)}, bf16[2,128,512]{2,1,0:T(8,128)(2,1)S(1)}, u32[]{:S(2)}, u32[]{:S(2)}) collective-permute-start(bf16[2,128,512]{2,1,0:T(8,128)(2,1)S(1)} %get-tuple-element.48), channel_id=1, source_target_pairs={{0,4},{8,16},{16,8},{24,28},{28,24},{20,12},{12,20},{4,0},{1,5},{9... | collective-permute-start | bytes 786440 | tf_op jit(solution)/shard_map/ppermute | solution.py:33
  6.2 2.2 %copy-start = (bf16[1024,2,1024]{2,1,0:T(2,128)(2,1)S(1)}, bf16[1024,2,1024]{2,1,0:T(2,128)(2,1)}, u32[]{:S(2)}) copy-start(bf16[1024,2,1024]{2,1,0:T(2,128)(2,1)} %amplitudes_ref.1) | copy-start | bytes 12582916
  8.4 0.7 %copy-start.2 = (s32[1024,2]{0,1:T(2,128)S(1)}, s32[1024,2]{0,1:T(2,128)}, u32[]{:S(2)}) copy-start(s32[1024,2]{0,1:T(2,128)} %param.7) | copy-start | bytes 24580
  9.1 12.9 %copy-start.1 = (bf16[2,128,1024]{2,1,0:T(8,128)(2,1)S(1)}, bf16[2,128,1024]{2,1,0:T(8,128)(2,1)}, u32[]{:S(2)}) copy-start(bf16[2,128,1024]{2,1,0:T(8,128)(2,1)} %refs_0_.1) | copy-start | bytes 1572868
  13.4 10.9 %collective-permute-start.4 = (bf16[2,128,512]{2,1,0:T(8,128)(2,1)S(1)}, bf16[2,128,512]{2,1,0:T(8,128)(2,1)S(1)}, u32[]{:S(2)}, u32[]{:S(2)}) collective-permute-start(bf16[2,128,512]{2,1,0:T(8,128)(2,1)S(1)} %collective-permute-done.3.refs_2_), channel_id=1, source_target_pairs={{0,8},{8,0},{16,24},{24,16},{28,20},{20,28},{12,4},{4,12},{1,9},{9... | collective-permute-start | bytes 786440 | tf_op jit(solution)/shard_map/ppermute | solution.py:33
  16.0 9.3 %collective-permute-start.2 = (bf16[2,128,512]{2,1,0:T(8,128)(2,1)S(1)}, bf16[2,128,512]{2,1,0:T(8,128)(2,1)S(1)}, u32[]{:S(2)}, u32[]{:S(2)}) collective-permute-start(bf16[2,128,512]{2,1,0:T(8,128)(2,1)S(1)} %get-tuple-element.49), channel_id=1, source_target_pairs={{0,4},{8,16},{16,8},{24,28},{28,24},{20,12},{12,20},{4,0},{1,5},{9... | collective-permute-start | bytes 786440 | tf_op jit(solution)/shard_map/ppermute | solution.py:33
  18.8 10.1 %collective-permute-start.7 = (bf16[2,128,512]{2,1,0:T(8,128)(2,1)S(1)}, bf16[2,128,512]{2,1,0:T(8,128)(2,1)S(1)}, u32[]{:S(2)}, u32[]{:S(2)}) collective-permute-start(bf16[2,128,512]{2,1,0:T(8,128)(2,1)S(1)} %collective-permute-done.refs_3_), channel_id=1, source_target_pairs={{0,8},{8,0},{16,24},{24,16},{28,20},{20,28},{12,4},{4,12},{1,9},{9... | collective-permute-start | bytes 786440 | tf_op jit(solution)/shard_map/ppermute | solution.py:33
  20.4 10.5 %collective-permute-start.8 = (bf16[2,128,512]{2,1,0:T(8,128)(2,1)S(1)}, bf16[2,128,512]{2,1,0:T(8,128)(2,1)S(1)}, u32[]{:S(2)}, u32[]{:S(2)}) collective-permute-start(bf16[2,128,512]{2,1,0:T(8,128)(2,1)S(1)} %get-tuple-element.50), channel_id=1, source_target_pairs={{0,4},{8,16},{16,8},{24,28},{28,24},{20,12},{12,20},{4,0},{1,5},{9... | collective-permute-start | bytes 786440 | tf_op jit(solution)/shard_map/ppermute | solution.py:33
  25.3 9.6 %collective-permute-start.5 = (bf16[2,128,512]{2,1,0:T(8,128)(2,1)S(1)}, bf16[2,128,512]{2,1,0:T(8,128)(2,1)S(1)}, u32[]{:S(2)}, u32[]{:S(2)}) collective-permute-start(bf16[2,128,512]{2,1,0:T(8,128)(2,1)S(1)} %collective-permute-done.2.refs_2_), channel_id=1, source_target_pairs={{0,8},{8,0},{16,24},{24,16},{28,20},{20,28},{12,4},{4,12},{1,9},{9... | collective-permute-start | bytes 786440 | tf_op jit(solution)/shard_map/ppermute | solution.py:33
  27.4 9.2 %collective-permute-start.6 = (bf16[2,128,512]{2,1,0:T(8,128)(2,1)S(1)}, bf16[2,128,512]{2,1,0:T(8,128)(2,1)S(1)}, u32[]{:S(2)}, u32[]{:S(2)}) collective-permute-start(bf16[2,128,512]{2,1,0:T(8,128)(2,1)S(1)} %collective-permute-done.4.refs_0_), channel_id=1, source_target_pairs={{0,4},{8,16},{16,8},{24,28},{28,24},{20,12},{12,20},{4,0},{1,5},{9... | collective-permute-start | bytes 786440 | tf_op jit(solution)/shard_map/ppermute | solution.py:33
  28.9 13.4 %collective-permute-start.14 = (bf16[2,128,512]{2,1,0:T(8,128)(2,1)S(1)}, bf16[2,128,512]{2,1,0:T(8,128)(2,1)S(1)}, u32[]{:S(2)}, u32[]{:S(2)}) collective-permute-start(bf16[2,128,512]{2,1,0:T(8,128)(2,1)S(1)} %collective-permute-done.7.refs_1_), channel_id=1, source_target_pairs={{0,4},{8,16},{16,8},{24,28},{28,24},{20,12},{12,20},{4,0},{1,5},{9... | collective-permute-start | bytes 786440 | tf_op jit(solution)/shard_map/ppermute | solution.py:33
  31.0 9.3 %collective-permute-start.10 = (bf16[2,128,512]{2,1,0:T(8,128)(2,1)S(1)}, bf16[2,128,512]{2,1,0:T(8,128)(2,1)S(1)}, u32[]{:S(2)}, u32[]{:S(2)}) collective-permute-start(bf16[2,128,512]{2,1,0:T(8,128)(2,1)S(1)} %collective-permute-done.8.refs_3_), channel_id=1, source_target_pairs={{0,8},{8,0},{16,24},{24,16},{28,20},{20,28},{12,4},{4,12},{1,9},{9... | collective-permute-start | bytes 786440 | tf_op jit(solution)/shard_map/ppermute | solution.py:33
  36.6 6.9 %collective-permute-start.9 = (bf16[2,128,512]{2,1,0:T(8,128)(2,1)S(1)}, bf16[2,128,512]{2,1,0:T(8,128)(2,1)S(1)}, u32[]{:S(2)}, u32[]{:S(2)}) collective-permute-start(bf16[2,128,512]{2,1,0:T(8,128)(2,1)S(1)} %collective-permute-done.6.refs_1_), channel_id=1, source_target_pairs={{0,8},{8,0},{16,24},{24,16},{28,20},{20,28},{12,4},{4,12},{1,9},{9... | collective-permute-start | bytes 786440 | tf_op jit(solution)/shard_map/ppermute | solution.py:33
  40.2 6.4 %collective-permute-start.13 = (bf16[2,128,512]{2,1,0:T(8,128)(2,1)S(1)}, bf16[2,128,512]{2,1,0:T(8,128)(2,1)S(1)}, u32[]{:S(2)}, u32[]{:S(2)}) collective-permute-start(bf16[2,128,512]{2,1,0:T(8,128)(2,1)S(1)} %collective-permute-done.10.refs_0_), channel_id=1, source_target_pairs={{0,4},{8,16},{16,8},{24,28},{28,24},{20,12},{12,20},{4,0},{1,5},{9... | collective-permute-start | bytes 786440 | tf_op jit(solution)/shard_map/ppermute | solution.py:33
  44.6 3.0 %collective-permute-start.12 = (bf16[256,512]{1,0:T(8,128)(2,1)S(1)}, bf16[256,512]{1,0:T(8,128)(2,1)S(1)}, u32[]{:S(2)}, u32[]{:S(2)}) collective-permute-start(bf16[256,512]{1,0:T(8,128)(2,1)S(1)} %get-tuple-element.39), channel_id=1, source_target_pairs={{0,1},{1,0},{2,3},{3,2},{4,5},{5,4},{6,7},{7,6},{8,9},{9,8},{10,11... | collective-permute-start | bytes 786440 | tf_op jit(solution)/shard_map/ppermute | solution.py:37
  47.6 14.8 %copy-start.3 = (f32[1024]{0:T(1024)S(1)}, f32[1024]{0:T(1024)}, u32[]{:S(2)}) copy-start(f32[1024]{0:T(1024)} %param.10) | copy-start | bytes 12292
  47.6 14.8 %copy-start.4 = (f32[256]{0:T(256)S(1)}, f32[256]{0:T(256)}, u32[]{:S(2)}) copy-start(f32[256]{0:T(256)} %param.9) | copy-start | bytes 3076
  47.7 2.5 %collective-permute-start.17 = (bf16[256,512]{1,0:T(8,128)(2,1)S(1)}, bf16[256,512]{1,0:T(8,128)(2,1)S(1)}, u32[]{:S(2)}, u32[]{:S(2)}) collective-permute-start(bf16[256,512]{1,0:T(8,128)(2,1)S(1)} %get-tuple-element.46), channel_id=1, source_target_pairs={{0,1},{1,0},{2,3},{3,2},{4,5},{5,4},{6,7},{7,6},{8,9},{9,8},{10,11... | collective-permute-start | bytes 786440 | tf_op jit(solution)/shard_map/ppermute | solution.py:37
  47.8 3.5 %collective-permute-start.11 = (bf16[256,512]{1,0:T(8,128)(2,1)S(1)}, bf16[256,512]{1,0:T(8,128)(2,1)S(1)}, u32[]{:S(2)}, u32[]{:S(2)}) collective-permute-start(bf16[256,512]{1,0:T(8,128)(2,1)S(1)} %get-tuple-element.37), channel_id=1, source_target_pairs={{0,1},{1,0},{2,3},{3,2},{4,5},{5,4},{6,7},{7,6},{8,9},{9,8},{10,11... | collective-permute-start | bytes 786440 | tf_op jit(solution)/shard_map/ppermute | solution.py:37
  48.3 9.1 %collective-permute-start.15 = (bf16[256,512]{1,0:T(8,128)(2,1)S(1)}, bf16[256,512]{1,0:T(8,128)(2,1)S(1)}, u32[]{:S(2)}, u32[]{:S(2)}) collective-permute-start(bf16[256,512]{1,0:T(8,128)(2,1)S(1)} %shard_map.69), channel_id=1, source_target_pairs={{0,2},{2,0},{1,3},{3,1},{4,6},{6,4},{5,7},{7,5},{8,10},{10,8},{9,1... | collective-permute-start | bytes 786440 | tf_op jit(solution)/shard_map/ppermute | solution.py:37
  50.2 7.4 %collective-permute-start.16 = (bf16[256,512]{1,0:T(8,128)(2,1)S(1)}, bf16[256,512]{1,0:T(8,128)(2,1)S(1)}, u32[]{:S(2)}, u32[]{:S(2)}) collective-permute-start(bf16[256,512]{1,0:T(8,128)(2,1)S(1)} %get-tuple-element.44), channel_id=1, source_target_pairs={{0,1},{1,0},{2,3},{3,2},{4,5},{5,4},{6,7},{7,6},{8,9},{9,8},{10,11... | collective-permute-start | bytes 786440 | tf_op jit(solution)/shard_map/ppermute | solution.py:37
  50.2 12.1 %collective-permute-start.18 = (bf16[256,512]{1,0:T(8,128)(2,1)S(1)}, bf16[256,512]{1,0:T(8,128)(2,1)S(1)}, u32[]{:S(2)}, u32[]{:S(2)}) collective-permute-start(bf16[256,512]{1,0:T(8,128)(2,1)S(1)} %shard_map.72), channel_id=1, source_target_pairs={{0,2},{2,0},{1,3},{3,1},{4,6},{6,4},{5,7},{7,5},{8,10},{10,8},{9,1... | collective-permute-start | bytes 786440 | tf_op jit(solution)/shard_map/ppermute | solution.py:37

commit v5 on v4

--- a/solution.py
+++ b/solution.py
@@ -67,25 +67,53 @@
 
 
 def added(kept, got):
-    def body(kept_ref, got_ref, out_ref):
-        out_ref[...] = (kept_ref[...] + got_ref[...].astype(F32)).astype(BF16)
+    def body(kept_ref, *refs):
+        for n, ref in enumerate(refs[:-1]):
+            here = pl.ds(n * ref.shape[0], ref.shape[0])
+            refs[-1][here] = (kept_ref[here] + ref[...].astype(F32)).astype(BF16)
 
     vmem = pl.BlockSpec(memory_space=pltpu.VMEM)
     return pl.pallas_call(
         body,
-        in_specs=[vmem, vmem],
+        in_specs=[vmem] * (1 + len(got)),
         out_specs=vmem,
         out_shape=jax.ShapeDtypeStruct(kept.shape, BF16),
         compiler_params=pltpu.CompilerParams(vmem_limit_bytes=4 * 2**20),
         cost_estimate=pl.CostEstimate(flops=0, bytes_accessed=0, transcendentals=0),
-    )(kept, got)
+    )(kept, *got)
+
+
+def quotient(kept, got, from_y, pair_energy, virt_energy, span, left=None, weight=1):
+    rows = kept.shape[0]
+
+    def body(kept_ref, got_ref, from_y_ref, pair_ref, virt_ref, *refs):
+        out_ref = refs[-1]
+        pair = jnp.transpose(jnp.concatenate([pair_ref[...]] * 8, axis=0))[:, :1]
+        ladder = kept_ref[...] + got_ref[...].astype(F32) + from_y_ref[...].astype(F32)
+        value = (ladder / (virt_ref[:, span[0] : span[1]] - pair)).astype(BF16)
+        if left is None:
+            out_ref[...] = value
+        else:
+            out_ref[:, : span[0]] = refs[0][...]
+            out_ref[:, span[0] :] = value
+
+    vmem = pl.BlockSpec(memory_space=pltpu.VMEM)
+    more = [] if left is None else [left]
+    return pl.pallas_call(
+        body,
+        in_specs=[vmem] * (5 + len(more)),
+        out_specs=vmem,
+        out_shape=jax.ShapeDtypeStruct((rows, span[1] - (span[0] if left is None else 0)), BF16),
+        compiler_params=pltpu.CompilerParams(vmem_limit_bytes=8 * 2**20),
+        cost_estimate=pl.CostEstimate(flops=weight * 10**8, bytes_accessed=weight * 10**6, transcendentals=0),
+    )(kept, got, from_y, pair_energy[None, :], virt_energy[None, :], *more)
 
 
 def tie(*values):
     return lax.optimization_barrier(values)
 
 
-def products(table, slots, a, blocks, span, total=None, finish=False, weight=1):
+def products(table, slots, a, blocks, span, total=None, finish=0, weight=1):
     blocks = [b if isinstance(b, list) else [b] for b in blocks]
     flat = [v for b in blocks for v in b]
     tiles, depth = flat[0].shape[:2]
@@ -113,7 +141,11 @@
             if total is not None:
                 acc += total_ref[i, :, lo:hi] if total.shape[2] > columns else total_ref[i]
             if finish:
-                outs[i - 1][...] = acc.astype(outs[i - 1].dtype)
+                if i > 0:
+                    outs[i - 1][...] = acc.astype(outs[i - 1].dtype)
+                else:
+                    for n, ref in enumerate(outs[3:]):
+                        ref[...] = acc[n * ref.shape[0] : (n + 1) * ref.shape[0]].astype(BF16)
             else:
                 outs[0][i] = acc
 
@@ -121,7 +153,8 @@
     smem = pl.BlockSpec(memory_space=pltpu.SMEM)
     operands = [a] + flat + ([] if total is None else [total])
     if finish:
-        out_shape = [jax.ShapeDtypeStruct((row, columns), t) for t in (BF16, F32, F32, BF16)]
+        out_shape = [jax.ShapeDtypeStruct((row, columns), t) for t in (BF16, F32, F32)]
+        out_shape += [jax.ShapeDtypeStruct((row // finish, columns), BF16)] * finish
     else:
         out_shape = [jax.ShapeDtypeStruct((4, row, columns), F32)]
     out = pl.pallas_call(
@@ -175,30 +208,24 @@
     e3b, total_a = tie(e3b, total_a)
     last_b = over_pair(e3b, ODD)
     total_b = products(table, [5, 6], a, [e3b, o3b], span_b, total=total)
-
-    here_a, keep_there_a, keep_here_a, there_a = products(
-        table, [7], a, [last_a], span_a, total=total_a, finish=True
-    )
-    got_there_a = over_virt(there_a, CORE)
-    here_b, keep_there_b, keep_here_b, there_b = products(
-        table, [7], a, [last_b], span_b, total=total_b, finish=True, weight=20
-    )
+    last_a, total_b = tie(last_a, total_b)
+
+    here_a, keep_there_a, keep_here_a, *there_a = products(
+        table, [7], a, [last_a], span_a, total=total_a, finish=2, weight=0
+    )
+    got_there_a = [over_virt(v, CORE) for v in there_a]
+    got_there_a[0], total_b = tie(got_there_a[0], total_b)
     mine_a = added(keep_there_a, got_there_a)
-    mine_a, there_b = tie(mine_a, there_b)
+    here_b, keep_there_b, keep_here_b, *there_b = products(
+        table, [7], a, [last_b], span_b, total=total_b, finish=2, weight=20
+    )
     from_y_a = over_virt(mine_a, YHOP)
-    got_there_b = over_virt(there_b, CORE)
+    got_there_b = [over_virt(v, CORE) for v in there_b]
     from_y_b = over_virt(added(keep_there_b, got_there_b), YHOP)
     got_here_a, got_here_b = over_virt(here_a, CORE), over_virt(here_b, CORE)
-
-    ladder = jnp.concatenate(
-        [
-            keep_here_a + got_here_a.astype(F32) + from_y_a.astype(F32),
-            keep_here_b + got_here_b.astype(F32) + from_y_b.astype(F32),
-        ],
-        axis=1,
-    )
-    denom = virt_energy[None, :] - pair_energy[:, None]
-    return (ladder / denom).astype(BF16)
+    left = quotient(keep_here_a, got_here_a, from_y_a, pair_energy, virt_energy, span_a, weight=20)
+    from_y_b, left = tie(from_y_b, left)
+    return quotient(keep_here_b, got_here_b, from_y_b, pair_energy, virt_energy, span_b, left=left)
 
 
 def solution(mesh):

time: 63.7 us -> 61.8 us (0.970)
  waiting for transfers between devices: 21.2 us -> 19.4 us
  Pallas kernels: 10.8 us -> 12.2 us
  other arithmetic: 1.21 us -> 0 us
    ppermute x13, waiting for transfers between devices: 10.3 us -> 8.41 us  [over_pair(): return lax.ppermute(value, 'pair', hops)]
    pallas_call x2 -> x4, Pallas kernels: 0.11 us -> 1.47 us  [the longest x2 1.35 us: quotient(): pl.pallas_call(body, in_specs=[vmem] * (5 + len(more)), out_specs=vmem, o...]
    convert_element_type x1 -> x0, other arithmetic: 1.01 us -> none  [scheduled(): return (ladder / denom).astype(BF16)]
    ppermute x6 -> x8, starting transfers between devices: 3.61 us -> 3.51 us  [over_virt(): return lax.ppermute(value, 'virt', hops)]
    ppermute x6 -> x8, waiting for transfers between devices: 10.9 us -> 11 us  [over_virt(): return lax.ppermute(value, 'virt', hops)]
  transfers between devices with their start and end apart: 19 -> 21, of which waited for: 10 -> 13; matrix products, arithmetic and copies ran while one was open for 3% -> 3% of each run, Pallas kernels for 17% -> 18%
where the time goes in v5:
time: 61.8 us; the launch traced here: 61.6 us
  starting transfers between devices  25.2 us (41%)
  waiting for transfers between devices  19.4 us (31%)
  Pallas kernels  12.2 us (20%)
  local copies, waits for them, and re-layouts  4.69 us (8%)
    ppermute x13, starting transfers between devices, over_pair(): return lax.ppermute(value, 'pair', hops)  21.7 us
    ppermute x8, waiting for transfers between devices, over_virt(): return lax.ppermute(value, 'virt', hops)  11 us
    pallas_call x6, Pallas kernels, products(): pl.pallas_call(body, in_specs=[smem] + [vmem] * len(operands), out_specs=...  8.89 us
    ppermute x13, waiting for transfers between devices, over_pair(): return lax.ppermute(value, 'pair', hops)  8.41 us
    ppermute x8, starting transfers between devices, over_virt(): return lax.ppermute(value, 'virt', hops)  3.51 us
    unnamed x10, local copies, waits for them, and re-layouts  2.9 us
    pallas_call x1, Pallas kernels, arranged(): pl.pallas_call(body, in_specs=[vmem, vmem], out_specs=vmem, out_shape=jax...  1.85 us
    pallas_call x2, Pallas kernels, quotient(): pl.pallas_call(body, in_specs=[vmem] * (5 + len(more)), out_specs=vmem, o...  1.35 us
  transfers between devices with their start and end apart: 21, of which 13 were waited for; matrix products, arithmetic and copies ran while one was open for 3% of the time, Pallas kernels for 18%

profile of v5, /device:TPU:0, one launch (start us, length us, event | category | flops | bytes accessed | tf_op | source)
XLA Modules:
  0.0 61.6 jit_solution(1384753904427588472)
XLA Ops:
  0.0 3.0 %collective-permute-start.1 = (bf16[2,128,1024]{2,1,0:T(8,128)(2,1)}, bf16[2,128,1024]{2,1,0:T(8,128)(2,1)S(1)}, u32[]{:S(2)}, u32[]{:S(2)}) collective-permute-start(bf16[2,128,1024]{2,1,0:T(8,128)(2,1)} %refs_0_.1), channel_id=1, source_target_pairs={{0,8},{8,0},{16,24},{24,16},{28,20},{20,28},{12,4},{4,12},{1,9},{9... | collective-permute-start | bytes 1572872 | tf_op jit(solution)/shard_map/ppermute | solution.py:33
  3.0 1.1 %fusion = (bf16[2,128,512]{2,1,0:T(8,128)(2,1)S(1)}, bf16[2,128,512]{2,1,0:T(8,128)(2,1)S(1)}) fusion(bf16[2,128,1024]{2,1,0:T(8,128)(2,1)} %refs_0_.1), kind=kLoop, calls=%fused_computation.1 | loop fusion | bytes 1048576 | tf_op jit(solution)/shard_map/slice | solution.py:192
  4.1 1.6 %collective-permute-start.5 = (bf16[2,128,512]{2,1,0:T(8,128)(2,1)S(1)}, bf16[2,128,512]{2,1,0:T(8,128)(2,1)S(1)}, u32[]{:S(2)}, u32[]{:S(2)}) collective-permute-start(bf16[2,128,512]{2,1,0:T(8,128)(2,1)S(1)} %get-tuple-element.59), channel_id=1, source_target_pairs={{0,4},{8,16},{16,8},{24,28},{28,24},{20,12},{12,20},{4,0},{1,5},{9... | collective-permute-start | bytes 786440 | tf_op jit(solution)/shard_map/ppermute | solution.py:33
  5.6 0.5 collective-permute-start
  6.2 0.0 copy-start
  6.2 2.2 %copy-done = bf16[1024,2,1024]{2,1,0:T(2,128)(2,1)S(1)} copy-done((bf16[1024,2,1024]{2,1,0:T(2,128)(2,1)S(1)}, bf16[1024,2,1024]{2,1,0:T(2,128)(2,1)}, u32[]{:S(2)}) %copy-start) | copy-done | bytes 4194328
  8.4 0.0 copy-start.2
  8.4 0.7 %copy-done.2 = s32[1024,2]{0,1:T(2,128)S(1)} copy-done((s32[1024,2]{0,1:T(2,128)S(1)}, s32[1024,2]{0,1:T(2,128)}, u32[]{:S(2)}) %copy-start.2) | copy-done | bytes 8216
  9.1 1.8 %shard_map.64.a_ref = bf16[2,1024,1024]{2,1,0:T(8,128)(2,1)S(1)} custom-call(bf16[1024,2,1024]{2,1,0:T(2,128)(2,1)S(1)} %copy-done, s32[2,1024]{1,0:T(2,128)S(1)} %bitcast.5), custom_call_target="tpu_custom_call" | custom-call | flops 2147483648 | bytes 8388608 | tf_op jit(solution)/shard_map/pallas_call | solution.py:57
  10.9 2.5 %collective-permute-done.5.refs_2_ = bf16[2,128,512]{2,1,0:T(8,128)(2,1)S(1)} collective-permute-done((bf16[2,128,512]{2,1,0:T(8,128)(2,1)S(1)}, bf16[2,128,512]{2,1,0:T(8,128)(2,1)S(1)}, u32[]{:S(2)}, u32[]{:S(2)}) %collective-permute-start.5) | collective-permute-done | bytes 262176 | tf_op jit(solution)/shard_map/ppermute | solution.py:33
  13.4 1.1 %collective-permute-start.6 = (bf16[2,128,512]{2,1,0:T(8,128)(2,1)S(1)}, bf16[2,128,512]{2,1,0:T(8,128)(2,1)S(1)}, u32[]{:S(2)}, u32[]{:S(2)}) collective-permute-start(bf16[2,128,512]{2,1,0:T(8,128)(2,1)S(1)} %collective-permute-done.5.refs_2_), channel_id=1, source_target_pairs={{0,8},{8,0},{16,24},{24,16},{28,20},{20,28},{12,4},{4,12},{1,9},{9... | collective-permute-start | bytes 786440 | tf_op jit(solution)/shard_map/ppermute | solution.py:33
  14.5 1.5 %collective-permute-done.1.refs_1_ = bf16[2,128,1024]{2,1,0:T(8,128)(2,1)S(1)} collective-permute-done((bf16[2,128,1024]{2,1,0:T(8,128)(2,1)}, bf16[2,128,1024]{2,1,0:T(8,128)(2,1)S(1)}, u32[]{:S(2)}, u32[]{:S(2)}) %collective-permute-start.1) | collective-permute-done | bytes 524320 | tf_op jit(solution)/shard_map/ppermute | solution.py:33
  16.0 2.0 %collective-permute-start.4 = (bf16[2,128,512]{2,1,0:T(8,128)(2,1)S(1)}, bf16[2,128,512]{2,1,0:T(8,128)(2,1)S(1)}, u32[]{:S(2)}, u32[]{:S(2)}) collective-permute-start(bf16[2,128,512]{2,1,0:T(8,128)(2,1)S(1)} %get-tuple-element.61), channel_id=1, source_target_pairs={{0,4},{8,16},{16,8},{24,28},{28,24},{20,12},{12,20},{4,0},{1,5},{9... | collective-permute-start | bytes 786440 | tf_op jit(solution)/shard_map/ppermute | solution.py:33
  18.1 0.7 %dynamic-slice_bitcast_fusion.table_ref = s32[12]{0:T(128)S(1)} fusion(s32[32,12]{1,0:T(8,128)} %constant.19.clone, s32[]{:T(128)S(6)} %select_n.4), kind=kLoop, calls=%fused_computation | loop fusion | bytes 100 | tf_op jit(solution)/shard_map/jit(dynamic_index_in_dim)/squeeze | solution.py:183
  18.8 0.0 collective-permute-done.refs_3_
  18.8 1.7 %collective-permute-start.9 = (bf16[2,128,512]{2,1,0:T(8,128)(2,1)S(1)}, bf16[2,128,512]{2,1,0:T(8,128)(2,1)S(1)}, u32[]{:S(2)}, u32[]{:S(2)}) collective-permute-start(bf16[2,128,512]{2,1,0:T(8,128)(2,1)S(1)} %collective-permute-done.refs_3_), channel_id=1, source_target_pairs={{0,8},{8,0},{16,24},{24,16},{28,20},{20,28},{12,4},{4,12},{1,9},{9... | collective-permute-start | bytes 786440 | tf_op jit(solution)/shard_map/ppermute | solution.py:33
  20.4 1.5 %collective-permute-start.2 = (bf16[2,128,512]{2,1,0:T(8,128)(2,1)S(1)}, bf16[2,128,512]{2,1,0:T(8,128)(2,1)S(1)}, u32[]{:S(2)}, u32[]{:S(2)}) collective-permute-start(bf16[2,128,512]{2,1,0:T(8,128)(2,1)S(1)} %get-tuple-element.62), channel_id=1, source_target_pairs={{0,4},{8,16},{16,8},{24,28},{28,24},{20,12},{12,20},{4,0},{1,5},{9... | collective-permute-start | bytes 786440 | tf_op jit(solution)/shard_map/ppermute | solution.py:33
  21.9 0.0 copy-done.1
  21.9 2.4 %shard_map.65.refs_4_ = f32[4,256,1024]{2,1,0:T(8,128)S(1)} custom-call(s32[12]{0:T(128)S(1)} %dynamic-slice_bitcast_fusion.table_ref, bf16[2,1024,1024]{2,1,0:T(8,128)(2,1)S(1)} %shard_map.64.a_ref, bf16[2,128,1024]{2,1,0:T(8,128)(2,1)S(1)} %copy-done.1, bf16[2,128,1024]{2,1,0:T(8,128)(2,1)S(1)} %collective-permute-done.1.refs_1_, ...), custom_call_target="tpu_custom_call" | custom-call | flops 1610612736 | bytes 6291456 | tf_op jit(solution)/shard_map/pallas_call | solution.py:160
  24.3 0.0 collective-permute-done.6.refs_0_
  24.3 1.0 %collective-permute-done.4.refs_2_ = bf16[2,128,512]{2,1,0:T(8,128)(2,1)S(1)} collective-permute-done((bf16[2,128,512]{2,1,0:T(8,128)(2,1)S(1)}, bf16[2,128,512]{2,1,0:T(8,128)(2,1)S(1)}, u32[]{:S(2)}, u32[]{:S(2)}) %collective-permute-start.4) | collective-permute-done | bytes 262176 | tf_op jit(solution)/shard_map/ppermute | solution.py:33
  25.3 2.1 %collective-permute-start.7 = (bf16[2,128,512]{2,1,0:T(8,128)(2,1)S(1)}, bf16[2,128,512]{2,1,0:T(8,128)(2,1)S(1)}, u32[]{:S(2)}, u32[]{:S(2)}) collective-permute-start(bf16[2,128,512]{2,1,0:T(8,128)(2,1)S(1)} %collective-permute-done.4.refs_2_), channel_id=1, source_target_pairs={{0,8},{8,0},{16,24},{24,16},{28,20},{20,28},{12,4},{4,12},{1,9},{9... | collective-permute-start | bytes 786440 | tf_op jit(solution)/shard_map/ppermute | solution.py:33
  27.4 1.5 %collective-permute-start.8 = (bf16[2,128,512]{2,1,0:T(8,128)(2,1)S(1)}, bf16[2,128,512]{2,1,0:T(8,128)(2,1)S(1)}, u32[]{:S(2)}, u32[]{:S(2)}) collective-permute-start(bf16[2,128,512]{2,1,0:T(8,128)(2,1)S(1)} %collective-permute-done.6.refs_0_), channel_id=1, source_target_pairs={{0,4},{8,16},{16,8},{24,28},{28,24},{20,12},{12,20},{4,0},{1,5},{9... | collective-permute-start | bytes 786440 | tf_op jit(solution)/shard_map/ppermute | solution.py:33
  28.9 0.0 collective-permute-done.9.refs_1_
  28.9 0.8 %collective-permute-start.12 = (bf16[2,128,512]{2,1,0:T(8,128)(2,1)S(1)}, bf16[2,128,512]{2,1,0:T(8,128)(2,1)S(1)}, u32[]{:S(2)}, u32[]{:S(2)}) collective-permute-start(bf16[2,128,512]{2,1,0:T(8,128)(2,1)S(1)} %collective-permute-done.9.refs_1_), channel_id=1, source_target_pairs={{0,4},{8,16},{16,8},{24,28},{28,24},{20,12},{12,20},{4,0},{1,5},{9... | collective-permute-start | bytes 786440 | tf_op jit(solution)/shard_map/ppermute | solution.py:33
  29.7 1.2 %collective-permute-done.2.refs_3_ = bf16[2,128,512]{2,1,0:T(8,128)(2,1)S(1)} collective-permute-done((bf16[2,128,512]{2,1,0:T(8,128)(2,1)S(1)}, bf16[2,128,512]{2,1,0:T(8,128)(2,1)S(1)}, u32[]{:S(2)}, u32[]{:S(2)}) %collective-permute-start.2) | collective-permute-done | bytes 262176 | tf_op jit(solution)/shard_map/ppermute | solution.py:33
  31.0 2.1 %collective-permute-start.3 = (bf16[2,128,512]{2,1,0:T(8,128)(2,1)S(1)}, bf16[2,128,512]{2,1,0:T(8,128)(2,1)S(1)}, u32[]{:S(2)}, u32[]{:S(2)}) collective-permute-start(bf16[2,128,512]{2,1,0:T(8,128)(2,1)S(1)} %collective-permute-done.2.refs_3_), channel_id=1, source_target_pairs={{0,8},{8,0},{16,24},{24,16},{28,20},{20,28},{12,4},{4,12},{1,9},{9... | collective-permute-start | bytes 786440 | tf_op jit(solution)/shard_map/ppermute | solution.py:33
  33.0 1.9 %shard_map.66.refs_2_ = f32[4,256,1024]{2,1,0:T(8,128)S(1)} custom-call(s32[12]{0:T(128)S(1)} %dynamic-slice_bitcast_fusion.table_ref, bf16[2,1024,1024]{2,1,0:T(8,128)(2,1)S(1)} %shard_map.64.a_ref, bf16[2,128,512]{2,1,0:T(8,128)(2,1)S(1)} %collective-permute-done.6.refs_0_, bf16[2,128,512]{2,1,0:T(8,128)(2,1)S(1)} %collective-permute-done.9.refs_1_, ...), custom_call_target="tpu_custom_call" | custom-call | flops 1073741824 | bytes 6291456 | tf_op jit(solution)/shard_map/pallas_call | solution.py:160
  34.9 0.0 collective-permute-done.7.refs_0_
  34.9 1.7 %collective-permute-done.8.refs_1_ = bf16[2,128,512]{2,1,0:T(8,128)(2,1)S(1)} collective-permute-done((bf16[2,128,512]{2,1,0:T(8,128)(2,1)S(1)}, bf16[2,128,512]{2,1,0:T(8,128)(2,1)S(1)}, u32[]{:S(2)}, u32[]{:S(2)}) %collective-permute-start.8) | collective-permute-done | bytes 262176 | tf_op jit(solution)/shard_map/ppermute | solution.py:33
  36.6 2.0 %collective-permute-start.11 = (bf16[2,128,512]{2,1,0:T(8,128)(2,1)S(1)}, bf16[2,128,512]{2,1,0:T(8,128)(2,1)S(1)}, u32[]{:S(2)}, u32[]{:S(2)}) collective-permute-start(bf16[2,128,512]{2,1,0:T(8,128)(2,1)S(1)} %collective-permute-done.8.refs_1_), channel_id=1, source_target_pairs={{0,8},{8,0},{16,24},{24,16},{28,20},{20,28},{12,4},{4,12},{1,9},{9... | collective-permute-start | bytes 786440 | tf_op jit(solution)/shard_map/ppermute | solution.py:33
  38.6 1.3 %shard_map.67.refs_1_ = f32[4,256,512]{2,1,0:T(8,128)S(1)} custom-call(s32[12]{0:T(128)S(1)} %dynamic-slice_bitcast_fusion.table_ref, bf16[2,1024,1024]{2,1,0:T(8,128)(2,1)S(1)} %shard_map.64.a_ref, bf16[2,128,512]{2,1,0:T(8,128)(2,1)S(1)} %collective-permute-done.7.refs_0_, bf16[2,128,512]{2,1,0:T(8,128)(2,1)S(1)} %collective-permute-done.8.refs_1_, ...), custom_call_target="tpu_custom_call" | custom-call | flops 10737418240 | bytes 4718592 | tf_op jit(solution)/shard_map/pallas_call | solution.py:160
  39.9 0.3 collective-permute-done.3.refs_0_
  40.2 1.9 %collective-permute-start.10 = (bf16[2,128,512]{2,1,0:T(8,128)(2,1)S(1)}, bf16[2,128,512]{2,1,0:T(8,128)(2,1)S(1)}, u32[]{:S(2)}, u32[]{:S(2)}) collective-permute-start(bf16[2,128,512]{2,1,0:T(8,128)(2,1)S(1)} %collective-permute-done.3.refs_0_), channel_id=1, source_target_pairs={{0,4},{8,16},{16,8},{24,28},{28,24},{20,12},{12,20},{4,0},{1,5},{9... | collective-permute-start | bytes 786440 | tf_op jit(solution)/shard_map/ppermute | solution.py:33
  42.1 0.2 collective-permute-done.12.refs_1_
  42.3 1.3 %shard_map.68.refs_1_ = f32[4,256,512]{2,1,0:T(8,128)S(1)} custom-call(s32[12]{0:T(128)S(1)} %dynamic-slice_bitcast_fusion.table_ref, bf16[2,1024,1024]{2,1,0:T(8,128)(2,1)S(1)} %shard_map.64.a_ref, bf16[2,128,512]{2,1,0:T(8,128)(2,1)S(1)} %collective-permute-done.3.refs_0_, bf16[2,128,512]{2,1,0:T(8,128)(2,1)S(1)} %collective-permute-done.12.refs_1_, ...), custom_call_target="tpu_custom_call" | custom-call | flops 536870912 | bytes 4718592 | tf_op jit(solution)/shard_map/pallas_call | solution.py:160
  43.6 0.0 collective-permute-done.11.refs_0_
  43.6 1.0 %shard_map.69 = (bf16[256,512]{1,0:T(8,128)(2,1)S(1)}, f32[256,512]{1,0:T(8,128)S(1)}, f32[256,512]{1,0:T(8,128)S(1)}, bf16[128,512]{1,0:T(8,128)(2,1)S(1)}, bf16[128,512]{1,0:T(8,128)(2,1)S(1)}) custom-call(s32[12]{0:T(128)S(1)} %dynamic-slice_bitcast_fusion.table_ref, bf16[2,1024,1024]{2,1,0:T(8,128)(2,1)S(1)} %shard_map.64.a_ref, ...), custom_call_target="tpu_custom_call" | custom-call | tf_op jit(solution)/shard_map/pallas_call | solution.py:160
  44.6 0.1 collective-permute-start.13
  44.7 0.5 collective-permute-start.19
  45.2 0.1 collective-permute-start.18
  45.3 0.8 %collective-permute-done.13.refs_0_ = bf16[128,512]{1,0:T(8,128)(2,1)S(1)} collective-permute-done((bf16[128,512]{1,0:T(8,128)(2,1)S(1)}, bf16[128,512]{1,0:T(8,128)(2,1)S(1)}, u32[]{:S(2)}, u32[]{:S(2)}) %collective-permute-start.13) | collective-permute-done | bytes 131104 | tf_op jit(solution)/shard_map/ppermute | solution.py:37
  46.0 0.2 collective-permute-done.19.refs_1_
  46.2 0.1 shard_map.72
  46.3 0.0 copy-start.3
  46.3 0.0 copy-start.4
  46.3 1.7 %collective-permute-start.20 = (bf16[256,512]{1,0:T(8,128)(2,1)S(1)}, bf16[256,512]{1,0:T(8,128)(2,1)S(1)}, u32[]{:S(2)}, u32[]{:S(2)}) collective-permute-start(bf16[256,512]{1,0:T(8,128)(2,1)S(1)} %shard_map.72), channel_id=1, source_target_pairs={{0,2},{2,0},{1,3},{3,1},{4,6},{6,4},{5,7},{7,5},{8,10},{10,8},{9,1... | collective-permute-start | bytes 786440 | tf_op jit(solution)/shard_map/ppermute | solution.py:37
  48.0 0.0 collective-permute-done.10.refs_0_
  48.0 1.0 %shard_map.70 = (bf16[256,512]{1,0:T(8,128)(2,1)S(1)}, f32[256,512]{1,0:T(8,128)S(1)}, f32[256,512]{1,0:T(8,128)S(1)}, bf16[128,512]{1,0:T(8,128)(2,1)S(1)}, bf16[128,512]{1,0:T(8,128)(2,1)S(1)}) custom-call(s32[12]{0:T(128)S(1)} %dynamic-slice_bitcast_fusion.table_ref, bf16[2,1024,1024]{2,1,0:T(8,128)(2,1)S(1)} %shard_map.64.a_ref, ...), custom_call_target="tpu_custom_call" | custom-call | flops 5368709120 | bytes 4456448 | tf_op jit(solution)/shard_map/pallas_call | solution.py:160
  49.0 0.1 collective-permute-start.15
  49.1 0.5 collective-permute-start.16
  49.5 0.8 %collective-permute-done.15.refs_0_ = bf16[128,512]{1,0:T(8,128)(2,1)S(1)} collective-permute-done((bf16[128,512]{1,0:T(8,128)(2,1)S(1)}, bf16[128,512]{1,0:T(8,128)(2,1)S(1)}, u32[]{:S(2)}, u32[]{:S(2)}) %collective-permute-start.15) | collective-permute-done | bytes 131104 | tf_op jit(solution)/shard_map/ppermute | solution.py:37
  50.4 0.2 collective-permute-done.16.refs_1_
  50.6 0.1 shard_map.71
  50.6 0.6 collective-permute-start.17
  51.2 0.0 collective-permute-start.14
  51.3 0.0 collective-permute-done.18.got_ref
  51.3 4.2 %collective-permute-done.20.from_y_ref = bf16[256,512]{1,0:T(8,128)(2,1)S(1)} collective-permute-done((bf16[256,512]{1,0:T(8,128)(2,1)S(1)}, bf16[256,512]{1,0:T(8,128)(2,1)S(1)}, u32[]{:S(2)}, u32[]{:S(2)}) %collective-permute-start.20) | collective-permute-done | bytes 262176 | tf_op jit(solution)/shard_map/ppermute | solution.py:37
  55.5 0.0 copy-done.3
  55.5 0.0 copy-done.4
  55.5 0.3 shard_map.73.refs_0_
  55.8 4.7 %collective-permute-done.17.from_y_ref = bf16[256,512]{1,0:T(8,128)(2,1)S(1)} collective-permute-done((bf16[256,512]{1,0:T(8,128)(2,1)S(1)}, bf16[256,512]{1,0:T(8,128)(2,1)S(1)}, u32[]{:S(2)}, u32[]{:S(2)}) %collective-permute-start.17) | collective-permute-done | bytes 262176 | tf_op jit(solution)/shard_map/ppermute | solution.py:37
  60.5 0.0 collective-permute-done.14.got_ref
  60.5 1.1 %shard_map.74 = bf16[256,1024]{1,0:T(8,128)(2,1)} custom-call(f32[256,512]{1,0:T(8,128)S(1)} %get-tuple-element.47.kept_ref, bf16[256,512]{1,0:T(8,128)(2,1)S(1)} %collective-permute-done.14.got_ref, bf16[256,512]{1,0:T(8,128)(2,1)S(1)} %collective-permute-done.17.from_y_ref, f32[1,256]{1,0:T(1,128)S(1)} %bitcast.9, f32[1,1024]{1,0:T(1,128)S(1)} %bitcast.7, ...), custom_call_target="tpu_custom_call" | custom-call | flops 100000000 | bytes 1000000 | tf_op jit(solution)/shard_map/pallas_call | solution.py:102
  (2 shorter events, 0.0 us)
Async XLA Ops:
  0.0 16.0 %collective-permute-start.1 = (bf16[2,128,1024]{2,1,0:T(8,128)(2,1)}, bf16[2,128,1024]{2,1,0:T(8,128)(2,1)S(1)}, u32[]{:S(2)}, u32[]{:S(2)}) collective-permute-start(bf16[2,128,1024]{2,1,0:T(8,128)(2,1)} %refs_0_.1), channel_id=1, source_target_pairs={{0,8},{8,0},{16,24},{24,16},{28,20},{20,28},{12,4},{4,12},{1,9},{9... | collective-permute-start | bytes 1572872 | tf_op jit(solution)/shard_map/ppermute | solution.py:33
  4.1 9.3 %collective-permute-start.5 = (bf16[2,128,512]{2,1,0:T(8,128)(2,1)S(1)}, bf16[2,128,512]{2,1,0:T(8,128)(2,1)S(1)}, u32[]{:S(2)}, u32[]{:S(2)}) collective-permute-start(bf16[2,128,512]{2,1,0:T(8,128)(2,1)S(1)} %get-tuple-element.59), channel_id=1, source_target_pairs={{0,4},{8,16},{16,8},{24,28},{28,24},{20,12},{12,20},{4,0},{1,5},{9... | collective-permute-start | bytes 786440 | tf_op jit(solution)/shard_map/ppermute | solution.py:33
  5.6 13.1 %collective-permute-start = (bf16[2,128,512]{2,1,0:T(8,128)(2,1)S(1)}, bf16[2,128,512]{2,1,0:T(8,128)(2,1)S(1)}, u32[]{:S(2)}, u32[]{:S(2)}) collective-permute-start(bf16[2,128,512]{2,1,0:T(8,128)(2,1)S(1)} %get-tuple-element.60), channel_id=1, source_target_pairs={{0,4},{8,16},{16,8},{24,28},{28,24},{20,12},{12,20},{4,0},{1,5},{9... | collective-permute-start | bytes 786440 | tf_op jit(solution)/shard_map/ppermute | solution.py:33
  6.2 2.2 %copy-start = (bf16[1024,2,1024]{2,1,0:T(2,128)(2,1)S(1)}, bf16[1024,2,1024]{2,1,0:T(2,128)(2,1)}, u32[]{:S(2)}) copy-start(bf16[1024,2,1024]{2,1,0:T(2,128)(2,1)} %amplitudes_ref.1) | copy-start | bytes 12582916
  8.4 0.7 %copy-start.2 = (s32[1024,2]{0,1:T(2,128)S(1)}, s32[1024,2]{0,1:T(2,128)}, u32[]{:S(2)}) copy-start(s32[1024,2]{0,1:T(2,128)} %param.7) | copy-start | bytes 24580
  9.1 12.9 %copy-start.1 = (bf16[2,128,1024]{2,1,0:T(8,128)(2,1)S(1)}, bf16[2,128,1024]{2,1,0:T(8,128)(2,1)}, u32[]{:S(2)}) copy-start(bf16[2,128,1024]{2,1,0:T(8,128)(2,1)} %refs_0_.1) | copy-start | bytes 1572868
  13.4 10.9 %collective-permute-start.6 = (bf16[2,128,512]{2,1,0:T(8,128)(2,1)S(1)}, bf16[2,128,512]{2,1,0:T(8,128)(2,1)S(1)}, u32[]{:S(2)}, u32[]{:S(2)}) collective-permute-start(bf16[2,128,512]{2,1,0:T(8,128)(2,1)S(1)} %collective-permute-done.5.refs_2_), channel_id=1, source_target_pairs={{0,8},{8,0},{16,24},{24,16},{28,20},{20,28},{12,4},{4,12},{1,9},{9... | collective-permute-start | bytes 786440 | tf_op jit(solution)/shard_map/ppermute | solution.py:33
  16.0 9.3 %collective-permute-start.4 = (bf16[2,128,512]{2,1,0:T(8,128)(2,1)S(1)}, bf16[2,128,512]{2,1,0:T(8,128)(2,1)S(1)}, u32[]{:S(2)}, u32[]{:S(2)}) collective-permute-start(bf16[2,128,512]{2,1,0:T(8,128)(2,1)S(1)} %get-tuple-element.61), channel_id=1, source_target_pairs={{0,4},{8,16},{16,8},{24,28},{28,24},{20,12},{12,20},{4,0},{1,5},{9... | collective-permute-start | bytes 786440 | tf_op jit(solution)/shard_map/ppermute | solution.py:33
  18.8 10.1 %collective-permute-start.9 = (bf16[2,128,512]{2,1,0:T(8,128)(2,1)S(1)}, bf16[2,128,512]{2,1,0:T(8,128)(2,1)S(1)}, u32[]{:S(2)}, u32[]{:S(2)}) collective-permute-start(bf16[2,128,512]{2,1,0:T(8,128)(2,1)S(1)} %collective-permute-done.refs_3_), channel_id=1, source_target_pairs={{0,8},{8,0},{16,24},{24,16},{28,20},{20,28},{12,4},{4,12},{1,9},{9... | collective-permute-start | bytes 786440 | tf_op jit(solution)/shard_map/ppermute | solution.py:33
  20.4 10.5 %collective-permute-start.2 = (bf16[2,128,512]{2,1,0:T(8,128)(2,1)S(1)}, bf16[2,128,512]{2,1,0:T(8,128)(2,1)S(1)}, u32[]{:S(2)}, u32[]{:S(2)}) collective-permute-start(bf16[2,128,512]{2,1,0:T(8,128)(2,1)S(1)} %get-tuple-element.62), channel_id=1, source_target_pairs={{0,4},{8,16},{16,8},{24,28},{28,24},{20,12},{12,20},{4,0},{1,5},{9... | collective-permute-start | bytes 786440 | tf_op jit(solution)/shard_map/ppermute | solution.py:33
  25.3 9.6 %collective-permute-start.7 = (bf16[2,128,512]{2,1,0:T(8,128)(2,1)S(1)}, bf16[2,128,512]{2,1,0:T(8,128)(2,1)S(1)}, u32[]{:S(2)}, u32[]{:S(2)}) collective-permute-start(bf16[2,128,512]{2,1,0:T(8,128)(2,1)S(1)} %collective-permute-done.4.refs_2_), channel_id=1, source_target_pairs={{0,8},{8,0},{16,24},{24,16},{28,20},{20,28},{12,4},{4,12},{1,9},{9... | collective-permute-start | bytes 786440 | tf_op jit(solution)/shard_map/ppermute | solution.py:33
  27.4 9.2 %collective-permute-start.8 = (bf16[2,128,512]{2,1,0:T(8,128)(2,1)S(1)}, bf16[2,128,512]{2,1,0:T(8,128)(2,1)S(1)}, u32[]{:S(2)}, u32[]{:S(2)}) collective-permute-start(bf16[2,128,512]{2,1,0:T(8,128)(2,1)S(1)} %collective-permute-done.6.refs_0_), channel_id=1, source_target_pairs={{0,4},{8,16},{16,8},{24,28},{28,24},{20,12},{12,20},{4,0},{1,5},{9... | collective-permute-start | bytes 786440 | tf_op jit(solution)/shard_map/ppermute | solution.py:33
  28.9 13.4 %collective-permute-start.12 = (bf16[2,128,512]{2,1,0:T(8,128)(2,1)S(1)}, bf16[2,128,512]{2,1,0:T(8,128)(2,1)S(1)}, u32[]{:S(2)}, u32[]{:S(2)}) collective-permute-start(bf16[2,128,512]{2,1,0:T(8,128)(2,1)S(1)} %collective-permute-done.9.refs_1_), channel_id=1, source_target_pairs={{0,4},{8,16},{16,8},{24,28},{28,24},{20,12},{12,20},{4,0},{1,5},{9... | collective-permute-start | bytes 786440 | tf_op jit(solution)/shard_map/ppermute | solution.py:33
  31.0 9.3 %collective-permute-start.3 = (bf16[2,128,512]{2,1,0:T(8,128)(2,1)S(1)}, bf16[2,128,512]{2,1,0:T(8,128)(2,1)S(1)}, u32[]{:S(2)}, u32[]{:S(2)}) collective-permute-start(bf16[2,128,512]{2,1,0:T(8,128)(2,1)S(1)} %collective-permute-done.2.refs_3_), channel_id=1, source_target_pairs={{0,8},{8,0},{16,24},{24,16},{28,20},{20,28},{12,4},{4,12},{1,9},{9... | collective-permute-start | bytes 786440 | tf_op jit(solution)/shard_map/ppermute | solution.py:33
  36.6 6.9 %collective-permute-start.11 = (bf16[2,128,512]{2,1,0:T(8,128)(2,1)S(1)}, bf16[2,128,512]{2,1,0:T(8,128)(2,1)S(1)}, u32[]{:S(2)}, u32[]{:S(2)}) collective-permute-start(bf16[2,128,512]{2,1,0:T(8,128)(2,1)S(1)} %collective-permute-done.8.refs_1_), channel_id=1, source_target_pairs={{0,8},{8,0},{16,24},{24,16},{28,20},{20,28},{12,4},{4,12},{1,9},{9... | collective-permute-start | bytes 786440 | tf_op jit(solution)/shard_map/ppermute | solution.py:33
  40.2 7.7 %collective-permute-start.10 = (bf16[2,128,512]{2,1,0:T(8,128)(2,1)S(1)}, bf16[2,128,512]{2,1,0:T(8,128)(2,1)S(1)}, u32[]{:S(2)}, u32[]{:S(2)}) collective-permute-start(bf16[2,128,512]{2,1,0:T(8,128)(2,1)S(1)} %collective-permute-done.3.refs_0_), channel_id=1, source_target_pairs={{0,4},{8,16},{16,8},{24,28},{28,24},{20,12},{12,20},{4,0},{1,5},{9... | collective-permute-start | bytes 786440 | tf_op jit(solution)/shard_map/ppermute | solution.py:33
  44.6 1.4 %collective-permute-start.13 = (bf16[128,512]{1,0:T(8,128)(2,1)S(1)}, bf16[128,512]{1,0:T(8,128)(2,1)S(1)}, u32[]{:S(2)}, u32[]{:S(2)}) collective-permute-start(bf16[128,512]{1,0:T(8,128)(2,1)S(1)} %get-tuple-element.44), channel_id=1, source_target_pairs={{0,1},{1,0},{2,3},{3,2},{4,5},{5,4},{6,7},{7,6},{8,9},{9,8},{10,11... | collective-permute-start | bytes 393224 | tf_op jit(solution)/shard_map/ppermute | solution.py:37
  44.7 1.5 %collective-permute-start.19 = (bf16[128,512]{1,0:T(8,128)(2,1)S(1)}, bf16[128,512]{1,0:T(8,128)(2,1)S(1)}, u32[]{:S(2)}, u32[]{:S(2)}) collective-permute-start(bf16[128,512]{1,0:T(8,128)(2,1)S(1)} %get-tuple-element.56), channel_id=1, source_target_pairs={{0,1},{1,0},{2,3},{3,2},{4,5},{5,4},{6,7},{7,6},{8,9},{9,8},{10,11... | collective-permute-start | bytes 393224 | tf_op jit(solution)/shard_map/ppermute | solution.py:37
  45.2 6.1 %collective-permute-start.18 = (bf16[256,512]{1,0:T(8,128)(2,1)S(1)}, bf16[256,512]{1,0:T(8,128)(2,1)S(1)}, u32[]{:S(2)}, u32[]{:S(2)}) collective-permute-start(bf16[256,512]{1,0:T(8,128)(2,1)S(1)} %get-tuple-element.53), channel_id=1, source_target_pairs={{0,1},{1,0},{2,3},{3,2},{4,5},{5,4},{6,7},{7,6},{8,9},{9,8},{10,11... | collective-permute-start | bytes 786440 | tf_op jit(solution)/shard_map/ppermute | solution.py:37
  46.3 9.2 %copy-start.3 = (f32[1024]{0:T(1024)S(1)}, f32[1024]{0:T(1024)}, u32[]{:S(2)}) copy-start(f32[1024]{0:T(1024)} %param.10) | copy-start | bytes 12292
  46.3 9.2 %copy-start.4 = (f32[256]{0:T(256)S(1)}, f32[256]{0:T(256)}, u32[]{:S(2)}) copy-start(f32[256]{0:T(256)} %param.9) | copy-start | bytes 3076
  46.3 9.2 %collective-permute-start.20 = (bf16[256,512]{1,0:T(8,128)(2,1)S(1)}, bf16[256,512]{1,0:T(8,128)(2,1)S(1)}, u32[]{:S(2)}, u32[]{:S(2)}) collective-permute-start(bf16[256,512]{1,0:T(8,128)(2,1)S(1)} %shard_map.72), channel_id=1, source_target_pairs={{0,2},{2,0},{1,3},{3,1},{4,6},{6,4},{5,7},{7,5},{8,10},{10,8},{9,1... | collective-permute-start | bytes 786440 | tf_op jit(solution)/shard_map/ppermute | solution.py:37
  49.0 1.4 %collective-permute-start.15 = (bf16[128,512]{1,0:T(8,128)(2,1)S(1)}, bf16[128,512]{1,0:T(8,128)(2,1)S(1)}, u32[]{:S(2)}, u32[]{:S(2)}) collective-permute-start(bf16[128,512]{1,0:T(8,128)(2,1)S(1)} %get-tuple-element.50), channel_id=1, source_target_pairs={{0,1},{1,0},{2,3},{3,2},{4,5},{5,4},{6,7},{7,6},{8,9},{9,8},{10,11... | collective-permute-start | bytes 393224 | tf_op jit(solution)/shard_map/ppermute | solution.py:37
  49.1 1.5 %collective-permute-start.16 = (bf16[128,512]{1,0:T(8,128)(2,1)S(1)}, bf16[128,512]{1,0:T(8,128)(2,1)S(1)}, u32[]{:S(2)}, u32[]{:S(2)}) collective-permute-start(bf16[128,512]{1,0:T(8,128)(2,1)S(1)} %get-tuple-element.51), channel_id=1, source_target_pairs={{0,1},{1,0},{2,3},{3,2},{4,5},{5,4},{6,7},{7,6},{8,9},{9,8},{10,11... | collective-permute-start | bytes 393224 | tf_op jit(solution)/shard_map/ppermute | solution.py:37
  50.6 9.9 %collective-permute-start.17 = (bf16[256,512]{1,0:T(8,128)(2,1)S(1)}, bf16[256,512]{1,0:T(8,128)(2,1)S(1)}, u32[]{:S(2)}, u32[]{:S(2)}) collective-permute-start(bf16[256,512]{1,0:T(8,128)(2,1)S(1)} %shard_map.71), channel_id=1, source_target_pairs={{0,2},{2,0},{1,3},{3,1},{4,6},{6,4},{5,7},{7,5},{8,10},{10,8},{9,1... | collective-permute-start | bytes 786440 | tf_op jit(solution)/shard_map/ppermute | solution.py:37
  51.2 9.3 %collective-permute-start.14 = (bf16[256,512]{1,0:T(8,128)(2,1)S(1)}, bf16[256,512]{1,0:T(8,128)(2,1)S(1)}, u32[]{:S(2)}, u32[]{:S(2)}) collective-permute-start(bf16[256,512]{1,0:T(8,128)(2,1)S(1)} %get-tuple-element.48), channel_id=1, source_target_pairs={{0,1},{1,0},{2,3},{3,2},{4,5},{5,4},{6,7},{7,6},{8,9},{9,8},{10,11... | collective-permute-start | bytes 786440 | tf_op jit(solution)/shard_map/ppermute | solution.py:37

commit v6 on v5

--- a/solution.py
+++ b/solution.py
@@ -113,20 +113,22 @@
     return lax.optimization_barrier(values)
 
 
-def products(table, slots, a, blocks, span, total=None, finish=0, weight=1):
+def products(table, slots, a, blocks, span, total=None, finish=(), weight=1):
     blocks = [b if isinstance(b, list) else [b] for b in blocks]
     flat = [v for b in blocks for v in b]
     tiles, depth = flat[0].shape[:2]
     lo, hi = span
     columns = hi - lo
     row = a.shape[1] // 4
+    pieces = (2, 1, 1, 1)
 
     def body(table_ref, a_ref, *refs):
         ins, outs = list(refs[: len(flat)]), refs[len(flat):]
         if total is not None:
             total_ref, outs = outs[0], outs[1:]
         groups = [[ins.pop(0) for _ in b] for b in blocks]
-        for i in range(4):
+        outs = list(outs)
+        for i in finish or range(4):
             here = pl.ds(pl.multiple_of(table_ref[8 + i] * row, row), row)
             left, right = [], []
             for slot, group in zip(slots, groups):
@@ -140,21 +142,21 @@
             )
             if total is not None:
                 acc += total_ref[i, :, lo:hi] if total.shape[2] > columns else total_ref[i]
-            if finish:
-                if i > 0:
-                    outs[i - 1][...] = acc.astype(outs[i - 1].dtype)
-                else:
-                    for n, ref in enumerate(outs[3:]):
-                        ref[...] = acc[n * ref.shape[0] : (n + 1) * ref.shape[0]].astype(BF16)
+            if not finish:
+                outs[0][i] = acc
             else:
-                outs[0][i] = acc
+                for n in range(pieces[i]):
+                    ref = outs.pop(0)
+                    ref[...] = acc[n * ref.shape[0] : (n + 1) * ref.shape[0]].astype(ref.dtype)
 
     vmem = pl.BlockSpec(memory_space=pltpu.VMEM)
     smem = pl.BlockSpec(memory_space=pltpu.SMEM)
     operands = [a] + flat + ([] if total is None else [total])
     if finish:
-        out_shape = [jax.ShapeDtypeStruct((row, columns), t) for t in (BF16, F32, F32)]
-        out_shape += [jax.ShapeDtypeStruct((row // finish, columns), BF16)] * finish
+        types = (BF16, BF16, F32, F32)
+        out_shape = [
+            jax.ShapeDtypeStruct((row // pieces[i], columns), types[i]) for i in finish for _ in range(pieces[i])
+        ]
     else:
         out_shape = [jax.ShapeDtypeStruct((4, row, columns), F32)]
     out = pl.pallas_call(
@@ -164,7 +166,7 @@
         out_shape=out_shape,
         compiler_params=pltpu.CompilerParams(vmem_limit_bytes=20 * 2**20),
         cost_estimate=pl.CostEstimate(
-            flops=weight * 2 * a.shape[1] * tiles * depth * len(blocks) * columns,
+            flops=weight * 2 * row * len(finish or range(4)) * tiles * depth * len(blocks) * columns,
             bytes_accessed=min(weight, 1) * (2 * a.size + 2 * len(flat) * tiles * depth * columns),
             transcendentals=0,
         ),
@@ -194,7 +196,7 @@
     e1 = over_pair(integrals, EVEN)
     o1a, o1b = over_pair(part(integrals, span_a), ODD), over_pair(part(integrals, span_b), ODD)
     a = arranged(amplitudes, tile_mask)
-    o1b, a, table = tie(o1b, a, table)
+    o1a, a, table = tie(o1a, a, table)
     e2a, o2a = over_pair(o1a, EVEN), over_pair(part(e1, span_a), ODD)
     e2b, o2b = over_pair(o1b, EVEN), over_pair(part(e1, span_b), ODD)
     total = products(table, [0, 1, 2], a, [integrals, e1, [o1a, o1b]], (0, columns))
@@ -207,20 +209,21 @@
     total_a = products(table, [5, 6], a, [e3a, o3a], span_a, total=total, weight=20)
     e3b, total_a = tie(e3b, total_a)
     last_b = over_pair(e3b, ODD)
+
+    there_a = products(table, [7], a, [last_a], span_a, total=total_a, finish=(0,), weight=0)
+    got_there_a = [over_virt(v, CORE) for v in there_a]
+    here_a, keep_there_a, keep_here_a = products(
+        table, [7], a, [last_a], span_a, total=total_a, finish=(1, 2, 3), weight=0
+    )
+    mine_a = added(keep_there_a, got_there_a)
+    total, mine_a = tie(total, mine_a)
     total_b = products(table, [5, 6], a, [e3b, o3b], span_b, total=total)
-    last_a, total_b = tie(last_a, total_b)
-
-    here_a, keep_there_a, keep_here_a, *there_a = products(
-        table, [7], a, [last_a], span_a, total=total_a, finish=2, weight=0
-    )
-    got_there_a = [over_virt(v, CORE) for v in there_a]
-    got_there_a[0], total_b = tie(got_there_a[0], total_b)
-    mine_a = added(keep_there_a, got_there_a)
-    here_b, keep_there_b, keep_here_b, *there_b = products(
-        table, [7], a, [last_b], span_b, total=total_b, finish=2, weight=20
-    )
+    there_b = products(table, [7], a, [last_b], span_b, total=total_b, finish=(0,), weight=20)
     from_y_a = over_virt(mine_a, YHOP)
     got_there_b = [over_virt(v, CORE) for v in there_b]
+    here_b, keep_there_b, keep_here_b = products(
+        table, [7], a, [last_b], span_b, total=total_b, finish=(1, 2, 3), weight=0
+    )
     from_y_b = over_virt(added(keep_there_b, got_there_b), YHOP)
     got_here_a, got_here_b = over_virt(here_a, CORE), over_virt(here_b, CORE)
     left = quotient(keep_here_a, got_here_a, from_y_a, pair_energy, virt_energy, span_a, weight=20)

time: 61.8 us -> 61.4 us (level)
  waiting for transfers between devices: 19.4 us -> 17.5 us
  Pallas kernels: 12.2 us -> 13.5 us
    ppermute x8, waiting for transfers between devices: 11 us -> 8.14 us  [over_virt(): return lax.ppermute(value, 'virt', hops)]
    pallas_call x6 -> x8, Pallas kernels: 8.89 us -> 10.3 us  [products(): pl.pallas_call(body, in_specs=[smem] + [vmem] * len(operands), out_specs=...]
    ppermute x13, waiting for transfers between devices: 8.41 us -> 9.39 us  [over_pair(): return lax.ppermute(value, 'pair', hops)]
  transfers between devices with their start and end apart: 21 -> 21, of which waited for: 13 -> 10; matrix products, arithmetic and copies ran while one was open for 3% -> 3% of each run, Pallas kernels for 18% -> 20%
where the time goes in v6:
time: 61.4 us; the launch traced here: 61.1 us
  starting transfers between devices  25.2 us (41%)
  waiting for transfers between devices  17.5 us (29%)
  Pallas kernels  13.5 us (22%)
  local copies, waits for them, and re-layouts  4.69 us (8%)
    ppermute x13, starting transfers between devices, over_pair(): return lax.ppermute(value, 'pair', hops)  21.7 us
    pallas_call x8, Pallas kernels, products(): pl.pallas_call(body, in_specs=[smem] + [vmem] * len(operands), out_specs=...  10.3 us
    ppermute x13, waiting for transfers between devices, over_pair(): return lax.ppermute(value, 'pair', hops)  9.39 us
    ppermute x8, waiting for transfers between devices, over_virt(): return lax.ppermute(value, 'virt', hops)  8.14 us
    ppermute x8, starting transfers between devices, over_virt(): return lax.ppermute(value, 'virt', hops)  3.52 us
    unnamed x10, local copies, waits for them, and re-layouts  2.9 us
    pallas_call x1, Pallas kernels, arranged(): pl.pallas_call(body, in_specs=[vmem, vmem], out_specs=vmem, out_shape=jax...  1.84 us
    pallas_call x2, Pallas kernels, quotient(): pl.pallas_call(body, in_specs=[vmem] * (5 + len(more)), out_specs=vmem, o...  1.35 us
  transfers between devices with their start and end apart: 21, of which 10 were waited for; matrix products, arithmetic and copies ran while one was open for 3% of the time, Pallas kernels for 20%

profile of v6, /device:TPU:0, one launch (start us, length us, event | category | flops | bytes accessed | tf_op | source)
XLA Modules:
  0.0 61.1 jit_solution(13652383117309239115)
XLA Ops:
  0.0 3.0 %collective-permute-start.1 = (bf16[2,128,1024]{2,1,0:T(8,128)(2,1)}, bf16[2,128,1024]{2,1,0:T(8,128)(2,1)S(1)}, u32[]{:S(2)}, u32[]{:S(2)}) collective-permute-start(bf16[2,128,1024]{2,1,0:T(8,128)(2,1)} %refs_0_.1), channel_id=1, source_target_pairs={{0,8},{8,0},{16,24},{24,16},{28,20},{20,28},{12,4},{4,12},{1,9},{9... | collective-permute-start | bytes 1572872 | tf_op jit(solution)/shard_map/ppermute | solution.py:33
  3.0 1.1 %fusion = (bf16[2,128,512]{2,1,0:T(8,128)(2,1)S(1)}, bf16[2,128,512]{2,1,0:T(8,128)(2,1)S(1)}) fusion(bf16[2,128,1024]{2,1,0:T(8,128)(2,1)} %refs_0_.1), kind=kLoop, calls=%fused_computation.1 | loop fusion | bytes 1048576 | tf_op jit(solution)/shard_map/slice | solution.py:194
  4.1 1.6 %collective-permute-start = (bf16[2,128,512]{2,1,0:T(8,128)(2,1)S(1)}, bf16[2,128,512]{2,1,0:T(8,128)(2,1)S(1)}, u32[]{:S(2)}, u32[]{:S(2)}) collective-permute-start(bf16[2,128,512]{2,1,0:T(8,128)(2,1)S(1)} %get-tuple-element.56), channel_id=1, source_target_pairs={{0,4},{8,16},{16,8},{24,28},{28,24},{20,12},{12,20},{4,0},{1,5},{9... | collective-permute-start | bytes 786440 | tf_op jit(solution)/shard_map/ppermute | solution.py:33
  5.6 0.5 collective-permute-start.6
  6.2 0.7 %dynamic-slice_bitcast_fusion.table_ref = s32[12]{0:T(128)S(1)} fusion(s32[32,12]{1,0:T(8,128)} %constant.19.clone, s32[]{:T(128)S(6)} %select_n.4), kind=kLoop, calls=%fused_computation | loop fusion | bytes 100 | tf_op jit(solution)/shard_map/jit(dynamic_index_in_dim)/squeeze | solution.py:185
  6.9 0.0 copy-start
  6.9 2.2 %copy-done = bf16[1024,2,1024]{2,1,0:T(2,128)(2,1)S(1)} copy-done((bf16[1024,2,1024]{2,1,0:T(2,128)(2,1)S(1)}, bf16[1024,2,1024]{2,1,0:T(2,128)(2,1)}, u32[]{:S(2)}) %copy-start) | copy-done | bytes 4194328
  9.1 0.0 copy-start.2
  9.1 0.7 %copy-done.2 = s32[1024,2]{0,1:T(2,128)S(1)} copy-done((s32[1024,2]{0,1:T(2,128)S(1)}, s32[1024,2]{0,1:T(2,128)}, u32[]{:S(2)}) %copy-start.2) | copy-done | bytes 8216
  9.8 1.8 %shard_map.64.a_ref = bf16[2,1024,1024]{2,1,0:T(8,128)(2,1)S(1)} custom-call(bf16[1024,2,1024]{2,1,0:T(2,128)(2,1)S(1)} %copy-done, s32[2,1024]{1,0:T(2,128)S(1)} %bitcast.5), custom_call_target="tpu_custom_call" | custom-call | flops 2147483648 | bytes 8388608 | tf_op jit(solution)/shard_map/pallas_call | solution.py:57
  11.6 1.8 %collective-permute-done.refs_2_ = bf16[2,128,512]{2,1,0:T(8,128)(2,1)S(1)} collective-permute-done((bf16[2,128,512]{2,1,0:T(8,128)(2,1)S(1)}, bf16[2,128,512]{2,1,0:T(8,128)(2,1)S(1)}, u32[]{:S(2)}, u32[]{:S(2)}) %collective-permute-start) | collective-permute-done | bytes 262176 | tf_op jit(solution)/shard_map/ppermute | solution.py:33
  13.4 1.1 %collective-permute-start.5 = (bf16[2,128,512]{2,1,0:T(8,128)(2,1)S(1)}, bf16[2,128,512]{2,1,0:T(8,128)(2,1)S(1)}, u32[]{:S(2)}, u32[]{:S(2)}) collective-permute-start(bf16[2,128,512]{2,1,0:T(8,128)(2,1)S(1)} %collective-permute-done.refs_2_), channel_id=1, source_target_pairs={{0,8},{8,0},{16,24},{24,16},{28,20},{20,28},{12,4},{4,12},{1,9},{9... | collective-permute-start | bytes 786440 | tf_op jit(solution)/shard_map/ppermute | solution.py:33
  14.5 1.5 %collective-permute-done.1.refs_1_ = bf16[2,128,1024]{2,1,0:T(8,128)(2,1)S(1)} collective-permute-done((bf16[2,128,1024]{2,1,0:T(8,128)(2,1)}, bf16[2,128,1024]{2,1,0:T(8,128)(2,1)S(1)}, u32[]{:S(2)}, u32[]{:S(2)}) %collective-permute-start.1) | collective-permute-done | bytes 524320 | tf_op jit(solution)/shard_map/ppermute | solution.py:33
  16.0 2.0 %collective-permute-start.4 = (bf16[2,128,512]{2,1,0:T(8,128)(2,1)S(1)}, bf16[2,128,512]{2,1,0:T(8,128)(2,1)S(1)}, u32[]{:S(2)}, u32[]{:S(2)}) collective-permute-start(bf16[2,128,512]{2,1,0:T(8,128)(2,1)S(1)} %get-tuple-element.57), channel_id=1, source_target_pairs={{0,4},{8,16},{16,8},{24,28},{28,24},{20,12},{12,20},{4,0},{1,5},{9... | collective-permute-start | bytes 786440 | tf_op jit(solution)/shard_map/ppermute | solution.py:33
  18.1 0.0 collective-permute-done.6.refs_3_
  18.1 1.7 %collective-permute-start.9 = (bf16[2,128,512]{2,1,0:T(8,128)(2,1)S(1)}, bf16[2,128,512]{2,1,0:T(8,128)(2,1)S(1)}, u32[]{:S(2)}, u32[]{:S(2)}) collective-permute-start(bf16[2,128,512]{2,1,0:T(8,128)(2,1)S(1)} %collective-permute-done.6.refs_3_), channel_id=1, source_target_pairs={{0,8},{8,0},{16,24},{24,16},{28,20},{20,28},{12,4},{4,12},{1,9},{9... | collective-permute-start | bytes 786440 | tf_op jit(solution)/shard_map/ppermute | solution.py:33
  19.7 1.5 %collective-permute-start.2 = (bf16[2,128,512]{2,1,0:T(8,128)(2,1)S(1)}, bf16[2,128,512]{2,1,0:T(8,128)(2,1)S(1)}, u32[]{:S(2)}, u32[]{:S(2)}) collective-permute-start(bf16[2,128,512]{2,1,0:T(8,128)(2,1)S(1)} %get-tuple-element.58), channel_id=1, source_target_pairs={{0,4},{8,16},{16,8},{24,28},{28,24},{20,12},{12,20},{4,0},{1,5},{9... | collective-permute-start | bytes 786440 | tf_op jit(solution)/shard_map/ppermute | solution.py:33
  21.2 0.0 copy-done.1
  21.2 2.4 %shard_map.65.refs_4_ = f32[4,256,1024]{2,1,0:T(8,128)S(1)} custom-call(s32[12]{0:T(128)S(1)} %dynamic-slice_bitcast_fusion.table_ref, bf16[2,1024,1024]{2,1,0:T(8,128)(2,1)S(1)} %shard_map.64.a_ref, bf16[2,128,1024]{2,1,0:T(8,128)(2,1)S(1)} %copy-done.1, bf16[2,128,1024]{2,1,0:T(8,128)(2,1)S(1)} %collective-permute-done.1.refs_1_, ...), custom_call_target="tpu_custom_call" | custom-call | flops 1610612736 | bytes 6291456 | tf_op jit(solution)/shard_map/pallas_call | solution.py:162
  23.6 0.0 collective-permute-done.5.refs_0_
  23.6 1.7 %collective-permute-done.4.refs_2_ = bf16[2,128,512]{2,1,0:T(8,128)(2,1)S(1)} collective-permute-done((bf16[2,128,512]{2,1,0:T(8,128)(2,1)S(1)}, bf16[2,128,512]{2,1,0:T(8,128)(2,1)S(1)}, u32[]{:S(2)}, u32[]{:S(2)}) %collective-permute-start.4) | collective-permute-done | bytes 262176 | tf_op jit(solution)/shard_map/ppermute | solution.py:33
  25.3 2.1 %collective-permute-start.7 = (bf16[2,128,512]{2,1,0:T(8,128)(2,1)S(1)}, bf16[2,128,512]{2,1,0:T(8,128)(2,1)S(1)}, u32[]{:S(2)}, u32[]{:S(2)}) collective-permute-start(bf16[2,128,512]{2,1,0:T(8,128)(2,1)S(1)} %collective-permute-done.4.refs_2_), channel_id=1, source_target_pairs={{0,8},{8,0},{16,24},{24,16},{28,20},{20,28},{12,4},{4,12},{1,9},{9... | collective-permute-start | bytes 786440 | tf_op jit(solution)/shard_map/ppermute | solution.py:33
  27.4 1.5 %collective-permute-start.8 = (bf16[2,128,512]{2,1,0:T(8,128)(2,1)S(1)}, bf16[2,128,512]{2,1,0:T(8,128)(2,1)S(1)}, u32[]{:S(2)}, u32[]{:S(2)}) collective-permute-start(bf16[2,128,512]{2,1,0:T(8,128)(2,1)S(1)} %collective-permute-done.5.refs_0_), channel_id=1, source_target_pairs={{0,4},{8,16},{16,8},{24,28},{28,24},{20,12},{12,20},{4,0},{1,5},{9... | collective-permute-start | bytes 786440 | tf_op jit(solution)/shard_map/ppermute | solution.py:33
  28.9 0.0 collective-permute-done.9.refs_1_
  28.9 0.8 %collective-permute-start.11 = (bf16[2,128,512]{2,1,0:T(8,128)(2,1)S(1)}, bf16[2,128,512]{2,1,0:T(8,128)(2,1)S(1)}, u32[]{:S(2)}, u32[]{:S(2)}) collective-permute-start(bf16[2,128,512]{2,1,0:T(8,128)(2,1)S(1)} %collective-permute-done.9.refs_1_), channel_id=1, source_target_pairs={{0,4},{8,16},{16,8},{24,28},{28,24},{20,12},{12,20},{4,0},{1,5},{9... | collective-permute-start | bytes 786440 | tf_op jit(solution)/shard_map/ppermute | solution.py:33
  29.7 1.2 %collective-permute-done.2.refs_3_ = bf16[2,128,512]{2,1,0:T(8,128)(2,1)S(1)} collective-permute-done((bf16[2,128,512]{2,1,0:T(8,128)(2,1)S(1)}, bf16[2,128,512]{2,1,0:T(8,128)(2,1)S(1)}, u32[]{:S(2)}, u32[]{:S(2)}) %collective-permute-start.2) | collective-permute-done | bytes 262176 | tf_op jit(solution)/shard_map/ppermute | solution.py:33
  31.0 2.1 %collective-permute-start.3 = (bf16[2,128,512]{2,1,0:T(8,128)(2,1)S(1)}, bf16[2,128,512]{2,1,0:T(8,128)(2,1)S(1)}, u32[]{:S(2)}, u32[]{:S(2)}) collective-permute-start(bf16[2,128,512]{2,1,0:T(8,128)(2,1)S(1)} %collective-permute-done.2.refs_3_), channel_id=1, source_target_pairs={{0,8},{8,0},{16,24},{24,16},{28,20},{20,28},{12,4},{4,12},{1,9},{9... | collective-permute-start | bytes 786440 | tf_op jit(solution)/shard_map/ppermute | solution.py:33
  33.0 1.9 %shard_map.66.refs_2_ = f32[4,256,1024]{2,1,0:T(8,128)S(1)} custom-call(s32[12]{0:T(128)S(1)} %dynamic-slice_bitcast_fusion.table_ref, bf16[2,1024,1024]{2,1,0:T(8,128)(2,1)S(1)} %shard_map.64.a_ref, bf16[2,128,512]{2,1,0:T(8,128)(2,1)S(1)} %collective-permute-done.5.refs_0_, bf16[2,128,512]{2,1,0:T(8,128)(2,1)S(1)} %collective-permute-done.9.refs_1_, ...), custom_call_target="tpu_custom_call" | custom-call | flops 1073741824 | bytes 6291456 | tf_op jit(solution)/shard_map/pallas_call | solution.py:162
  34.9 0.0 collective-permute-done.7.refs_0_
  34.9 1.7 %collective-permute-done.8.refs_1_ = bf16[2,128,512]{2,1,0:T(8,128)(2,1)S(1)} collective-permute-done((bf16[2,128,512]{2,1,0:T(8,128)(2,1)S(1)}, bf16[2,128,512]{2,1,0:T(8,128)(2,1)S(1)}, u32[]{:S(2)}, u32[]{:S(2)}) %collective-permute-start.8) | collective-permute-done | bytes 262176 | tf_op jit(solution)/shard_map/ppermute | solution.py:33
  36.6 2.0 %collective-permute-start.12 = (bf16[2,128,512]{2,1,0:T(8,128)(2,1)S(1)}, bf16[2,128,512]{2,1,0:T(8,128)(2,1)S(1)}, u32[]{:S(2)}, u32[]{:S(2)}) collective-permute-start(bf16[2,128,512]{2,1,0:T(8,128)(2,1)S(1)} %collective-permute-done.8.refs_1_), channel_id=1, source_target_pairs={{0,8},{8,0},{16,24},{24,16},{28,20},{20,28},{12,4},{4,12},{1,9},{9... | collective-permute-start | bytes 786440 | tf_op jit(solution)/shard_map/ppermute | solution.py:33
  38.6 1.3 %shard_map.67.refs_1_ = f32[4,256,512]{2,1,0:T(8,128)S(1)} custom-call(s32[12]{0:T(128)S(1)} %dynamic-slice_bitcast_fusion.table_ref, bf16[2,1024,1024]{2,1,0:T(8,128)(2,1)S(1)} %shard_map.64.a_ref, bf16[2,128,512]{2,1,0:T(8,128)(2,1)S(1)} %collective-permute-done.7.refs_0_, bf16[2,128,512]{2,1,0:T(8,128)(2,1)S(1)} %collective-permute-done.8.refs_1_, ...), custom_call_target="tpu_custom_call" | custom-call | flops 10737418240 | bytes 4718592 | tf_op jit(solution)/shard_map/pallas_call | solution.py:162
  40.0 0.3 collective-permute-done.3.refs_0_
  40.2 1.9 %collective-permute-start.10 = (bf16[2,128,512]{2,1,0:T(8,128)(2,1)S(1)}, bf16[2,128,512]{2,1,0:T(8,128)(2,1)S(1)}, u32[]{:S(2)}, u32[]{:S(2)}) collective-permute-start(bf16[2,128,512]{2,1,0:T(8,128)(2,1)S(1)} %collective-permute-done.3.refs_0_), channel_id=1, source_target_pairs={{0,4},{8,16},{16,8},{24,28},{28,24},{20,12},{12,20},{4,0},{1,5},{9... | collective-permute-start | bytes 786440 | tf_op jit(solution)/shard_map/ppermute | solution.py:33
  42.1 1.1 %collective-permute-done.12.refs_0_ = bf16[2,128,512]{2,1,0:T(8,128)(2,1)S(1)} collective-permute-done((bf16[2,128,512]{2,1,0:T(8,128)(2,1)S(1)}, bf16[2,128,512]{2,1,0:T(8,128)(2,1)S(1)}, u32[]{:S(2)}, u32[]{:S(2)}) %collective-permute-start.12) | collective-permute-done | bytes 262176 | tf_op jit(solution)/shard_map/ppermute | solution.py:33
  43.2 0.8 %shard_map.69 = (bf16[128,512]{1,0:T(8,128)(2,1)S(1)}, bf16[128,512]{1,0:T(8,128)(2,1)S(1)}) custom-call(s32[12]{0:T(128)S(1)} %dynamic-slice_bitcast_fusion.table_ref, bf16[2,1024,1024]{2,1,0:T(8,128)(2,1)S(1)} %shard_map.64.a_ref, bf16[2,128,512]{2,1,0:T(8,128)(2,1)S(1)} %collective-permute-done.12.refs_0_, f32[4,256,512]{2,1,0:T(8,128)S(1)} %shard_map.67.refs_1_), custom_call_target="tpu_custom_call" | custom-call | tf_op jit(solution)/shard_map/pallas_call | solution.py:162
  44.0 0.1 collective-permute-start.13
  44.1 0.5 collective-permute-start.14
  44.6 0.9 %shard_map.68 = (bf16[256,512]{1,0:T(8,128)(2,1)S(1)}, f32[256,512]{1,0:T(8,128)S(1)}, f32[256,512]{1,0:T(8,128)S(1)}) custom-call(s32[12]{0:T(128)S(1)} %dynamic-slice_bitcast_fusion.table_ref, bf16[2,1024,1024]{2,1,0:T(8,128)(2,1)S(1)} %shard_map.64.a_ref, bf16[2,128,512]{2,1,0:T(8,128)(2,1)S(1)} %collective-permute-done.12.refs_0_, ...), custom_call_target="tpu_custom_call" | custom-call | tf_op jit(solution)/shard_map/pallas_call | solution.py:162
  45.5 0.1 collective-permute-start.19
  45.7 0.0 collective-permute-done.13.refs_0_
  45.7 0.0 collective-permute-done.14.refs_1_
  45.7 1.8 %collective-permute-start.20 = (bf16[256,512]{1,0:T(8,128)(2,1)S(1)}, bf16[256,512]{1,0:T(8,128)(2,1)S(1)}, u32[]{:S(2)}, u32[]{:S(2)}) collective-permute-start(bf16[256,512]{1,0:T(8,128)(2,1)S(1)} %shard_map.70), channel_id=1, source_target_pairs={{0,2},{2,0},{1,3},{3,1},{4,6},{6,4},{5,7},{7,5},{8,10},{10,8},{9,1... | collective-permute-start | bytes 786440 | tf_op jit(solution)/shard_map/ppermute | solution.py:37
  47.5 0.0 collective-permute-done.11.refs_1_
  47.5 1.3 %shard_map.71.refs_1_ = f32[4,256,512]{2,1,0:T(8,128)S(1)} custom-call(s32[12]{0:T(128)S(1)} %dynamic-slice_bitcast_fusion.table_ref, bf16[2,1024,1024]{2,1,0:T(8,128)(2,1)S(1)} %shard_map.64.a_ref, bf16[2,128,512]{2,1,0:T(8,128)(2,1)S(1)} %collective-permute-done.3.refs_0_, bf16[2,128,512]{2,1,0:T(8,128)(2,1)S(1)} %collective-permute-done.11.refs_1_, ...), custom_call_target="tpu_custom_call" | custom-call | flops 536870912 | bytes 4718592 | tf_op jit(solution)/shard_map/pallas_call | solution.py:162
  48.8 0.0 collective-permute-done.10.refs_0_
  48.8 0.8 %shard_map.73 = (bf16[128,512]{1,0:T(8,128)(2,1)S(1)}, bf16[128,512]{1,0:T(8,128)(2,1)S(1)}) custom-call(s32[12]{0:T(128)S(1)} %dynamic-slice_bitcast_fusion.table_ref, bf16[2,1024,1024]{2,1,0:T(8,128)(2,1)S(1)} %shard_map.64.a_ref, bf16[2,128,512]{2,1,0:T(8,128)(2,1)S(1)} %collective-permute-done.10.refs_0_, f32[4,256,512]{2,1,0:T(8,128)S(1)} %shard_map.71.refs_1_), custom_call_target="tpu_custom_call" | custom-call | flops 1342177280 | bytes 4456448 | tf_op jit(solution)/shard_map/pallas_call | solution.py:162
  49.6 0.0 copy-start.3
  49.6 0.0 copy-start.4
  49.6 0.2 collective-permute-start.16
  49.8 0.4 collective-permute-start.17
  50.2 0.9 %shard_map.72 = (bf16[256,512]{1,0:T(8,128)(2,1)S(1)}, f32[256,512]{1,0:T(8,128)S(1)}, f32[256,512]{1,0:T(8,128)S(1)}) custom-call(s32[12]{0:T(128)S(1)} %dynamic-slice_bitcast_fusion.table_ref, bf16[2,1024,1024]{2,1,0:T(8,128)(2,1)S(1)} %shard_map.64.a_ref, bf16[2,128,512]{2,1,0:T(8,128)(2,1)S(1)} %collective-permute-done.10.refs_0_, ...), custom_call_target="tpu_custom_call" | custom-call | tf_op jit(solution)/shard_map/pallas_call | solution.py:162
  51.1 0.0 collective-permute-done.16.refs_0_
  51.1 0.1 collective-permute-done.17.refs_1_
  51.3 0.4 collective-permute-start.18
  51.6 0.1 collective-permute-start.15
  51.7 0.0 collective-permute-done.19.got_ref
  51.7 2.8 %collective-permute-done.20.from_y_ref = bf16[256,512]{1,0:T(8,128)(2,1)S(1)} collective-permute-done((bf16[256,512]{1,0:T(8,128)(2,1)S(1)}, bf16[256,512]{1,0:T(8,128)(2,1)S(1)}, u32[]{:S(2)}, u32[]{:S(2)}) %collective-permute-start.20) | collective-permute-done | bytes 262176 | tf_op jit(solution)/shard_map/ppermute | solution.py:37
  54.6 0.0 copy-done.3
  54.6 0.0 copy-done.4
  54.6 0.3 shard_map.75.refs_0_
  54.8 5.2 %collective-permute-done.18.from_y_ref = bf16[256,512]{1,0:T(8,128)(2,1)S(1)} collective-permute-done((bf16[256,512]{1,0:T(8,128)(2,1)S(1)}, bf16[256,512]{1,0:T(8,128)(2,1)S(1)}, u32[]{:S(2)}, u32[]{:S(2)}) %collective-permute-start.18) | collective-permute-done | bytes 262176 | tf_op jit(solution)/shard_map/ppermute | solution.py:37
  60.1 0.0 collective-permute-done.15.got_ref
  60.1 1.1 %shard_map.76 = bf16[256,1024]{1,0:T(8,128)(2,1)} custom-call(f32[256,512]{1,0:T(8,128)S(1)} %get-tuple-element.45.kept_ref, bf16[256,512]{1,0:T(8,128)(2,1)S(1)} %collective-permute-done.15.got_ref, bf16[256,512]{1,0:T(8,128)(2,1)S(1)} %collective-permute-done.18.from_y_ref, f32[1,256]{1,0:T(1,128)S(1)} %bitcast.9, f32[1,1024]{1,0:T(1,128)S(1)} %bitcast.7, ...), custom_call_target="tpu_custom_call" | custom-call | flops 100000000 | bytes 1000000 | tf_op jit(solution)/shard_map/pallas_call | solution.py:102
  (4 shorter events, 0.1 us)
Async XLA Ops:
  0.0 16.0 %collective-permute-start.1 = (bf16[2,128,1024]{2,1,0:T(8,128)(2,1)}, bf16[2,128,1024]{2,1,0:T(8,128)(2,1)S(1)}, u32[]{:S(2)}, u32[]{:S(2)}) collective-permute-start(bf16[2,128,1024]{2,1,0:T(8,128)(2,1)} %refs_0_.1), channel_id=1, source_target_pairs={{0,8},{8,0},{16,24},{24,16},{28,20},{20,28},{12,4},{4,12},{1,9},{9... | collective-permute-start | bytes 1572872 | tf_op jit(solution)/shard_map/ppermute | solution.py:33
  4.1 9.3 %collective-permute-start = (bf16[2,128,512]{2,1,0:T(8,128)(2,1)S(1)}, bf16[2,128,512]{2,1,0:T(8,128)(2,1)S(1)}, u32[]{:S(2)}, u32[]{:S(2)}) collective-permute-start(bf16[2,128,512]{2,1,0:T(8,128)(2,1)S(1)} %get-tuple-element.56), channel_id=1, source_target_pairs={{0,4},{8,16},{16,8},{24,28},{28,24},{20,12},{12,20},{4,0},{1,5},{9... | collective-permute-start | bytes 786440 | tf_op jit(solution)/shard_map/ppermute | solution.py:33
  5.6 12.4 %collective-permute-start.6 = (bf16[2,128,512]{2,1,0:T(8,128)(2,1)S(1)}, bf16[2,128,512]{2,1,0:T(8,128)(2,1)S(1)}, u32[]{:S(2)}, u32[]{:S(2)}) collective-permute-start(bf16[2,128,512]{2,1,0:T(8,128)(2,1)S(1)} %get-tuple-element.55), channel_id=1, source_target_pairs={{0,4},{8,16},{16,8},{24,28},{28,24},{20,12},{12,20},{4,0},{1,5},{9... | collective-permute-start | bytes 786440 | tf_op jit(solution)/shard_map/ppermute | solution.py:33
  6.9 2.2 %copy-start = (bf16[1024,2,1024]{2,1,0:T(2,128)(2,1)S(1)}, bf16[1024,2,1024]{2,1,0:T(2,128)(2,1)}, u32[]{:S(2)}) copy-start(bf16[1024,2,1024]{2,1,0:T(2,128)(2,1)} %amplitudes_ref.1) | copy-start | bytes 12582916
  9.1 0.7 %copy-start.2 = (s32[1024,2]{0,1:T(2,128)S(1)}, s32[1024,2]{0,1:T(2,128)}, u32[]{:S(2)}) copy-start(s32[1024,2]{0,1:T(2,128)} %param.7) | copy-start | bytes 24580
  9.8 11.5 %copy-start.1 = (bf16[2,128,1024]{2,1,0:T(8,128)(2,1)S(1)}, bf16[2,128,1024]{2,1,0:T(8,128)(2,1)}, u32[]{:S(2)}) copy-start(bf16[2,128,1024]{2,1,0:T(8,128)(2,1)} %refs_0_.1) | copy-start | bytes 1572868
  13.4 10.2 %collective-permute-start.5 = (bf16[2,128,512]{2,1,0:T(8,128)(2,1)S(1)}, bf16[2,128,512]{2,1,0:T(8,128)(2,1)S(1)}, u32[]{:S(2)}, u32[]{:S(2)}) collective-permute-start(bf16[2,128,512]{2,1,0:T(8,128)(2,1)S(1)} %collective-permute-done.refs_2_), channel_id=1, source_target_pairs={{0,8},{8,0},{16,24},{24,16},{28,20},{20,28},{12,4},{4,12},{1,9},{9... | collective-permute-start | bytes 786440 | tf_op jit(solution)/shard_map/ppermute | solution.py:33
  16.0 9.3 %collective-permute-start.4 = (bf16[2,128,512]{2,1,0:T(8,128)(2,1)S(1)}, bf16[2,128,512]{2,1,0:T(8,128)(2,1)S(1)}, u32[]{:S(2)}, u32[]{:S(2)}) collective-permute-start(bf16[2,128,512]{2,1,0:T(8,128)(2,1)S(1)} %get-tuple-element.57), channel_id=1, source_target_pairs={{0,4},{8,16},{16,8},{24,28},{28,24},{20,12},{12,20},{4,0},{1,5},{9... | collective-permute-start | bytes 786440 | tf_op jit(solution)/shard_map/ppermute | solution.py:33
  18.1 10.8 %collective-permute-start.9 = (bf16[2,128,512]{2,1,0:T(8,128)(2,1)S(1)}, bf16[2,128,512]{2,1,0:T(8,128)(2,1)S(1)}, u32[]{:S(2)}, u32[]{:S(2)}) collective-permute-start(bf16[2,128,512]{2,1,0:T(8,128)(2,1)S(1)} %collective-permute-done.6.refs_3_), channel_id=1, source_target_pairs={{0,8},{8,0},{16,24},{24,16},{28,20},{20,28},{12,4},{4,12},{1,9},{9... | collective-permute-start | bytes 786440 | tf_op jit(solution)/shard_map/ppermute | solution.py:33
  19.7 11.2 %collective-permute-start.2 = (bf16[2,128,512]{2,1,0:T(8,128)(2,1)S(1)}, bf16[2,128,512]{2,1,0:T(8,128)(2,1)S(1)}, u32[]{:S(2)}, u32[]{:S(2)}) collective-permute-start(bf16[2,128,512]{2,1,0:T(8,128)(2,1)S(1)} %get-tuple-element.58), channel_id=1, source_target_pairs={{0,4},{8,16},{16,8},{24,28},{28,24},{20,12},{12,20},{4,0},{1,5},{9... | collective-permute-start | bytes 786440 | tf_op jit(solution)/shard_map/ppermute | solution.py:33
  25.3 9.6 %collective-permute-start.7 = (bf16[2,128,512]{2,1,0:T(8,128)(2,1)S(1)}, bf16[2,128,512]{2,1,0:T(8,128)(2,1)S(1)}, u32[]{:S(2)}, u32[]{:S(2)}) collective-permute-start(bf16[2,128,512]{2,1,0:T(8,128)(2,1)S(1)} %collective-permute-done.4.refs_2_), channel_id=1, source_target_pairs={{0,8},{8,0},{16,24},{24,16},{28,20},{20,28},{12,4},{4,12},{1,9},{9... | collective-permute-start | bytes 786440 | tf_op jit(solution)/shard_map/ppermute | solution.py:33
  27.4 9.2 %collective-permute-start.8 = (bf16[2,128,512]{2,1,0:T(8,128)(2,1)S(1)}, bf16[2,128,512]{2,1,0:T(8,128)(2,1)S(1)}, u32[]{:S(2)}, u32[]{:S(2)}) collective-permute-start(bf16[2,128,512]{2,1,0:T(8,128)(2,1)S(1)} %collective-permute-done.5.refs_0_), channel_id=1, source_target_pairs={{0,4},{8,16},{16,8},{24,28},{28,24},{20,12},{12,20},{4,0},{1,5},{9... | collective-permute-start | bytes 786440 | tf_op jit(solution)/shard_map/ppermute | solution.py:33
  28.9 18.6 %collective-permute-start.11 = (bf16[2,128,512]{2,1,0:T(8,128)(2,1)S(1)}, bf16[2,128,512]{2,1,0:T(8,128)(2,1)S(1)}, u32[]{:S(2)}, u32[]{:S(2)}) collective-permute-start(bf16[2,128,512]{2,1,0:T(8,128)(2,1)S(1)} %collective-permute-done.9.refs_1_), channel_id=1, source_target_pairs={{0,4},{8,16},{16,8},{24,28},{28,24},{20,12},{12,20},{4,0},{1,5},{9... | collective-permute-start | bytes 786440 | tf_op jit(solution)/shard_map/ppermute | solution.py:33
  31.0 9.3 %collective-permute-start.3 = (bf16[2,128,512]{2,1,0:T(8,128)(2,1)S(1)}, bf16[2,128,512]{2,1,0:T(8,128)(2,1)S(1)}, u32[]{:S(2)}, u32[]{:S(2)}) collective-permute-start(bf16[2,128,512]{2,1,0:T(8,128)(2,1)S(1)} %collective-permute-done.2.refs_3_), channel_id=1, source_target_pairs={{0,8},{8,0},{16,24},{24,16},{28,20},{20,28},{12,4},{4,12},{1,9},{9... | collective-permute-start | bytes 786440 | tf_op jit(solution)/shard_map/ppermute | solution.py:33
  36.6 6.6 %collective-permute-start.12 = (bf16[2,128,512]{2,1,0:T(8,128)(2,1)S(1)}, bf16[2,128,512]{2,1,0:T(8,128)(2,1)S(1)}, u32[]{:S(2)}, u32[]{:S(2)}) collective-permute-start(bf16[2,128,512]{2,1,0:T(8,128)(2,1)S(1)} %collective-permute-done.8.refs_1_), channel_id=1, source_target_pairs={{0,8},{8,0},{16,24},{24,16},{28,20},{20,28},{12,4},{4,12},{1,9},{9... | collective-permute-start | bytes 786440 | tf_op jit(solution)/shard_map/ppermute | solution.py:33
  40.2 8.6 %collective-permute-start.10 = (bf16[2,128,512]{2,1,0:T(8,128)(2,1)S(1)}, bf16[2,128,512]{2,1,0:T(8,128)(2,1)S(1)}, u32[]{:S(2)}, u32[]{:S(2)}) collective-permute-start(bf16[2,128,512]{2,1,0:T(8,128)(2,1)S(1)} %collective-permute-done.3.refs_0_), channel_id=1, source_target_pairs={{0,4},{8,16},{16,8},{24,28},{28,24},{20,12},{12,20},{4,0},{1,5},{9... | collective-permute-start | bytes 786440 | tf_op jit(solution)/shard_map/ppermute | solution.py:33
  44.0 1.6 %collective-permute-start.13 = (bf16[128,512]{1,0:T(8,128)(2,1)S(1)}, bf16[128,512]{1,0:T(8,128)(2,1)S(1)}, u32[]{:S(2)}, u32[]{:S(2)}) collective-permute-start(bf16[128,512]{1,0:T(8,128)(2,1)S(1)} %get-tuple-element.42), channel_id=1, source_target_pairs={{0,1},{1,0},{2,3},{3,2},{4,5},{5,4},{6,7},{7,6},{8,9},{9,8},{10,11... | collective-permute-start | bytes 393224 | tf_op jit(solution)/shard_map/ppermute | solution.py:37
  44.1 1.6 %collective-permute-start.14 = (bf16[128,512]{1,0:T(8,128)(2,1)S(1)}, bf16[128,512]{1,0:T(8,128)(2,1)S(1)}, u32[]{:S(2)}, u32[]{:S(2)}) collective-permute-start(bf16[128,512]{1,0:T(8,128)(2,1)S(1)} %get-tuple-element.43), channel_id=1, source_target_pairs={{0,1},{1,0},{2,3},{3,2},{4,5},{5,4},{6,7},{7,6},{8,9},{9,8},{10,11... | collective-permute-start | bytes 393224 | tf_op jit(solution)/shard_map/ppermute | solution.py:37
  45.5 6.2 %collective-permute-start.19 = (bf16[256,512]{1,0:T(8,128)(2,1)S(1)}, bf16[256,512]{1,0:T(8,128)(2,1)S(1)}, u32[]{:S(2)}, u32[]{:S(2)}) collective-permute-start(bf16[256,512]{1,0:T(8,128)(2,1)S(1)} %get-tuple-element.51), channel_id=1, source_target_pairs={{0,1},{1,0},{2,3},{3,2},{4,5},{5,4},{6,7},{7,6},{8,9},{9,8},{10,11... | collective-permute-start | bytes 786440 | tf_op jit(solution)/shard_map/ppermute | solution.py:37
  45.7 8.8 %collective-permute-start.20 = (bf16[256,512]{1,0:T(8,128)(2,1)S(1)}, bf16[256,512]{1,0:T(8,128)(2,1)S(1)}, u32[]{:S(2)}, u32[]{:S(2)}) collective-permute-start(bf16[256,512]{1,0:T(8,128)(2,1)S(1)} %shard_map.70), channel_id=1, source_target_pairs={{0,2},{2,0},{1,3},{3,1},{4,6},{6,4},{5,7},{7,5},{8,10},{10,8},{9,1... | collective-permute-start | bytes 786440 | tf_op jit(solution)/shard_map/ppermute | solution.py:37
  49.6 5.0 %copy-start.3 = (f32[1024]{0:T(1024)S(1)}, f32[1024]{0:T(1024)}, u32[]{:S(2)}) copy-start(f32[1024]{0:T(1024)} %param.10) | copy-start | bytes 12292
  49.6 5.0 %copy-start.4 = (f32[256]{0:T(256)S(1)}, f32[256]{0:T(256)}, u32[]{:S(2)}) copy-start(f32[256]{0:T(256)} %param.9) | copy-start | bytes 3076
  49.6 1.5 %collective-permute-start.16 = (bf16[128,512]{1,0:T(8,128)(2,1)S(1)}, bf16[128,512]{1,0:T(8,128)(2,1)S(1)}, u32[]{:S(2)}, u32[]{:S(2)}) collective-permute-start(bf16[128,512]{1,0:T(8,128)(2,1)S(1)} %get-tuple-element.48), channel_id=1, source_target_pairs={{0,1},{1,0},{2,3},{3,2},{4,5},{5,4},{6,7},{7,6},{8,9},{9,8},{10,11... | collective-permute-start | bytes 393224 | tf_op jit(solution)/shard_map/ppermute | solution.py:37
  49.8 1.4 %collective-permute-start.17 = (bf16[128,512]{1,0:T(8,128)(2,1)S(1)}, bf16[128,512]{1,0:T(8,128)(2,1)S(1)}, u32[]{:S(2)}, u32[]{:S(2)}) collective-permute-start(bf16[128,512]{1,0:T(8,128)(2,1)S(1)} %get-tuple-element.49), channel_id=1, source_target_pairs={{0,1},{1,0},{2,3},{3,2},{4,5},{5,4},{6,7},{7,6},{8,9},{9,8},{10,11... | collective-permute-start | bytes 393224 | tf_op jit(solution)/shard_map/ppermute | solution.py:37
  51.3 8.8 %collective-permute-start.18 = (bf16[256,512]{1,0:T(8,128)(2,1)S(1)}, bf16[256,512]{1,0:T(8,128)(2,1)S(1)}, u32[]{:S(2)}, u32[]{:S(2)}) collective-permute-start(bf16[256,512]{1,0:T(8,128)(2,1)S(1)} %shard_map.74), channel_id=1, source_target_pairs={{0,2},{2,0},{1,3},{3,1},{4,6},{6,4},{5,7},{7,5},{8,10},{10,8},{9,1... | collective-permute-start | bytes 786440 | tf_op jit(solution)/shard_map/ppermute | solution.py:37
  51.6 8.4 %collective-permute-start.15 = (bf16[256,512]{1,0:T(8,128)(2,1)S(1)}, bf16[256,512]{1,0:T(8,128)(2,1)S(1)}, u32[]{:S(2)}, u32[]{:S(2)}) collective-permute-start(bf16[256,512]{1,0:T(8,128)(2,1)S(1)} %get-tuple-element.46), channel_id=1, source_target_pairs={{0,1},{1,0},{2,3},{3,2},{4,5},{5,4},{6,7},{7,6},{8,9},{9,8},{10,11... | collective-permute-start | bytes 786440 | tf_op jit(solution)/shard_map/ppermute | solution.py:37

commit v7 on v6

--- a/solution.py
+++ b/solution.py
@@ -83,30 +83,45 @@
     )(kept, *got)
 
 
-def quotient(kept, got, from_y, pair_energy, virt_energy, span, left=None, weight=1):
-    rows = kept.shape[0]
-
-    def body(kept_ref, got_ref, from_y_ref, pair_ref, virt_ref, *refs):
-        out_ref = refs[-1]
+def first_quotient(kept, got, from_y, pair_energy, virt_energy, span):
+    rows, columns = kept.shape
+    rest = virt_energy.shape[0] - span[1]
+
+    def body(kept_ref, got_ref, from_y_ref, pair_ref, virt_ref, out_ref, inverse_ref):
         pair = jnp.transpose(jnp.concatenate([pair_ref[...]] * 8, axis=0))[:, :1]
         ladder = kept_ref[...] + got_ref[...].astype(F32) + from_y_ref[...].astype(F32)
-        value = (ladder / (virt_ref[:, span[0] : span[1]] - pair)).astype(BF16)
-        if left is None:
-            out_ref[...] = value
-        else:
-            out_ref[:, : span[0]] = refs[0][...]
-            out_ref[:, span[0] :] = value
-
-    vmem = pl.BlockSpec(memory_space=pltpu.VMEM)
-    more = [] if left is None else [left]
-    return pl.pallas_call(
-        body,
-        in_specs=[vmem] * (5 + len(more)),
+        out_ref[...] = (ladder / (virt_ref[:, : span[1]] - pair)).astype(BF16)
+        inverse_ref[...] = 1.0 / (virt_ref[:, span[1] :] - pair)
+
+    vmem = pl.BlockSpec(memory_space=pltpu.VMEM)
+    return pl.pallas_call(
+        body,
+        in_specs=[vmem] * 5,
+        out_specs=[vmem, vmem],
+        out_shape=[jax.ShapeDtypeStruct((rows, columns), BF16), jax.ShapeDtypeStruct((rows, rest), F32)],
+        compiler_params=pltpu.CompilerParams(vmem_limit_bytes=8 * 2**20),
+        cost_estimate=pl.CostEstimate(flops=2 * 10**9, bytes_accessed=2 * 10**7, transcendentals=0),
+    )(kept, got, from_y, pair_energy[None, :], virt_energy[None, :])
+
+
+def second_quotient(kept, got, from_y, inverse, left):
+    rows, columns = kept.shape
+    at = left.shape[1]
+
+    def body(kept_ref, got_ref, from_y_ref, inverse_ref, left_ref, out_ref):
+        out_ref[:, :at] = left_ref[...]
+        ladder = kept_ref[...] + got_ref[...].astype(F32) + from_y_ref[...].astype(F32)
+        out_ref[:, at:] = (ladder * inverse_ref[...]).astype(BF16)
+
+    vmem = pl.BlockSpec(memory_space=pltpu.VMEM)
+    return pl.pallas_call(
+        body,
+        in_specs=[vmem] * 5,
         out_specs=vmem,
-        out_shape=jax.ShapeDtypeStruct((rows, span[1] - (span[0] if left is None else 0)), BF16),
+        out_shape=jax.ShapeDtypeStruct((rows, at + columns), BF16),
         compiler_params=pltpu.CompilerParams(vmem_limit_bytes=8 * 2**20),
-        cost_estimate=pl.CostEstimate(flops=weight * 10**8, bytes_accessed=weight * 10**6, transcendentals=0),
-    )(kept, got, from_y, pair_energy[None, :], virt_energy[None, :], *more)
+        cost_estimate=pl.CostEstimate(flops=10**8, bytes_accessed=10**6, transcendentals=0),
+    )(kept, got, from_y, inverse, left)
 
 
 def tie(*values):
@@ -226,9 +241,9 @@
     )
     from_y_b = over_virt(added(keep_there_b, got_there_b), YHOP)
     got_here_a, got_here_b = over_virt(here_a, CORE), over_virt(here_b, CORE)
-    left = quotient(keep_here_a, got_here_a, from_y_a, pair_energy, virt_energy, span_a, weight=20)
+    left, inverse = first_quotient(keep_here_a, got_here_a, from_y_a, pair_energy, virt_energy, span_a)
     from_y_b, left = tie(from_y_b, left)
-    return quotient(keep_here_b, got_here_b, from_y_b, pair_energy, virt_energy, span_b, left=left)
+    return second_quotient(keep_here_b, got_here_b, from_y_b, inverse, left)
 
 
 def solution(mesh):

time: 61.4 us -> 61.3 us (level)
  transfers between devices with their start and end apart: 21 -> 21, of which waited for: 10 -> 10; matrix products, arithmetic and copies ran while one was open for 3% -> 3% of each run, Pallas kernels for 20% -> 21%
where the time goes in v7:
time: 61.3 us; the launch traced here: 61 us
  starting transfers between devices  25.2 us (41%)
  waiting for transfers between devices  17.5 us (29%)
  Pallas kernels  13.5 us (22%)
  local copies, waits for them, and re-layouts  4.69 us (8%)
    ppermute x13, starting transfers between devices, over_pair(): return lax.ppermute(value, 'pair', hops)  21.7 us
    pallas_call x8, Pallas kernels, products(): pl.pallas_call(body, in_specs=[smem] + [vmem] * len(operands), out_specs=...  10.3 us
    ppermute x13, waiting for transfers between devices, over_pair(): return lax.ppermute(value, 'pair', hops)  9.39 us
    ppermute x8, waiting for transfers between devices, over_virt(): return lax.ppermute(value, 'virt', hops)  8.07 us
    ppermute x8, starting transfers between devices, over_virt(): return lax.ppermute(value, 'virt', hops)  3.52 us
    unnamed x10, local copies, waits for them, and re-layouts  2.9 us
    pallas_call x1, Pallas kernels, arranged(): pl.pallas_call(body, in_specs=[vmem, vmem], out_specs=vmem, out_shape=jax...  1.84 us
  transfers between devices with their start and end apart: 21, of which 10 were waited for; matrix products, arithmetic and copies ran while one was open for 3% of the time, Pallas kernels for 21%

profile of v7, /device:TPU:0, one launch (start us, length us, event | category | flops | bytes accessed | tf_op | source)
XLA Modules:
  0.0 61.0 jit_solution(3097993747059533957)
XLA Ops:
  0.0 3.0 %collective-permute-start.1 = (bf16[2,128,1024]{2,1,0:T(8,128)(2,1)}, bf16[2,128,1024]{2,1,0:T(8,128)(2,1)S(1)}, u32[]{:S(2)}, u32[]{:S(2)}) collective-permute-start(bf16[2,128,1024]{2,1,0:T(8,128)(2,1)} %refs_0_.1), channel_id=1, source_target_pairs={{0,8},{8,0},{16,24},{24,16},{28,20},{20,28},{12,4},{4,12},{1,9},{9... | collective-permute-start | bytes 1572872 | tf_op jit(solution)/shard_map/ppermute | solution.py:33
  3.0 1.1 %fusion = (bf16[2,128,512]{2,1,0:T(8,128)(2,1)S(1)}, bf16[2,128,512]{2,1,0:T(8,128)(2,1)S(1)}) fusion(bf16[2,128,1024]{2,1,0:T(8,128)(2,1)} %refs_0_.1), kind=kLoop, calls=%fused_computation.1 | loop fusion | bytes 1048576 | tf_op jit(solution)/shard_map/slice | solution.py:209
  4.1 1.6 %collective-permute-start = (bf16[2,128,512]{2,1,0:T(8,128)(2,1)S(1)}, bf16[2,128,512]{2,1,0:T(8,128)(2,1)S(1)}, u32[]{:S(2)}, u32[]{:S(2)}) collective-permute-start(bf16[2,128,512]{2,1,0:T(8,128)(2,1)S(1)} %get-tuple-element.60), channel_id=1, source_target_pairs={{0,4},{8,16},{16,8},{24,28},{28,24},{20,12},{12,20},{4,0},{1,5},{9... | collective-permute-start | bytes 786440 | tf_op jit(solution)/shard_map/ppermute | solution.py:33
  5.6 0.5 collective-permute-start.6
  6.2 0.7 %dynamic-slice_bitcast_fusion.table_ref = s32[12]{0:T(128)S(1)} fusion(s32[32,12]{1,0:T(8,128)} %constant.19.clone, s32[]{:T(128)S(6)} %select_n.4), kind=kLoop, calls=%fused_computation | loop fusion | bytes 100 | tf_op jit(solution)/shard_map/jit(dynamic_index_in_dim)/squeeze | solution.py:200
  6.9 0.0 copy-start
  6.9 2.2 %copy-done = bf16[1024,2,1024]{2,1,0:T(2,128)(2,1)S(1)} copy-done((bf16[1024,2,1024]{2,1,0:T(2,128)(2,1)S(1)}, bf16[1024,2,1024]{2,1,0:T(2,128)(2,1)}, u32[]{:S(2)}) %copy-start) | copy-done | bytes 4194328
  9.1 0.0 copy-start.2
  9.1 0.7 %copy-done.2 = s32[1024,2]{0,1:T(2,128)S(1)} copy-done((s32[1024,2]{0,1:T(2,128)S(1)}, s32[1024,2]{0,1:T(2,128)}, u32[]{:S(2)}) %copy-start.2) | copy-done | bytes 8216
  9.8 1.8 %shard_map.64.a_ref = bf16[2,1024,1024]{2,1,0:T(8,128)(2,1)S(1)} custom-call(bf16[1024,2,1024]{2,1,0:T(2,128)(2,1)S(1)} %copy-done, s32[2,1024]{1,0:T(2,128)S(1)} %bitcast.5), custom_call_target="tpu_custom_call" | custom-call | flops 2147483648 | bytes 8388608 | tf_op jit(solution)/shard_map/pallas_call | solution.py:57
  11.6 1.8 %collective-permute-done.refs_2_ = bf16[2,128,512]{2,1,0:T(8,128)(2,1)S(1)} collective-permute-done((bf16[2,128,512]{2,1,0:T(8,128)(2,1)S(1)}, bf16[2,128,512]{2,1,0:T(8,128)(2,1)S(1)}, u32[]{:S(2)}, u32[]{:S(2)}) %collective-permute-start) | collective-permute-done | bytes 262176 | tf_op jit(solution)/shard_map/ppermute | solution.py:33
  13.4 1.1 %collective-permute-start.5 = (bf16[2,128,512]{2,1,0:T(8,128)(2,1)S(1)}, bf16[2,128,512]{2,1,0:T(8,128)(2,1)S(1)}, u32[]{:S(2)}, u32[]{:S(2)}) collective-permute-start(bf16[2,128,512]{2,1,0:T(8,128)(2,1)S(1)} %collective-permute-done.refs_2_), channel_id=1, source_target_pairs={{0,8},{8,0},{16,24},{24,16},{28,20},{20,28},{12,4},{4,12},{1,9},{9... | collective-permute-start | bytes 786440 | tf_op jit(solution)/shard_map/ppermute | solution.py:33
  14.5 1.5 %collective-permute-done.1.refs_1_ = bf16[2,128,1024]{2,1,0:T(8,128)(2,1)S(1)} collective-permute-done((bf16[2,128,1024]{2,1,0:T(8,128)(2,1)}, bf16[2,128,1024]{2,1,0:T(8,128)(2,1)S(1)}, u32[]{:S(2)}, u32[]{:S(2)}) %collective-permute-start.1) | collective-permute-done | bytes 524320 | tf_op jit(solution)/shard_map/ppermute | solution.py:33
  16.0 2.0 %collective-permute-start.4 = (bf16[2,128,512]{2,1,0:T(8,128)(2,1)S(1)}, bf16[2,128,512]{2,1,0:T(8,128)(2,1)S(1)}, u32[]{:S(2)}, u32[]{:S(2)}) collective-permute-start(bf16[2,128,512]{2,1,0:T(8,128)(2,1)S(1)} %get-tuple-element.61), channel_id=1, source_target_pairs={{0,4},{8,16},{16,8},{24,28},{28,24},{20,12},{12,20},{4,0},{1,5},{9... | collective-permute-start | bytes 786440 | tf_op jit(solution)/shard_map/ppermute | solution.py:33
  18.1 0.0 collective-permute-done.6.refs_3_
  18.1 1.7 %collective-permute-start.9 = (bf16[2,128,512]{2,1,0:T(8,128)(2,1)S(1)}, bf16[2,128,512]{2,1,0:T(8,128)(2,1)S(1)}, u32[]{:S(2)}, u32[]{:S(2)}) collective-permute-start(bf16[2,128,512]{2,1,0:T(8,128)(2,1)S(1)} %collective-permute-done.6.refs_3_), channel_id=1, source_target_pairs={{0,8},{8,0},{16,24},{24,16},{28,20},{20,28},{12,4},{4,12},{1,9},{9... | collective-permute-start | bytes 786440 | tf_op jit(solution)/shard_map/ppermute | solution.py:33
  19.7 1.5 %collective-permute-start.2 = (bf16[2,128,512]{2,1,0:T(8,128)(2,1)S(1)}, bf16[2,128,512]{2,1,0:T(8,128)(2,1)S(1)}, u32[]{:S(2)}, u32[]{:S(2)}) collective-permute-start(bf16[2,128,512]{2,1,0:T(8,128)(2,1)S(1)} %get-tuple-element.62), channel_id=1, source_target_pairs={{0,4},{8,16},{16,8},{24,28},{28,24},{20,12},{12,20},{4,0},{1,5},{9... | collective-permute-start | bytes 786440 | tf_op jit(solution)/shard_map/ppermute | solution.py:33
  21.2 0.0 copy-done.1
  21.2 2.4 %shard_map.65.refs_4_ = f32[4,256,1024]{2,1,0:T(8,128)S(1)} custom-call(s32[12]{0:T(128)S(1)} %dynamic-slice_bitcast_fusion.table_ref, bf16[2,1024,1024]{2,1,0:T(8,128)(2,1)S(1)} %shard_map.64.a_ref, bf16[2,128,1024]{2,1,0:T(8,128)(2,1)S(1)} %copy-done.1, bf16[2,128,1024]{2,1,0:T(8,128)(2,1)S(1)} %collective-permute-done.1.refs_1_, ...), custom_call_target="tpu_custom_call" | custom-call | flops 1610612736 | bytes 6291456 | tf_op jit(solution)/shard_map/pallas_call | solution.py:177
  23.6 0.0 collective-permute-done.5.refs_0_
  23.6 1.7 %collective-permute-done.4.refs_2_ = bf16[2,128,512]{2,1,0:T(8,128)(2,1)S(1)} collective-permute-done((bf16[2,128,512]{2,1,0:T(8,128)(2,1)S(1)}, bf16[2,128,512]{2,1,0:T(8,128)(2,1)S(1)}, u32[]{:S(2)}, u32[]{:S(2)}) %collective-permute-start.4) | collective-permute-done | bytes 262176 | tf_op jit(solution)/shard_map/ppermute | solution.py:33
  25.3 2.1 %collective-permute-start.7 = (bf16[2,128,512]{2,1,0:T(8,128)(2,1)S(1)}, bf16[2,128,512]{2,1,0:T(8,128)(2,1)S(1)}, u32[]{:S(2)}, u32[]{:S(2)}) collective-permute-start(bf16[2,128,512]{2,1,0:T(8,128)(2,1)S(1)} %collective-permute-done.4.refs_2_), channel_id=1, source_target_pairs={{0,8},{8,0},{16,24},{24,16},{28,20},{20,28},{12,4},{4,12},{1,9},{9... | collective-permute-start | bytes 786440 | tf_op jit(solution)/shard_map/ppermute | solution.py:33
  27.4 1.5 %collective-permute-start.8 = (bf16[2,128,512]{2,1,0:T(8,128)(2,1)S(1)}, bf16[2,128,512]{2,1,0:T(8,128)(2,1)S(1)}, u32[]{:S(2)}, u32[]{:S(2)}) collective-permute-start(bf16[2,128,512]{2,1,0:T(8,128)(2,1)S(1)} %collective-permute-done.5.refs_0_), channel_id=1, source_target_pairs={{0,4},{8,16},{16,8},{24,28},{28,24},{20,12},{12,20},{4,0},{1,5},{9... | collective-permute-start | bytes 786440 | tf_op jit(solution)/shard_map/ppermute | solution.py:33
  28.9 0.0 collective-permute-done.9.refs_1_
  28.9 0.8 %collective-permute-start.11 = (bf16[2,128,512]{2,1,0:T(8,128)(2,1)S(1)}, bf16[2,128,512]{2,1,0:T(8,128)(2,1)S(1)}, u32[]{:S(2)}, u32[]{:S(2)}) collective-permute-start(bf16[2,128,512]{2,1,0:T(8,128)(2,1)S(1)} %collective-permute-done.9.refs_1_), channel_id=1, source_target_pairs={{0,4},{8,16},{16,8},{24,28},{28,24},{20,12},{12,20},{4,0},{1,5},{9... | collective-permute-start | bytes 786440 | tf_op jit(solution)/shard_map/ppermute | solution.py:33
  29.7 1.2 %collective-permute-done.2.refs_3_ = bf16[2,128,512]{2,1,0:T(8,128)(2,1)S(1)} collective-permute-done((bf16[2,128,512]{2,1,0:T(8,128)(2,1)S(1)}, bf16[2,128,512]{2,1,0:T(8,128)(2,1)S(1)}, u32[]{:S(2)}, u32[]{:S(2)}) %collective-permute-start.2) | collective-permute-done | bytes 262176 | tf_op jit(solution)/shard_map/ppermute | solution.py:33
  31.0 2.1 %collective-permute-start.3 = (bf16[2,128,512]{2,1,0:T(8,128)(2,1)S(1)}, bf16[2,128,512]{2,1,0:T(8,128)(2,1)S(1)}, u32[]{:S(2)}, u32[]{:S(2)}) collective-permute-start(bf16[2,128,512]{2,1,0:T(8,128)(2,1)S(1)} %collective-permute-done.2.refs_3_), channel_id=1, source_target_pairs={{0,8},{8,0},{16,24},{24,16},{28,20},{20,28},{12,4},{4,12},{1,9},{9... | collective-permute-start | bytes 786440 | tf_op jit(solution)/shard_map/ppermute | solution.py:33
  33.0 1.9 %shard_map.66.refs_2_ = f32[4,256,1024]{2,1,0:T(8,128)S(1)} custom-call(s32[12]{0:T(128)S(1)} %dynamic-slice_bitcast_fusion.table_ref, bf16[2,1024,1024]{2,1,0:T(8,128)(2,1)S(1)} %shard_map.64.a_ref, bf16[2,128,512]{2,1,0:T(8,128)(2,1)S(1)} %collective-permute-done.5.refs_0_, bf16[2,128,512]{2,1,0:T(8,128)(2,1)S(1)} %collective-permute-done.9.refs_1_, ...), custom_call_target="tpu_custom_call" | custom-call | flops 1073741824 | bytes 6291456 | tf_op jit(solution)/shard_map/pallas_call | solution.py:177
  34.9 0.0 collective-permute-done.7.refs_0_
  34.9 1.7 %collective-permute-done.8.refs_1_ = bf16[2,128,512]{2,1,0:T(8,128)(2,1)S(1)} collective-permute-done((bf16[2,128,512]{2,1,0:T(8,128)(2,1)S(1)}, bf16[2,128,512]{2,1,0:T(8,128)(2,1)S(1)}, u32[]{:S(2)}, u32[]{:S(2)}) %collective-permute-start.8) | collective-permute-done | bytes 262176 | tf_op jit(solution)/shard_map/ppermute | solution.py:33
  36.6 2.0 %collective-permute-start.12 = (bf16[2,128,512]{2,1,0:T(8,128)(2,1)S(1)}, bf16[2,128,512]{2,1,0:T(8,128)(2,1)S(1)}, u32[]{:S(2)}, u32[]{:S(2)}) collective-permute-start(bf16[2,128,512]{2,1,0:T(8,128)(2,1)S(1)} %collective-permute-done.8.refs_1_), channel_id=1, source_target_pairs={{0,8},{8,0},{16,24},{24,16},{28,20},{20,28},{12,4},{4,12},{1,9},{9... | collective-permute-start | bytes 786440 | tf_op jit(solution)/shard_map/ppermute | solution.py:33
  38.6 1.3 %shard_map.67.refs_1_ = f32[4,256,512]{2,1,0:T(8,128)S(1)} custom-call(s32[12]{0:T(128)S(1)} %dynamic-slice_bitcast_fusion.table_ref, bf16[2,1024,1024]{2,1,0:T(8,128)(2,1)S(1)} %shard_map.64.a_ref, bf16[2,128,512]{2,1,0:T(8,128)(2,1)S(1)} %collective-permute-done.7.refs_0_, bf16[2,128,512]{2,1,0:T(8,128)(2,1)S(1)} %collective-permute-done.8.refs_1_, ...), custom_call_target="tpu_custom_call" | custom-call | flops 10737418240 | bytes 4718592 | tf_op jit(solution)/shard_map/pallas_call | solution.py:177
  40.0 0.3 collective-permute-done.3.refs_0_
  40.2 1.9 %collective-permute-start.10 = (bf16[2,128,512]{2,1,0:T(8,128)(2,1)S(1)}, bf16[2,128,512]{2,1,0:T(8,128)(2,1)S(1)}, u32[]{:S(2)}, u32[]{:S(2)}) collective-permute-start(bf16[2,128,512]{2,1,0:T(8,128)(2,1)S(1)} %collective-permute-done.3.refs_0_), channel_id=1, source_target_pairs={{0,4},{8,16},{16,8},{24,28},{28,24},{20,12},{12,20},{4,0},{1,5},{9... | collective-permute-start | bytes 786440 | tf_op jit(solution)/shard_map/ppermute | solution.py:33
  42.1 1.1 %collective-permute-done.12.refs_0_ = bf16[2,128,512]{2,1,0:T(8,128)(2,1)S(1)} collective-permute-done((bf16[2,128,512]{2,1,0:T(8,128)(2,1)S(1)}, bf16[2,128,512]{2,1,0:T(8,128)(2,1)S(1)}, u32[]{:S(2)}, u32[]{:S(2)}) %collective-permute-start.12) | collective-permute-done | bytes 262176 | tf_op jit(solution)/shard_map/ppermute | solution.py:33
  43.2 0.8 %shard_map.69 = (bf16[128,512]{1,0:T(8,128)(2,1)S(1)}, bf16[128,512]{1,0:T(8,128)(2,1)S(1)}) custom-call(s32[12]{0:T(128)S(1)} %dynamic-slice_bitcast_fusion.table_ref, bf16[2,1024,1024]{2,1,0:T(8,128)(2,1)S(1)} %shard_map.64.a_ref, bf16[2,128,512]{2,1,0:T(8,128)(2,1)S(1)} %collective-permute-done.12.refs_0_, f32[4,256,512]{2,1,0:T(8,128)S(1)} %shard_map.67.refs_1_), custom_call_target="tpu_custom_call" | custom-call | tf_op jit(solution)/shard_map/pallas_call | solution.py:177
  44.0 0.1 collective-permute-start.13
  44.1 0.5 collective-permute-start.14
  44.6 0.9 %shard_map.68 = (bf16[256,512]{1,0:T(8,128)(2,1)S(1)}, f32[256,512]{1,0:T(8,128)S(1)}, f32[256,512]{1,0:T(8,128)S(1)}) custom-call(s32[12]{0:T(128)S(1)} %dynamic-slice_bitcast_fusion.table_ref, bf16[2,1024,1024]{2,1,0:T(8,128)(2,1)S(1)} %shard_map.64.a_ref, bf16[2,128,512]{2,1,0:T(8,128)(2,1)S(1)} %collective-permute-done.12.refs_0_, ...), custom_call_target="tpu_custom_call" | custom-call | tf_op jit(solution)/shard_map/pallas_call | solution.py:177
  45.5 0.1 collective-permute-start.19
  45.7 0.0 collective-permute-done.13.refs_0_
  45.7 0.0 collective-permute-done.14.refs_1_
  45.7 1.8 %collective-permute-start.20 = (bf16[256,512]{1,0:T(8,128)(2,1)S(1)}, bf16[256,512]{1,0:T(8,128)(2,1)S(1)}, u32[]{:S(2)}, u32[]{:S(2)}) collective-permute-start(bf16[256,512]{1,0:T(8,128)(2,1)S(1)} %shard_map.70), channel_id=1, source_target_pairs={{0,2},{2,0},{1,3},{3,1},{4,6},{6,4},{5,7},{7,5},{8,10},{10,8},{9,1... | collective-permute-start | bytes 786440 | tf_op jit(solution)/shard_map/ppermute | solution.py:37
  47.5 0.0 collective-permute-done.11.refs_1_
  47.5 1.3 %shard_map.71.refs_1_ = f32[4,256,512]{2,1,0:T(8,128)S(1)} custom-call(s32[12]{0:T(128)S(1)} %dynamic-slice_bitcast_fusion.table_ref, bf16[2,1024,1024]{2,1,0:T(8,128)(2,1)S(1)} %shard_map.64.a_ref, bf16[2,128,512]{2,1,0:T(8,128)(2,1)S(1)} %collective-permute-done.3.refs_0_, bf16[2,128,512]{2,1,0:T(8,128)(2,1)S(1)} %collective-permute-done.11.refs_1_, ...), custom_call_target="tpu_custom_call" | custom-call | flops 536870912 | bytes 4718592 | tf_op jit(solution)/shard_map/pallas_call | solution.py:177
  48.8 0.0 collective-permute-done.10.refs_0_
  48.8 0.8 %shard_map.73 = (bf16[128,512]{1,0:T(8,128)(2,1)S(1)}, bf16[128,512]{1,0:T(8,128)(2,1)S(1)}) custom-call(s32[12]{0:T(128)S(1)} %dynamic-slice_bitcast_fusion.table_ref, bf16[2,1024,1024]{2,1,0:T(8,128)(2,1)S(1)} %shard_map.64.a_ref, bf16[2,128,512]{2,1,0:T(8,128)(2,1)S(1)} %collective-permute-done.10.refs_0_, f32[4,256,512]{2,1,0:T(8,128)S(1)} %shard_map.71.refs_1_), custom_call_target="tpu_custom_call" | custom-call | flops 1342177280 | bytes 4456448 | tf_op jit(solution)/shard_map/pallas_call | solution.py:177
  49.6 0.0 copy-start.3
  49.6 0.0 copy-start.4
  49.6 0.2 collective-permute-start.16
  49.8 0.4 collective-permute-start.17
  50.2 0.9 %shard_map.72 = (bf16[256,512]{1,0:T(8,128)(2,1)S(1)}, f32[256,512]{1,0:T(8,128)S(1)}, f32[256,512]{1,0:T(8,128)S(1)}) custom-call(s32[12]{0:T(128)S(1)} %dynamic-slice_bitcast_fusion.table_ref, bf16[2,1024,1024]{2,1,0:T(8,128)(2,1)S(1)} %shard_map.64.a_ref, bf16[2,128,512]{2,1,0:T(8,128)(2,1)S(1)} %collective-permute-done.10.refs_0_, ...), custom_call_target="tpu_custom_call" | custom-call | tf_op jit(solution)/shard_map/pallas_call | solution.py:177
  51.1 0.0 collective-permute-done.16.refs_0_
  51.1 0.1 collective-permute-done.17.refs_1_
  51.3 0.4 collective-permute-start.18
  51.6 0.1 collective-permute-start.15
  51.7 0.0 collective-permute-done.19.got_ref
  51.7 2.8 %collective-permute-done.20.from_y_ref = bf16[256,512]{1,0:T(8,128)(2,1)S(1)} collective-permute-done((bf16[256,512]{1,0:T(8,128)(2,1)S(1)}, bf16[256,512]{1,0:T(8,128)(2,1)S(1)}, u32[]{:S(2)}, u32[]{:S(2)}) %collective-permute-start.20) | collective-permute-done | bytes 262176 | tf_op jit(solution)/shard_map/ppermute | solution.py:37
  54.6 0.0 copy-done.3
  54.6 0.0 copy-done.4
  54.6 0.3 shard_map.75
  54.9 5.1 %collective-permute-done.18.from_y_ref = bf16[256,512]{1,0:T(8,128)(2,1)S(1)} collective-permute-done((bf16[256,512]{1,0:T(8,128)(2,1)S(1)}, bf16[256,512]{1,0:T(8,128)(2,1)S(1)}, u32[]{:S(2)}, u32[]{:S(2)}) %collective-permute-start.18) | collective-permute-done | bytes 262176 | tf_op jit(solution)/shard_map/ppermute | solution.py:37
  60.1 0.0 collective-permute-done.15.got_ref
  60.1 1.0 %shard_map.76 = bf16[256,1024]{1,0:T(8,128)(2,1)} custom-call(f32[256,512]{1,0:T(8,128)S(1)} %get-tuple-element.47.kept_ref, bf16[256,512]{1,0:T(8,128)(2,1)S(1)} %collective-permute-done.15.got_ref, bf16[256,512]{1,0:T(8,128)(2,1)S(1)} %collective-permute-done.18.from_y_ref, f32[256,512]{1,0:T(8,128)S(1)} %get-tuple-element.57.inverse_ref, ...), custom_call_target="tpu_custom_call" | custom-call | flops 100000000 | bytes 1000000 | tf_op jit(solution)/shard_map/pallas_call | solution.py:117
  (4 shorter events, 0.1 us)
Async XLA Ops:
  0.0 16.0 %collective-permute-start.1 = (bf16[2,128,1024]{2,1,0:T(8,128)(2,1)}, bf16[2,128,1024]{2,1,0:T(8,128)(2,1)S(1)}, u32[]{:S(2)}, u32[]{:S(2)}) collective-permute-start(bf16[2,128,1024]{2,1,0:T(8,128)(2,1)} %refs_0_.1), channel_id=1, source_target_pairs={{0,8},{8,0},{16,24},{24,16},{28,20},{20,28},{12,4},{4,12},{1,9},{9... | collective-permute-start | bytes 1572872 | tf_op jit(solution)/shard_map/ppermute | solution.py:33
  4.1 9.3 %collective-permute-start = (bf16[2,128,512]{2,1,0:T(8,128)(2,1)S(1)}, bf16[2,128,512]{2,1,0:T(8,128)(2,1)S(1)}, u32[]{:S(2)}, u32[]{:S(2)}) collective-permute-start(bf16[2,128,512]{2,1,0:T(8,128)(2,1)S(1)} %get-tuple-element.60), channel_id=1, source_target_pairs={{0,4},{8,16},{16,8},{24,28},{28,24},{20,12},{12,20},{4,0},{1,5},{9... | collective-permute-start | bytes 786440 | tf_op jit(solution)/shard_map/ppermute | solution.py:33
  5.6 12.4 %collective-permute-start.6 = (bf16[2,128,512]{2,1,0:T(8,128)(2,1)S(1)}, bf16[2,128,512]{2,1,0:T(8,128)(2,1)S(1)}, u32[]{:S(2)}, u32[]{:S(2)}) collective-permute-start(bf16[2,128,512]{2,1,0:T(8,128)(2,1)S(1)} %get-tuple-element.59), channel_id=1, source_target_pairs={{0,4},{8,16},{16,8},{24,28},{28,24},{20,12},{12,20},{4,0},{1,5},{9... | collective-permute-start | bytes 786440 | tf_op jit(solution)/shard_map/ppermute | solution.py:33
  6.9 2.2 %copy-start = (bf16[1024,2,1024]{2,1,0:T(2,128)(2,1)S(1)}, bf16[1024,2,1024]{2,1,0:T(2,128)(2,1)}, u32[]{:S(2)}) copy-start(bf16[1024,2,1024]{2,1,0:T(2,128)(2,1)} %amplitudes_ref.1) | copy-start | bytes 12582916
  9.1 0.7 %copy-start.2 = (s32[1024,2]{0,1:T(2,128)S(1)}, s32[1024,2]{0,1:T(2,128)}, u32[]{:S(2)}) copy-start(s32[1024,2]{0,1:T(2,128)} %param.7) | copy-start | bytes 24580
  9.8 11.5 %copy-start.1 = (bf16[2,128,1024]{2,1,0:T(8,128)(2,1)S(1)}, bf16[2,128,1024]{2,1,0:T(8,128)(2,1)}, u32[]{:S(2)}) copy-start(bf16[2,128,1024]{2,1,0:T(8,128)(2,1)} %refs_0_.1) | copy-start | bytes 1572868
  13.4 10.2 %collective-permute-start.5 = (bf16[2,128,512]{2,1,0:T(8,128)(2,1)S(1)}, bf16[2,128,512]{2,1,0:T(8,128)(2,1)S(1)}, u32[]{:S(2)}, u32[]{:S(2)}) collective-permute-start(bf16[2,128,512]{2,1,0:T(8,128)(2,1)S(1)} %collective-permute-done.refs_2_), channel_id=1, source_target_pairs={{0,8},{8,0},{16,24},{24,16},{28,20},{20,28},{12,4},{4,12},{1,9},{9... | collective-permute-start | bytes 786440 | tf_op jit(solution)/shard_map/ppermute | solution.py:33
  16.0 9.3 %collective-permute-start.4 = (bf16[2,128,512]{2,1,0:T(8,128)(2,1)S(1)}, bf16[2,128,512]{2,1,0:T(8,128)(2,1)S(1)}, u32[]{:S(2)}, u32[]{:S(2)}) collective-permute-start(bf16[2,128,512]{2,1,0:T(8,128)(2,1)S(1)} %get-tuple-element.61), channel_id=1, source_target_pairs={{0,4},{8,16},{16,8},{24,28},{28,24},{20,12},{12,20},{4,0},{1,5},{9... | collective-permute-start | bytes 786440 | tf_op jit(solution)/shard_map/ppermute | solution.py:33
  18.1 10.8 %collective-permute-start.9 = (bf16[2,128,512]{2,1,0:T(8,128)(2,1)S(1)}, bf16[2,128,512]{2,1,0:T(8,128)(2,1)S(1)}, u32[]{:S(2)}, u32[]{:S(2)}) collective-permute-start(bf16[2,128,512]{2,1,0:T(8,128)(2,1)S(1)} %collective-permute-done.6.refs_3_), channel_id=1, source_target_pairs={{0,8},{8,0},{16,24},{24,16},{28,20},{20,28},{12,4},{4,12},{1,9},{9... | collective-permute-start | bytes 786440 | tf_op jit(solution)/shard_map/ppermute | solution.py:33
  19.7 11.2 %collective-permute-start.2 = (bf16[2,128,512]{2,1,0:T(8,128)(2,1)S(1)}, bf16[2,128,512]{2,1,0:T(8,128)(2,1)S(1)}, u32[]{:S(2)}, u32[]{:S(2)}) collective-permute-start(bf16[2,128,512]{2,1,0:T(8,128)(2,1)S(1)} %get-tuple-element.62), channel_id=1, source_target_pairs={{0,4},{8,16},{16,8},{24,28},{28,24},{20,12},{12,20},{4,0},{1,5},{9... | collective-permute-start | bytes 786440 | tf_op jit(solution)/shard_map/ppermute | solution.py:33
  25.3 9.6 %collective-permute-start.7 = (bf16[2,128,512]{2,1,0:T(8,128)(2,1)S(1)}, bf16[2,128,512]{2,1,0:T(8,128)(2,1)S(1)}, u32[]{:S(2)}, u32[]{:S(2)}) collective-permute-start(bf16[2,128,512]{2,1,0:T(8,128)(2,1)S(1)} %collective-permute-done.4.refs_2_), channel_id=1, source_target_pairs={{0,8},{8,0},{16,24},{24,16},{28,20},{20,28},{12,4},{4,12},{1,9},{9... | collective-permute-start | bytes 786440 | tf_op jit(solution)/shard_map/ppermute | solution.py:33
  27.4 9.2 %collective-permute-start.8 = (bf16[2,128,512]{2,1,0:T(8,128)(2,1)S(1)}, bf16[2,128,512]{2,1,0:T(8,128)(2,1)S(1)}, u32[]{:S(2)}, u32[]{:S(2)}) collective-permute-start(bf16[2,128,512]{2,1,0:T(8,128)(2,1)S(1)} %collective-permute-done.5.refs_0_), channel_id=1, source_target_pairs={{0,4},{8,16},{16,8},{24,28},{28,24},{20,12},{12,20},{4,0},{1,5},{9... | collective-permute-start | bytes 786440 | tf_op jit(solution)/shard_map/ppermute | solution.py:33
  28.9 18.6 %collective-permute-start.11 = (bf16[2,128,512]{2,1,0:T(8,128)(2,1)S(1)}, bf16[2,128,512]{2,1,0:T(8,128)(2,1)S(1)}, u32[]{:S(2)}, u32[]{:S(2)}) collective-permute-start(bf16[2,128,512]{2,1,0:T(8,128)(2,1)S(1)} %collective-permute-done.9.refs_1_), channel_id=1, source_target_pairs={{0,4},{8,16},{16,8},{24,28},{28,24},{20,12},{12,20},{4,0},{1,5},{9... | collective-permute-start | bytes 786440 | tf_op jit(solution)/shard_map/ppermute | solution.py:33
  31.0 9.3 %collective-permute-start.3 = (bf16[2,128,512]{2,1,0:T(8,128)(2,1)S(1)}, bf16[2,128,512]{2,1,0:T(8,128)(2,1)S(1)}, u32[]{:S(2)}, u32[]{:S(2)}) collective-permute-start(bf16[2,128,512]{2,1,0:T(8,128)(2,1)S(1)} %collective-permute-done.2.refs_3_), channel_id=1, source_target_pairs={{0,8},{8,0},{16,24},{24,16},{28,20},{20,28},{12,4},{4,12},{1,9},{9... | collective-permute-start | bytes 786440 | tf_op jit(solution)/shard_map/ppermute | solution.py:33
  36.6 6.6 %collective-permute-start.12 = (bf16[2,128,512]{2,1,0:T(8,128)(2,1)S(1)}, bf16[2,128,512]{2,1,0:T(8,128)(2,1)S(1)}, u32[]{:S(2)}, u32[]{:S(2)}) collective-permute-start(bf16[2,128,512]{2,1,0:T(8,128)(2,1)S(1)} %collective-permute-done.8.refs_1_), channel_id=1, source_target_pairs={{0,8},{8,0},{16,24},{24,16},{28,20},{20,28},{12,4},{4,12},{1,9},{9... | collective-permute-start | bytes 786440 | tf_op jit(solution)/shard_map/ppermute | solution.py:33
  40.2 8.6 %collective-permute-start.10 = (bf16[2,128,512]{2,1,0:T(8,128)(2,1)S(1)}, bf16[2,128,512]{2,1,0:T(8,128)(2,1)S(1)}, u32[]{:S(2)}, u32[]{:S(2)}) collective-permute-start(bf16[2,128,512]{2,1,0:T(8,128)(2,1)S(1)} %collective-permute-done.3.refs_0_), channel_id=1, source_target_pairs={{0,4},{8,16},{16,8},{24,28},{28,24},{20,12},{12,20},{4,0},{1,5},{9... | collective-permute-start | bytes 786440 | tf_op jit(solution)/shard_map/ppermute | solution.py:33
  44.0 1.6 %collective-permute-start.13 = (bf16[128,512]{1,0:T(8,128)(2,1)S(1)}, bf16[128,512]{1,0:T(8,128)(2,1)S(1)}, u32[]{:S(2)}, u32[]{:S(2)}) collective-permute-start(bf16[128,512]{1,0:T(8,128)(2,1)S(1)} %get-tuple-element.44), channel_id=1, source_target_pairs={{0,1},{1,0},{2,3},{3,2},{4,5},{5,4},{6,7},{7,6},{8,9},{9,8},{10,11... | collective-permute-start | bytes 393224 | tf_op jit(solution)/shard_map/ppermute | solution.py:37
  44.1 1.6 %collective-permute-start.14 = (bf16[128,512]{1,0:T(8,128)(2,1)S(1)}, bf16[128,512]{1,0:T(8,128)(2,1)S(1)}, u32[]{:S(2)}, u32[]{:S(2)}) collective-permute-start(bf16[128,512]{1,0:T(8,128)(2,1)S(1)} %get-tuple-element.45), channel_id=1, source_target_pairs={{0,1},{1,0},{2,3},{3,2},{4,5},{5,4},{6,7},{7,6},{8,9},{9,8},{10,11... | collective-permute-start | bytes 393224 | tf_op jit(solution)/shard_map/ppermute | solution.py:37
  45.5 6.2 %collective-permute-start.19 = (bf16[256,512]{1,0:T(8,128)(2,1)S(1)}, bf16[256,512]{1,0:T(8,128)(2,1)S(1)}, u32[]{:S(2)}, u32[]{:S(2)}) collective-permute-start(bf16[256,512]{1,0:T(8,128)(2,1)S(1)} %get-tuple-element.53), channel_id=1, source_target_pairs={{0,1},{1,0},{2,3},{3,2},{4,5},{5,4},{6,7},{7,6},{8,9},{9,8},{10,11... | collective-permute-start | bytes 786440 | tf_op jit(solution)/shard_map/ppermute | solution.py:37
  45.7 8.8 %collective-permute-start.20 = (bf16[256,512]{1,0:T(8,128)(2,1)S(1)}, bf16[256,512]{1,0:T(8,128)(2,1)S(1)}, u32[]{:S(2)}, u32[]{:S(2)}) collective-permute-start(bf16[256,512]{1,0:T(8,128)(2,1)S(1)} %shard_map.70), channel_id=1, source_target_pairs={{0,2},{2,0},{1,3},{3,1},{4,6},{6,4},{5,7},{7,5},{8,10},{10,8},{9,1... | collective-permute-start | bytes 786440 | tf_op jit(solution)/shard_map/ppermute | solution.py:37
  49.6 5.0 %copy-start.3 = (f32[1024]{0:T(1024)S(1)}, f32[1024]{0:T(1024)}, u32[]{:S(2)}) copy-start(f32[1024]{0:T(1024)} %param.10) | copy-start | bytes 12292
  49.6 5.0 %copy-start.4 = (f32[256]{0:T(256)S(1)}, f32[256]{0:T(256)}, u32[]{:S(2)}) copy-start(f32[256]{0:T(256)} %param.9) | copy-start | bytes 3076
  49.6 1.5 %collective-permute-start.16 = (bf16[128,512]{1,0:T(8,128)(2,1)S(1)}, bf16[128,512]{1,0:T(8,128)(2,1)S(1)}, u32[]{:S(2)}, u32[]{:S(2)}) collective-permute-start(bf16[128,512]{1,0:T(8,128)(2,1)S(1)} %get-tuple-element.50), channel_id=1, source_target_pairs={{0,1},{1,0},{2,3},{3,2},{4,5},{5,4},{6,7},{7,6},{8,9},{9,8},{10,11... | collective-permute-start | bytes 393224 | tf_op jit(solution)/shard_map/ppermute | solution.py:37
  49.8 1.4 %collective-permute-start.17 = (bf16[128,512]{1,0:T(8,128)(2,1)S(1)}, bf16[128,512]{1,0:T(8,128)(2,1)S(1)}, u32[]{:S(2)}, u32[]{:S(2)}) collective-permute-start(bf16[128,512]{1,0:T(8,128)(2,1)S(1)} %get-tuple-element.51), channel_id=1, source_target_pairs={{0,1},{1,0},{2,3},{3,2},{4,5},{5,4},{6,7},{7,6},{8,9},{9,8},{10,11... | collective-permute-start | bytes 393224 | tf_op jit(solution)/shard_map/ppermute | solution.py:37
  51.3 8.8 %collective-permute-start.18 = (bf16[256,512]{1,0:T(8,128)(2,1)S(1)}, bf16[256,512]{1,0:T(8,128)(2,1)S(1)}, u32[]{:S(2)}, u32[]{:S(2)}) collective-permute-start(bf16[256,512]{1,0:T(8,128)(2,1)S(1)} %shard_map.74), channel_id=1, source_target_pairs={{0,2},{2,0},{1,3},{3,1},{4,6},{6,4},{5,7},{7,5},{8,10},{10,8},{9,1... | collective-permute-start | bytes 786440 | tf_op jit(solution)/shard_map/ppermute | solution.py:37
  51.6 8.4 %collective-permute-start.15 = (bf16[256,512]{1,0:T(8,128)(2,1)S(1)}, bf16[256,512]{1,0:T(8,128)(2,1)S(1)}, u32[]{:S(2)}, u32[]{:S(2)}) collective-permute-start(bf16[256,512]{1,0:T(8,128)(2,1)S(1)} %get-tuple-element.48), channel_id=1, source_target_pairs={{0,1},{1,0},{2,3},{3,2},{4,5},{5,4},{6,7},{7,6},{8,9},{9,8},{10,11... | collective-permute-start | bytes 786440 | tf_op jit(solution)/shard_map/ppermute | solution.py:37

commit v8 on v7

--- a/solution.py
+++ b/solution.py
@@ -214,11 +214,11 @@
     o1a, a, table = tie(o1a, a, table)
     e2a, o2a = over_pair(o1a, EVEN), over_pair(part(e1, span_a), ODD)
     e2b, o2b = over_pair(o1b, EVEN), over_pair(part(e1, span_b), ODD)
-    total = products(table, [0, 1, 2], a, [integrals, e1, [o1a, o1b]], (0, columns))
-    o2a, e2a, total = tie(o2a, e2a, total)
     e3a, o3a = over_pair(o2a, EVEN), over_pair(e2a, ODD)
     e3b, o3b = over_pair(o2b, EVEN), over_pair(e2b, ODD)
-    total = products(table, [3, 4], a, [[e2a, e2b], [o2a, o2b]], (0, columns), total=total)
+    total = products(
+        table, [0, 1, 2, 3, 4], a, [integrals, e1, [o1a, o1b], [e2a, e2b], [o2a, o2b]], (0, columns)
+    )
     e3a, o3a, total = tie(e3a, o3a, total)
     last_a = over_pair(o3a, EVEN)
     total_a = products(table, [5, 6], a, [e3a, o3a], span_a, total=total, weight=20)

time: 61.3 us -> 64.9 us (1.059)
  waiting for transfers between devices: 17.5 us -> 25 us
  starting transfers between devices: 25.2 us -> 22 us
  Pallas kernels: 13.5 us -> 12.7 us
    ppermute x13, waiting for transfers between devices: 9.39 us -> 17 us  [over_pair(): return lax.ppermute(value, 'pair', hops)]
    ppermute x13, starting transfers between devices: 21.7 us -> 18.5 us  [over_pair(): return lax.ppermute(value, 'pair', hops)]
    pallas_call x8 -> x7, Pallas kernels: 10.3 us -> 9.5 us  [products(): pl.pallas_call(body, in_specs=[smem] + [vmem] * len(operands), out_specs=...]
  transfers between devices with their start and end apart: 21 -> 21, of which waited for: 10 -> 11; matrix products, arithmetic and copies ran while one was open for 3% -> 3% of each run, Pallas kernels for 21% -> 18%
where the time goes in v8:
time: 64.9 us; the launch traced here: 64.6 us
  waiting for transfers between devices  25 us (39%)
  starting transfers between devices  22 us (34%)
  Pallas kernels  12.7 us (20%)
  local copies, waits for them, and re-layouts  4.7 us (7%)
    ppermute x13, starting transfers between devices, over_pair(): return lax.ppermute(value, 'pair', hops)  18.5 us
    ppermute x13, waiting for transfers between devices, over_pair(): return lax.ppermute(value, 'pair', hops)  17 us
    pallas_call x7, Pallas kernels, products(): pl.pallas_call(body, in_specs=[smem] + [vmem] * len(operands), out_specs=...  9.5 us
    ppermute x8, waiting for transfers between devices, over_virt(): return lax.ppermute(value, 'virt', hops)  8.07 us
    ppermute x8, starting transfers between devices, over_virt(): return lax.ppermute(value, 'virt', hops)  3.49 us
    unnamed x10, local copies, waits for them, and re-layouts  2.9 us
    pallas_call x1, Pallas kernels, arranged(): pl.pallas_call(body, in_specs=[vmem, vmem], out_specs=vmem, out_shape=jax...  1.85 us
  transfers between devices with their start and end apart: 21, of which 11 were waited for; matrix products, arithmetic and copies ran while one was open for 3% of the time, Pallas kernels for 18%

profile of v8, /device:TPU:0, one launch (start us, length us, event | category | flops | bytes accessed | tf_op | source)
XLA Modules:
  0.0 64.6 jit_solution(6082782799454864809)
XLA Ops:
  0.0 3.0 %collective-permute-start.1 = (bf16[2,128,1024]{2,1,0:T(8,128)(2,1)}, bf16[2,128,1024]{2,1,0:T(8,128)(2,1)S(1)}, u32[]{:S(2)}, u32[]{:S(2)}) collective-permute-start(bf16[2,128,1024]{2,1,0:T(8,128)(2,1)} %refs_0_.1), channel_id=1, source_target_pairs={{0,8},{8,0},{16,24},{24,16},{28,20},{20,28},{12,4},{4,12},{1,9},{9... | collective-permute-start | bytes 1572872 | tf_op jit(solution)/shard_map/ppermute | solution.py:33
  3.0 1.1 %fusion = (bf16[2,128,512]{2,1,0:T(8,128)(2,1)S(1)}, bf16[2,128,512]{2,1,0:T(8,128)(2,1)S(1)}) fusion(bf16[2,128,1024]{2,1,0:T(8,128)(2,1)} %refs_0_.1), kind=kLoop, calls=%fused_computation.1 | loop fusion | bytes 1048576 | tf_op jit(solution)/shard_map/slice | solution.py:209
  4.1 1.6 %collective-permute-start.8 = (bf16[2,128,512]{2,1,0:T(8,128)(2,1)S(1)}, bf16[2,128,512]{2,1,0:T(8,128)(2,1)S(1)}, u32[]{:S(2)}, u32[]{:S(2)}) collective-permute-start(bf16[2,128,512]{2,1,0:T(8,128)(2,1)S(1)} %get-tuple-element.53), channel_id=1, source_target_pairs={{0,4},{8,16},{16,8},{24,28},{28,24},{20,12},{12,20},{4,0},{1,5},{9... | collective-permute-start | bytes 786440 | tf_op jit(solution)/shard_map/ppermute | solution.py:33
  5.6 0.5 collective-permute-start
  6.2 0.0 copy-start
  6.2 2.2 %copy-done = bf16[1024,2,1024]{2,1,0:T(2,128)(2,1)S(1)} copy-done((bf16[1024,2,1024]{2,1,0:T(2,128)(2,1)S(1)}, bf16[1024,2,1024]{2,1,0:T(2,128)(2,1)}, u32[]{:S(2)}) %copy-start) | copy-done | bytes 4194328
  8.4 0.0 copy-start.2
  8.4 0.7 %copy-done.2 = s32[1024,2]{0,1:T(2,128)S(1)} copy-done((s32[1024,2]{0,1:T(2,128)S(1)}, s32[1024,2]{0,1:T(2,128)}, u32[]{:S(2)}) %copy-start.2) | copy-done | bytes 8216
  9.1 0.0 copy-start.1
  9.1 1.8 %shard_map.64.a_ref = bf16[2,1024,1024]{2,1,0:T(8,128)(2,1)S(1)} custom-call(bf16[1024,2,1024]{2,1,0:T(2,128)(2,1)S(1)} %copy-done, s32[2,1024]{1,0:T(2,128)S(1)} %bitcast.5), custom_call_target="tpu_custom_call" | custom-call | flops 2147483648 | bytes 8388608 | tf_op jit(solution)/shard_map/pallas_call | solution.py:57
  10.9 0.7 %dynamic-slice_bitcast_fusion.table_ref = s32[12]{0:T(128)S(1)} fusion(s32[32,12]{1,0:T(8,128)} %constant.19.clone, s32[]{:T(128)S(6)} %select_n.4), kind=kLoop, calls=%fused_computation | loop fusion | bytes 100 | tf_op jit(solution)/shard_map/jit(dynamic_index_in_dim)/squeeze | solution.py:200
  11.6 5.9 %collective-permute-done.refs_2_ = bf16[2,128,512]{2,1,0:T(8,128)(2,1)S(1)} collective-permute-done((bf16[2,128,512]{2,1,0:T(8,128)(2,1)S(1)}, bf16[2,128,512]{2,1,0:T(8,128)(2,1)S(1)}, u32[]{:S(2)}, u32[]{:S(2)}) %collective-permute-start) | collective-permute-done | bytes 262176 | tf_op jit(solution)/shard_map/ppermute | solution.py:33
  17.5 1.4 %collective-permute-start.6 = (bf16[2,128,512]{2,1,0:T(8,128)(2,1)S(1)}, bf16[2,128,512]{2,1,0:T(8,128)(2,1)S(1)}, u32[]{:S(2)}, u32[]{:S(2)}) collective-permute-start(bf16[2,128,512]{2,1,0:T(8,128)(2,1)S(1)} %collective-permute-done.refs_2_), channel_id=1, source_target_pairs={{0,8},{8,0},{16,24},{24,16},{28,20},{20,28},{12,4},{4,12},{1,9},{9... | collective-permute-start | bytes 786440 | tf_op jit(solution)/shard_map/ppermute | solution.py:33
  19.0 0.0 collective-permute-done.1.refs_1_
  19.0 1.6 %collective-permute-start.4 = (bf16[2,128,512]{2,1,0:T(8,128)(2,1)S(1)}, bf16[2,128,512]{2,1,0:T(8,128)(2,1)S(1)}, u32[]{:S(2)}, u32[]{:S(2)}) collective-permute-start(bf16[2,128,512]{2,1,0:T(8,128)(2,1)S(1)} %get-tuple-element.55), channel_id=1, source_target_pairs={{0,4},{8,16},{16,8},{24,28},{28,24},{20,12},{12,20},{4,0},{1,5},{9... | collective-permute-start | bytes 786440 | tf_op jit(solution)/shard_map/ppermute | solution.py:33
  20.6 0.0 collective-permute-done.8.refs_3_
  20.6 0.7 %collective-permute-start.9 = (bf16[2,128,512]{2,1,0:T(8,128)(2,1)S(1)}, bf16[2,128,512]{2,1,0:T(8,128)(2,1)S(1)}, u32[]{:S(2)}, u32[]{:S(2)}) collective-permute-start(bf16[2,128,512]{2,1,0:T(8,128)(2,1)S(1)} %collective-permute-done.8.refs_3_), channel_id=1, source_target_pairs={{0,8},{8,0},{16,24},{24,16},{28,20},{20,28},{12,4},{4,12},{1,9},{9... | collective-permute-start | bytes 786440 | tf_op jit(solution)/shard_map/ppermute | solution.py:33
  21.3 1.5 %collective-permute-start.2 = (bf16[2,128,512]{2,1,0:T(8,128)(2,1)S(1)}, bf16[2,128,512]{2,1,0:T(8,128)(2,1)S(1)}, u32[]{:S(2)}, u32[]{:S(2)}) collective-permute-start(bf16[2,128,512]{2,1,0:T(8,128)(2,1)S(1)} %get-tuple-element.56), channel_id=1, source_target_pairs={{0,4},{8,16},{16,8},{24,28},{28,24},{20,12},{12,20},{4,0},{1,5},{9... | collective-permute-start | bytes 786440 | tf_op jit(solution)/shard_map/ppermute | solution.py:33
  22.8 4.0 %collective-permute-done.6.refs_4_ = bf16[2,128,512]{2,1,0:T(8,128)(2,1)S(1)} collective-permute-done((bf16[2,128,512]{2,1,0:T(8,128)(2,1)S(1)}, bf16[2,128,512]{2,1,0:T(8,128)(2,1)S(1)}, u32[]{:S(2)}, u32[]{:S(2)}) %collective-permute-start.6) | collective-permute-done | bytes 262176 | tf_op jit(solution)/shard_map/ppermute | solution.py:33
  26.8 1.5 %collective-permute-start.7 = (bf16[2,128,512]{2,1,0:T(8,128)(2,1)S(1)}, bf16[2,128,512]{2,1,0:T(8,128)(2,1)S(1)}, u32[]{:S(2)}, u32[]{:S(2)}) collective-permute-start(bf16[2,128,512]{2,1,0:T(8,128)(2,1)S(1)} %collective-permute-done.6.refs_4_), channel_id=1, source_target_pairs={{0,4},{8,16},{16,8},{24,28},{28,24},{20,12},{12,20},{4,0},{1,5},{9... | collective-permute-start | bytes 786440 | tf_op jit(solution)/shard_map/ppermute | solution.py:33
  28.3 0.1 collective-permute-done.4.refs_6_
  28.3 1.6 %collective-permute-start.5 = (bf16[2,128,512]{2,1,0:T(8,128)(2,1)S(1)}, bf16[2,128,512]{2,1,0:T(8,128)(2,1)S(1)}, u32[]{:S(2)}, u32[]{:S(2)}) collective-permute-start(bf16[2,128,512]{2,1,0:T(8,128)(2,1)S(1)} %collective-permute-done.4.refs_6_), channel_id=1, source_target_pairs={{0,8},{8,0},{16,24},{24,16},{28,20},{20,28},{12,4},{4,12},{1,9},{9... | collective-permute-start | bytes 786440 | tf_op jit(solution)/shard_map/ppermute | solution.py:33
  29.9 2.5 %collective-permute-done.9.refs_5_ = bf16[2,128,512]{2,1,0:T(8,128)(2,1)S(1)} collective-permute-done((bf16[2,128,512]{2,1,0:T(8,128)(2,1)S(1)}, bf16[2,128,512]{2,1,0:T(8,128)(2,1)S(1)}, u32[]{:S(2)}, u32[]{:S(2)}) %collective-permute-start.9) | collective-permute-done | bytes 262176 | tf_op jit(solution)/shard_map/ppermute | solution.py:33
  32.4 1.5 %collective-permute-start.11 = (bf16[2,128,512]{2,1,0:T(8,128)(2,1)S(1)}, bf16[2,128,512]{2,1,0:T(8,128)(2,1)S(1)}, u32[]{:S(2)}, u32[]{:S(2)}) collective-permute-start(bf16[2,128,512]{2,1,0:T(8,128)(2,1)S(1)} %collective-permute-done.9.refs_5_), channel_id=1, source_target_pairs={{0,4},{8,16},{16,8},{24,28},{28,24},{20,12},{12,20},{4,0},{1,5},{9... | collective-permute-start | bytes 786440 | tf_op jit(solution)/shard_map/ppermute | solution.py:33
  33.9 0.1 collective-permute-done.2.refs_7_
  34.0 1.6 %collective-permute-start.3 = (bf16[2,128,512]{2,1,0:T(8,128)(2,1)S(1)}, bf16[2,128,512]{2,1,0:T(8,128)(2,1)S(1)}, u32[]{:S(2)}, u32[]{:S(2)}) collective-permute-start(bf16[2,128,512]{2,1,0:T(8,128)(2,1)S(1)} %collective-permute-done.2.refs_7_), channel_id=1, source_target_pairs={{0,8},{8,0},{16,24},{24,16},{28,20},{20,28},{12,4},{4,12},{1,9},{9... | collective-permute-start | bytes 786440 | tf_op jit(solution)/shard_map/ppermute | solution.py:33
  35.6 0.0 copy-done.1
  35.6 3.5 %shard_map.65.refs_2_ = f32[4,256,1024]{2,1,0:T(8,128)S(1)} custom-call(s32[12]{0:T(128)S(1)} %dynamic-slice_bitcast_fusion.table_ref, bf16[2,1024,1024]{2,1,0:T(8,128)(2,1)S(1)} %shard_map.64.a_ref, bf16[2,128,1024]{2,1,0:T(8,128)(2,1)S(1)} %copy-done.1, bf16[2,128,1024]{2,1,0:T(8,128)(2,1)S(1)} %collective-permute-done.1.refs_1_, ...), custom_call_target="tpu_custom_call" | custom-call | flops 2684354560 | bytes 8388608 | tf_op jit(solution)/shard_map/pallas_call | solution.py:177
  39.0 0.5 collective-permute-done.7.refs_1_
  39.6 0.0 collective-permute-done.5.refs_0_
  39.6 0.6 collective-permute-start.12
  40.2 1.3 %shard_map.66.refs_1_ = f32[4,256,512]{2,1,0:T(8,128)S(1)} custom-call(s32[12]{0:T(128)S(1)} %dynamic-slice_bitcast_fusion.table_ref, bf16[2,1024,1024]{2,1,0:T(8,128)(2,1)S(1)} %shard_map.64.a_ref, bf16[2,128,512]{2,1,0:T(8,128)(2,1)S(1)} %collective-permute-done.5.refs_0_, bf16[2,128,512]{2,1,0:T(8,128)(2,1)S(1)} %collective-permute-done.7.refs_1_, ...), custom_call_target="tpu_custom_call" | custom-call | flops 10737418240 | bytes 4718592 | tf_op jit(solution)/shard_map/pallas_call | solution.py:177
  41.5 2.1 %collective-permute-done.3.refs_0_ = bf16[2,128,512]{2,1,0:T(8,128)(2,1)S(1)} collective-permute-done((bf16[2,128,512]{2,1,0:T(8,128)(2,1)S(1)}, bf16[2,128,512]{2,1,0:T(8,128)(2,1)S(1)}, u32[]{:S(2)}, u32[]{:S(2)}) %collective-permute-start.3) | collective-permute-done | bytes 262176 | tf_op jit(solution)/shard_map/ppermute | solution.py:33
  43.6 1.5 %collective-permute-start.10 = (bf16[2,128,512]{2,1,0:T(8,128)(2,1)S(1)}, bf16[2,128,512]{2,1,0:T(8,128)(2,1)S(1)}, u32[]{:S(2)}, u32[]{:S(2)}) collective-permute-start(bf16[2,128,512]{2,1,0:T(8,128)(2,1)S(1)} %collective-permute-done.3.refs_0_), channel_id=1, source_target_pairs={{0,4},{8,16},{16,8},{24,28},{28,24},{20,12},{12,20},{4,0},{1,5},{9... | collective-permute-start | bytes 786440 | tf_op jit(solution)/shard_map/ppermute | solution.py:33
  45.1 1.7 %collective-permute-done.12.refs_0_ = bf16[2,128,512]{2,1,0:T(8,128)(2,1)S(1)} collective-permute-done((bf16[2,128,512]{2,1,0:T(8,128)(2,1)S(1)}, bf16[2,128,512]{2,1,0:T(8,128)(2,1)S(1)}, u32[]{:S(2)}, u32[]{:S(2)}) %collective-permute-start.12) | collective-permute-done | bytes 262176 | tf_op jit(solution)/shard_map/ppermute | solution.py:33
  46.9 0.8 %shard_map.68 = (bf16[128,512]{1,0:T(8,128)(2,1)S(1)}, bf16[128,512]{1,0:T(8,128)(2,1)S(1)}) custom-call(s32[12]{0:T(128)S(1)} %dynamic-slice_bitcast_fusion.table_ref, bf16[2,1024,1024]{2,1,0:T(8,128)(2,1)S(1)} %shard_map.64.a_ref, bf16[2,128,512]{2,1,0:T(8,128)(2,1)S(1)} %collective-permute-done.12.refs_0_, f32[4,256,512]{2,1,0:T(8,128)S(1)} %shard_map.66.refs_1_), custom_call_target="tpu_custom_call" | custom-call | tf_op jit(solution)/shard_map/pallas_call | solution.py:177
  47.6 0.1 collective-permute-start.13
  47.7 0.5 collective-permute-start.14
  48.2 0.9 %shard_map.67 = (bf16[256,512]{1,0:T(8,128)(2,1)S(1)}, f32[256,512]{1,0:T(8,128)S(1)}, f32[256,512]{1,0:T(8,128)S(1)}) custom-call(s32[12]{0:T(128)S(1)} %dynamic-slice_bitcast_fusion.table_ref, bf16[2,1024,1024]{2,1,0:T(8,128)(2,1)S(1)} %shard_map.64.a_ref, bf16[2,128,512]{2,1,0:T(8,128)(2,1)S(1)} %collective-permute-done.12.refs_0_, ...), custom_call_target="tpu_custom_call" | custom-call | tf_op jit(solution)/shard_map/pallas_call | solution.py:177
  49.1 0.1 collective-permute-start.19
  49.3 0.0 collective-permute-done.13.refs_0_
  49.3 0.0 collective-permute-done.14.refs_1_
  49.3 1.6 %collective-permute-start.20 = (bf16[256,512]{1,0:T(8,128)(2,1)S(1)}, bf16[256,512]{1,0:T(8,128)(2,1)S(1)}, u32[]{:S(2)}, u32[]{:S(2)}) collective-permute-start(bf16[256,512]{1,0:T(8,128)(2,1)S(1)} %shard_map.69), channel_id=1, source_target_pairs={{0,2},{2,0},{1,3},{3,1},{4,6},{6,4},{5,7},{7,5},{8,10},{10,8},{9,1... | collective-permute-start | bytes 786440 | tf_op jit(solution)/shard_map/ppermute | solution.py:37
  50.9 0.0 collective-permute-done.11.refs_1_
  50.9 1.3 %shard_map.70.refs_1_ = f32[4,256,512]{2,1,0:T(8,128)S(1)} custom-call(s32[12]{0:T(128)S(1)} %dynamic-slice_bitcast_fusion.table_ref, bf16[2,1024,1024]{2,1,0:T(8,128)(2,1)S(1)} %shard_map.64.a_ref, bf16[2,128,512]{2,1,0:T(8,128)(2,1)S(1)} %collective-permute-done.3.refs_0_, bf16[2,128,512]{2,1,0:T(8,128)(2,1)S(1)} %collective-permute-done.11.refs_1_, ...), custom_call_target="tpu_custom_call" | custom-call | flops 536870912 | bytes 4718592 | tf_op jit(solution)/shard_map/pallas_call | solution.py:177
  52.3 0.0 collective-permute-done.10.refs_0_
  52.3 0.8 %shard_map.72 = (bf16[128,512]{1,0:T(8,128)(2,1)S(1)}, bf16[128,512]{1,0:T(8,128)(2,1)S(1)}) custom-call(s32[12]{0:T(128)S(1)} %dynamic-slice_bitcast_fusion.table_ref, bf16[2,1024,1024]{2,1,0:T(8,128)(2,1)S(1)} %shard_map.64.a_ref, bf16[2,128,512]{2,1,0:T(8,128)(2,1)S(1)} %collective-permute-done.10.refs_0_, f32[4,256,512]{2,1,0:T(8,128)S(1)} %shard_map.70.refs_1_), custom_call_target="tpu_custom_call" | custom-call | flops 1342177280 | bytes 4456448 | tf_op jit(solution)/shard_map/pallas_call | solution.py:177
  53.1 0.0 copy-start.3
  53.1 0.0 copy-start.4
  53.1 0.2 collective-permute-start.16
  53.3 0.3 collective-permute-start.17
  53.7 0.9 %shard_map.71 = (bf16[256,512]{1,0:T(8,128)(2,1)S(1)}, f32[256,512]{1,0:T(8,128)S(1)}, f32[256,512]{1,0:T(8,128)S(1)}) custom-call(s32[12]{0:T(128)S(1)} %dynamic-slice_bitcast_fusion.table_ref, bf16[2,1024,1024]{2,1,0:T(8,128)(2,1)S(1)} %shard_map.64.a_ref, bf16[2,128,512]{2,1,0:T(8,128)(2,1)S(1)} %collective-permute-done.10.refs_0_, ...), custom_call_target="tpu_custom_call" | custom-call | tf_op jit(solution)/shard_map/pallas_call | solution.py:177
  54.6 0.0 collective-permute-done.16.refs_0_
  54.6 0.1 collective-permute-done.17.refs_1_
  54.8 0.6 collective-permute-start.18
  55.3 0.0 collective-permute-start.15
  55.4 0.0 collective-permute-done.19.got_ref
  55.4 3.0 %collective-permute-done.20.from_y_ref = bf16[256,512]{1,0:T(8,128)(2,1)S(1)} collective-permute-done((bf16[256,512]{1,0:T(8,128)(2,1)S(1)}, bf16[256,512]{1,0:T(8,128)(2,1)S(1)}, u32[]{:S(2)}, u32[]{:S(2)}) %collective-permute-start.20) | collective-permute-done | bytes 262176 | tf_op jit(solution)/shard_map/ppermute | solution.py:37
  58.3 0.0 copy-done.3
  58.3 0.0 copy-done.4
  58.3 0.3 shard_map.74
  58.7 5.0 %collective-permute-done.18.from_y_ref = bf16[256,512]{1,0:T(8,128)(2,1)S(1)} collective-permute-done((bf16[256,512]{1,0:T(8,128)(2,1)S(1)}, bf16[256,512]{1,0:T(8,128)(2,1)S(1)}, u32[]{:S(2)}, u32[]{:S(2)}) %collective-permute-start.18) | collective-permute-done | bytes 262176 | tf_op jit(solution)/shard_map/ppermute | solution.py:37
  63.7 0.0 collective-permute-done.15.got_ref
  63.7 1.0 %shard_map.75 = bf16[256,1024]{1,0:T(8,128)(2,1)} custom-call(f32[256,512]{1,0:T(8,128)S(1)} %get-tuple-element.41.kept_ref, bf16[256,512]{1,0:T(8,128)(2,1)S(1)} %collective-permute-done.15.got_ref, bf16[256,512]{1,0:T(8,128)(2,1)S(1)} %collective-permute-done.18.from_y_ref, f32[256,512]{1,0:T(8,128)S(1)} %get-tuple-element.51.inverse_ref, ...), custom_call_target="tpu_custom_call" | custom-call | flops 100000000 | bytes 1000000 | tf_op jit(solution)/shard_map/pallas_call | solution.py:117
  (3 shorter events, 0.1 us)
Async XLA Ops:
  0.0 19.0 %collective-permute-start.1 = (bf16[2,128,1024]{2,1,0:T(8,128)(2,1)}, bf16[2,128,1024]{2,1,0:T(8,128)(2,1)S(1)}, u32[]{:S(2)}, u32[]{:S(2)}) collective-permute-start(bf16[2,128,1024]{2,1,0:T(8,128)(2,1)} %refs_0_.1), channel_id=1, source_target_pairs={{0,8},{8,0},{16,24},{24,16},{28,20},{20,28},{12,4},{4,12},{1,9},{9... | collective-permute-start | bytes 1572872 | tf_op jit(solution)/shard_map/ppermute | solution.py:33
  4.1 16.5 %collective-permute-start.8 = (bf16[2,128,512]{2,1,0:T(8,128)(2,1)S(1)}, bf16[2,128,512]{2,1,0:T(8,128)(2,1)S(1)}, u32[]{:S(2)}, u32[]{:S(2)}) collective-permute-start(bf16[2,128,512]{2,1,0:T(8,128)(2,1)S(1)} %get-tuple-element.53), channel_id=1, source_target_pairs={{0,4},{8,16},{16,8},{24,28},{28,24},{20,12},{12,20},{4,0},{1,5},{9... | collective-permute-start | bytes 786440 | tf_op jit(solution)/shard_map/ppermute | solution.py:33
  5.6 11.9 %collective-permute-start = (bf16[2,128,512]{2,1,0:T(8,128)(2,1)S(1)}, bf16[2,128,512]{2,1,0:T(8,128)(2,1)S(1)}, u32[]{:S(2)}, u32[]{:S(2)}) collective-permute-start(bf16[2,128,512]{2,1,0:T(8,128)(2,1)S(1)} %get-tuple-element.54), channel_id=1, source_target_pairs={{0,4},{8,16},{16,8},{24,28},{28,24},{20,12},{12,20},{4,0},{1,5},{9... | collective-permute-start | bytes 786440 | tf_op jit(solution)/shard_map/ppermute | solution.py:33
  6.2 2.2 %copy-start = (bf16[1024,2,1024]{2,1,0:T(2,128)(2,1)S(1)}, bf16[1024,2,1024]{2,1,0:T(2,128)(2,1)}, u32[]{:S(2)}) copy-start(bf16[1024,2,1024]{2,1,0:T(2,128)(2,1)} %amplitudes_ref.1) | copy-start | bytes 12582916
  8.4 0.7 %copy-start.2 = (s32[1024,2]{0,1:T(2,128)S(1)}, s32[1024,2]{0,1:T(2,128)}, u32[]{:S(2)}) copy-start(s32[1024,2]{0,1:T(2,128)} %param.7) | copy-start | bytes 24580
  9.1 26.5 %copy-start.1 = (bf16[2,128,1024]{2,1,0:T(8,128)(2,1)S(1)}, bf16[2,128,1024]{2,1,0:T(8,128)(2,1)}, u32[]{:S(2)}) copy-start(bf16[2,128,1024]{2,1,0:T(8,128)(2,1)} %refs_0_.1) | copy-start | bytes 1572868
  17.5 9.2 %collective-permute-start.6 = (bf16[2,128,512]{2,1,0:T(8,128)(2,1)S(1)}, bf16[2,128,512]{2,1,0:T(8,128)(2,1)S(1)}, u32[]{:S(2)}, u32[]{:S(2)}) collective-permute-start(bf16[2,128,512]{2,1,0:T(8,128)(2,1)S(1)} %collective-permute-done.refs_2_), channel_id=1, source_target_pairs={{0,8},{8,0},{16,24},{24,16},{28,20},{20,28},{12,4},{4,12},{1,9},{9... | collective-permute-start | bytes 786440 | tf_op jit(solution)/shard_map/ppermute | solution.py:33
  19.0 9.3 %collective-permute-start.4 = (bf16[2,128,512]{2,1,0:T(8,128)(2,1)S(1)}, bf16[2,128,512]{2,1,0:T(8,128)(2,1)S(1)}, u32[]{:S(2)}, u32[]{:S(2)}) collective-permute-start(bf16[2,128,512]{2,1,0:T(8,128)(2,1)S(1)} %get-tuple-element.55), channel_id=1, source_target_pairs={{0,4},{8,16},{16,8},{24,28},{28,24},{20,12},{12,20},{4,0},{1,5},{9... | collective-permute-start | bytes 786440 | tf_op jit(solution)/shard_map/ppermute | solution.py:33
  20.6 11.8 %collective-permute-start.9 = (bf16[2,128,512]{2,1,0:T(8,128)(2,1)S(1)}, bf16[2,128,512]{2,1,0:T(8,128)(2,1)S(1)}, u32[]{:S(2)}, u32[]{:S(2)}) collective-permute-start(bf16[2,128,512]{2,1,0:T(8,128)(2,1)S(1)} %collective-permute-done.8.refs_3_), channel_id=1, source_target_pairs={{0,8},{8,0},{16,24},{24,16},{28,20},{20,28},{12,4},{4,12},{1,9},{9... | collective-permute-start | bytes 786440 | tf_op jit(solution)/shard_map/ppermute | solution.py:33
  21.3 12.7 %collective-permute-start.2 = (bf16[2,128,512]{2,1,0:T(8,128)(2,1)S(1)}, bf16[2,128,512]{2,1,0:T(8,128)(2,1)S(1)}, u32[]{:S(2)}, u32[]{:S(2)}) collective-permute-start(bf16[2,128,512]{2,1,0:T(8,128)(2,1)S(1)} %get-tuple-element.56), channel_id=1, source_target_pairs={{0,4},{8,16},{16,8},{24,28},{28,24},{20,12},{12,20},{4,0},{1,5},{9... | collective-permute-start | bytes 786440 | tf_op jit(solution)/shard_map/ppermute | solution.py:33
  26.8 12.8 %collective-permute-start.7 = (bf16[2,128,512]{2,1,0:T(8,128)(2,1)S(1)}, bf16[2,128,512]{2,1,0:T(8,128)(2,1)S(1)}, u32[]{:S(2)}, u32[]{:S(2)}) collective-permute-start(bf16[2,128,512]{2,1,0:T(8,128)(2,1)S(1)} %collective-permute-done.6.refs_4_), channel_id=1, source_target_pairs={{0,4},{8,16},{16,8},{24,28},{28,24},{20,12},{12,20},{4,0},{1,5},{9... | collective-permute-start | bytes 786440 | tf_op jit(solution)/shard_map/ppermute | solution.py:33
  28.3 11.2 %collective-permute-start.5 = (bf16[2,128,512]{2,1,0:T(8,128)(2,1)S(1)}, bf16[2,128,512]{2,1,0:T(8,128)(2,1)S(1)}, u32[]{:S(2)}, u32[]{:S(2)}) collective-permute-start(bf16[2,128,512]{2,1,0:T(8,128)(2,1)S(1)} %collective-permute-done.4.refs_6_), channel_id=1, source_target_pairs={{0,8},{8,0},{16,24},{24,16},{28,20},{20,28},{12,4},{4,12},{1,9},{9... | collective-permute-start | bytes 786440 | tf_op jit(solution)/shard_map/ppermute | solution.py:33
  32.4 18.5 %collective-permute-start.11 = (bf16[2,128,512]{2,1,0:T(8,128)(2,1)S(1)}, bf16[2,128,512]{2,1,0:T(8,128)(2,1)S(1)}, u32[]{:S(2)}, u32[]{:S(2)}) collective-permute-start(bf16[2,128,512]{2,1,0:T(8,128)(2,1)S(1)} %collective-permute-done.9.refs_5_), channel_id=1, source_target_pairs={{0,4},{8,16},{16,8},{24,28},{28,24},{20,12},{12,20},{4,0},{1,5},{9... | collective-permute-start | bytes 786440 | tf_op jit(solution)/shard_map/ppermute | solution.py:33
  34.0 9.7 %collective-permute-start.3 = (bf16[2,128,512]{2,1,0:T(8,128)(2,1)S(1)}, bf16[2,128,512]{2,1,0:T(8,128)(2,1)S(1)}, u32[]{:S(2)}, u32[]{:S(2)}) collective-permute-start(bf16[2,128,512]{2,1,0:T(8,128)(2,1)S(1)} %collective-permute-done.2.refs_7_), channel_id=1, source_target_pairs={{0,8},{8,0},{16,24},{24,16},{28,20},{20,28},{12,4},{4,12},{1,9},{9... | collective-permute-start | bytes 786440 | tf_op jit(solution)/shard_map/ppermute | solution.py:33
  39.6 7.3 %collective-permute-start.12 = (bf16[2,128,512]{2,1,0:T(8,128)(2,1)S(1)}, bf16[2,128,512]{2,1,0:T(8,128)(2,1)S(1)}, u32[]{:S(2)}, u32[]{:S(2)}) collective-permute-start(bf16[2,128,512]{2,1,0:T(8,128)(2,1)S(1)} %collective-permute-done.7.refs_1_), channel_id=1, source_target_pairs={{0,8},{8,0},{16,24},{24,16},{28,20},{20,28},{12,4},{4,12},{1,9},{9... | collective-permute-start | bytes 786440 | tf_op jit(solution)/shard_map/ppermute | solution.py:33
  43.6 8.7 %collective-permute-start.10 = (bf16[2,128,512]{2,1,0:T(8,128)(2,1)S(1)}, bf16[2,128,512]{2,1,0:T(8,128)(2,1)S(1)}, u32[]{:S(2)}, u32[]{:S(2)}) collective-permute-start(bf16[2,128,512]{2,1,0:T(8,128)(2,1)S(1)} %collective-permute-done.3.refs_0_), channel_id=1, source_target_pairs={{0,4},{8,16},{16,8},{24,28},{28,24},{20,12},{12,20},{4,0},{1,5},{9... | collective-permute-start | bytes 786440 | tf_op jit(solution)/shard_map/ppermute | solution.py:33
  47.6 1.7 %collective-permute-start.13 = (bf16[128,512]{1,0:T(8,128)(2,1)S(1)}, bf16[128,512]{1,0:T(8,128)(2,1)S(1)}, u32[]{:S(2)}, u32[]{:S(2)}) collective-permute-start(bf16[128,512]{1,0:T(8,128)(2,1)S(1)} %get-tuple-element.38), channel_id=1, source_target_pairs={{0,1},{1,0},{2,3},{3,2},{4,5},{5,4},{6,7},{7,6},{8,9},{9,8},{10,11... | collective-permute-start | bytes 393224 | tf_op jit(solution)/shard_map/ppermute | solution.py:37
  47.7 1.6 %collective-permute-start.14 = (bf16[128,512]{1,0:T(8,128)(2,1)S(1)}, bf16[128,512]{1,0:T(8,128)(2,1)S(1)}, u32[]{:S(2)}, u32[]{:S(2)}) collective-permute-start(bf16[128,512]{1,0:T(8,128)(2,1)S(1)} %get-tuple-element.39), channel_id=1, source_target_pairs={{0,1},{1,0},{2,3},{3,2},{4,5},{5,4},{6,7},{7,6},{8,9},{9,8},{10,11... | collective-permute-start | bytes 393224 | tf_op jit(solution)/shard_map/ppermute | solution.py:37
  49.1 6.2 %collective-permute-start.19 = (bf16[256,512]{1,0:T(8,128)(2,1)S(1)}, bf16[256,512]{1,0:T(8,128)(2,1)S(1)}, u32[]{:S(2)}, u32[]{:S(2)}) collective-permute-start(bf16[256,512]{1,0:T(8,128)(2,1)S(1)} %get-tuple-element.47), channel_id=1, source_target_pairs={{0,1},{1,0},{2,3},{3,2},{4,5},{5,4},{6,7},{7,6},{8,9},{9,8},{10,11... | collective-permute-start | bytes 786440 | tf_op jit(solution)/shard_map/ppermute | solution.py:37
  49.3 9.0 %collective-permute-start.20 = (bf16[256,512]{1,0:T(8,128)(2,1)S(1)}, bf16[256,512]{1,0:T(8,128)(2,1)S(1)}, u32[]{:S(2)}, u32[]{:S(2)}) collective-permute-start(bf16[256,512]{1,0:T(8,128)(2,1)S(1)} %shard_map.69), channel_id=1, source_target_pairs={{0,2},{2,0},{1,3},{3,1},{4,6},{6,4},{5,7},{7,5},{8,10},{10,8},{9,1... | collective-permute-start | bytes 786440 | tf_op jit(solution)/shard_map/ppermute | solution.py:37
  53.1 5.3 %copy-start.3 = (f32[1024]{0:T(1024)S(1)}, f32[1024]{0:T(1024)}, u32[]{:S(2)}) copy-start(f32[1024]{0:T(1024)} %param.10) | copy-start | bytes 12292
  53.1 5.3 %copy-start.4 = (f32[256]{0:T(256)S(1)}, f32[256]{0:T(256)}, u32[]{:S(2)}) copy-start(f32[256]{0:T(256)} %param.9) | copy-start | bytes 3076
  53.1 1.5 %collective-permute-start.16 = (bf16[128,512]{1,0:T(8,128)(2,1)S(1)}, bf16[128,512]{1,0:T(8,128)(2,1)S(1)}, u32[]{:S(2)}, u32[]{:S(2)}) collective-permute-start(bf16[128,512]{1,0:T(8,128)(2,1)S(1)} %get-tuple-element.44), channel_id=1, source_target_pairs={{0,1},{1,0},{2,3},{3,2},{4,5},{5,4},{6,7},{7,6},{8,9},{9,8},{10,11... | collective-permute-start | bytes 393224 | tf_op jit(solution)/shard_map/ppermute | solution.py:37
  53.3 1.4 %collective-permute-start.17 = (bf16[128,512]{1,0:T(8,128)(2,1)S(1)}, bf16[128,512]{1,0:T(8,128)(2,1)S(1)}, u32[]{:S(2)}, u32[]{:S(2)}) collective-permute-start(bf16[128,512]{1,0:T(8,128)(2,1)S(1)} %get-tuple-element.45), channel_id=1, source_target_pairs={{0,1},{1,0},{2,3},{3,2},{4,5},{5,4},{6,7},{7,6},{8,9},{9,8},{10,11... | collective-permute-start | bytes 393224 | tf_op jit(solution)/shard_map/ppermute | solution.py:37
  54.8 8.9 %collective-permute-start.18 = (bf16[256,512]{1,0:T(8,128)(2,1)S(1)}, bf16[256,512]{1,0:T(8,128)(2,1)S(1)}, u32[]{:S(2)}, u32[]{:S(2)}) collective-permute-start(bf16[256,512]{1,0:T(8,128)(2,1)S(1)} %shard_map.73), channel_id=1, source_target_pairs={{0,2},{2,0},{1,3},{3,1},{4,6},{6,4},{5,7},{7,5},{8,10},{10,8},{9,1... | collective-permute-start | bytes 786440 | tf_op jit(solution)/shard_map/ppermute | solution.py:37
  55.3 8.4 %collective-permute-start.15 = (bf16[256,512]{1,0:T(8,128)(2,1)S(1)}, bf16[256,512]{1,0:T(8,128)(2,1)S(1)}, u32[]{:S(2)}, u32[]{:S(2)}) collective-permute-start(bf16[256,512]{1,0:T(8,128)(2,1)S(1)} %get-tuple-element.42), channel_id=1, source_target_pairs={{0,1},{1,0},{2,3},{3,2},{4,5},{5,4},{6,7},{7,6},{8,9},{9,8},{10,11... | collective-permute-start | bytes 786440 | tf_op jit(solution)/shard_map/ppermute | solution.py:37

commit v9 on v7

--- a/solution.py
+++ b/solution.py
@@ -122,6 +122,30 @@
         compiler_params=pltpu.CompilerParams(vmem_limit_bytes=8 * 2**20),
         cost_estimate=pl.CostEstimate(flops=10**8, bytes_accessed=10**6, transcendentals=0),
     )(kept, got, from_y, inverse, left)
+
+
+def halves(integrals):
+    tiles, depth, columns = integrals.shape
+    half = columns // 2
+
+    def body(in_ref, a_ref, b_ref, sem):
+        copies = [
+            pltpu.make_async_copy(in_ref.at[:, :, :half], a_ref, sem.at[0]),
+            pltpu.make_async_copy(in_ref.at[:, :, half:], b_ref, sem.at[1]),
+        ]
+        for copy in copies:
+            copy.start()
+        for copy in copies:
+            copy.wait()
+
+    return pl.pallas_call(
+        body,
+        in_specs=[pl.BlockSpec(memory_space=pl.ANY)],
+        out_specs=[pl.BlockSpec(memory_space=pltpu.VMEM)] * 2,
+        out_shape=[jax.ShapeDtypeStruct((tiles, depth, half), BF16)] * 2,
+        scratch_shapes=[pltpu.SemaphoreType.DMA((2,))],
+        compiler_params=pltpu.CompilerParams(vmem_limit_bytes=4 * 2**20),
+    )(integrals)
 
 
 def tie(*values):
@@ -209,7 +233,8 @@
         return v[:, :, span[0] : span[1]]
 
     e1 = over_pair(integrals, EVEN)
-    o1a, o1b = over_pair(part(integrals, span_a), ODD), over_pair(part(integrals, span_b), ODD)
+    own_a, own_b = halves(integrals)
+    o1a, o1b = over_pair(own_a, ODD), over_pair(own_b, ODD)
     a = arranged(amplitudes, tile_mask)
     o1a, a, table = tie(o1a, a, table)
     e2a, o2a = over_pair(o1a, EVEN), over_pair(part(e1, span_a), ODD)

time: 61.3 us -> 61.3 us (level)
    unnamed x10 -> x12, local copies, waits for them, and re-layouts: 2.9 us -> 3.97 us
    slice x2 -> x1, local copies, waits for them, and re-layouts: 1.1 us -> 0.04 us  [part(): return v[:, :, span[0]:span[1]]]
  transfers between devices with their start and end apart: 21 -> 21, of which waited for: 10 -> 10; matrix products, arithmetic and copies ran while one was open for 3% -> 1% of each run, Pallas kernels for 21% -> 21%
where the time goes in v9:
time: 61.3 us; the launch traced here: 61 us
  starting transfers between devices  25.3 us (41%)
  waiting for transfers between devices  17.3 us (28%)
  Pallas kernels  13.5 us (22%)
  local copies, waits for them, and re-layouts  4.7 us (8%)
    ppermute x13, starting transfers between devices, over_pair(): return lax.ppermute(value, 'pair', hops)  21.8 us
    pallas_call x8, Pallas kernels, products(): pl.pallas_call(body, in_specs=[smem] + [vmem] * len(operands), out_specs=...  10.2 us
    ppermute x13, waiting for transfers between devices, over_pair(): return lax.ppermute(value, 'pair', hops)  9.18 us
    ppermute x8, waiting for transfers between devices, over_virt(): return lax.ppermute(value, 'virt', hops)  8.08 us
    unnamed x12, local copies, waits for them, and re-layouts  3.97 us
    ppermute x8, starting transfers between devices, over_virt(): return lax.ppermute(value, 'virt', hops)  3.53 us
    pallas_call x1, Pallas kernels, arranged(): pl.pallas_call(body, in_specs=[vmem, vmem], out_specs=vmem, out_shape=jax...  1.84 us
  transfers between devices with their start and end apart: 21, of which 10 were waited for; matrix products, arithmetic and copies ran while one was open for 1% of the time, Pallas kernels for 21%

profile of v9, /device:TPU:0, one launch (start us, length us, event | category | flops | bytes accessed | tf_op | source)
XLA Modules:
  0.0 61.0 jit_solution(11369804196022458310)
XLA Ops:
  0.0 3.0 %collective-permute-start.1 = (bf16[2,128,1024]{2,1,0:T(8,128)(2,1)}, bf16[2,128,1024]{2,1,0:T(8,128)(2,1)S(1)}, u32[]{:S(2)}, u32[]{:S(2)}) collective-permute-start(bf16[2,128,1024]{2,1,0:T(8,128)(2,1)} %refs_0_.1), channel_id=1, source_target_pairs={{0,8},{8,0},{16,24},{24,16},{28,20},{20,28},{12,4},{4,12},{1,9},{9... | collective-permute-start | bytes 1572872 | tf_op jit(solution)/shard_map/ppermute | solution.py:33
  3.0 0.0 copy-start.1
  3.0 1.1 %copy-done.1 = bf16[2,128,1024]{2,1,0:T(8,128)(2,1)S(1)} copy-done((bf16[2,128,1024]{2,1,0:T(8,128)(2,1)S(1)}, bf16[2,128,1024]{2,1,0:T(8,128)(2,1)}, u32[]{:S(2)}) %copy-start.1) | copy-done | bytes 524312
  4.1 0.1 shard_map.64
  4.2 1.6 %collective-permute-start = (bf16[2,128,512]{2,1,0:T(8,128)(2,1)S(1)}, bf16[2,128,512]{2,1,0:T(8,128)(2,1)S(1)}, u32[]{:S(2)}, u32[]{:S(2)}) collective-permute-start(bf16[2,128,512]{2,1,0:T(8,128)(2,1)S(1)} %get-tuple-element.34), channel_id=1, source_target_pairs={{0,4},{8,16},{16,8},{24,28},{28,24},{20,12},{12,20},{4,0},{1,5},{9... | collective-permute-start | bytes 786440 | tf_op jit(solution)/shard_map/ppermute | solution.py:33
  5.7 0.5 collective-permute-start.6
  6.3 0.7 %dynamic-slice_bitcast_fusion.table_ref = s32[12]{0:T(128)S(1)} fusion(s32[32,12]{1,0:T(8,128)} %constant.19.clone, s32[]{:T(128)S(6)} %select_n.4), kind=kLoop, calls=%fused_computation | loop fusion | bytes 100 | tf_op jit(solution)/shard_map/jit(dynamic_index_in_dim)/squeeze | solution.py:224
  7.0 2.2 %copy-done = bf16[1024,2,1024]{2,1,0:T(2,128)(2,1)S(1)} copy-done((bf16[1024,2,1024]{2,1,0:T(2,128)(2,1)S(1)}, bf16[1024,2,1024]{2,1,0:T(2,128)(2,1)}, u32[]{:S(2)}) %copy-start) | copy-done | bytes 4194328
  9.1 0.7 %copy-done.3 = s32[1024,2]{0,1:T(2,128)S(1)} copy-done((s32[1024,2]{0,1:T(2,128)S(1)}, s32[1024,2]{0,1:T(2,128)}, u32[]{:S(2)}) %copy-start.3) | copy-done | bytes 8216
  9.8 1.8 %shard_map.65.a_ref = bf16[2,1024,1024]{2,1,0:T(8,128)(2,1)S(1)} custom-call(bf16[1024,2,1024]{2,1,0:T(2,128)(2,1)S(1)} %copy-done, s32[2,1024]{1,0:T(2,128)S(1)} %bitcast.5), custom_call_target="tpu_custom_call" | custom-call | flops 2147483648 | bytes 8388608 | tf_op jit(solution)/shard_map/pallas_call | solution.py:57
  11.7 1.8 %collective-permute-done.refs_2_ = bf16[2,128,512]{2,1,0:T(8,128)(2,1)S(1)} collective-permute-done((bf16[2,128,512]{2,1,0:T(8,128)(2,1)S(1)}, bf16[2,128,512]{2,1,0:T(8,128)(2,1)S(1)}, u32[]{:S(2)}, u32[]{:S(2)}) %collective-permute-start) | collective-permute-done | bytes 262176 | tf_op jit(solution)/shard_map/ppermute | solution.py:33
  13.5 1.1 %collective-permute-start.5 = (bf16[2,128,512]{2,1,0:T(8,128)(2,1)S(1)}, bf16[2,128,512]{2,1,0:T(8,128)(2,1)S(1)}, u32[]{:S(2)}, u32[]{:S(2)}) collective-permute-start(bf16[2,128,512]{2,1,0:T(8,128)(2,1)S(1)} %collective-permute-done.refs_2_), channel_id=1, source_target_pairs={{0,8},{8,0},{16,24},{24,16},{28,20},{20,28},{12,4},{4,12},{1,9},{9... | collective-permute-start | bytes 786440 | tf_op jit(solution)/shard_map/ppermute | solution.py:33
  14.6 1.4 %collective-permute-done.1.refs_1_ = bf16[2,128,1024]{2,1,0:T(8,128)(2,1)S(1)} collective-permute-done((bf16[2,128,1024]{2,1,0:T(8,128)(2,1)}, bf16[2,128,1024]{2,1,0:T(8,128)(2,1)S(1)}, u32[]{:S(2)}, u32[]{:S(2)}) %collective-permute-start.1) | collective-permute-done | bytes 524320 | tf_op jit(solution)/shard_map/ppermute | solution.py:33
  16.0 2.0 %collective-permute-start.4 = (bf16[2,128,512]{2,1,0:T(8,128)(2,1)S(1)}, bf16[2,128,512]{2,1,0:T(8,128)(2,1)S(1)}, u32[]{:S(2)}, u32[]{:S(2)}) collective-permute-start(bf16[2,128,512]{2,1,0:T(8,128)(2,1)S(1)} %get-tuple-element.63), channel_id=1, source_target_pairs={{0,4},{8,16},{16,8},{24,28},{28,24},{20,12},{12,20},{4,0},{1,5},{9... | collective-permute-start | bytes 786440 | tf_op jit(solution)/shard_map/ppermute | solution.py:33
  18.1 0.0 collective-permute-done.6.refs_3_
  18.1 1.7 %collective-permute-start.9 = (bf16[2,128,512]{2,1,0:T(8,128)(2,1)S(1)}, bf16[2,128,512]{2,1,0:T(8,128)(2,1)S(1)}, u32[]{:S(2)}, u32[]{:S(2)}) collective-permute-start(bf16[2,128,512]{2,1,0:T(8,128)(2,1)S(1)} %collective-permute-done.6.refs_3_), channel_id=1, source_target_pairs={{0,8},{8,0},{16,24},{24,16},{28,20},{20,28},{12,4},{4,12},{1,9},{9... | collective-permute-start | bytes 786440 | tf_op jit(solution)/shard_map/ppermute | solution.py:33
  19.7 1.5 %collective-permute-start.2 = (bf16[2,128,512]{2,1,0:T(8,128)(2,1)S(1)}, bf16[2,128,512]{2,1,0:T(8,128)(2,1)S(1)}, u32[]{:S(2)}, u32[]{:S(2)}) collective-permute-start(bf16[2,128,512]{2,1,0:T(8,128)(2,1)S(1)} %get-tuple-element.64), channel_id=1, source_target_pairs={{0,4},{8,16},{16,8},{24,28},{28,24},{20,12},{12,20},{4,0},{1,5},{9... | collective-permute-start | bytes 786440 | tf_op jit(solution)/shard_map/ppermute | solution.py:33
  21.2 0.0 copy-done.2
  21.2 2.4 %shard_map.66.refs_4_ = f32[4,256,1024]{2,1,0:T(8,128)S(1)} custom-call(s32[12]{0:T(128)S(1)} %dynamic-slice_bitcast_fusion.table_ref, bf16[2,1024,1024]{2,1,0:T(8,128)(2,1)S(1)} %shard_map.65.a_ref, bf16[2,128,1024]{2,1,0:T(8,128)(2,1)S(1)} %copy-done.2, bf16[2,128,1024]{2,1,0:T(8,128)(2,1)S(1)} %collective-permute-done.1.refs_1_, ...), custom_call_target="tpu_custom_call" | custom-call | flops 1610612736 | bytes 6291456 | tf_op jit(solution)/shard_map/pallas_call | solution.py:201
  23.6 0.0 collective-permute-done.5.refs_0_
  23.6 1.7 %collective-permute-done.4.refs_2_ = bf16[2,128,512]{2,1,0:T(8,128)(2,1)S(1)} collective-permute-done((bf16[2,128,512]{2,1,0:T(8,128)(2,1)S(1)}, bf16[2,128,512]{2,1,0:T(8,128)(2,1)S(1)}, u32[]{:S(2)}, u32[]{:S(2)}) %collective-permute-start.4) | collective-permute-done | bytes 262176 | tf_op jit(solution)/shard_map/ppermute | solution.py:33
  25.3 2.1 %collective-permute-start.7 = (bf16[2,128,512]{2,1,0:T(8,128)(2,1)S(1)}, bf16[2,128,512]{2,1,0:T(8,128)(2,1)S(1)}, u32[]{:S(2)}, u32[]{:S(2)}) collective-permute-start(bf16[2,128,512]{2,1,0:T(8,128)(2,1)S(1)} %collective-permute-done.4.refs_2_), channel_id=1, source_target_pairs={{0,8},{8,0},{16,24},{24,16},{28,20},{20,28},{12,4},{4,12},{1,9},{9... | collective-permute-start | bytes 786440 | tf_op jit(solution)/shard_map/ppermute | solution.py:33
  27.4 1.5 %collective-permute-start.8 = (bf16[2,128,512]{2,1,0:T(8,128)(2,1)S(1)}, bf16[2,128,512]{2,1,0:T(8,128)(2,1)S(1)}, u32[]{:S(2)}, u32[]{:S(2)}) collective-permute-start(bf16[2,128,512]{2,1,0:T(8,128)(2,1)S(1)} %collective-permute-done.5.refs_0_), channel_id=1, source_target_pairs={{0,4},{8,16},{16,8},{24,28},{28,24},{20,12},{12,20},{4,0},{1,5},{9... | collective-permute-start | bytes 786440 | tf_op jit(solution)/shard_map/ppermute | solution.py:33
  28.9 0.0 collective-permute-done.9.refs_1_
  28.9 0.9 %collective-permute-start.11 = (bf16[2,128,512]{2,1,0:T(8,128)(2,1)S(1)}, bf16[2,128,512]{2,1,0:T(8,128)(2,1)S(1)}, u32[]{:S(2)}, u32[]{:S(2)}) collective-permute-start(bf16[2,128,512]{2,1,0:T(8,128)(2,1)S(1)} %collective-permute-done.9.refs_1_), channel_id=1, source_target_pairs={{0,4},{8,16},{16,8},{24,28},{28,24},{20,12},{12,20},{4,0},{1,5},{9... | collective-permute-start | bytes 786440 | tf_op jit(solution)/shard_map/ppermute | solution.py:33
  29.8 1.1 %collective-permute-done.2.refs_3_ = bf16[2,128,512]{2,1,0:T(8,128)(2,1)S(1)} collective-permute-done((bf16[2,128,512]{2,1,0:T(8,128)(2,1)S(1)}, bf16[2,128,512]{2,1,0:T(8,128)(2,1)S(1)}, u32[]{:S(2)}, u32[]{:S(2)}) %collective-permute-start.2) | collective-permute-done | bytes 262176 | tf_op jit(solution)/shard_map/ppermute | solution.py:33
  31.0 2.1 %collective-permute-start.3 = (bf16[2,128,512]{2,1,0:T(8,128)(2,1)S(1)}, bf16[2,128,512]{2,1,0:T(8,128)(2,1)S(1)}, u32[]{:S(2)}, u32[]{:S(2)}) collective-permute-start(bf16[2,128,512]{2,1,0:T(8,128)(2,1)S(1)} %collective-permute-done.2.refs_3_), channel_id=1, source_target_pairs={{0,8},{8,0},{16,24},{24,16},{28,20},{20,28},{12,4},{4,12},{1,9},{9... | collective-permute-start | bytes 786440 | tf_op jit(solution)/shard_map/ppermute | solution.py:33
  33.0 1.9 %shard_map.67.refs_2_ = f32[4,256,1024]{2,1,0:T(8,128)S(1)} custom-call(s32[12]{0:T(128)S(1)} %dynamic-slice_bitcast_fusion.table_ref, bf16[2,1024,1024]{2,1,0:T(8,128)(2,1)S(1)} %shard_map.65.a_ref, bf16[2,128,512]{2,1,0:T(8,128)(2,1)S(1)} %collective-permute-done.5.refs_0_, bf16[2,128,512]{2,1,0:T(8,128)(2,1)S(1)} %collective-permute-done.9.refs_1_, ...), custom_call_target="tpu_custom_call" | custom-call | flops 1073741824 | bytes 6291456 | tf_op jit(solution)/shard_map/pallas_call | solution.py:201
  34.9 0.0 collective-permute-done.7.refs_0_
  34.9 1.7 %collective-permute-done.8.refs_1_ = bf16[2,128,512]{2,1,0:T(8,128)(2,1)S(1)} collective-permute-done((bf16[2,128,512]{2,1,0:T(8,128)(2,1)S(1)}, bf16[2,128,512]{2,1,0:T(8,128)(2,1)S(1)}, u32[]{:S(2)}, u32[]{:S(2)}) %collective-permute-start.8) | collective-permute-done | bytes 262176 | tf_op jit(solution)/shard_map/ppermute | solution.py:33
  36.7 2.0 %collective-permute-start.12 = (bf16[2,128,512]{2,1,0:T(8,128)(2,1)S(1)}, bf16[2,128,512]{2,1,0:T(8,128)(2,1)S(1)}, u32[]{:S(2)}, u32[]{:S(2)}) collective-permute-start(bf16[2,128,512]{2,1,0:T(8,128)(2,1)S(1)} %collective-permute-done.8.refs_1_), channel_id=1, source_target_pairs={{0,8},{8,0},{16,24},{24,16},{28,20},{20,28},{12,4},{4,12},{1,9},{9... | collective-permute-start | bytes 786440 | tf_op jit(solution)/shard_map/ppermute | solution.py:33
  38.6 1.3 %shard_map.68.refs_1_ = f32[4,256,512]{2,1,0:T(8,128)S(1)} custom-call(s32[12]{0:T(128)S(1)} %dynamic-slice_bitcast_fusion.table_ref, bf16[2,1024,1024]{2,1,0:T(8,128)(2,1)S(1)} %shard_map.65.a_ref, bf16[2,128,512]{2,1,0:T(8,128)(2,1)S(1)} %collective-permute-done.7.refs_0_, bf16[2,128,512]{2,1,0:T(8,128)(2,1)S(1)} %collective-permute-done.8.refs_1_, ...), custom_call_target="tpu_custom_call" | custom-call | flops 10737418240 | bytes 4718592 | tf_op jit(solution)/shard_map/pallas_call | solution.py:201
  40.0 0.2 collective-permute-done.3.refs_0_
  40.2 1.9 %collective-permute-start.10 = (bf16[2,128,512]{2,1,0:T(8,128)(2,1)S(1)}, bf16[2,128,512]{2,1,0:T(8,128)(2,1)S(1)}, u32[]{:S(2)}, u32[]{:S(2)}) collective-permute-start(bf16[2,128,512]{2,1,0:T(8,128)(2,1)S(1)} %collective-permute-done.3.refs_0_), channel_id=1, source_target_pairs={{0,4},{8,16},{16,8},{24,28},{28,24},{20,12},{12,20},{4,0},{1,5},{9... | collective-permute-start | bytes 786440 | tf_op jit(solution)/shard_map/ppermute | solution.py:33
  42.1 1.1 %collective-permute-done.12.refs_0_ = bf16[2,128,512]{2,1,0:T(8,128)(2,1)S(1)} collective-permute-done((bf16[2,128,512]{2,1,0:T(8,128)(2,1)S(1)}, bf16[2,128,512]{2,1,0:T(8,128)(2,1)S(1)}, u32[]{:S(2)}, u32[]{:S(2)}) %collective-permute-start.12) | collective-permute-done | bytes 262176 | tf_op jit(solution)/shard_map/ppermute | solution.py:33
  43.2 0.8 %shard_map.70 = (bf16[128,512]{1,0:T(8,128)(2,1)S(1)}, bf16[128,512]{1,0:T(8,128)(2,1)S(1)}) custom-call(s32[12]{0:T(128)S(1)} %dynamic-slice_bitcast_fusion.table_ref, bf16[2,1024,1024]{2,1,0:T(8,128)(2,1)S(1)} %shard_map.65.a_ref, bf16[2,128,512]{2,1,0:T(8,128)(2,1)S(1)} %collective-permute-done.12.refs_0_, f32[4,256,512]{2,1,0:T(8,128)S(1)} %shard_map.68.refs_1_), custom_call_target="tpu_custom_call" | custom-call | tf_op jit(solution)/shard_map/pallas_call | solution.py:201
  44.0 0.1 collective-permute-start.13
  44.1 0.5 collective-permute-start.14
  44.6 0.9 %shard_map.69 = (bf16[256,512]{1,0:T(8,128)(2,1)S(1)}, f32[256,512]{1,0:T(8,128)S(1)}, f32[256,512]{1,0:T(8,128)S(1)}) custom-call(s32[12]{0:T(128)S(1)} %dynamic-slice_bitcast_fusion.table_ref, bf16[2,1024,1024]{2,1,0:T(8,128)(2,1)S(1)} %shard_map.65.a_ref, bf16[2,128,512]{2,1,0:T(8,128)(2,1)S(1)} %collective-permute-done.12.refs_0_, ...), custom_call_target="tpu_custom_call" | custom-call | tf_op jit(solution)/shard_map/pallas_call | solution.py:201
  45.5 0.1 collective-permute-start.19
  45.7 0.0 collective-permute-done.13.refs_0_
  45.7 0.0 collective-permute-done.14.refs_1_
  45.7 1.8 %collective-permute-start.20 = (bf16[256,512]{1,0:T(8,128)(2,1)S(1)}, bf16[256,512]{1,0:T(8,128)(2,1)S(1)}, u32[]{:S(2)}, u32[]{:S(2)}) collective-permute-start(bf16[256,512]{1,0:T(8,128)(2,1)S(1)} %shard_map.71), channel_id=1, source_target_pairs={{0,2},{2,0},{1,3},{3,1},{4,6},{6,4},{5,7},{7,5},{8,10},{10,8},{9,1... | collective-permute-start | bytes 786440 | tf_op jit(solution)/shard_map/ppermute | solution.py:37
  47.5 0.0 collective-permute-done.11.refs_1_
  47.5 1.3 %shard_map.72.refs_1_ = f32[4,256,512]{2,1,0:T(8,128)S(1)} custom-call(s32[12]{0:T(128)S(1)} %dynamic-slice_bitcast_fusion.table_ref, bf16[2,1024,1024]{2,1,0:T(8,128)(2,1)S(1)} %shard_map.65.a_ref, bf16[2,128,512]{2,1,0:T(8,128)(2,1)S(1)} %collective-permute-done.3.refs_0_, bf16[2,128,512]{2,1,0:T(8,128)(2,1)S(1)} %collective-permute-done.11.refs_1_, ...), custom_call_target="tpu_custom_call" | custom-call | flops 536870912 | bytes 4718592 | tf_op jit(solution)/shard_map/pallas_call | solution.py:201
  48.8 0.0 collective-permute-done.10.refs_0_
  48.8 0.8 %shard_map.74 = (bf16[128,512]{1,0:T(8,128)(2,1)S(1)}, bf16[128,512]{1,0:T(8,128)(2,1)S(1)}) custom-call(s32[12]{0:T(128)S(1)} %dynamic-slice_bitcast_fusion.table_ref, bf16[2,1024,1024]{2,1,0:T(8,128)(2,1)S(1)} %shard_map.65.a_ref, bf16[2,128,512]{2,1,0:T(8,128)(2,1)S(1)} %collective-permute-done.10.refs_0_, f32[4,256,512]{2,1,0:T(8,128)S(1)} %shard_map.72.refs_1_), custom_call_target="tpu_custom_call" | custom-call | flops 1342177280 | bytes 4456448 | tf_op jit(solution)/shard_map/pallas_call | solution.py:201
  49.6 0.0 copy-start.4
  49.6 0.0 copy-start.5
  49.6 0.2 collective-permute-start.16
  49.8 0.3 collective-permute-start.17
  50.2 0.9 %shard_map.73 = (bf16[256,512]{1,0:T(8,128)(2,1)S(1)}, f32[256,512]{1,0:T(8,128)S(1)}, f32[256,512]{1,0:T(8,128)S(1)}) custom-call(s32[12]{0:T(128)S(1)} %dynamic-slice_bitcast_fusion.table_ref, bf16[2,1024,1024]{2,1,0:T(8,128)(2,1)S(1)} %shard_map.65.a_ref, bf16[2,128,512]{2,1,0:T(8,128)(2,1)S(1)} %collective-permute-done.10.refs_0_, ...), custom_call_target="tpu_custom_call" | custom-call | tf_op jit(solution)/shard_map/pallas_call | solution.py:201
  51.1 0.0 collective-permute-done.16.refs_0_
  51.1 0.1 collective-permute-done.17.refs_1_
  51.3 0.4 collective-permute-start.18
  51.6 0.1 collective-permute-start.15
  51.7 0.0 collective-permute-done.19.got_ref
  51.7 2.8 %collective-permute-done.20.from_y_ref = bf16[256,512]{1,0:T(8,128)(2,1)S(1)} collective-permute-done((bf16[256,512]{1,0:T(8,128)(2,1)S(1)}, bf16[256,512]{1,0:T(8,128)(2,1)S(1)}, u32[]{:S(2)}, u32[]{:S(2)}) %collective-permute-start.20) | collective-permute-done | bytes 262176 | tf_op jit(solution)/shard_map/ppermute | solution.py:37
  54.6 0.0 copy-done.4
  54.6 0.0 copy-done.5
  54.6 0.3 shard_map.76
  54.9 5.1 %collective-permute-done.18.from_y_ref = bf16[256,512]{1,0:T(8,128)(2,1)S(1)} collective-permute-done((bf16[256,512]{1,0:T(8,128)(2,1)S(1)}, bf16[256,512]{1,0:T(8,128)(2,1)S(1)}, u32[]{:S(2)}, u32[]{:S(2)}) %collective-permute-start.18) | collective-permute-done | bytes 262176 | tf_op jit(solution)/shard_map/ppermute | solution.py:37
  60.1 0.0 collective-permute-done.15.got_ref
  60.1 1.0 %shard_map.77 = bf16[256,1024]{1,0:T(8,128)(2,1)} custom-call(f32[256,512]{1,0:T(8,128)S(1)} %get-tuple-element.51.kept_ref, bf16[256,512]{1,0:T(8,128)(2,1)S(1)} %collective-permute-done.15.got_ref, bf16[256,512]{1,0:T(8,128)(2,1)S(1)} %collective-permute-done.18.from_y_ref, f32[256,512]{1,0:T(8,128)S(1)} %get-tuple-element.61.inverse_ref, ...), custom_call_target="tpu_custom_call" | custom-call | flops 100000000 | bytes 1000000 | tf_op jit(solution)/shard_map/pallas_call | solution.py:117
  (6 shorter events, 0.1 us)
Async XLA Ops:
  0.0 16.0 %collective-permute-start.1 = (bf16[2,128,1024]{2,1,0:T(8,128)(2,1)}, bf16[2,128,1024]{2,1,0:T(8,128)(2,1)S(1)}, u32[]{:S(2)}, u32[]{:S(2)}) collective-permute-start(bf16[2,128,1024]{2,1,0:T(8,128)(2,1)} %refs_0_.1), channel_id=1, source_target_pairs={{0,8},{8,0},{16,24},{24,16},{28,20},{20,28},{12,4},{4,12},{1,9},{9... | collective-permute-start | bytes 1572872 | tf_op jit(solution)/shard_map/ppermute | solution.py:33
  3.0 1.1 %copy-start.1 = (bf16[2,128,1024]{2,1,0:T(8,128)(2,1)S(1)}, bf16[2,128,1024]{2,1,0:T(8,128)(2,1)}, u32[]{:S(2)}) copy-start(bf16[2,128,1024]{2,1,0:T(8,128)(2,1)} %refs_0_.1) | copy-start | bytes 1572868
  4.2 9.3 %collective-permute-start = (bf16[2,128,512]{2,1,0:T(8,128)(2,1)S(1)}, bf16[2,128,512]{2,1,0:T(8,128)(2,1)S(1)}, u32[]{:S(2)}, u32[]{:S(2)}) collective-permute-start(bf16[2,128,512]{2,1,0:T(8,128)(2,1)S(1)} %get-tuple-element.34), channel_id=1, source_target_pairs={{0,4},{8,16},{16,8},{24,28},{28,24},{20,12},{12,20},{4,0},{1,5},{9... | collective-permute-start | bytes 786440 | tf_op jit(solution)/shard_map/ppermute | solution.py:33
  5.7 12.4 %collective-permute-start.6 = (bf16[2,128,512]{2,1,0:T(8,128)(2,1)S(1)}, bf16[2,128,512]{2,1,0:T(8,128)(2,1)S(1)}, u32[]{:S(2)}, u32[]{:S(2)}) collective-permute-start(bf16[2,128,512]{2,1,0:T(8,128)(2,1)S(1)} %get-tuple-element.38), channel_id=1, source_target_pairs={{0,4},{8,16},{16,8},{24,28},{28,24},{20,12},{12,20},{4,0},{1,5},{9... | collective-permute-start | bytes 786440 | tf_op jit(solution)/shard_map/ppermute | solution.py:33
  6.9 2.2 %copy-start = (bf16[1024,2,1024]{2,1,0:T(2,128)(2,1)S(1)}, bf16[1024,2,1024]{2,1,0:T(2,128)(2,1)}, u32[]{:S(2)}) copy-start(bf16[1024,2,1024]{2,1,0:T(2,128)(2,1)} %amplitudes_ref.1) | copy-start | bytes 12582916
  9.1 0.7 %copy-start.3 = (s32[1024,2]{0,1:T(2,128)S(1)}, s32[1024,2]{0,1:T(2,128)}, u32[]{:S(2)}) copy-start(s32[1024,2]{0,1:T(2,128)} %param.7) | copy-start | bytes 24580
  9.8 11.4 %copy-start.2 = (bf16[2,128,1024]{2,1,0:T(8,128)(2,1)S(1)}, bf16[2,128,1024]{2,1,0:T(8,128)(2,1)}, u32[]{:S(2)}) copy-start(bf16[2,128,1024]{2,1,0:T(8,128)(2,1)} %refs_0_.1) | copy-start | bytes 1572868
  13.5 10.1 %collective-permute-start.5 = (bf16[2,128,512]{2,1,0:T(8,128)(2,1)S(1)}, bf16[2,128,512]{2,1,0:T(8,128)(2,1)S(1)}, u32[]{:S(2)}, u32[]{:S(2)}) collective-permute-start(bf16[2,128,512]{2,1,0:T(8,128)(2,1)S(1)} %collective-permute-done.refs_2_), channel_id=1, source_target_pairs={{0,8},{8,0},{16,24},{24,16},{28,20},{20,28},{12,4},{4,12},{1,9},{9... | collective-permute-start | bytes 786440 | tf_op jit(solution)/shard_map/ppermute | solution.py:33
  16.0 9.3 %collective-permute-start.4 = (bf16[2,128,512]{2,1,0:T(8,128)(2,1)S(1)}, bf16[2,128,512]{2,1,0:T(8,128)(2,1)S(1)}, u32[]{:S(2)}, u32[]{:S(2)}) collective-permute-start(bf16[2,128,512]{2,1,0:T(8,128)(2,1)S(1)} %get-tuple-element.63), channel_id=1, source_target_pairs={{0,4},{8,16},{16,8},{24,28},{28,24},{20,12},{12,20},{4,0},{1,5},{9... | collective-permute-start | bytes 786440 | tf_op jit(solution)/shard_map/ppermute | solution.py:33
  18.1 10.8 %collective-permute-start.9 = (bf16[2,128,512]{2,1,0:T(8,128)(2,1)S(1)}, bf16[2,128,512]{2,1,0:T(8,128)(2,1)S(1)}, u32[]{:S(2)}, u32[]{:S(2)}) collective-permute-start(bf16[2,128,512]{2,1,0:T(8,128)(2,1)S(1)} %collective-permute-done.6.refs_3_), channel_id=1, source_target_pairs={{0,8},{8,0},{16,24},{24,16},{28,20},{20,28},{12,4},{4,12},{1,9},{9... | collective-permute-start | bytes 786440 | tf_op jit(solution)/shard_map/ppermute | solution.py:33
  19.7 11.2 %collective-permute-start.2 = (bf16[2,128,512]{2,1,0:T(8,128)(2,1)S(1)}, bf16[2,128,512]{2,1,0:T(8,128)(2,1)S(1)}, u32[]{:S(2)}, u32[]{:S(2)}) collective-permute-start(bf16[2,128,512]{2,1,0:T(8,128)(2,1)S(1)} %get-tuple-element.64), channel_id=1, source_target_pairs={{0,4},{8,16},{16,8},{24,28},{28,24},{20,12},{12,20},{4,0},{1,5},{9... | collective-permute-start | bytes 786440 | tf_op jit(solution)/shard_map/ppermute | solution.py:33
  25.3 9.6 %collective-permute-start.7 = (bf16[2,128,512]{2,1,0:T(8,128)(2,1)S(1)}, bf16[2,128,512]{2,1,0:T(8,128)(2,1)S(1)}, u32[]{:S(2)}, u32[]{:S(2)}) collective-permute-start(bf16[2,128,512]{2,1,0:T(8,128)(2,1)S(1)} %collective-permute-done.4.refs_2_), channel_id=1, source_target_pairs={{0,8},{8,0},{16,24},{24,16},{28,20},{20,28},{12,4},{4,12},{1,9},{9... | collective-permute-start | bytes 786440 | tf_op jit(solution)/shard_map/ppermute | solution.py:33
  27.4 9.2 %collective-permute-start.8 = (bf16[2,128,512]{2,1,0:T(8,128)(2,1)S(1)}, bf16[2,128,512]{2,1,0:T(8,128)(2,1)S(1)}, u32[]{:S(2)}, u32[]{:S(2)}) collective-permute-start(bf16[2,128,512]{2,1,0:T(8,128)(2,1)S(1)} %collective-permute-done.5.refs_0_), channel_id=1, source_target_pairs={{0,4},{8,16},{16,8},{24,28},{28,24},{20,12},{12,20},{4,0},{1,5},{9... | collective-permute-start | bytes 786440 | tf_op jit(solution)/shard_map/ppermute | solution.py:33
  28.9 18.6 %collective-permute-start.11 = (bf16[2,128,512]{2,1,0:T(8,128)(2,1)S(1)}, bf16[2,128,512]{2,1,0:T(8,128)(2,1)S(1)}, u32[]{:S(2)}, u32[]{:S(2)}) collective-permute-start(bf16[2,128,512]{2,1,0:T(8,128)(2,1)S(1)} %collective-permute-done.9.refs_1_), channel_id=1, source_target_pairs={{0,4},{8,16},{16,8},{24,28},{28,24},{20,12},{12,20},{4,0},{1,5},{9... | collective-permute-start | bytes 786440 | tf_op jit(solution)/shard_map/ppermute | solution.py:33
  31.0 9.2 %collective-permute-start.3 = (bf16[2,128,512]{2,1,0:T(8,128)(2,1)S(1)}, bf16[2,128,512]{2,1,0:T(8,128)(2,1)S(1)}, u32[]{:S(2)}, u32[]{:S(2)}) collective-permute-start(bf16[2,128,512]{2,1,0:T(8,128)(2,1)S(1)} %collective-permute-done.2.refs_3_), channel_id=1, source_target_pairs={{0,8},{8,0},{16,24},{24,16},{28,20},{20,28},{12,4},{4,12},{1,9},{9... | collective-permute-start | bytes 786440 | tf_op jit(solution)/shard_map/ppermute | solution.py:33
  36.7 6.6 %collective-permute-start.12 = (bf16[2,128,512]{2,1,0:T(8,128)(2,1)S(1)}, bf16[2,128,512]{2,1,0:T(8,128)(2,1)S(1)}, u32[]{:S(2)}, u32[]{:S(2)}) collective-permute-start(bf16[2,128,512]{2,1,0:T(8,128)(2,1)S(1)} %collective-permute-done.8.refs_1_), channel_id=1, source_target_pairs={{0,8},{8,0},{16,24},{24,16},{28,20},{20,28},{12,4},{4,12},{1,9},{9... | collective-permute-start | bytes 786440 | tf_op jit(solution)/shard_map/ppermute | solution.py:33
  40.2 8.6 %collective-permute-start.10 = (bf16[2,128,512]{2,1,0:T(8,128)(2,1)S(1)}, bf16[2,128,512]{2,1,0:T(8,128)(2,1)S(1)}, u32[]{:S(2)}, u32[]{:S(2)}) collective-permute-start(bf16[2,128,512]{2,1,0:T(8,128)(2,1)S(1)} %collective-permute-done.3.refs_0_), channel_id=1, source_target_pairs={{0,4},{8,16},{16,8},{24,28},{28,24},{20,12},{12,20},{4,0},{1,5},{9... | collective-permute-start | bytes 786440 | tf_op jit(solution)/shard_map/ppermute | solution.py:33
  44.0 1.6 %collective-permute-start.13 = (bf16[128,512]{1,0:T(8,128)(2,1)S(1)}, bf16[128,512]{1,0:T(8,128)(2,1)S(1)}, u32[]{:S(2)}, u32[]{:S(2)}) collective-permute-start(bf16[128,512]{1,0:T(8,128)(2,1)S(1)} %get-tuple-element.48), channel_id=1, source_target_pairs={{0,1},{1,0},{2,3},{3,2},{4,5},{5,4},{6,7},{7,6},{8,9},{9,8},{10,11... | collective-permute-start | bytes 393224 | tf_op jit(solution)/shard_map/ppermute | solution.py:37
  44.1 1.6 %collective-permute-start.14 = (bf16[128,512]{1,0:T(8,128)(2,1)S(1)}, bf16[128,512]{1,0:T(8,128)(2,1)S(1)}, u32[]{:S(2)}, u32[]{:S(2)}) collective-permute-start(bf16[128,512]{1,0:T(8,128)(2,1)S(1)} %get-tuple-element.49), channel_id=1, source_target_pairs={{0,1},{1,0},{2,3},{3,2},{4,5},{5,4},{6,7},{7,6},{8,9},{9,8},{10,11... | collective-permute-start | bytes 393224 | tf_op jit(solution)/shard_map/ppermute | solution.py:37
  45.5 6.2 %collective-permute-start.19 = (bf16[256,512]{1,0:T(8,128)(2,1)S(1)}, bf16[256,512]{1,0:T(8,128)(2,1)S(1)}, u32[]{:S(2)}, u32[]{:S(2)}) collective-permute-start(bf16[256,512]{1,0:T(8,128)(2,1)S(1)} %get-tuple-element.57), channel_id=1, source_target_pairs={{0,1},{1,0},{2,3},{3,2},{4,5},{5,4},{6,7},{7,6},{8,9},{9,8},{10,11... | collective-permute-start | bytes 786440 | tf_op jit(solution)/shard_map/ppermute | solution.py:37
  45.7 8.9 %collective-permute-start.20 = (bf16[256,512]{1,0:T(8,128)(2,1)S(1)}, bf16[256,512]{1,0:T(8,128)(2,1)S(1)}, u32[]{:S(2)}, u32[]{:S(2)}) collective-permute-start(bf16[256,512]{1,0:T(8,128)(2,1)S(1)} %shard_map.71), channel_id=1, source_target_pairs={{0,2},{2,0},{1,3},{3,1},{4,6},{6,4},{5,7},{7,5},{8,10},{10,8},{9,1... | collective-permute-start | bytes 786440 | tf_op jit(solution)/shard_map/ppermute | solution.py:37
  49.6 5.0 %copy-start.4 = (f32[1024]{0:T(1024)S(1)}, f32[1024]{0:T(1024)}, u32[]{:S(2)}) copy-start(f32[1024]{0:T(1024)} %param.10) | copy-start | bytes 12292
  49.6 5.0 %copy-start.5 = (f32[256]{0:T(256)S(1)}, f32[256]{0:T(256)}, u32[]{:S(2)}) copy-start(f32[256]{0:T(256)} %param.9) | copy-start | bytes 3076
  49.6 1.5 %collective-permute-start.16 = (bf16[128,512]{1,0:T(8,128)(2,1)S(1)}, bf16[128,512]{1,0:T(8,128)(2,1)S(1)}, u32[]{:S(2)}, u32[]{:S(2)}) collective-permute-start(bf16[128,512]{1,0:T(8,128)(2,1)S(1)} %get-tuple-element.54), channel_id=1, source_target_pairs={{0,1},{1,0},{2,3},{3,2},{4,5},{5,4},{6,7},{7,6},{8,9},{9,8},{10,11... | collective-permute-start | bytes 393224 | tf_op jit(solution)/shard_map/ppermute | solution.py:37
  49.8 1.4 %collective-permute-start.17 = (bf16[128,512]{1,0:T(8,128)(2,1)S(1)}, bf16[128,512]{1,0:T(8,128)(2,1)S(1)}, u32[]{:S(2)}, u32[]{:S(2)}) collective-permute-start(bf16[128,512]{1,0:T(8,128)(2,1)S(1)} %get-tuple-element.55), channel_id=1, source_target_pairs={{0,1},{1,0},{2,3},{3,2},{4,5},{5,4},{6,7},{7,6},{8,9},{9,8},{10,11... | collective-permute-start | bytes 393224 | tf_op jit(solution)/shard_map/ppermute | solution.py:37
  51.3 8.8 %collective-permute-start.18 = (bf16[256,512]{1,0:T(8,128)(2,1)S(1)}, bf16[256,512]{1,0:T(8,128)(2,1)S(1)}, u32[]{:S(2)}, u32[]{:S(2)}) collective-permute-start(bf16[256,512]{1,0:T(8,128)(2,1)S(1)} %shard_map.75), channel_id=1, source_target_pairs={{0,2},{2,0},{1,3},{3,1},{4,6},{6,4},{5,7},{7,5},{8,10},{10,8},{9,1... | collective-permute-start | bytes 786440 | tf_op jit(solution)/shard_map/ppermute | solution.py:37
  51.6 8.4 %collective-permute-start.15 = (bf16[256,512]{1,0:T(8,128)(2,1)S(1)}, bf16[256,512]{1,0:T(8,128)(2,1)S(1)}, u32[]{:S(2)}, u32[]{:S(2)}) collective-permute-start(bf16[256,512]{1,0:T(8,128)(2,1)S(1)} %get-tuple-element.52), channel_id=1, source_target_pairs={{0,1},{1,0},{2,3},{3,2},{4,5},{5,4},{6,7},{7,6},{8,9},{9,8},{10,11... | collective-permute-start | bytes 786440 | tf_op jit(solution)/shard_map/ppermute | solution.py:37
